TPU v7x, 32 devices: a whole 2x2x4 slice. The times are simulated.
32 devices in a mesh: groups: 2 (over x), experts: 16 (over z, y, core).
Axes of the slice: x: 2, y: 2, z: 4, core: 2. Of those that a mesh axis runs over, the one named last changes fastest.
Arguments:
- queries: bfloat16 [128, 576, 64], P(('groups', 'experts')), parts along dimension 0, may hold values from -21 to 21
- cache: bfloat16 [128, 576, 4096], P(('groups', 'experts')), parts along dimension 0, may hold values from -6 to 6
- cache_len: int32 [128], P(('groups', 'experts')), parts along dimension 0, may hold values from 2 to 4096, as said below
- residual_in: bfloat16 [128, 7168], P(('groups', 'experts')), parts along dimension 0, may hold values from -24 to 24
- w_absorb: bfloat16 [64, 512, 128], P('experts'), may hold values from -0.5 to 0.5
- w_out: bfloat16 [8192, 7168], P('experts'), may hold values from -0.0625 to 0.0625
- norm_gain: float32 [7168], replicated, may hold values from 0.1 to 1.9
- expert_ids: int32 [128, 2], P('groups'), parts along dimension 0, may hold values from 0 to 1, as said below
- route_gates: float32 [128, 2], P(('groups', 'experts')), parts along dimension 0, may hold values from 0.3 to 1.5
- w_gate: bfloat16 [7168, 4096], P(None, 'experts'), may hold values from -0.0625 to 0.0625
- w_up: bfloat16 [7168, 4096], P(None, 'experts'), may hold values from -0.0625 to 0.0625
- w_down: bfloat16 [4096, 7168], P('experts'), may hold values from -0.125 to 0.125
Outputs:
- attended: bfloat16 [128, 7168], P(('groups', 'experts')), parts along dimension 0
- expert_out: bfloat16 [128, 7168], P(('groups', 'experts')), parts along dimension 0
There are 2 independent parts, one for each index of `groups`. A program takes and returns all parts, laid end to end along the dimension named above; an argument that names none is the same for every part. Nothing has to cross between parts.
Inputs may be any that keep to these rules, and one draw needn't show every extreme that they name: `expert_ids`: each row names 2 different experts; one expert, the same for all rows of a draw, is named by every row. `cache_len`: some request has exactly 4096 valid positions.
All inputs are finite; a program needn't handle non-finite values.
Results may differ from a plain program's by a relative error of at most 0.0097.
Values may be sent and summed in bfloat16 or wider, within the bound.
No kernel may reach another device: no remote copies, remote signals or barrier semaphores. Data moves between devices by JAX's collectives and lax.ppermute only.
A program may use at most 128 MiB of HBM per device.

v0:
```python
import jax
import jax.numpy as jnp
from jax import lax
from jax.sharding import PartitionSpec as P

QK = 192
FF = 2048


def rms_scale(stream, norm_gain):
    widened = stream.astype(jnp.float32)
    inverse = lax.rsqrt(jnp.mean(widened * widened, axis=-1, keepdims=True) + 1e-06)
    return (widened * inverse * norm_gain).astype(jnp.bfloat16)


def shards(
    queries,
    cache,
    cache_len,
    residual_in,
    w_absorb,
    w_out,
    norm_gain,
    expert_ids,
    route_gates,
    w_gate,
    w_up,
    w_down,
):
    devices = lax.axis_size("experts")
    rank_here = lax.axis_index("experts")
    own_rows = queries.shape[0]
    all_rows = expert_ids.shape[0]
    latent_rank = w_absorb.shape[1]
    width = residual_in.shape[1]
    split_ways = FF // w_gate.shape[1]
    experts_held = devices // split_ways
    positions = lax.broadcasted_iota(jnp.int32, (1, 1, cache.shape[2]), 2)
    scores = jnp.einsum(
        "rch,rcp->rhp", queries, cache, preferred_element_type=jnp.float32
    ) * QK ** (-0.5)
    scores = jnp.where(positions < cache_len[:, None, None], scores, -jnp.inf)
    soft_w = jax.nn.softmax(scores, axis=-1).astype(jnp.bfloat16)
    latent = jnp.einsum(
        "rhp,rcp->rhc", soft_w, cache[:, :latent_rank, :], preferred_element_type=jnp.float32
    ).astype(jnp.bfloat16)
    by_head = lax.all_to_all(latent, "experts", split_axis=1, concat_axis=0, tiled=True)
    own_ids = lax.dynamic_slice_in_dim(expert_ids, rank_here * own_rows, own_rows, 0)
    expert_iota = jnp.arange(experts_held, dtype=jnp.int32)
    matches = (own_ids[:, :, None] == expert_iota[None, None, :]).astype(jnp.float32)
    head_values = jnp.einsum(
        "rhc,hcv->rhv", by_head, w_absorb, preferred_element_type=jnp.float32
    ).astype(jnp.bfloat16)
    head_term = jnp.dot(
        head_values.reshape(all_rows, -1), w_out, preferred_element_type=jnp.float32
    )
    own_part = lax.dynamic_update_slice_in_dim(
        jnp.zeros_like(head_term), residual_in.astype(jnp.float32), rank_here * own_rows, 0
    )
    summed = lax.psum(head_term + own_part, "experts")
    attended_all = summed.astype(jnp.bfloat16)
    attended = lax.dynamic_slice_in_dim(attended_all, rank_here * own_rows, own_rows, 0)
    normed_all = rms_scale(attended_all, norm_gain)
    expert_here = rank_here // split_ways
    chosen = jnp.any(expert_ids == expert_here, axis=1).astype(jnp.bfloat16)
    incoming = (normed_all * chosen[:, None]).reshape(devices, own_rows, width)
    flattened = incoming.reshape(-1, incoming.shape[-1])
    gate_proj = jnp.dot(flattened, w_gate, preferred_element_type=jnp.float32)
    up_proj = jnp.dot(flattened, w_up, preferred_element_type=jnp.float32)
    activated = (jax.nn.silu(gate_proj) * up_proj).astype(jnp.bfloat16)
    partials = jnp.dot(activated, w_down, preferred_element_type=jnp.float32).reshape(
        incoming.shape
    )
    returned = lax.all_to_all(partials, "experts", split_axis=0, concat_axis=0, tiled=True)
    gathered = returned.reshape(experts_held, split_ways, own_rows, width).sum(axis=1)
    mixing = jnp.sum(route_gates[:, :, None] * matches, axis=1)
    expert_out = jnp.sum(mixing.T[:, :, None] * gathered, axis=0)
    return (attended, expert_out.astype(jnp.bfloat16))


def solution(mesh):
    placed = (
        P(("groups", "experts"), None, None),
        P(("groups", "experts"), None, None),
        P(("groups", "experts")),
        P(("groups", "experts"), None),
        P("experts", None, None),
        P("experts", None),
        P(),
        P("groups", None),
        P(("groups", "experts"), None),
        P(None, "experts"),
        P(None, "experts"),
        P("experts", None),
    )
    return jax.shard_map(
        shards,
        mesh=mesh,
        in_specs=placed,
        out_specs=(P(("groups", "experts"), None), P(("groups", "experts"), None)),
        check_vma=False,
    )
```

profile of v0, /device:TPU:13, one launch (start us, length us, event | category | flops | bytes accessed | tf_op | source)
XLA Modules:
  0.0 177.8 jit_solution(17029793138728281451)
XLA Ops:
  0.6 0.0 copy-start
  0.6 0.8 iota_compare_fusion
  1.4 12.6 %fusion.32 = (f32[4,64]{1,0:T(4,128)S(1)}, f32[4,64,4096]{2,1,0:T(8,128)}) fusion(bf16[4,576,64]{1,2,0:T(8,128)(2,1)} %param.12, bf16[4,576,4096]{2,1,0:T(8,128)(2,1)} %param.13, pred[4,4096]{1,0:T(4,128)(4,1)S(1)} %iota_compare_fusion), kind=kOutput, calls=%fused_computation.43 | convolution fusion | flops 1212157952 | bytes 23380992 | tf_op jit(solution)/shard_map/sub | solution.py:43
  14.1 12.3 %fusion.10 = bf16[4,64,512]{2,1,0:T(8,128)(2,1)S(1)} fusion(bf16[4,576,4096]{2,1,0:T(8,128)(2,1)} %param.13, f32[4,64,4096]{2,1,0:T(8,128)} %get-tuple-element.3, f32[4,64]{1,0:T(4,128)S(1)} %get-tuple-element.2), kind=kOutput, calls=%fused_computation.15 | convolution fusion | flops 1075970048 | bytes 21234688 | tf_op jit(solution)/shard_map/rhp,rcp->rhc/dot_general | solution.py:44
  26.4 0.9 copy.29
  27.3 6.6 %all-to-all-start = ((bf16[4,64,512]{2,0,1:T(4,128)(2,1)}), bf16[4,64,512]{2,0,1:T(4,128)(2,1)S(1)}, u32[]{:S(2)}, u32[]{:S(2)}) async-start(bf16[4,64,512]{2,0,1:T(4,128)(2,1)} %copy.29), calls=%async_computation | async-start | bytes 524288 | tf_op jit(solution)/shard_map/all_to_all | solution.py:47
  33.9 7.9 %all-to-all-done = bf16[4,64,512]{2,0,1:T(4,128)(2,1)S(1)} async-done(((bf16[4,64,512]{2,0,1:T(4,128)(2,1)}), bf16[4,64,512]{2,0,1:T(4,128)(2,1)S(1)}, u32[]{:S(2)}, u32[]{:S(2)}) %all-to-all-start) | async-done | bytes 262176 | tf_op jit(solution)/shard_map/all_to_all | solution.py:47
  41.8 0.1 copy.38
  41.9 0.1 all_to_all.19
  42.0 0.2 fusion.13
  42.2 4.5 %fusion.17 = f32[64,7168]{1,0:T(8,128)S(1)} fusion(bf16[512,7168]{1,0:T(8,128)(2,1)} %param.17, bf16[4,8,8,128]{3,2,1,0:T(8,128)(2,1)S(1)} %fusion.13), kind=kOutput, calls=%fused_computation.25 | convolution fusion | flops 469762048 | bytes 9240576 | tf_op jit(solution)/shard_map/dot_general | solution.py:54
  46.7 0.1 add_dynamic-update-slice_fusion
  46.8 58.5 %all-reduce.1 = bf16[64,7168]{1,0:T(8,128)(2,1)S(1)} all-reduce(f32[64,7168]{1,0:T(8,128)S(1)} %add_dynamic-update-slice_fusion), channel_id=1, replica_groups=mesh['groups'=2,'experts'=16] {'experts'}, use_global_device_ids=true, to_apply=%region_2.3 | all-reduce | flops 458752 | bytes 2752512 | tf_op jit(solution)/shard_map/psum | solution.py:60
  105.2 0.3 fusion.7
  105.5 2.8 %fusion.30 = f32[64,256]{1,0:T(8,128)S(1)} fusion(bf16[7168,256]{1,0:T(8,128)(2,1)} %param.21, bf16[64,7168]{1,0:T(8,128)(2,1)S(1)} %all-reduce.1, f32[7168]{0:T(1024)S(1)} %copy-done.1, f32[64]{0:T(128)S(1)} %add_rsqrt_fusion, bf16[64]{0:T(256)(128)(2,1)S(1)} %convert_element_type.46), kind=kOutput, calls=%fused_computation.42 | convolution fusion | flops 237174784 | bytes 4682112 | tf_op jit(solution)/shard_map/dot_general | solution.py:68
  108.4 5.5 %fusion.15 = f32[64,7168]{1,0:T(8,128)S(1)} fusion(bf16[256,7168]{1,0:T(8,128)(2,1)} %param.23, bf16[7168,256]{1,0:T(8,128)(2,1)} %param.22, f32[64,256]{1,0:T(8,128)S(1)} %fusion.30, bf16[64,7168]{1,0:T(8,128)(2,1)S(1)} %all-reduce.1, f32[7168]{0:T(1024)S(1)} %copy-done.1, f32[64]{0:T(128)S(1)} %add_rsqrt_fusion, bf16[64]{0:T(256)(128)(2,1)S(1)} %convert_element_type.46), kind=kOutput, calls=%fused_computation.20 | convolution fusion | flops 472154112 | bytes 10187136 | tf_op jit(solution)/shard_map/dot_general | solution.py:71
  113.9 0.0 copy-start.4
  113.9 1.8 %reshape.52 = f32[16,4,7168]{2,1,0:T(4,128)} reshape(f32[64,7168]{1,0:T(8,128)S(1)} %fusion.15) | data formatting | bytes 3670016 | tf_op jit(solution)/shard_map/reshape | solution.py:71
  115.7 19.4 %all-to-all-start.1 = ((f32[16,4,7168]{2,1,0:T(4,128)}), f32[16,4,7168]{2,1,0:T(4,128)S(1)}, u32[]{:S(2)}, u32[]{:S(2)}) async-start(f32[16,4,7168]{2,1,0:T(4,128)} %reshape.52), calls=%async_computation.1 | async-start | bytes 3670016 | tf_op jit(solution)/shard_map/all_to_all | solution.py:74
  135.1 0.1 constant_dynamic-slice_fusion
  135.2 0.7 constant_dynamic-slice_fusion.1
  135.8 41.1 %all-to-all-done.1 = f32[16,4,7168]{2,1,0:T(4,128)S(1)} async-done(((f32[16,4,7168]{2,1,0:T(4,128)}), f32[16,4,7168]{2,1,0:T(4,128)S(1)}, u32[]{:S(2)}, u32[]{:S(2)}) %all-to-all-start.1) | async-done | bytes 1835040 | tf_op jit(solution)/shard_map/all_to_all | solution.py:74
  176.9 0.2 bitcast_reduce_fusion
  177.1 0.7 multiply_reduce_fusion
  (12 shorter events, 0.1 us)
Async XLA Ops:
  0.6 41.3 %copy-start = (bf16[4,512,128]{2,1,0:T(8,128)(2,1)S(1)}, bf16[4,512,128]{2,1,0:T(8,128)(2,1)}, u32[]{:S(2)}) copy-start(bf16[4,512,128]{2,1,0:T(8,128)(2,1)} %param.16) | copy-start | bytes 1572868
  14.1 19.7 %copy-start.3 = (s32[64,2]{0,1:T(2,128)S(1)}, s32[64,2]{0,1:T(2,128)}, u32[]{:S(2)}) copy-start(s32[64,2]{0,1:T(2,128)} %param.19) | copy-start | bytes 1540
  27.3 14.5 %all-to-all-start = ((bf16[4,64,512]{2,0,1:T(4,128)(2,1)}), bf16[4,64,512]{2,0,1:T(4,128)(2,1)S(1)}, u32[]{:S(2)}, u32[]{:S(2)}) async-start(bf16[4,64,512]{2,0,1:T(4,128)(2,1)} %copy.29), calls=%async_computation | async-start | bytes 524288 | tf_op jit(solution)/shard_map/all_to_all | solution.py:47
  42.2 4.5 %copy-start.2 = (bf16[4,7168]{1,0:T(4,128)(2,1)S(1)}, bf16[4,7168]{1,0:T(4,128)(2,1)}, u32[]{:S(2)}) copy-start(bf16[4,7168]{1,0:T(4,128)(2,1)} %param.15) | copy-start | bytes 172036
  46.7 58.8 %copy-start.1 = (f32[7168]{0:T(1024)S(1)}, f32[7168]{0:T(1024)}, u32[]{:S(2)}) copy-start(f32[7168]{0:T(1024)} %param.18) | copy-start | bytes 86020
  113.9 21.3 %copy-start.4 = (f32[4,2]{0,1:T(2,128)S(1)}, f32[4,2]{0,1:T(2,128)}, u32[]{:S(2)}) copy-start(f32[4,2]{0,1:T(2,128)} %param.20) | copy-start | bytes 100
  115.7 61.2 %all-to-all-start.1 = ((f32[16,4,7168]{2,1,0:T(4,128)}), f32[16,4,7168]{2,1,0:T(4,128)S(1)}, u32[]{:S(2)}, u32[]{:S(2)}) async-start(f32[16,4,7168]{2,1,0:T(4,128)} %reshape.52), calls=%async_computation.1 | async-start | bytes 3670016 | tf_op jit(solution)/shard_map/all_to_all | solution.py:74
where the time goes:
time: 178 us
  blocking collectives  58.5 us (33%)
  waiting for transfers between devices  49 us (28%)
  matrix products  38 us (21%)
  starting transfers between devices  25.9 us (15%)
  local copies, waits for them, and re-layouts  3.62 us (2%)
  other arithmetic  2.15 us (1%)
    psum x1, blocking collectives, shards(): summed = lax.psum(head_term + own_part, 'experts')  58.5 us
    all_to_all x1, waiting for transfers between devices, shards(): lax.all_to_all(partials, 'experts', split_axis=0, concat_axis=0, tiled=True)  41.1 us
    all_to_all x1, starting transfers between devices, shards(): lax.all_to_all(partials, 'experts', split_axis=0, concat_axis=0, tiled=True)  19.4 us
    sub x1, matrix products, shards(): soft_w = jax.nn.softmax(scores, axis=-1).astype(jnp.bfloat16)  12.6 us
    dot_general x1, matrix products, shards(): jnp.einsum('rhp,rcp->rhc', soft_w, cache[:, :latent_rank, :], preferred_e...  12.3 us
    all_to_all x1, waiting for transfers between devices, shards(): lax.all_to_all(latent, 'experts', split_axis=1, concat_axis=0, tiled=True)  7.92 us
    all_to_all x1, starting transfers between devices, shards(): lax.all_to_all(latent, 'experts', split_axis=1, concat_axis=0, tiled=True)  6.56 us
    dot_general x1, matrix products, shards(): jnp.dot(activated, w_down, preferred_element_type=jnp.float32)  5.5 us
  transfers between devices with their start and end apart: 2, of which 2 were waited for; matrix products, arithmetic and copies ran while one was open for 0% of the time, Pallas kernels for 0%

commit v1 on v0

v1 whole, which is shorter than its diff:
```python
import jax
import jax.numpy as jnp
from jax import lax
from jax.sharding import PartitionSpec as P

QK = 192
FF = 2048


def rms_scale(stream, norm_gain):
    widened = stream.astype(jnp.float32)
    inverse = lax.rsqrt(jnp.mean(widened * widened, axis=-1, keepdims=True) + 1e-06)
    return (widened * inverse * norm_gain).astype(jnp.bfloat16)


def shards(
    queries,
    cache,
    cache_len,
    residual_in,
    w_absorb,
    w_out,
    norm_gain,
    expert_ids,
    route_gates,
    w_gate,
    w_up,
    w_down,
):
    devices = lax.axis_size("experts")
    rank_here = lax.axis_index("experts")
    own_rows = queries.shape[0]
    all_rows = expert_ids.shape[0]
    latent_rank = w_absorb.shape[1]
    width = residual_in.shape[1]
    split_ways = FF // w_gate.shape[1]
    gates_all = lax.all_gather(route_gates, "experts", axis=0, tiled=True)
    expert_here = rank_here // split_ways
    mixing = jnp.sum(
        gates_all * (expert_ids == expert_here).astype(jnp.float32), axis=1, keepdims=True
    )
    positions = lax.broadcasted_iota(jnp.int32, (1, 1, cache.shape[2]), 2)
    scores = jnp.einsum(
        "rch,rcp->rhp", queries, cache, preferred_element_type=jnp.float32
    ) * QK ** (-0.5)
    scores = jnp.where(positions < cache_len[:, None, None], scores, -jnp.inf)
    soft_w = jax.nn.softmax(scores, axis=-1).astype(jnp.bfloat16)
    latent = jnp.einsum(
        "rhp,rcp->rhc", soft_w, cache[:, :latent_rank, :], preferred_element_type=jnp.float32
    ).astype(jnp.bfloat16)
    by_head = lax.all_to_all(latent, "experts", split_axis=1, concat_axis=0, tiled=True)
    head_values = jnp.einsum(
        "rhc,hcv->rhv", by_head, w_absorb, preferred_element_type=jnp.float32
    ).astype(jnp.bfloat16)
    head_term = jnp.dot(
        head_values.reshape(all_rows, -1), w_out, preferred_element_type=jnp.float32
    ).astype(jnp.bfloat16)
    terms = lax.all_to_all(
        head_term.reshape(devices, own_rows, width), "experts", split_axis=0, concat_axis=0, tiled=True
    )
    summed = jnp.sum(terms.astype(jnp.float32), axis=0)
    attended = (residual_in.astype(jnp.float32) + summed).astype(jnp.bfloat16)
    attended_all = lax.all_gather(attended, "experts", axis=0, tiled=True)
    normed_all = rms_scale(attended_all, norm_gain)
    gate_proj = jnp.dot(normed_all, w_gate, preferred_element_type=jnp.float32)
    up_proj = jnp.dot(normed_all, w_up, preferred_element_type=jnp.float32)
    activated = (jax.nn.silu(gate_proj) * up_proj).astype(jnp.bfloat16)
    partials = jnp.dot(activated, w_down, preferred_element_type=jnp.float32)
    sent = (partials * mixing).astype(jnp.bfloat16).reshape(devices, own_rows, width)
    returned = lax.all_to_all(sent, "experts", split_axis=0, concat_axis=0, tiled=True)
    expert_out = jnp.sum(returned.astype(jnp.float32), axis=0)
    return (attended, expert_out.astype(jnp.bfloat16))


def solution(mesh):
    placed = (
        P(("groups", "experts"), None, None),
        P(("groups", "experts"), None, None),
        P(("groups", "experts")),
        P(("groups", "experts"), None),
        P("experts", None, None),
        P("experts", None),
        P(),
        P("groups", None),
        P(("groups", "experts"), None),
        P(None, "experts"),
        P(None, "experts"),
        P("experts", None),
    )
    return jax.shard_map(
        shards,
        mesh=mesh,
        in_specs=placed,
        out_specs=(P(("groups", "experts"), None), P(("groups", "experts"), None)),
        check_vma=False,
    )
```

time: 178 us -> 145 us (0.81)
  the two profiles are of different devices: /device:TPU:13 before, /device:TPU:0 now
where the time goes in v1:
time: 145 us; the launch traced here: 144 us
  blocking collectives  97.2 us (67%)
  matrix products  38 us (26%)
  starting transfers between devices  3.63 us (3%)
  other arithmetic  2.5 us (2%)
  local copies, waits for them, and re-layouts  2.21 us (2%)
    all_gather x1, blocking collectives, shards(): gates_all = lax.all_gather(route_gates, 'experts', axis=0, tiled=True)  31.1 us
    all_to_all x1, blocking collectives, shards(): lax.all_to_all(sent, 'experts', split_axis=0, concat_axis=0, tiled=True)  25.1 us
    all_gather x1, blocking collectives, shards(): attended_all = lax.all_gather(attended, 'experts', axis=0, tiled=True)  23.7 us
    all_to_all x1, blocking collectives, shards(): lax.all_to_all(latent, 'experts', split_axis=1, concat_axis=0, tiled=True)  17.2 us
    sub x1, matrix products, shards(): soft_w = jax.nn.softmax(scores, axis=-1).astype(jnp.bfloat16)  12.6 us
    dot_general x1, matrix products, shards(): jnp.einsum('rhp,rcp->rhc', soft_w, cache[:, :latent_rank, :], preferred_e...  12.3 us
    dot_general x1, matrix products, shards(): partials = jnp.dot(activated, w_down, preferred_element_type=jnp.float32)  5.5 us
    dot_general x1, matrix products, shards(): jnp.dot(head_values.reshape(all_rows, -1), w_out, preferred_element_type=...  4.51 us
  transfers between devices with their start and end apart: 1, of which 0 were waited for; matrix products, arithmetic and copies ran while one was open for 0% of the time, Pallas kernels for 0%

profile of v1, /device:TPU:0, one launch (start us, length us, event | category | flops | bytes accessed | tf_op | source)
XLA Modules:
  0.0 144.3 jit_solution(1132271093405454406)
XLA Ops:
  0.6 0.0 copy-start
  0.6 0.8 iota_compare_fusion
  1.4 12.6 %fusion.24 = (f32[4,64]{1,0:T(4,128)S(1)}, f32[4,64,4096]{2,1,0:T(8,128)}) fusion(bf16[4,576,64]{1,2,0:T(8,128)(2,1)} %param.12, bf16[4,576,4096]{2,1,0:T(8,128)(2,1)} %param.13, pred[4,4096]{1,0:T(4,128)(4,1)S(1)} %iota_compare_fusion), kind=kOutput, calls=%fused_computation.36 | convolution fusion | flops 1212157952 | bytes 23380992 | tf_op jit(solution)/shard_map/sub | solution.py:47
  14.1 12.3 %fusion.8 = bf16[4,64,512]{2,1,0:T(8,128)(2,1)S(1)} fusion(bf16[4,576,4096]{2,1,0:T(8,128)(2,1)} %param.13, f32[4,64,4096]{2,1,0:T(8,128)} %get-tuple-element.3, f32[4,64]{1,0:T(4,128)S(1)} %get-tuple-element.2), kind=kOutput, calls=%fused_computation.15 | convolution fusion | flops 1075970048 | bytes 21234688 | tf_op jit(solution)/shard_map/rhp,rcp->rhc/dot_general | solution.py:48
  26.4 0.2 copy.19
  26.6 17.2 %all_to_all.28 = bf16[4,64,512]{2,0,1:T(4,128)(2,1)S(1)} all-to-all(bf16[4,64,512]{2,0,1:T(4,128)(2,1)S(1)} %copy.19), channel_id=1, replica_groups=mesh['groups'=2,'experts'=16] {'experts'}, dimensions={1} | all-to-all | bytes 524288 | tf_op jit(solution)/shard_map/all_to_all | solution.py:51
  43.8 0.1 copy.29
  43.9 0.1 all_to_all.22
  44.0 0.2 fusion.11
  44.2 4.5 %convolution_convert_fusion = bf16[64,7168]{1,0:T(8,128)(2,1)S(1)} fusion(bf16[512,7168]{1,0:T(8,128)(2,1)} %param.17, bf16[4,8,8,128]{3,2,1,0:T(8,128)(2,1)S(1)} %fusion.11), kind=kOutput, calls=%fused_computation.4 | convolution fusion | flops 470220800 | bytes 8323072 | tf_op jit(solution)/shard_map/dot_general | solution.py:55
  48.8 1.3 reshape.47
  50.0 3.6 %all-to-all-start.1 = ((bf16[16,4,7168]{2,1,0:T(4,128)(2,1)}), bf16[16,4,7168]{2,1,0:T(4,128)(2,1)S(1)}, u32[]{:S(2)}, u32[]{:S(2)}) async-start(bf16[16,4,7168]{2,1,0:T(4,128)(2,1)} %reshape.47), calls=%async_computation.1 | async-start | bytes 1835008 | tf_op jit(solution)/shard_map/all_to_all | solution.py:58
  53.7 31.1 %all-gather.1 = f32[16,4,2]{1,2,0:T(2,128)S(1)} all-gather(f32[1,4,2]{1,2,0:T(2,128)S(1)} %bitcast.27), channel_id=1, replica_groups=mesh['groups'=2,'experts'=16] {'experts'}, dimensions={0}, use_global_device_ids=true | all-gather | bytes 544 | tf_op jit(solution)/shard_map/all_gather | solution.py:37
  84.8 0.1 reshape.52
  85.0 0.4 convert_reduce_fusion
  85.4 0.0 copy-start.1
  85.4 23.7 %all-gather = bf16[16,4,7168]{2,1,0:T(4,128)(2,1)S(1)} all-gather(bf16[1,4,7168]{2,1,0:T(4,128)(2,1)S(1)} %bitcast.26), channel_id=1, replica_groups=mesh['groups'=2,'experts'=16] {'experts'}, dimensions={0}, use_global_device_ids=true | all-gather | bytes 974848 | tf_op jit(solution)/shard_map/all_gather | solution.py:63
  109.1 0.1 reshape.53
  109.2 0.2 multiply_reduce_fusion
  109.5 2.8 %fusion.23 = f32[64,256]{1,0:T(8,128)S(1)} fusion(bf16[7168,256]{1,0:T(8,128)(2,1)} %param.21, f32[64,7168]{1,0:T(8,128)S(1)} %reshape.53, f32[7168]{0:T(1024)S(1)} %copy-done.2, f32[64]{0:T(128)S(1)} %add_rsqrt_fusion), kind=kOutput, calls=%fused_computation.35 | convolution fusion | flops 236257280 | bytes 5599488 | tf_op jit(solution)/shard_map/dot_general | solution.py:65
  112.3 5.5 %fusion.3 = bf16[64,7168]{1,0:T(8,128)(2,1)S(1)} fusion(bf16[256,7168]{1,0:T(8,128)(2,1)} %param.23, bf16[7168,256]{1,0:T(8,128)(2,1)} %param.22, f32[64]{0:T(128)S(1)} %fusion.21, f32[64,256]{1,0:T(8,128)S(1)} %fusion.23, f32[64,7168]{1,0:T(8,128)S(1)} %reshape.53, f32[7168]{0:T(1024)S(1)} %copy-done.2, f32[64]{0:T(128)S(1)} %add_rsqrt_fusion), kind=kOutput, calls=%fused_computation.5 | convolution fusion | flops 472154112 | bytes 10187264 | tf_op jit(solution)/shard_map/dot_general | solution.py:68
  117.8 0.3 reshape.48
  118.2 25.1 %all_to_all.29 = bf16[16,4,7168]{2,1,0:T(4,128)(2,1)S(1)} all-to-all(bf16[16,4,7168]{2,1,0:T(4,128)(2,1)S(1)} %reshape.48), channel_id=1, replica_groups=mesh['groups'=2,'experts'=16] {'experts'}, dimensions={0} | all-to-all | bytes 1835008 | tf_op jit(solution)/shard_map/all_to_all | solution.py:70
  143.3 1.0 reduce_sum.52
  (15 shorter events, 0.1 us)
Async XLA Ops:
  0.6 43.3 %copy-start = (bf16[4,512,128]{2,1,0:T(8,128)(2,1)S(1)}, bf16[4,512,128]{2,1,0:T(8,128)(2,1)}, u32[]{:S(2)}) copy-start(bf16[4,512,128]{2,1,0:T(8,128)(2,1)} %param.16) | copy-start | bytes 1572868
  48.7 5.0 %copy-start.4 = (f32[4,2]{0,1:T(2,128)S(1)}, f32[4,2]{0,1:T(2,128)}, u32[]{:S(2)}) copy-start(f32[4,2]{0,1:T(2,128)} %param.20) | copy-start | bytes 100
  48.7 36.2 %copy-start.5 = (s32[64,2]{0,1:T(2,128)S(1)}, s32[64,2]{0,1:T(2,128)}, u32[]{:S(2)}) copy-start(s32[64,2]{0,1:T(2,128)} %param.19) | copy-start | bytes 1540
  48.7 36.6 %copy-start.3 = (bf16[4,7168]{1,0:T(4,128)(2,1)S(1)}, bf16[4,7168]{1,0:T(4,128)(2,1)}, u32[]{:S(2)}) copy-start(bf16[4,7168]{1,0:T(4,128)(2,1)} %param.15) | copy-start | bytes 172036
  50.0 35.0 %all-to-all-start.1 = ((bf16[16,4,7168]{2,1,0:T(4,128)(2,1)}), bf16[16,4,7168]{2,1,0:T(4,128)(2,1)S(1)}, u32[]{:S(2)}, u32[]{:S(2)}) async-start(bf16[16,4,7168]{2,1,0:T(4,128)(2,1)} %reshape.47), calls=%async_computation.1 | async-start | bytes 1835008 | tf_op jit(solution)/shard_map/all_to_all | solution.py:58
  53.7 55.8 %copy-start.2 = (f32[7168]{0:T(1024)S(1)}, f32[7168]{0:T(1024)}, u32[]{:S(2)}) copy-start(f32[7168]{0:T(1024)} %param.18) | copy-start | bytes 86020
  85.4 26.9 %copy-start.1 = (bf16[4,7168]{1,0:T(4,128)(2,1)}, bf16[4,7168]{1,0:T(4,128)(2,1)S(1)}, u32[]{:S(2)}) copy-start(bf16[4,7168]{1,0:T(4,128)(2,1)S(1)} %add_convert_fusion) | copy-start | bytes 172036

commit v2 on v1

v2 whole, which is shorter than its diff:
```python
import jax
import jax.numpy as jnp
from jax import lax
from jax.experimental import pallas as pl
from jax.experimental.pallas import tpu as pltpu
from jax.sharding import PartitionSpec as P

QK = 192
FF = 2048
BLOCK = 512
LANES = 128


def attend_kernel(
    len_ref, queries_ref, cache_ref, latent_ref, held, scores, summed, arrived
):
    own_rows, _, heads = queries_ref.shape
    rank = latent_ref.shape[2]

    def block_copy(row, block):
        return pltpu.make_async_copy(
            cache_ref.at[row, :, pl.ds(pl.multiple_of(block * BLOCK, BLOCK), BLOCK)],
            held.at[row, block],
            arrived.at[row, block],
        )

    counts = [(len_ref[row] + BLOCK - 1) // BLOCK for row in range(own_rows)]
    for row in range(own_rows):

        def begin(block, _, row=row):
            block_copy(row, block).start()
            return 0

        lax.fori_loop(0, counts[row], begin, 0)
    for row in range(own_rows):
        length = len_ref[row]
        query = queries_ref[row].T
        column = lax.broadcasted_iota(jnp.int32, (heads, BLOCK), 1)

        def score(block, highest, row=row, length=length, query=query):
            block_copy(row, block).wait()
            found = jnp.dot(
                query, held[row, block], preferred_element_type=jnp.float32
            ) * QK ** (-0.5)
            found = jnp.where(column + block * BLOCK < length, found, -jnp.inf)
            scores[block] = found
            for at in range(0, BLOCK, LANES):
                highest = jnp.maximum(highest, found[:, at : at + LANES])
            return highest

        highest = lax.fori_loop(
            0, counts[row], score, jnp.full((heads, LANES), -jnp.inf, jnp.float32)
        )
        highest = jnp.max(highest, axis=1, keepdims=True)
        summed[...] = jnp.zeros_like(summed)

        def weigh(block, total, row=row, highest=highest):
            weight = jnp.exp(scores[block] - highest)
            summed[...] += lax.dot_general(
                weight.astype(jnp.bfloat16),
                held[row, block, :rank, :],
                (((1,), (1,)), ((), ())),
                preferred_element_type=jnp.float32,
            )
            for at in range(0, BLOCK, LANES):
                total = total + weight[:, at : at + LANES]
            return total

        total = lax.fori_loop(
            0, counts[row], weigh, jnp.zeros((heads, LANES), jnp.float32)
        )
        total = jnp.sum(total, axis=1, keepdims=True)
        latent_ref[row] = (summed[...] / total).astype(latent_ref.dtype)


def attend(queries, cache, cache_len, rank):
    own_rows, depth, heads = queries.shape
    blocks = cache.shape[2] // BLOCK
    return pl.pallas_call(
        attend_kernel,
        out_shape=jax.ShapeDtypeStruct((own_rows, heads, rank), jnp.bfloat16),
        in_specs=[
            pl.BlockSpec(memory_space=pltpu.SMEM),
            pl.BlockSpec(memory_space=pltpu.VMEM),
            pl.BlockSpec(memory_space=pl.ANY),
        ],
        out_specs=pl.BlockSpec(memory_space=pltpu.VMEM),
        scratch_shapes=[
            pltpu.VMEM((own_rows, blocks, depth, BLOCK), jnp.bfloat16),
            pltpu.VMEM((blocks, heads, BLOCK), jnp.float32),
            pltpu.VMEM((heads, rank), jnp.float32),
            pltpu.SemaphoreType.DMA((own_rows, blocks)),
        ],
        compiler_params=pltpu.CompilerParams(vmem_limit_bytes=32 * 2**20),
        cost_estimate=pl.CostEstimate(
            flops=2 * own_rows * heads * cache.shape[2] * (depth + rank),
            bytes_accessed=2 * cache.size,
            transcendentals=own_rows * heads * cache.shape[2],
        ),
        name="attend",
    )(cache_len, queries, cache)


def swap(array, distance):
    pairs = [(at, at ^ distance) for at in range(lax.axis_size("experts"))]
    return lax.ppermute(array, "experts", pairs)


def add(ours, theirs):
    return (ours.astype(jnp.float32) + theirs.astype(jnp.float32)).astype(jnp.bfloat16)


def shards(
    queries,
    cache,
    cache_len,
    residual_in,
    w_absorb,
    w_out,
    norm_gain,
    expert_ids,
    route_gates,
    w_gate,
    w_up,
    w_down,
):
    devices = lax.axis_size("experts")
    rank_here = lax.axis_index("experts")
    own_rows = queries.shape[0]
    all_rows = expert_ids.shape[0]
    half, quarter = all_rows // 2, all_rows // 4
    far = devices // 4
    split_ways = FF // w_gate.shape[1]

    latent = attend(queries, cache, cache_len, w_absorb.shape[1])
    by_head = lax.all_to_all(latent, "experts", split_axis=1, concat_axis=0, tiled=True)
    head_values = jnp.einsum(
        "rhc,hcv->rhv", by_head, w_absorb, preferred_element_type=jnp.float32
    ).astype(jnp.bfloat16)
    slot = jnp.arange(all_rows, dtype=jnp.int32) // own_rows
    distance = slot // (2 * far) + slot // far % 2 * 2 + slot % far * 4
    source = (rank_here ^ distance) * own_rows + jnp.arange(all_rows) % own_rows
    order = (source[:, None] == jnp.arange(all_rows)[None, :]).astype(jnp.bfloat16)
    relative = jnp.dot(
        order, head_values.reshape(all_rows, -1), preferred_element_type=jnp.float32
    ).astype(jnp.bfloat16)

    term = jnp.dot(relative, w_out, preferred_element_type=jnp.float32).astype(jnp.bfloat16)
    term = add(term[:half], swap(term[half:], 1))
    term = add(term[:quarter], swap(term[quarter:], 2))
    blocks = [term[at * own_rows : (at + 1) * own_rows] for at in range(far)]
    blocks = [blocks[0]] + [swap(blocks[at], 4 * at) for at in range(1, far)]
    attention = sum(block.astype(jnp.float32) for block in blocks)
    attended = (residual_in.astype(jnp.float32) + attention).astype(jnp.bfloat16)
    widened = attended.astype(jnp.float32)
    inverse = lax.rsqrt(jnp.mean(widened * widened, axis=-1, keepdims=True) + 1e-06)
    normed = (widened * inverse * norm_gain).astype(jnp.bfloat16)

    normed = jnp.concatenate([normed] + [swap(normed, 4 * at) for at in range(1, far)])
    normed = jnp.concatenate([normed, swap(normed, 2)])
    normed = jnp.concatenate([normed, swap(normed, 1)])
    gate_proj = jnp.dot(normed, w_gate, preferred_element_type=jnp.float32)
    up_proj = jnp.dot(normed, w_up, preferred_element_type=jnp.float32)
    activated = (jax.nn.silu(gate_proj) * up_proj).astype(jnp.bfloat16)
    term = jnp.dot(activated, w_down, preferred_element_type=jnp.float32).astype(jnp.bfloat16)

    term = add(term[:half], swap(term[half:], 1))
    own_ids = lax.dynamic_slice_in_dim(expert_ids, rank_here * own_rows, own_rows, 0)
    expert_out = 0.0
    for at in range(devices // 2):
        block = term[at * own_rows : (at + 1) * own_rows]
        distance = at // far * 2 + at % far * 4
        block = swap(block, distance) if distance else block
        expert = (rank_here ^ distance) // split_ways
        mixing = jnp.sum(
            route_gates * (own_ids == expert).astype(jnp.float32), axis=1, keepdims=True
        )
        expert_out = expert_out + mixing * block.astype(jnp.float32)
    return (attended, expert_out.astype(jnp.bfloat16))


def solution(mesh):
    placed = (
        P(("groups", "experts"), None, None),
        P(("groups", "experts"), None, None),
        P(("groups", "experts")),
        P(("groups", "experts"), None),
        P("experts", None, None),
        P("experts", None),
        P(),
        P("groups", None),
        P(("groups", "experts"), None),
        P(None, "experts"),
        P(None, "experts"),
        P("experts", None),
    )
    return jax.shard_map(
        shards,
        mesh=mesh,
        in_specs=placed,
        out_specs=(P(("groups", "experts"), None), P(("groups", "experts"), None)),
        check_vma=False,
    )
```

time: 145 us -> 105 us (0.72)
  blocking collectives: 97.2 us -> 0 us
  waiting for transfers between devices: 0.01 us -> 40.3 us
  starting transfers between devices: 3.63 us -> 31.6 us
  matrix products: 38 us -> 13.1 us
  local copies, waits for them, and re-layouts: 2.21 us -> 10.4 us
  Pallas kernels: 0 us -> 6.67 us
    all_gather x2 -> x0, blocking collectives: 54.8 us -> none  [the longest x1 31.1 us: shards(): gates_all = lax.all_gather(route_gates, 'experts', axis=0, tiled=True)]
    all_to_all x2 -> x0, blocking collectives: 42.4 us -> none  [the longest x1 25.1 us: shards(): lax.all_to_all(sent, 'experts', split_axis=0, concat_axis=0, tiled=True)]
    ppermute x0 -> x18, waiting for transfers between devices: none -> 30.3 us  [swap(): return lax.ppermute(array, 'experts', pairs)]
    ppermute x0 -> x18, starting transfers between devices: none -> 21.1 us  [swap(): return lax.ppermute(array, 'experts', pairs)]
    sub x1 -> x0, matrix products: 12.6 us -> none  [shards(): soft_w = jax.nn.softmax(scores, axis=-1).astype(jnp.bfloat16)]
    dot_general x4 -> x3, matrix products: 25.1 us -> 12.8 us  [the longest x1 5.46 us: shards(): jnp.dot(activated, w_down, preferred_element_type=jnp.float32)]
    all_to_all x1, waiting for transfers between devices: 0.01 us -> 10 us  [shards(): lax.all_to_all(latent, 'experts', split_axis=1, concat_axis=0, tiled=True)]
    unnamed x13 -> x17, local copies, waits for them, and re-layouts: 0.13 us -> 8.38 us
  transfers between devices with their start and end apart: 1 -> 19, of which waited for: 0 -> 13; matrix products, arithmetic and copies ran while one was open for 0% -> 0% of each run, Pallas kernels for 0% -> 0%
where the time goes in v2:
time: 105 us
  waiting for transfers between devices  40.3 us (38%)
  starting transfers between devices  31.6 us (30%)
  matrix products  13.1 us (12%)
  local copies, waits for them, and re-layouts  10.4 us (10%)
  Pallas kernels  6.67 us (6%)
  other arithmetic  1.72 us (2%)
    ppermute x18, waiting for transfers between devices, swap(): return lax.ppermute(array, 'experts', pairs)  30.3 us
    ppermute x18, starting transfers between devices, swap(): return lax.ppermute(array, 'experts', pairs)  21.1 us
    all_to_all x1, starting transfers between devices, shards(): lax.all_to_all(latent, 'experts', split_axis=1, concat_axis=0, tiled=True)  10.5 us
    all_to_all x1, waiting for transfers between devices, shards(): lax.all_to_all(latent, 'experts', split_axis=1, concat_axis=0, tiled=True)  10 us
    unnamed x17, local copies, waits for them, and re-layouts  8.38 us
    pallas_call x1, Pallas kernels, attend(): pl.pallas_call(attend_kernel, out_shape=jax.ShapeDtypeStruct((own_rows, h...  6.67 us
    dot_general x1, matrix products, shards(): jnp.dot(activated, w_down, preferred_element_type=jnp.float32)  5.46 us
    dot_general x1, matrix products, shards(): jnp.dot(relative, w_out, preferred_element_type=jnp.float32)  4.64 us
  transfers between devices with their start and end apart: 19, of which 13 were waited for; matrix products, arithmetic and copies ran while one was open for 0% of the time, Pallas kernels for 0%

profile of v2, /device:TPU:0, one launch (start us, length us, event | category | flops | bytes accessed | tf_op | source)
XLA Modules:
  0.0 104.7 jit_solution(5615511520290464760)
XLA Ops:
  0.6 1.3 %copy.19.queries_ref = bf16[4,576,64]{2,1,0:T(8,128)(2,1)S(1)} copy(bf16[4,576,64]{1,2,0:T(8,128)(2,1)} %param.12) | data formatting | bytes 589824 | tf_op args[0]
  2.0 6.4 %copy-done.1 = bf16[4,576,4096]{2,1,0:T(8,128)(2,1)S(1)} copy-done((bf16[4,576,4096]{2,1,0:T(8,128)(2,1)S(1)}, bf16[4,576,4096]{2,1,0:T(8,128)(2,1)}, u32[]{:S(2)}) %copy-start.1) | copy-done | bytes 18874392
  9.0 6.7 %attend.1 = bf16[4,64,512]{2,1,0:T(8,128)(2,1)S(1)} custom-call(s32[4]{0:T(128)S(1)} %copy-done.2, bf16[4,576,64]{2,1,0:T(8,128)(2,1)S(1)} %copy.19.queries_ref, bf16[4,576,4096]{2,1,0:T(8,128)(2,1)S(1)} %copy-done.1), custom_call_target="tpu_custom_call" | custom-call | flops 2281701376 | bytes 18874368 | tf_op jit(solution)/shard_map/attend/pallas_call | solution.py:79
  16.6 10.5 %all-to-all-start = ((bf16[4,64,512]{2,0,1:T(4,128)(2,1)}), bf16[4,64,512]{2,0,1:T(4,128)(2,1)S(1)}, u32[]{:S(2)}, u32[]{:S(2)}) async-start(bf16[4,64,512]{2,0,1:T(4,128)(2,1)} %copy.20), calls=%async_computation | async-start | bytes 524288 | tf_op jit(solution)/shard_map/all_to_all | solution.py:136
  27.1 10.0 %all-to-all-done = bf16[4,64,512]{2,0,1:T(4,128)(2,1)S(1)} async-done(((bf16[4,64,512]{2,0,1:T(4,128)(2,1)}), bf16[4,64,512]{2,0,1:T(4,128)(2,1)S(1)}, u32[]{:S(2)}, u32[]{:S(2)}) %all-to-all-start) | async-done | bytes 262176 | tf_op jit(solution)/shard_map/all_to_all | solution.py:136
  37.5 4.6 %convolution_convert_fusion = bf16[64,7168]{1,0:T(8,128)(2,1)S(1)} fusion(bf16[512,7168]{1,0:T(8,128)(2,1)} %param.17, bf16[4,8,8,128]{3,2,1,0:T(8,128)(2,1)S(1)} %fusion, s32[64]{0:T(128)S(1)} %fusion.19), kind=kOutput, calls=%fused_computation | convolution fusion | flops 474451968 | bytes 8323328 | tf_op jit(solution)/shard_map/dot_general | solution.py:148
  42.3 1.8 %collective-permute-done = bf16[32,7168]{1,0:T(8,128)(2,1)S(1)} collective-permute-done((bf16[32,7168]{1,0:T(8,128)(2,1)S(1)}, bf16[32,7168]{1,0:T(8,128)(2,1)S(1)}, u32[]{:S(2)}, u32[]{:S(2)}) %collective-permute-start) | collective-permute-done | bytes 458784 | tf_op jit(solution)/shard_map/ppermute | solution.py:106
  44.5 7.5 %collective-permute-done.1 = bf16[16,7168]{1,0:T(8,128)(2,1)S(1)} collective-permute-done((bf16[16,7168]{1,0:T(8,128)(2,1)S(1)}, bf16[16,7168]{1,0:T(8,128)(2,1)S(1)}, u32[]{:S(2)}, u32[]{:S(2)}) %collective-permute-start.1) | collective-permute-done | bytes 229408 | tf_op jit(solution)/shard_map/ppermute | solution.py:106
  53.9 2.6 %collective-permute-start.4 = (bf16[4,7168]{1,0:T(4,128)(2,1)S(1)}, bf16[4,7168]{1,0:T(4,128)(2,1)S(1)}, u32[]{:S(2)}, u32[]{:S(2)}) collective-permute-start(bf16[4,7168]{1,0:T(4,128)(2,1)S(1)} %get-tuple-element.20), channel_id=1, source_target_pairs={{0,12},{1,13},{2,14},{3,15},{4,8},{5,9},{6,10},{7,11},{8,4},{9,5},... | collective-permute-start | bytes 172040 | tf_op jit(solution)/shard_map/ppermute | solution.py:106
  56.7 2.5 %collective-permute-done.3 = bf16[4,7168]{1,0:T(4,128)(2,1)S(1)} collective-permute-done((bf16[4,7168]{1,0:T(4,128)(2,1)S(1)}, bf16[4,7168]{1,0:T(4,128)(2,1)S(1)}, u32[]{:S(2)}, u32[]{:S(2)}) %collective-permute-start.3) | collective-permute-done | bytes 57376 | tf_op jit(solution)/shard_map/ppermute | solution.py:106
  61.4 2.1 %collective-permute-start.6 = (bf16[4,7168]{1,0:T(4,128)(2,1)S(1)}, bf16[4,7168]{1,0:T(4,128)(2,1)S(1)}, u32[]{:S(2)}, u32[]{:S(2)}) collective-permute-start(bf16[4,7168]{1,0:T(4,128)(2,1)S(1)} %fusion.3), channel_id=1, source_target_pairs={{0,8},{1,9},{2,10},{3,11},{4,12},{5,13},{6,14},{7,15},{8,0},{9,1},... | collective-permute-start | bytes 172040 | tf_op jit(solution)/shard_map/ppermute | solution.py:106
  63.5 1.3 %collective-permute-start.7 = (bf16[4,7168]{1,0:T(4,128)(2,1)S(1)}, bf16[4,7168]{1,0:T(4,128)(2,1)S(1)}, u32[]{:S(2)}, u32[]{:S(2)}) collective-permute-start(bf16[4,7168]{1,0:T(4,128)(2,1)S(1)} %fusion.3), channel_id=1, source_target_pairs={{0,12},{1,13},{2,14},{3,15},{4,8},{5,9},{6,10},{7,11},{8,4},{9,5},... | collective-permute-start | bytes 172040 | tf_op jit(solution)/shard_map/ppermute | solution.py:106
  64.8 2.3 %collective-permute-done.6 = bf16[4,7168]{1,0:T(4,128)(2,1)S(1)} collective-permute-done((bf16[4,7168]{1,0:T(4,128)(2,1)S(1)}, bf16[4,7168]{1,0:T(4,128)(2,1)S(1)}, u32[]{:S(2)}, u32[]{:S(2)}) %collective-permute-start.6) | collective-permute-done | bytes 57376 | tf_op jit(solution)/shard_map/ppermute | solution.py:106
  67.1 2.4 %collective-permute-done.7 = bf16[4,7168]{1,0:T(4,128)(2,1)S(1)} collective-permute-done((bf16[4,7168]{1,0:T(4,128)(2,1)S(1)}, bf16[4,7168]{1,0:T(4,128)(2,1)S(1)}, u32[]{:S(2)}, u32[]{:S(2)}) %collective-permute-start.7) | collective-permute-done | bytes 57376 | tf_op jit(solution)/shard_map/ppermute | solution.py:106
  70.1 5.6 %collective-permute-done.8 = bf16[16,7168]{1,0:T(8,128)(2,1)S(1)} collective-permute-done((bf16[16,7168]{1,0:T(8,128)(2,1)S(1)}, bf16[16,7168]{1,0:T(8,128)(2,1)S(1)}, u32[]{:S(2)}, u32[]{:S(2)}) %collective-permute-start.8) | collective-permute-done | bytes 229408 | tf_op jit(solution)/shard_map/ppermute | solution.py:106
  76.0 1.8 %collective-permute-done.9 = bf16[32,7168]{1,0:T(8,128)(2,1)S(1)} collective-permute-done((bf16[32,7168]{1,0:T(8,128)(2,1)S(1)}, bf16[32,7168]{1,0:T(8,128)(2,1)S(1)}, u32[]{:S(2)}, u32[]{:S(2)}) %collective-permute-start.9) | collective-permute-done | bytes 458784 | tf_op jit(solution)/shard_map/ppermute | solution.py:106
  78.2 2.8 %fusion.30 = f32[64,256]{1,0:T(8,128)S(1)} fusion(bf16[64,7168]{1,0:T(8,128)(2,1)S(1)} %concatenate.13, bf16[7168,256]{1,0:T(8,128)(2,1)} %param.21), kind=kOutput, calls=%fused_computation.67 | convolution fusion | flops 234881024 | bytes 4653056 | tf_op jit(solution)/shard_map/dot_general | solution.py:162
  81.0 5.5 %convolution_convert_fusion.1 = bf16[64,7168]{1,0:T(8,128)(2,1)S(1)} fusion(bf16[256,7168]{1,0:T(8,128)(2,1)} %param.23, f32[64,256]{1,0:T(8,128)S(1)} %fusion.30, bf16[64,7168]{1,0:T(8,128)(2,1)S(1)} %concatenate.13, bf16[7168,256]{1,0:T(8,128)(2,1)} %param.22), kind=kOutput, calls=%fused_computation.1 | convolution fusion | flops 470319104 | bytes 9240576 | tf_op jit(solution)/shard_map/dot_general | solution.py:165
  86.7 1.7 %collective-permute-done.10 = bf16[32,7168]{1,0:T(8,128)(2,1)S(1)} collective-permute-done((bf16[32,7168]{1,0:T(8,128)(2,1)S(1)}, bf16[32,7168]{1,0:T(8,128)(2,1)S(1)}, u32[]{:S(2)}, u32[]{:S(2)}) %collective-permute-start.10) | collective-permute-done | bytes 458784 | tf_op jit(solution)/shard_map/ppermute | solution.py:106
  88.8 1.9 %collective-permute-start.12 = (bf16[4,7168]{1,0:T(4,128)(2,1)S(1)}, bf16[4,7168]{1,0:T(4,128)(2,1)S(1)}, u32[]{:S(2)}, u32[]{:S(2)}) collective-permute-start(bf16[4,7168]{1,0:T(4,128)(2,1)S(1)} %get-tuple-element.18), channel_id=1, source_target_pairs={{0,8},{1,9},{2,10},{3,11},{4,12},{5,13},{6,14},{7,15},{8,0},{9,1},... | collective-permute-start | bytes 172040 | tf_op jit(solution)/shard_map/ppermute | solution.py:106
  90.6 2.5 %collective-permute-start.13 = (bf16[4,7168]{1,0:T(4,128)(2,1)S(1)}, bf16[4,7168]{1,0:T(4,128)(2,1)S(1)}, u32[]{:S(2)}, u32[]{:S(2)}) collective-permute-start(bf16[4,7168]{1,0:T(4,128)(2,1)S(1)} %get-tuple-element.17), channel_id=1, source_target_pairs={{0,12},{1,13},{2,14},{3,15},{4,8},{5,9},{6,10},{7,11},{8,4},{9,5},... | collective-permute-start | bytes 172040 | tf_op jit(solution)/shard_map/ppermute | solution.py:106
  93.8 3.1 %collective-permute-start.16 = (bf16[4,7168]{1,0:T(4,128)(2,1)S(1)}, bf16[4,7168]{1,0:T(4,128)(2,1)S(1)}, u32[]{:S(2)}, u32[]{:S(2)}) collective-permute-start(bf16[4,7168]{1,0:T(4,128)(2,1)S(1)} %get-tuple-element.14), channel_id=1, source_target_pairs={{0,10},{1,11},{2,8},{3,9},{4,14},{5,15},{6,12},{7,13},{8,2},{9,3},... | collective-permute-start | bytes 172040 | tf_op jit(solution)/shard_map/ppermute | solution.py:106
  96.9 3.0 %collective-permute-start.17 = (bf16[4,7168]{1,0:T(4,128)(2,1)S(1)}, bf16[4,7168]{1,0:T(4,128)(2,1)S(1)}, u32[]{:S(2)}, u32[]{:S(2)}) collective-permute-start(bf16[4,7168]{1,0:T(4,128)(2,1)S(1)} %get-tuple-element.13), channel_id=1, source_target_pairs={{0,14},{1,15},{2,12},{3,13},{4,10},{5,11},{6,8},{7,9},{8,6},{9,7},... | collective-permute-start | bytes 172040 | tf_op jit(solution)/shard_map/ppermute | solution.py:106
  100.4 3.4 %collective-permute-done.17 = bf16[4,7168]{1,0:T(4,128)(2,1)S(1)} collective-permute-done((bf16[4,7168]{1,0:T(4,128)(2,1)S(1)}, bf16[4,7168]{1,0:T(4,128)(2,1)S(1)}, u32[]{:S(2)}, u32[]{:S(2)}) %collective-permute-start.17) | collective-permute-done | bytes 57376 | tf_op jit(solution)/shard_map/ppermute | solution.py:106
  (56 shorter events, 10.6 us)
Async XLA Ops:
  0.6 36.6 %copy-start = (bf16[4,512,128]{2,1,0:T(8,128)(2,1)S(1)}, bf16[4,512,128]{2,1,0:T(8,128)(2,1)}, u32[]{:S(2)}) copy-start(bf16[4,512,128]{2,1,0:T(8,128)(2,1)} %param.16) | copy-start | bytes 1572868
  16.6 20.5 %all-to-all-start = ((bf16[4,64,512]{2,0,1:T(4,128)(2,1)}), bf16[4,64,512]{2,0,1:T(4,128)(2,1)S(1)}, u32[]{:S(2)}, u32[]{:S(2)}) async-start(bf16[4,64,512]{2,0,1:T(4,128)(2,1)} %copy.20), calls=%async_computation | async-start | bytes 524288 | tf_op jit(solution)/shard_map/all_to_all | solution.py:136
  42.2 18.1 %copy-start.5 = (f32[7168]{0:T(1024)S(1)}, f32[7168]{0:T(1024)}, u32[]{:S(2)}) copy-start(f32[7168]{0:T(1024)} %param.18) | copy-start | bytes 86020
  42.2 1.9 %collective-permute-start = (bf16[32,7168]{1,0:T(8,128)(2,1)S(1)}, bf16[32,7168]{1,0:T(8,128)(2,1)S(1)}, u32[]{:S(2)}, u32[]{:S(2)}) collective-permute-start(bf16[32,7168]{1,0:T(8,128)(2,1)S(1)} %slice.73), channel_id=1, source_target_pairs={{0,1},{1,0},{2,3},{3,2},{4,5},{5,4},{6,7},{7,6},{8,9},{9,8},{10,11... | collective-permute-start | bytes 1376264 | tf_op jit(solution)/shard_map/ppermute | solution.py:106
  44.2 7.7 %collective-permute-start.1 = (bf16[16,7168]{1,0:T(8,128)(2,1)S(1)}, bf16[16,7168]{1,0:T(8,128)(2,1)S(1)}, u32[]{:S(2)}, u32[]{:S(2)}) collective-permute-start(bf16[16,7168]{1,0:T(8,128)(2,1)S(1)} %slice.75), channel_id=1, source_target_pairs={{0,2},{1,3},{2,0},{3,1},{4,6},{5,7},{6,4},{7,5},{8,10},{9,11},{10,... | collective-permute-start | bytes 688136 | tf_op jit(solution)/shard_map/ppermute | solution.py:106
  52.1 4.6 %collective-permute-start.2 = (bf16[4,7168]{1,0:T(4,128)(2,1)S(1)}, bf16[4,7168]{1,0:T(4,128)(2,1)S(1)}, u32[]{:S(2)}, u32[]{:S(2)}) collective-permute-start(bf16[4,7168]{1,0:T(4,128)(2,1)S(1)} %get-tuple-element.19), channel_id=1, source_target_pairs={{0,4},{1,5},{2,6},{3,7},{4,0},{5,1},{6,2},{7,3},{8,12},{9,13},{10,... | collective-permute-start | bytes 172040 | tf_op jit(solution)/shard_map/ppermute | solution.py:106
  52.7 6.5 %collective-permute-start.3 = (bf16[4,7168]{1,0:T(4,128)(2,1)S(1)}, bf16[4,7168]{1,0:T(4,128)(2,1)S(1)}, u32[]{:S(2)}, u32[]{:S(2)}) collective-permute-start(bf16[4,7168]{1,0:T(4,128)(2,1)S(1)} %get-tuple-element.21), channel_id=1, source_target_pairs={{0,8},{1,9},{2,10},{3,11},{4,12},{5,13},{6,14},{7,15},{8,0},{9,1},... | collective-permute-start | bytes 172040 | tf_op jit(solution)/shard_map/ppermute | solution.py:106
  53.9 6.1 %collective-permute-start.4 = (bf16[4,7168]{1,0:T(4,128)(2,1)S(1)}, bf16[4,7168]{1,0:T(4,128)(2,1)S(1)}, u32[]{:S(2)}, u32[]{:S(2)}) collective-permute-start(bf16[4,7168]{1,0:T(4,128)(2,1)S(1)} %get-tuple-element.20), channel_id=1, source_target_pairs={{0,12},{1,13},{2,14},{3,15},{4,8},{5,9},{6,10},{7,11},{8,4},{9,5},... | collective-permute-start | bytes 172040 | tf_op jit(solution)/shard_map/ppermute | solution.py:106
  60.2 20.8 %copy-start.3 = (bf16[4,7168]{1,0:T(4,128)(2,1)}, bf16[4,7168]{1,0:T(4,128)(2,1)S(1)}, u32[]{:S(2)}) copy-start(bf16[4,7168]{1,0:T(4,128)(2,1)S(1)} %get-tuple-element.11) | copy-start | bytes 172036
  60.4 4.5 %collective-permute-start.5 = (bf16[4,7168]{1,0:T(4,128)(2,1)S(1)}, bf16[4,7168]{1,0:T(4,128)(2,1)S(1)}, u32[]{:S(2)}, u32[]{:S(2)}) collective-permute-start(bf16[4,7168]{1,0:T(4,128)(2,1)S(1)} %fusion.3), channel_id=1, source_target_pairs={{0,4},{1,5},{2,6},{3,7},{4,0},{5,1},{6,2},{7,3},{8,12},{9,13},{10,... | collective-permute-start | bytes 172040 | tf_op jit(solution)/shard_map/ppermute | solution.py:106
  61.4 5.7 %collective-permute-start.6 = (bf16[4,7168]{1,0:T(4,128)(2,1)S(1)}, bf16[4,7168]{1,0:T(4,128)(2,1)S(1)}, u32[]{:S(2)}, u32[]{:S(2)}) collective-permute-start(bf16[4,7168]{1,0:T(4,128)(2,1)S(1)} %fusion.3), channel_id=1, source_target_pairs={{0,8},{1,9},{2,10},{3,11},{4,12},{5,13},{6,14},{7,15},{8,0},{9,1},... | collective-permute-start | bytes 172040 | tf_op jit(solution)/shard_map/ppermute | solution.py:106
  63.5 6.0 %collective-permute-start.7 = (bf16[4,7168]{1,0:T(4,128)(2,1)S(1)}, bf16[4,7168]{1,0:T(4,128)(2,1)S(1)}, u32[]{:S(2)}, u32[]{:S(2)}) collective-permute-start(bf16[4,7168]{1,0:T(4,128)(2,1)S(1)} %fusion.3), channel_id=1, source_target_pairs={{0,12},{1,13},{2,14},{3,15},{4,8},{5,9},{6,10},{7,11},{8,4},{9,5},... | collective-permute-start | bytes 172040 | tf_op jit(solution)/shard_map/ppermute | solution.py:106
  69.6 6.1 %collective-permute-start.8 = (bf16[16,7168]{1,0:T(8,128)(2,1)S(1)}, bf16[16,7168]{1,0:T(8,128)(2,1)S(1)}, u32[]{:S(2)}, u32[]{:S(2)}) collective-permute-start(bf16[16,7168]{1,0:T(8,128)(2,1)S(1)} %pad_maximum_fusion), channel_id=1, source_target_pairs={{0,2},{1,3},{2,0},{3,1},{4,6},{5,7},{6,4},{7,5},{8,10},{9,11},{10,... | collective-permute-start | bytes 688136 | tf_op jit(solution)/shard_map/ppermute | solution.py:106
  76.0 1.9 %collective-permute-start.9 = (bf16[32,7168]{1,0:T(8,128)(2,1)S(1)}, bf16[32,7168]{1,0:T(8,128)(2,1)S(1)}, u32[]{:S(2)}, u32[]{:S(2)}) collective-permute-start(bf16[32,7168]{1,0:T(8,128)(2,1)S(1)} %concatenate.12), channel_id=1, source_target_pairs={{0,1},{1,0},{2,3},{3,2},{4,5},{5,4},{6,7},{7,6},{8,9},{9,8},{10,11... | collective-permute-start | bytes 1376264 | tf_op jit(solution)/shard_map/ppermute | solution.py:106
  81.0 18.9 %copy-start.6 = (f32[4,2]{0,1:T(2,128)S(1)}, f32[4,2]{0,1:T(2,128)}, u32[]{:S(2)}) copy-start(f32[4,2]{0,1:T(2,128)} %param.20) | copy-start | bytes 100
  81.0 18.9 %copy-start.7 = (s32[64,2]{0,1:T(2,128)S(1)}, s32[64,2]{0,1:T(2,128)}, u32[]{:S(2)}) copy-start(s32[64,2]{0,1:T(2,128)} %param.19) | copy-start | bytes 1540
  86.5 1.9 %collective-permute-start.10 = (bf16[32,7168]{1,0:T(8,128)(2,1)S(1)}, bf16[32,7168]{1,0:T(8,128)(2,1)S(1)}, u32[]{:S(2)}, u32[]{:S(2)}) collective-permute-start(bf16[32,7168]{1,0:T(8,128)(2,1)S(1)} %slice.81), channel_id=1, source_target_pairs={{0,1},{1,0},{2,3},{3,2},{4,5},{5,4},{6,7},{7,6},{8,9},{9,8},{10,11... | collective-permute-start | bytes 1376264 | tf_op jit(solution)/shard_map/ppermute | solution.py:106
  88.7 5.1 %collective-permute-start.11 = (bf16[4,7168]{1,0:T(4,128)(2,1)S(1)}, bf16[4,7168]{1,0:T(4,128)(2,1)S(1)}, u32[]{:S(2)}, u32[]{:S(2)}) collective-permute-start(bf16[4,7168]{1,0:T(4,128)(2,1)S(1)} %get-tuple-element.12), channel_id=1, source_target_pairs={{0,4},{1,5},{2,6},{3,7},{4,0},{5,1},{6,2},{7,3},{8,12},{9,13},{10,... | collective-permute-start | bytes 172040 | tf_op jit(solution)/shard_map/ppermute | solution.py:106
  88.8 8.2 %collective-permute-start.12 = (bf16[4,7168]{1,0:T(4,128)(2,1)S(1)}, bf16[4,7168]{1,0:T(4,128)(2,1)S(1)}, u32[]{:S(2)}, u32[]{:S(2)}) collective-permute-start(bf16[4,7168]{1,0:T(4,128)(2,1)S(1)} %get-tuple-element.18), channel_id=1, source_target_pairs={{0,8},{1,9},{2,10},{3,11},{4,12},{5,13},{6,14},{7,15},{8,0},{9,1},... | collective-permute-start | bytes 172040 | tf_op jit(solution)/shard_map/ppermute | solution.py:106
  90.6 9.4 %collective-permute-start.13 = (bf16[4,7168]{1,0:T(4,128)(2,1)S(1)}, bf16[4,7168]{1,0:T(4,128)(2,1)S(1)}, u32[]{:S(2)}, u32[]{:S(2)}) collective-permute-start(bf16[4,7168]{1,0:T(4,128)(2,1)S(1)} %get-tuple-element.17), channel_id=1, source_target_pairs={{0,12},{1,13},{2,14},{3,15},{4,8},{5,9},{6,10},{7,11},{8,4},{9,5},... | collective-permute-start | bytes 172040 | tf_op jit(solution)/shard_map/ppermute | solution.py:106
  93.1 6.9 %collective-permute-start.14 = (bf16[4,7168]{1,0:T(4,128)(2,1)S(1)}, bf16[4,7168]{1,0:T(4,128)(2,1)S(1)}, u32[]{:S(2)}, u32[]{:S(2)}) collective-permute-start(bf16[4,7168]{1,0:T(4,128)(2,1)S(1)} %get-tuple-element.16), channel_id=1, source_target_pairs={{0,2},{1,3},{2,0},{3,1},{4,6},{5,7},{6,4},{7,5},{8,10},{9,11},{10,... | collective-permute-start | bytes 172040 | tf_op jit(solution)/shard_map/ppermute | solution.py:106
  93.5 6.5 %collective-permute-start.15 = (bf16[4,7168]{1,0:T(4,128)(2,1)S(1)}, bf16[4,7168]{1,0:T(4,128)(2,1)S(1)}, u32[]{:S(2)}, u32[]{:S(2)}) collective-permute-start(bf16[4,7168]{1,0:T(4,128)(2,1)S(1)} %get-tuple-element.15), channel_id=1, source_target_pairs={{0,6},{1,7},{2,4},{3,5},{4,2},{5,3},{6,0},{7,1},{8,14},{9,15},{10,... | collective-permute-start | bytes 172040 | tf_op jit(solution)/shard_map/ppermute | solution.py:106
  93.8 6.6 %collective-permute-start.16 = (bf16[4,7168]{1,0:T(4,128)(2,1)S(1)}, bf16[4,7168]{1,0:T(4,128)(2,1)S(1)}, u32[]{:S(2)}, u32[]{:S(2)}) collective-permute-start(bf16[4,7168]{1,0:T(4,128)(2,1)S(1)} %get-tuple-element.14), channel_id=1, source_target_pairs={{0,10},{1,11},{2,8},{3,9},{4,14},{5,15},{6,12},{7,13},{8,2},{9,3},... | collective-permute-start | bytes 172040 | tf_op jit(solution)/shard_map/ppermute | solution.py:106
  96.9 6.9 %collective-permute-start.17 = (bf16[4,7168]{1,0:T(4,128)(2,1)S(1)}, bf16[4,7168]{1,0:T(4,128)(2,1)S(1)}, u32[]{:S(2)}, u32[]{:S(2)}) collective-permute-start(bf16[4,7168]{1,0:T(4,128)(2,1)S(1)} %get-tuple-element.13), channel_id=1, source_target_pairs={{0,14},{1,15},{2,12},{3,13},{4,10},{5,11},{6,8},{7,9},{8,6},{9,7},... | collective-permute-start | bytes 172040 | tf_op jit(solution)/shard_map/ppermute | solution.py:106
  (3 other events, 24.9 us)

commit v3 on v2

v3 whole, which is shorter than its diff:
```python
import functools

import jax
import jax.numpy as jnp
from jax import lax
from jax.experimental import pallas as pl
from jax.experimental.pallas import tpu as pltpu
from jax.sharding import PartitionSpec as P

QK = 192
FF = 2048
BLOCK = 512
GROUP = 4
LANES = 128
TILE = 256
MIB = 2**20


def in_groups(count, step):
    whole = count // GROUP

    def body(at, _):
        step(at * GROUP, GROUP)
        return 0

    lax.fori_loop(0, whole, body, 0)
    pl.when((count & 2) != 0)(lambda: step(whole * GROUP, 2))
    pl.when((count & 1) != 0)(lambda: step(count - 1, 1))


def lane_tiles(array):
    return [array[:, at : at + LANES] for at in range(0, array.shape[1], LANES)]


def attend_kernel(
    info_ref,
    queries_ref,
    cache_ref,
    near_ref,
    across_ref,
    held,
    scores,
    highest,
    total,
    summed,
    staged,
    arrived,
):
    own_rows, heads, _ = queries_ref.shape
    devices, _, rank = staged.shape
    own_heads = heads // devices

    def block_copy(row, block):
        return pltpu.make_async_copy(
            cache_ref.at[row, :, pl.ds(pl.multiple_of(block * BLOCK, BLOCK), BLOCK)],
            held.at[row, block],
            arrived.at[row, block],
        )

    counts = [(info_ref[row] + BLOCK - 1) // BLOCK for row in range(own_rows)]
    for row in range(own_rows):

        def begin(block, _, row=row):
            block_copy(row, block).start()
            return 0

        lax.fori_loop(0, counts[row], begin, 0)
    column = lax.broadcasted_iota(jnp.int32, (heads, BLOCK), 1)
    for row in range(own_rows):
        length = info_ref[row]
        query = queries_ref[row]
        highest[...] = jnp.full_like(highest, -jnp.inf)
        total[...] = jnp.zeros_like(total)
        summed[...] = jnp.zeros_like(summed)

        def score(first, many, row=row, length=length, query=query):
            for block in [first + at for at in range(many)]:
                block_copy(row, block).wait()
            tops = []
            for block in [first + at for at in range(many)]:
                found = jnp.dot(
                    query, held[row, block], preferred_element_type=jnp.float32
                ) * QK ** (-0.5)
                found = jnp.where(column + block * BLOCK < length, found, -jnp.inf)
                scores[block] = found
                tops.append(functools.reduce(jnp.maximum, lane_tiles(found)))
            highest[...] = functools.reduce(jnp.maximum, tops, highest[...])

        in_groups(counts[row], score)
        top = jnp.max(highest[...], axis=1, keepdims=True)

        def lift(first, many, top=top):
            sums = []
            for block in [first + at for at in range(many)]:
                weight = jnp.exp(scores[block] - top)
                scores[block] = weight
                sums.append(sum(lane_tiles(weight)))
            total[...] += sum(sums)

        in_groups(counts[row], lift)
        inverse = 1.0 / jnp.sum(total[...], axis=1, keepdims=True)

        def gather(first, many, row=row, inverse=inverse):
            terms = []
            for block in [first + at for at in range(many)]:
                weight = (scores[block] * inverse).astype(jnp.bfloat16)
                terms.append(
                    lax.dot_general(
                        weight,
                        held[row, block, :rank, :],
                        (((1,), (1,)), ((), ())),
                        preferred_element_type=jnp.float32,
                    )
                )
            summed[...] += sum(terms)

        in_groups(counts[row], gather)
        latent = summed[...]
        for device in range(devices):
            staged[device, row * own_heads : (row + 1) * own_heads, :] = latent[
                device * own_heads : (device + 1) * own_heads
            ]
    here = info_ref[own_rows]
    for at in range(devices // 2):
        near_ref[at] = staged[here ^ (2 * at)].astype(near_ref.dtype)
        across_ref[at] = staged[here ^ (2 * at + 1)].astype(across_ref.dtype)


def attend(queries, cache, cache_len, rank_here, devices, rank):
    own_rows, depth, heads = queries.shape
    blocks = cache.shape[2] // BLOCK
    packed = own_rows * heads // devices
    info = jnp.concatenate([cache_len, rank_here.astype(jnp.int32)[None]])
    part = jax.ShapeDtypeStruct((devices // 2, packed, rank), jnp.bfloat16)
    return pl.pallas_call(
        attend_kernel,
        out_shape=(part, part),
        in_specs=[
            pl.BlockSpec(memory_space=pltpu.SMEM),
            pl.BlockSpec(memory_space=pltpu.VMEM),
            pl.BlockSpec(memory_space=pl.ANY),
        ],
        out_specs=(pl.BlockSpec(memory_space=pltpu.VMEM),) * 2,
        scratch_shapes=[
            pltpu.VMEM((own_rows, blocks, depth, BLOCK), jnp.bfloat16),
            pltpu.VMEM((blocks, heads, BLOCK), jnp.float32),
            pltpu.VMEM((heads, LANES), jnp.float32),
            pltpu.VMEM((heads, LANES), jnp.float32),
            pltpu.VMEM((heads, rank), jnp.float32),
            pltpu.VMEM((devices, packed, rank), jnp.float32),
            pltpu.SemaphoreType.DMA((own_rows, blocks)),
        ],
        compiler_params=pltpu.CompilerParams(vmem_limit_bytes=48 * MIB),
        cost_estimate=pl.CostEstimate(
            flops=own_rows * heads * cache.shape[2] * (depth + rank),
            bytes_accessed=cache.size,
            transcendentals=own_rows * heads * cache.shape[2],
        ),
        name="attend",
    )(info, jnp.swapaxes(queries, 1, 2), cache)


def column_copies(source, target, semaphores, parts):
    width = source.shape[1] // parts
    return [
        pltpu.make_async_copy(
            source.at[:, at * width : (at + 1) * width],
            target.at[:, at * width : (at + 1) * width],
            semaphores.at[at],
        )
        for at in range(parts)
    ]


def row_copies(source, target, semaphores, parts):
    depth = source.shape[0] // parts
    return [
        pltpu.make_async_copy(
            source.at[at * depth : (at + 1) * depth, :],
            target.at[at * depth : (at + 1) * depth, :],
            semaphores.at[at],
        )
        for at in range(parts)
    ]


PARTS = 4


def project_kernel(own_rows, far, *refs):
    *pieces, absorb_ref, w_ref, keep_ref, send_ref, joined, held, arrived = refs
    copies = column_copies(w_ref, held, arrived, PARTS)
    for copy in copies:
        copy.start()
    packed = 2 * pieces[0].shape[0]
    joined[0 : packed // 2, :] = pieces[0][...]
    joined[packed // 2 : packed, :] = pieces[1][...]
    for at, piece in enumerate(pieces[2:], 1):
        joined[at * packed : (at + 1) * packed, :] = piece[...]
    own_heads = absorb_ref.shape[0]
    half, width = keep_ref.shape
    rows = 2 * half
    shape = (rows, joined.shape[0])
    row = lax.broadcasted_iota(jnp.int32, shape, 0)
    place = lax.broadcasted_iota(jnp.int32, shape, 1)
    turn = own_rows.bit_length() - 1
    far_bits = far.bit_length() - 1
    request, slot = row & (own_rows - 1), row >> turn
    far_at, slot = slot & (far - 1), slot >> far_bits
    source = (far_at << 3) + ((slot & 1) << 2) + ((slot >> 1 & 1) << 1) + (slot >> 2)
    values = []
    for head in range(own_heads):
        wanted = ((source << turn) + request) * own_heads + head
        choice = (place == wanted).astype(jnp.float32).astype(jnp.bfloat16)
        latent = jnp.dot(choice, joined[...], preferred_element_type=jnp.float32)
        value = jnp.dot(
            latent.astype(jnp.bfloat16), absorb_ref[head], preferred_element_type=jnp.float32
        )
        values.append(value.astype(jnp.bfloat16))
    values = jnp.concatenate(values, axis=1)
    for part in range(PARTS):
        copies[part].wait()
        for at in range(part * width // PARTS, (part + 1) * width // PARTS, TILE):
            term = jnp.dot(values, held[:, at : at + TILE], preferred_element_type=jnp.float32)
            keep_ref[:, at : at + TILE] = term[:half]
            send_ref[:, at : at + TILE] = term[half:].astype(send_ref.dtype)


def project(pieces, w_absorb, w_out, own_rows, rows, far):
    depth, width = w_out.shape
    rank = w_absorb.shape[1]
    joined = sum(piece.shape[0] for piece in pieces)
    return pl.pallas_call(
        functools.partial(project_kernel, own_rows, far),
        out_shape=(
            jax.ShapeDtypeStruct((rows // 2, width), jnp.float32),
            jax.ShapeDtypeStruct((rows // 2, width), jnp.bfloat16),
        ),
        in_specs=[pl.BlockSpec(memory_space=pltpu.VMEM)] * (len(pieces) + 1)
        + [pl.BlockSpec(memory_space=pl.ANY)],
        out_specs=(pl.BlockSpec(memory_space=pltpu.VMEM),) * 2,
        scratch_shapes=[
            pltpu.VMEM((joined, rank), jnp.bfloat16),
            pltpu.VMEM((depth, width), jnp.bfloat16),
            pltpu.SemaphoreType.DMA((PARTS,)),
        ],
        compiler_params=pltpu.CompilerParams(vmem_limit_bytes=24 * MIB),
        cost_estimate=pl.CostEstimate(
            flops=2 * rows * depth * width, bytes_accessed=2 * depth * width, transcendentals=0
        ),
        name="project",
    )(*pieces, w_absorb, w_out)


def expert_kernel(
    far_rows,
    first_own,
    first_other,
    second_own,
    second_other,
    gate_ref,
    up_ref,
    down_ref,
    keep_ref,
    send_ref,
    gate_held,
    up_held,
    down_held,
    gate_arrived,
    up_arrived,
    down_arrived,
):
    gate_copies = row_copies(gate_ref, gate_held, gate_arrived, PARTS)
    up_copies = row_copies(up_ref, up_held, up_arrived, PARTS)
    down_copies = column_copies(down_ref, down_held, down_arrived, PARTS)
    for part in range(PARTS):
        gate_copies[part].start()
        up_copies[part].start()
    for part in range(PARTS):
        down_copies[part].start()
    half, width = keep_ref.shape
    depth = width // PARTS
    side = width // 2

    def arrange(array):
        eighths = [array[at * far_rows : (at + 1) * far_rows] for at in range(8)]
        return jnp.concatenate([eighths[at] for at in (0, 2, 1, 3, 4, 6, 5, 7)], axis=0)

    gates, ups = [], []
    for part in range(PARTS):
        own, other = (
            (first_own, first_other) if part < PARTS // 2 else (second_own, second_other)
        )
        at = part * depth % side
        tokens = jnp.concatenate(
            [own[:, at : at + depth], other[:, at : at + depth]], axis=0
        )
        span = slice(part * depth, (part + 1) * depth)
        gate_copies[part].wait()
        gates.append(jnp.dot(tokens, gate_held[span, :], preferred_element_type=jnp.float32))
        up_copies[part].wait()
        ups.append(jnp.dot(tokens, up_held[span, :], preferred_element_type=jnp.float32))
    middle = PARTS // 2
    gate = sum(gates[:middle]) + arrange(sum(gates[middle:]))
    up = sum(ups[:middle]) + arrange(sum(ups[middle:]))
    active = (gate / (1.0 + jnp.exp(-gate)) * up).astype(jnp.bfloat16)
    for part in range(PARTS):
        down_copies[part].wait()
        for at in range(part * depth, (part + 1) * depth, TILE):
            term = jnp.dot(
                active, down_held[:, at : at + TILE], preferred_element_type=jnp.float32
            )
            keep_ref[:, at : at + TILE] = term[:half]
            send_ref[:, at : at + TILE] = term[half:].astype(send_ref.dtype)


def run_expert(tokens, w_gate, w_up, w_down, far_rows):
    half, side = tokens[0].shape
    width, hidden = w_gate.shape
    return pl.pallas_call(
        functools.partial(expert_kernel, far_rows),
        out_shape=(
            jax.ShapeDtypeStruct((half, width), jnp.float32),
            jax.ShapeDtypeStruct((half, width), jnp.bfloat16),
        ),
        in_specs=[pl.BlockSpec(memory_space=pltpu.VMEM)] * 4
        + [pl.BlockSpec(memory_space=pl.ANY)] * 3,
        out_specs=(pl.BlockSpec(memory_space=pltpu.VMEM),) * 2,
        scratch_shapes=[
            pltpu.VMEM((width, hidden), jnp.bfloat16),
            pltpu.VMEM((width, hidden), jnp.bfloat16),
            pltpu.VMEM((hidden, width), jnp.bfloat16),
            pltpu.SemaphoreType.DMA((PARTS,)),
            pltpu.SemaphoreType.DMA((PARTS,)),
            pltpu.SemaphoreType.DMA((PARTS,)),
        ],
        compiler_params=pltpu.CompilerParams(vmem_limit_bytes=24 * MIB),
        cost_estimate=pl.CostEstimate(
            flops=12 * half * hidden * width,
            bytes_accessed=6 * hidden * width,
            transcendentals=2 * half * hidden,
        ),
        name="expert",
    )(*tokens, w_gate, w_up, w_down)


def swap(array, distance):
    pairs = [(at, at ^ distance) for at in range(lax.axis_size("experts"))]
    return lax.ppermute(array, "experts", pairs)


def join(ours, theirs, distance):
    return ours + swap(theirs.astype(jnp.bfloat16), distance).astype(jnp.float32)


def halve(keep, send, far):
    half, width = keep.shape
    whole = join(keep, send, 1)
    first, second = whole[:, : width // 2], whole[:, width // 2 :]
    second = second.reshape(2, 2, half // 4, width // 2)
    first = join(first[: half // 2], first[half // 2 :], 2)
    second = join(second[:, 0], second[:, 1], 4)
    first = join(first[: half // 4], first[half // 4 :], 4)
    second = join(second[0], second[1], 2)
    own_rows = half // 4 // far
    found = []
    for at in range(far):
        span = slice(at * own_rows, (at + 1) * own_rows)
        if at == 0:
            found.append((first[span], second[span]))
        else:
            found.append(
                tuple(
                    swap(side[span].astype(jnp.bfloat16), 8 * at).astype(jnp.float32)
                    for side in (first, second)
                )
            )
    return found


def shards(
    queries,
    cache,
    cache_len,
    residual_in,
    w_absorb,
    w_out,
    norm_gain,
    expert_ids,
    route_gates,
    w_gate,
    w_up,
    w_down,
):
    devices = lax.axis_size("experts")
    rank_here = lax.axis_index("experts")
    own_rows = queries.shape[0]
    all_rows = expert_ids.shape[0]
    width = residual_in.shape[1]
    far = devices // 8
    split_ways = FF // w_gate.shape[1]
    assert split_ways == 8

    near, across = attend(
        queries, cache, cache_len, rank_here, devices, w_absorb.shape[1]
    )
    other = swap(across, 1)
    pieces = [near[0], other[0]]
    for at in range(1, devices // 2):
        pieces.append(swap(jnp.concatenate([near[at], other[at]]), 2 * at))
    keep, send = project(pieces, w_absorb, w_out, own_rows, all_rows, far)

    found = halve(keep, send, far)
    residual = residual_in.astype(jnp.float32)
    attended = jnp.concatenate(
        [
            residual[:, : width // 2] + sum(one[0] for one in found),
            residual[:, width // 2 :] + sum(one[1] for one in found),
        ],
        axis=1,
    ).astype(jnp.bfloat16)
    widened = attended.astype(jnp.float32)
    inverse = lax.rsqrt(jnp.mean(widened * widened, axis=-1, keepdims=True) + 1e-06)
    normed = (widened * inverse * norm_gain).astype(jnp.bfloat16)

    normed = jnp.concatenate([normed] + [swap(normed, 8 * at) for at in range(1, far)])
    first, second = normed[:, : width // 2], normed[:, width // 2 :]
    first = jnp.concatenate([first, swap(first, 4)])
    second = jnp.concatenate([second, swap(second, 2)])
    first = jnp.concatenate([first, swap(first, 2)])
    second = jnp.concatenate([second, swap(second, 4)])
    tokens = (first, swap(first, 1), second, swap(second, 1))
    keep, send = run_expert(tokens, w_gate, w_up, w_down, far * own_rows)

    found = halve(keep, send, far)
    own_ids = lax.dynamic_slice_in_dim(expert_ids, rank_here * own_rows, own_rows, 0)
    sides = [0.0, 0.0]
    for at, one in enumerate(found):
        expert = (rank_here ^ (8 * at)) // split_ways
        mixing = jnp.sum(
            route_gates * (own_ids == expert).astype(jnp.float32), axis=1, keepdims=True
        )
        sides = [side + mixing * block for side, block in zip(sides, one)]
    expert_out = jnp.concatenate(sides, axis=1)
    return (attended, expert_out.astype(jnp.bfloat16))


def solution(mesh):
    placed = (
        P(("groups", "experts"), None, None),
        P(("groups", "experts"), None, None),
        P(("groups", "experts")),
        P(("groups", "experts"), None),
        P("experts", None, None),
        P("experts", None),
        P(),
        P("groups", None),
        P(("groups", "experts"), None),
        P(None, "experts"),
        P(None, "experts"),
        P("experts", None),
    )
    return jax.shard_map(
        shards,
        mesh=mesh,
        in_specs=placed,
        out_specs=(P(("groups", "experts"), None), P(("groups", "experts"), None)),
        check_vma=False,
    )
```

time: 105 us -> 94.3 us (0.90)
  matrix products: 13.1 us -> 0 us
  Pallas kernels: 6.67 us -> 18.4 us
  local copies, waits for them, and re-layouts: 10.4 us -> 1.41 us
  starting transfers between devices: 31.6 us -> 30 us
    dot_general x4 -> x0, matrix products: 13.1 us -> none  [the longest x1 5.46 us: shards(): jnp.dot(activated, w_down, preferred_element_type=jnp.float32)]
    pallas_call x1 -> x3, Pallas kernels: 6.67 us -> 18.4 us  [the longest x1 9.22 us: attend(): pl.pallas_call(attend_kernel, out_shape=(part, part), in_specs=[pl.BlockS...]
    ppermute x18 -> x29, waiting for transfers between devices: 30.3 us -> 41.1 us  [swap(): return lax.ppermute(array, 'experts', pairs)]
    all_to_all x1 -> x0, starting transfers between devices: 10.5 us -> none  [shards(): lax.all_to_all(latent, 'experts', split_axis=1, concat_axis=0, tiled=True)]
    all_to_all x1 -> x0, waiting for transfers between devices: 10 us -> none  [shards(): lax.all_to_all(latent, 'experts', split_axis=1, concat_axis=0, tiled=True)]
    ppermute x18 -> x29, starting transfers between devices: 21.1 us -> 30 us  [swap(): return lax.ppermute(array, 'experts', pairs)]
    unnamed x17 -> x24, local copies, waits for them, and re-layouts: 8.38 us -> 1.18 us
    concatenate x1 -> x14, other arithmetic: 0.14 us -> 1.52 us  [the longest x1 0.73 us: attend(): info = jnp.concatenate([cache_len, rank_here.astype(jnp.int32)[None]])]
  transfers between devices with their start and end apart: 19 -> 29, of which waited for: 13 -> 22; matrix products, arithmetic and copies ran while one was open for 0% -> 0% of each run, Pallas kernels for 0% -> 0%
where the time goes in v3:
time: 94.3 us
  waiting for transfers between devices  41.1 us (44%)
  starting transfers between devices  30 us (32%)
  Pallas kernels  18.4 us (20%)
  other arithmetic  2.36 us (3%)
  local copies, waits for them, and re-layouts  1.41 us (1%)
  between operations  1.01 us (1%)
    ppermute x29, waiting for transfers between devices, swap(): return lax.ppermute(array, 'experts', pairs)  41.1 us
    ppermute x29, starting transfers between devices, swap(): return lax.ppermute(array, 'experts', pairs)  30 us
    pallas_call x1, Pallas kernels, attend(): pl.pallas_call(attend_kernel, out_shape=(part, part), in_specs=[pl.BlockS...  9.22 us
    pallas_call x1, Pallas kernels, run_expert(): pl.pallas_call(functools.partial(expert_kernel, far_rows), out_shape=(jax...  5.52 us
    pallas_call x1, Pallas kernels, project(): pl.pallas_call(functools.partial(project_kernel, own_rows, far), out_shap...  3.67 us
  transfers between devices with their start and end apart: 29, of which 22 were waited for; matrix products, arithmetic and copies ran while one was open for 0% of the time, Pallas kernels for 0%

profile of v3, /device:TPU:0, one launch (start us, length us, event | category | flops | bytes accessed | tf_op | source)
XLA Modules:
  0.0 94.3 jit_solution(1383147381738548890)
XLA Ops:
  2.5 9.2 %attend.1 = (bf16[8,16,512]{2,1,0:T(8,128)(2,1)S(1)}, bf16[8,16,512]{2,1,0:T(8,128)(2,1)S(1)}) custom-call(s32[5]{0:T(128)S(1)} %pad_add_fusion.info_ref, bf16[4,64,576]{2,1,0:T(8,128)(2,1)S(1)} %bitcast.62, bf16[4,576,4096]{2,1,0:T(8,128)(2,1)} %cache_ref.1), custom_call_target="tpu_custom_call" | custom-call | flops 1140850688 | bytes 9437184 | tf_op jit(solution)/shard_map/attend/pallas_call | solution.py:135
  13.2 5.5 %collective-permute-start.5 = (bf16[32,512]{1,0:T(8,128)(2,1)S(1)}, bf16[32,512]{1,0:T(8,128)(2,1)S(1)}, u32[]{:S(2)}, u32[]{:S(2)}) collective-permute-start(bf16[32,512]{1,0:T(8,128)(2,1)S(1)} %pad_maximum_fusion.11), channel_id=1, source_target_pairs={{0,10},{1,11},{2,8},{3,9},{4,14},{5,15},{6,12},{7,13},{8,2},{9,3},... | collective-permute-start | bytes 98312 | tf_op jit(solution)/shard_map/ppermute | solution.py:349
  18.6 2.5 %collective-permute-start.7 = (bf16[32,512]{1,0:T(8,128)(2,1)S(1)}, bf16[32,512]{1,0:T(8,128)(2,1)S(1)}, u32[]{:S(2)}, u32[]{:S(2)}) collective-permute-start(bf16[32,512]{1,0:T(8,128)(2,1)S(1)} %pad_maximum_fusion.13), channel_id=1, source_target_pairs={{0,14},{1,15},{2,12},{3,13},{4,10},{5,11},{6,8},{7,9},{8,6},{9,7},... | collective-permute-start | bytes 98312 | tf_op jit(solution)/shard_map/ppermute | solution.py:349
  21.2 2.8 %collective-permute-start.3 = (bf16[32,512]{1,0:T(8,128)(2,1)S(1)}, bf16[32,512]{1,0:T(8,128)(2,1)S(1)}, u32[]{:S(2)}, u32[]{:S(2)}) collective-permute-start(bf16[32,512]{1,0:T(8,128)(2,1)S(1)} %pad_maximum_fusion.9), channel_id=1, source_target_pairs={{0,6},{1,7},{2,4},{3,5},{4,2},{5,3},{6,0},{7,1},{8,14},{9,15},{10,... | collective-permute-start | bytes 98312 | tf_op jit(solution)/shard_map/ppermute | solution.py:349
  24.0 1.5 %collective-permute-start.2 = (bf16[32,512]{1,0:T(8,128)(2,1)S(1)}, bf16[32,512]{1,0:T(8,128)(2,1)S(1)}, u32[]{:S(2)}, u32[]{:S(2)}) collective-permute-start(bf16[32,512]{1,0:T(8,128)(2,1)S(1)} %pad_maximum_fusion.8), channel_id=1, source_target_pairs={{0,4},{1,5},{2,6},{3,7},{4,0},{5,1},{6,2},{7,3},{8,12},{9,13},{10,... | collective-permute-start | bytes 98312 | tf_op jit(solution)/shard_map/ppermute | solution.py:349
  29.5 3.7 %project.1 = (f32[32,7168]{1,0:T(8,128)S(1)}, bf16[32,7168]{1,0:T(8,128)(2,1)S(1)}) custom-call(bf16[16,512]{1,0:T(8,128)(2,1)S(1)} %get-tuple-element.25.refs_0_, bf16[16,512]{1,0:T(8,128)(2,1)S(1)} %get-tuple-element.33.refs_1_, bf16[32,512]{1,0:T(8,128)(2,1)S(1)} %collective-permute-done.1.refs_2_, bf16[32,512]{1,0:T(8,128)(2,1)S(1)} %collective-permute-done.2.refs_3_, ...), custom_call_target="tpu_custom_call" | custom-call | flops 469762048 | bytes 7340032 | tf_op jit(solution)/shard_map/project/pallas_call | solution.py:233
  33.3 1.8 %collective-permute-done.8 = bf16[32,7168]{1,0:T(8,128)(2,1)S(1)} collective-permute-done((bf16[32,7168]{1,0:T(8,128)(2,1)S(1)}, bf16[32,7168]{1,0:T(8,128)(2,1)S(1)}, u32[]{:S(2)}, u32[]{:S(2)}) %collective-permute-start.8) | collective-permute-done | bytes 458784 | tf_op jit(solution)/shard_map/ppermute | solution.py:349
  36.5 4.0 %collective-permute-done.12 = bf16[2,8,3584]{2,1,0:T(8,128)(2,1)S(1)} collective-permute-done((bf16[2,8,3584]{2,1,0:T(8,128)(2,1)S(1)}, bf16[2,8,3584]{2,1,0:T(8,128)(2,1)S(1)}, u32[]{:S(2)}, u32[]{:S(2)}) %collective-permute-start.12) | collective-permute-done | bytes 114720 | tf_op jit(solution)/shard_map/ppermute | solution.py:349
  40.9 1.5 %collective-permute-start.10 = (bf16[8,3584]{1,0:T(8,128)(2,1)S(1)}, bf16[8,3584]{1,0:T(8,128)(2,1)S(1)}, u32[]{:S(2)}, u32[]{:S(2)}) collective-permute-start(bf16[8,3584]{1,0:T(8,128)(2,1)S(1)} %slice.311), channel_id=1, source_target_pairs={{0,4},{1,5},{2,6},{3,7},{4,0},{5,1},{6,2},{7,3},{8,12},{9,13},{10,... | collective-permute-start | bytes 172040 | tf_op jit(solution)/shard_map/ppermute | solution.py:349
  42.4 2.3 %collective-permute-done.13 = bf16[8,3584]{1,0:T(8,128)(2,1)S(1)} collective-permute-done((bf16[8,3584]{1,0:T(8,128)(2,1)S(1)}, bf16[8,3584]{1,0:T(8,128)(2,1)S(1)}, u32[]{:S(2)}, u32[]{:S(2)}) %collective-permute-start.13) | collective-permute-done | bytes 57376 | tf_op jit(solution)/shard_map/ppermute | solution.py:349
  44.8 2.9 %collective-permute-start.14 = (bf16[4,3584]{1,0:T(4,128)(2,1)S(1)}, bf16[4,3584]{1,0:T(4,128)(2,1)S(1)}, u32[]{:S(2)}, u32[]{:S(2)}) collective-permute-start(bf16[4,3584]{1,0:T(4,128)(2,1)S(1)} %slice.314), channel_id=1, source_target_pairs={{0,8},{1,9},{2,10},{3,11},{4,12},{5,13},{6,14},{7,15},{8,0},{9,1},... | collective-permute-start | bytes 86024 | tf_op jit(solution)/shard_map/ppermute | solution.py:349
  48.2 2.2 %collective-permute-done.14 = bf16[4,3584]{1,0:T(4,128)(2,1)S(1)} collective-permute-done((bf16[4,3584]{1,0:T(4,128)(2,1)S(1)}, bf16[4,3584]{1,0:T(4,128)(2,1)S(1)}, u32[]{:S(2)}, u32[]{:S(2)}) %collective-permute-start.14) | collective-permute-done | bytes 28704 | tf_op jit(solution)/shard_map/ppermute | solution.py:349
  50.4 2.3 %collective-permute-done.11 = bf16[4,3584]{1,0:T(4,128)(2,1)S(1)} collective-permute-done((bf16[4,3584]{1,0:T(4,128)(2,1)S(1)}, bf16[4,3584]{1,0:T(4,128)(2,1)S(1)}, u32[]{:S(2)}, u32[]{:S(2)}) %collective-permute-start.11) | collective-permute-done | bytes 28704 | tf_op jit(solution)/shard_map/ppermute | solution.py:349
  53.5 5.1 %collective-permute-done.15 = bf16[4,7168]{1,0:T(4,128)(2,1)S(1)} collective-permute-done((bf16[4,7168]{1,0:T(4,128)(2,1)S(1)}, bf16[4,7168]{1,0:T(4,128)(2,1)S(1)}, u32[]{:S(2)}, u32[]{:S(2)}) %collective-permute-start.15) | collective-permute-done | bytes 57376 | tf_op jit(solution)/shard_map/ppermute | solution.py:349
  59.0 4.2 %collective-permute-done.19 = bf16[8,3584]{1,0:T(8,128)(2,1)S(1)} collective-permute-done((bf16[8,3584]{1,0:T(8,128)(2,1)S(1)}, bf16[8,3584]{1,0:T(8,128)(2,1)S(1)}, u32[]{:S(2)}, u32[]{:S(2)}) %collective-permute-start.19) | collective-permute-done | bytes 57376 | tf_op jit(solution)/shard_map/ppermute | solution.py:349
  63.3 1.6 %collective-permute-start.17 = (bf16[16,3584]{1,0:T(8,128)(2,1)S(1)}, bf16[16,3584]{1,0:T(8,128)(2,1)S(1)}, u32[]{:S(2)}, u32[]{:S(2)}) collective-permute-start(bf16[16,3584]{1,0:T(8,128)(2,1)S(1)} %pad_maximum_fusion.2), channel_id=1, source_target_pairs={{0,2},{1,3},{2,0},{3,1},{4,6},{5,7},{6,4},{7,5},{8,10},{9,11},{10,... | collective-permute-start | bytes 344072 | tf_op jit(solution)/shard_map/ppermute | solution.py:349
  64.9 3.1 %collective-permute-done.20 = bf16[16,3584]{1,0:T(8,128)(2,1)S(1)} collective-permute-done((bf16[16,3584]{1,0:T(8,128)(2,1)S(1)}, bf16[16,3584]{1,0:T(8,128)(2,1)S(1)}, u32[]{:S(2)}, u32[]{:S(2)}) %collective-permute-start.20) | collective-permute-done | bytes 114720 | tf_op jit(solution)/shard_map/ppermute | solution.py:349
  70.0 5.5 %expert.1 = (f32[32,7168]{1,0:T(8,128)S(1)}, bf16[32,7168]{1,0:T(8,128)(2,1)S(1)}) custom-call(bf16[32,3584]{1,0:T(8,128)(2,1)S(1)} %pad_maximum_fusion.first_own, bf16[32,3584]{1,0:T(8,128)(2,1)S(1)} %collective-permute-done.18.first_other, bf16[32,3584]{1,0:T(8,128)(2,1)S(1)} %pad_maximum_fusion.1.second_own, ...), custom_call_target="tpu_custom_call" | custom-call | flops 704643072 | bytes 11010048 | tf_op jit(solution)/shard_map/expert/pallas_call | solution.py:320
  75.9 1.5 %collective-permute-done.22 = bf16[32,7168]{1,0:T(8,128)(2,1)S(1)} collective-permute-done((bf16[32,7168]{1,0:T(8,128)(2,1)S(1)}, bf16[32,7168]{1,0:T(8,128)(2,1)S(1)}, u32[]{:S(2)}, u32[]{:S(2)}) %collective-permute-start.22) | collective-permute-done | bytes 458784 | tf_op jit(solution)/shard_map/ppermute | solution.py:349
  77.6 1.8 %collective-permute-start.26 = (bf16[2,8,3584]{2,1,0:T(8,128)(2,1)S(1)}, bf16[2,8,3584]{2,1,0:T(8,128)(2,1)S(1)}, u32[]{:S(2)}, u32[]{:S(2)}) collective-permute-start(bf16[2,8,3584]{2,1,0:T(8,128)(2,1)S(1)} %fusion.6), channel_id=1, source_target_pairs={{0,4},{1,5},{2,6},{3,7},{4,0},{5,1},{6,2},{7,3},{8,12},{9,13},{10,... | collective-permute-start | bytes 344072 | tf_op jit(solution)/shard_map/ppermute | solution.py:349
  80.0 2.9 %collective-permute-done.26 = bf16[2,8,3584]{2,1,0:T(8,128)(2,1)S(1)} collective-permute-done((bf16[2,8,3584]{2,1,0:T(8,128)(2,1)S(1)}, bf16[2,8,3584]{2,1,0:T(8,128)(2,1)S(1)}, u32[]{:S(2)}, u32[]{:S(2)}) %collective-permute-start.26) | collective-permute-done | bytes 114720 | tf_op jit(solution)/shard_map/ppermute | solution.py:349
  85.4 1.9 %collective-permute-done.27 = bf16[8,3584]{1,0:T(8,128)(2,1)S(1)} collective-permute-done((bf16[8,3584]{1,0:T(8,128)(2,1)S(1)}, bf16[8,3584]{1,0:T(8,128)(2,1)S(1)}, u32[]{:S(2)}, u32[]{:S(2)}) %collective-permute-start.27) | collective-permute-done | bytes 57376 | tf_op jit(solution)/shard_map/ppermute | solution.py:349
  88.7 1.6 %collective-permute-start.25 = (bf16[4,3584]{1,0:T(4,128)(2,1)S(1)}, bf16[4,3584]{1,0:T(4,128)(2,1)S(1)}, u32[]{:S(2)}, u32[]{:S(2)}) collective-permute-start(bf16[4,3584]{1,0:T(4,128)(2,1)S(1)} %slice.313), channel_id=1, source_target_pairs={{0,8},{1,9},{2,10},{3,11},{4,12},{5,13},{6,14},{7,15},{8,0},{9,1},... | collective-permute-start | bytes 86024 | tf_op jit(solution)/shard_map/ppermute | solution.py:349
  90.5 1.6 %collective-permute-done.28 = bf16[4,3584]{1,0:T(4,128)(2,1)S(1)} collective-permute-done((bf16[4,3584]{1,0:T(4,128)(2,1)S(1)}, bf16[4,3584]{1,0:T(4,128)(2,1)S(1)}, u32[]{:S(2)}, u32[]{:S(2)}) %collective-permute-start.28) | collective-permute-done | bytes 28704 | tf_op jit(solution)/shard_map/ppermute | solution.py:349
  (109 shorter events, 20.1 us)
Async XLA Ops:
  13.2 10.8 %collective-permute-start.5 = (bf16[32,512]{1,0:T(8,128)(2,1)S(1)}, bf16[32,512]{1,0:T(8,128)(2,1)S(1)}, u32[]{:S(2)}, u32[]{:S(2)}) collective-permute-start(bf16[32,512]{1,0:T(8,128)(2,1)S(1)} %pad_maximum_fusion.11), channel_id=1, source_target_pairs={{0,10},{1,11},{2,8},{3,9},{4,14},{5,15},{6,12},{7,13},{8,2},{9,3},... | collective-permute-start | bytes 98312 | tf_op jit(solution)/shard_map/ppermute | solution.py:349
  18.6 6.9 %collective-permute-start.6 = (bf16[32,512]{1,0:T(8,128)(2,1)S(1)}, bf16[32,512]{1,0:T(8,128)(2,1)S(1)}, u32[]{:S(2)}, u32[]{:S(2)}) collective-permute-start(bf16[32,512]{1,0:T(8,128)(2,1)S(1)} %pad_maximum_fusion.12), channel_id=1, source_target_pairs={{0,12},{1,13},{2,14},{3,15},{4,8},{5,9},{6,10},{7,11},{8,4},{9,5},... | collective-permute-start | bytes 98312 | tf_op jit(solution)/shard_map/ppermute | solution.py:349
  18.6 6.9 %collective-permute-start.7 = (bf16[32,512]{1,0:T(8,128)(2,1)S(1)}, bf16[32,512]{1,0:T(8,128)(2,1)S(1)}, u32[]{:S(2)}, u32[]{:S(2)}) collective-permute-start(bf16[32,512]{1,0:T(8,128)(2,1)S(1)} %pad_maximum_fusion.13), channel_id=1, source_target_pairs={{0,14},{1,15},{2,12},{3,13},{4,10},{5,11},{6,8},{7,9},{8,6},{9,7},... | collective-permute-start | bytes 98312 | tf_op jit(solution)/shard_map/ppermute | solution.py:349
  21.1 5.1 %collective-permute-start.4 = (bf16[32,512]{1,0:T(8,128)(2,1)S(1)}, bf16[32,512]{1,0:T(8,128)(2,1)S(1)}, u32[]{:S(2)}, u32[]{:S(2)}) collective-permute-start(bf16[32,512]{1,0:T(8,128)(2,1)S(1)} %pad_maximum_fusion.10), channel_id=1, source_target_pairs={{0,8},{1,9},{2,10},{3,11},{4,12},{5,13},{6,14},{7,15},{8,0},{9,1},... | collective-permute-start | bytes 98312 | tf_op jit(solution)/shard_map/ppermute | solution.py:349
  21.2 5.6 %collective-permute-start.3 = (bf16[32,512]{1,0:T(8,128)(2,1)S(1)}, bf16[32,512]{1,0:T(8,128)(2,1)S(1)}, u32[]{:S(2)}, u32[]{:S(2)}) collective-permute-start(bf16[32,512]{1,0:T(8,128)(2,1)S(1)} %pad_maximum_fusion.9), channel_id=1, source_target_pairs={{0,6},{1,7},{2,4},{3,5},{4,2},{5,3},{6,0},{7,1},{8,14},{9,15},{10,... | collective-permute-start | bytes 98312 | tf_op jit(solution)/shard_map/ppermute | solution.py:349
  24.0 4.0 %collective-permute-start.2 = (bf16[32,512]{1,0:T(8,128)(2,1)S(1)}, bf16[32,512]{1,0:T(8,128)(2,1)S(1)}, u32[]{:S(2)}, u32[]{:S(2)}) collective-permute-start(bf16[32,512]{1,0:T(8,128)(2,1)S(1)} %pad_maximum_fusion.8), channel_id=1, source_target_pairs={{0,4},{1,5},{2,6},{3,7},{4,0},{5,1},{6,2},{7,3},{8,12},{9,13},{10,... | collective-permute-start | bytes 98312 | tf_op jit(solution)/shard_map/ppermute | solution.py:349
  25.5 3.9 %collective-permute-start.1 = (bf16[32,512]{1,0:T(8,128)(2,1)S(1)}, bf16[32,512]{1,0:T(8,128)(2,1)S(1)}, u32[]{:S(2)}, u32[]{:S(2)}) collective-permute-start(bf16[32,512]{1,0:T(8,128)(2,1)S(1)} %pad_maximum_fusion.7), channel_id=1, source_target_pairs={{0,2},{1,3},{2,0},{3,1},{4,6},{5,7},{6,4},{7,5},{8,10},{9,11},{10,... | collective-permute-start | bytes 98312 | tf_op jit(solution)/shard_map/ppermute | solution.py:349
  35.2 5.3 %collective-permute-start.12 = (bf16[2,8,3584]{2,1,0:T(8,128)(2,1)S(1)}, bf16[2,8,3584]{2,1,0:T(8,128)(2,1)S(1)}, u32[]{:S(2)}, u32[]{:S(2)}) collective-permute-start(bf16[2,8,3584]{2,1,0:T(8,128)(2,1)S(1)} %fusion.5), channel_id=1, source_target_pairs={{0,4},{1,5},{2,6},{3,7},{4,0},{5,1},{6,2},{7,3},{8,12},{9,13},{10,... | collective-permute-start | bytes 344072 | tf_op jit(solution)/shard_map/ppermute | solution.py:349
  35.9 5.0 %collective-permute-start.9 = (bf16[16,3584]{1,0:T(8,128)(2,1)S(1)}, bf16[16,3584]{1,0:T(8,128)(2,1)S(1)}, u32[]{:S(2)}, u32[]{:S(2)}) collective-permute-start(bf16[16,3584]{1,0:T(8,128)(2,1)S(1)} %slice.309), channel_id=1, source_target_pairs={{0,2},{1,3},{2,0},{3,1},{4,6},{5,7},{6,4},{7,5},{8,10},{9,11},{10,... | collective-permute-start | bytes 344072 | tf_op jit(solution)/shard_map/ppermute | solution.py:349
  40.5 4.2 %collective-permute-start.13 = (bf16[8,3584]{1,0:T(8,128)(2,1)S(1)}, bf16[8,3584]{1,0:T(8,128)(2,1)S(1)}, u32[]{:S(2)}, u32[]{:S(2)}) collective-permute-start(bf16[8,3584]{1,0:T(8,128)(2,1)S(1)} %fusion.10), channel_id=1, source_target_pairs={{0,2},{1,3},{2,0},{3,1},{4,6},{5,7},{6,4},{7,5},{8,10},{9,11},{10,... | collective-permute-start | bytes 172040 | tf_op jit(solution)/shard_map/ppermute | solution.py:349
  40.9 6.8 %collective-permute-start.10 = (bf16[8,3584]{1,0:T(8,128)(2,1)S(1)}, bf16[8,3584]{1,0:T(8,128)(2,1)S(1)}, u32[]{:S(2)}, u32[]{:S(2)}) collective-permute-start(bf16[8,3584]{1,0:T(8,128)(2,1)S(1)} %slice.311), channel_id=1, source_target_pairs={{0,4},{1,5},{2,6},{3,7},{4,0},{5,1},{6,2},{7,3},{8,12},{9,13},{10,... | collective-permute-start | bytes 172040 | tf_op jit(solution)/shard_map/ppermute | solution.py:349
  44.8 5.6 %collective-permute-start.14 = (bf16[4,3584]{1,0:T(4,128)(2,1)S(1)}, bf16[4,3584]{1,0:T(4,128)(2,1)S(1)}, u32[]{:S(2)}, u32[]{:S(2)}) collective-permute-start(bf16[4,3584]{1,0:T(4,128)(2,1)S(1)} %slice.314), channel_id=1, source_target_pairs={{0,8},{1,9},{2,10},{3,11},{4,12},{5,13},{6,14},{7,15},{8,0},{9,1},... | collective-permute-start | bytes 86024 | tf_op jit(solution)/shard_map/ppermute | solution.py:349
  47.8 4.9 %collective-permute-start.11 = (bf16[4,3584]{1,0:T(4,128)(2,1)S(1)}, bf16[4,3584]{1,0:T(4,128)(2,1)S(1)}, u32[]{:S(2)}, u32[]{:S(2)}) collective-permute-start(bf16[4,3584]{1,0:T(4,128)(2,1)S(1)} %slice.315), channel_id=1, source_target_pairs={{0,8},{1,9},{2,10},{3,11},{4,12},{5,13},{6,14},{7,15},{8,0},{9,1},... | collective-permute-start | bytes 86024 | tf_op jit(solution)/shard_map/ppermute | solution.py:349
  53.0 5.5 %collective-permute-start.15 = (bf16[4,7168]{1,0:T(4,128)(2,1)S(1)}, bf16[4,7168]{1,0:T(4,128)(2,1)S(1)}, u32[]{:S(2)}, u32[]{:S(2)}) collective-permute-start(bf16[4,7168]{1,0:T(4,128)(2,1)S(1)} %fusion.4), channel_id=1, source_target_pairs={{0,8},{1,9},{2,10},{3,11},{4,12},{5,13},{6,14},{7,15},{8,0},{9,1},... | collective-permute-start | bytes 172040 | tf_op jit(solution)/shard_map/ppermute | solution.py:349
  58.6 4.6 %collective-permute-start.19 = (bf16[8,3584]{1,0:T(8,128)(2,1)S(1)}, bf16[8,3584]{1,0:T(8,128)(2,1)S(1)}, u32[]{:S(2)}, u32[]{:S(2)}) collective-permute-start(bf16[8,3584]{1,0:T(8,128)(2,1)S(1)} %get-tuple-element.34), channel_id=1, source_target_pairs={{0,2},{1,3},{2,0},{3,1},{4,6},{5,7},{6,4},{7,5},{8,10},{9,11},{10,... | collective-permute-start | bytes 172040 | tf_op jit(solution)/shard_map/ppermute | solution.py:349
  59.0 4.3 %collective-permute-start.16 = (bf16[8,3584]{1,0:T(8,128)(2,1)S(1)}, bf16[8,3584]{1,0:T(8,128)(2,1)S(1)}, u32[]{:S(2)}, u32[]{:S(2)}) collective-permute-start(bf16[8,3584]{1,0:T(8,128)(2,1)S(1)} %get-tuple-element.35), channel_id=1, source_target_pairs={{0,4},{1,5},{2,6},{3,7},{4,0},{5,1},{6,2},{7,3},{8,12},{9,13},{10,... | collective-permute-start | bytes 172040 | tf_op jit(solution)/shard_map/ppermute | solution.py:349
  63.2 4.9 %collective-permute-start.20 = (bf16[16,3584]{1,0:T(8,128)(2,1)S(1)}, bf16[16,3584]{1,0:T(8,128)(2,1)S(1)}, u32[]{:S(2)}, u32[]{:S(2)}) collective-permute-start(bf16[16,3584]{1,0:T(8,128)(2,1)S(1)} %pad_maximum_fusion.3), channel_id=1, source_target_pairs={{0,4},{1,5},{2,6},{3,7},{4,0},{5,1},{6,2},{7,3},{8,12},{9,13},{10,... | collective-permute-start | bytes 344072 | tf_op jit(solution)/shard_map/ppermute | solution.py:349
  63.3 4.9 %collective-permute-start.17 = (bf16[16,3584]{1,0:T(8,128)(2,1)S(1)}, bf16[16,3584]{1,0:T(8,128)(2,1)S(1)}, u32[]{:S(2)}, u32[]{:S(2)}) collective-permute-start(bf16[16,3584]{1,0:T(8,128)(2,1)S(1)} %pad_maximum_fusion.2), channel_id=1, source_target_pairs={{0,2},{1,3},{2,0},{3,1},{4,6},{5,7},{6,4},{7,5},{8,10},{9,11},{10,... | collective-permute-start | bytes 344072 | tf_op jit(solution)/shard_map/ppermute | solution.py:349
  77.6 5.4 %collective-permute-start.26 = (bf16[2,8,3584]{2,1,0:T(8,128)(2,1)S(1)}, bf16[2,8,3584]{2,1,0:T(8,128)(2,1)S(1)}, u32[]{:S(2)}, u32[]{:S(2)}) collective-permute-start(bf16[2,8,3584]{2,1,0:T(8,128)(2,1)S(1)} %fusion.6), channel_id=1, source_target_pairs={{0,4},{1,5},{2,6},{3,7},{4,0},{5,1},{6,2},{7,3},{8,12},{9,13},{10,... | collective-permute-start | bytes 344072 | tf_op jit(solution)/shard_map/ppermute | solution.py:349
  79.4 5.0 %collective-permute-start.23 = (bf16[16,3584]{1,0:T(8,128)(2,1)S(1)}, bf16[16,3584]{1,0:T(8,128)(2,1)S(1)}, u32[]{:S(2)}, u32[]{:S(2)}) collective-permute-start(bf16[16,3584]{1,0:T(8,128)(2,1)S(1)} %slice.308), channel_id=1, source_target_pairs={{0,2},{1,3},{2,0},{3,1},{4,6},{5,7},{6,4},{7,5},{8,10},{9,11},{10,... | collective-permute-start | bytes 344072 | tf_op jit(solution)/shard_map/ppermute | solution.py:349
  83.0 4.2 %collective-permute-start.27 = (bf16[8,3584]{1,0:T(8,128)(2,1)S(1)}, bf16[8,3584]{1,0:T(8,128)(2,1)S(1)}, u32[]{:S(2)}, u32[]{:S(2)}) collective-permute-start(bf16[8,3584]{1,0:T(8,128)(2,1)S(1)} %fusion.11), channel_id=1, source_target_pairs={{0,2},{1,3},{2,0},{3,1},{4,6},{5,7},{6,4},{7,5},{8,10},{9,11},{10,... | collective-permute-start | bytes 172040 | tf_op jit(solution)/shard_map/ppermute | solution.py:349
  84.4 4.3 %collective-permute-start.24 = (bf16[8,3584]{1,0:T(8,128)(2,1)S(1)}, bf16[8,3584]{1,0:T(8,128)(2,1)S(1)}, u32[]{:S(2)}, u32[]{:S(2)}) collective-permute-start(bf16[8,3584]{1,0:T(8,128)(2,1)S(1)} %slice.310), channel_id=1, source_target_pairs={{0,4},{1,5},{2,6},{3,7},{4,0},{5,1},{6,2},{7,3},{8,12},{9,13},{10,... | collective-permute-start | bytes 172040 | tf_op jit(solution)/shard_map/ppermute | solution.py:349
  87.3 4.8 %collective-permute-start.28 = (bf16[4,3584]{1,0:T(4,128)(2,1)S(1)}, bf16[4,3584]{1,0:T(4,128)(2,1)S(1)}, u32[]{:S(2)}, u32[]{:S(2)}) collective-permute-start(bf16[4,3584]{1,0:T(4,128)(2,1)S(1)} %slice.312), channel_id=1, source_target_pairs={{0,8},{1,9},{2,10},{3,11},{4,12},{5,13},{6,14},{7,15},{8,0},{9,1},... | collective-permute-start | bytes 86024 | tf_op jit(solution)/shard_map/ppermute | solution.py:349
  88.7 4.8 %collective-permute-start.25 = (bf16[4,3584]{1,0:T(4,128)(2,1)S(1)}, bf16[4,3584]{1,0:T(4,128)(2,1)S(1)}, u32[]{:S(2)}, u32[]{:S(2)}) collective-permute-start(bf16[4,3584]{1,0:T(4,128)(2,1)S(1)} %slice.313), channel_id=1, source_target_pairs={{0,8},{1,9},{2,10},{3,11},{4,12},{5,13},{6,14},{7,15},{8,0},{9,1},... | collective-permute-start | bytes 86024 | tf_op jit(solution)/shard_map/ppermute | solution.py:349
  (17 other events, 289.0 us)

commit v4 on v1

v4 whole, which is shorter than its diff:
```python
import functools

import jax
import jax.numpy as jnp
from jax import lax
from jax.experimental import pallas as pl
from jax.experimental.pallas import tpu as pltpu
from jax.sharding import PartitionSpec as P

QK = 192
FF = 2048
BLOCK = 512
GROUP = 4
LANES = 128
TILE = 256
MIB = 2**20


def lane_tiles(array):
    return [array[:, at : at + LANES] for at in range(0, array.shape[1], LANES)]


def attend_kernel(
    len_ref,
    queries_ref,
    cache_ref,
    latent_ref,
    length,
    queries,
    held,
    scores,
    highest,
    sums,
    inverse,
    summed,
    staged,
    item_row,
    item_block,
    length_arrived,
    queries_arrived,
    arrived,
):
    own_rows, heads, _ = queries.shape
    devices, _, rank = staged.shape
    own_heads = heads // devices
    blocks = held.shape[1]

    length_copy = pltpu.make_async_copy(len_ref, length, length_arrived)
    length_copy.start()
    queries_copy = pltpu.make_async_copy(queries_ref, queries, queries_arrived)
    queries_copy.start()

    def block_copy(row, block):
        return pltpu.make_async_copy(
            cache_ref.at[row, :, pl.ds(pl.multiple_of(block * BLOCK, BLOCK), BLOCK)],
            held.at[row, block],
            arrived.at[row, block],
        )

    length_copy.wait()
    items = 0
    for row in range(own_rows):
        count = (length[row] + BLOCK - 1) // BLOCK

        def begin(block, first, row=row):
            block_copy(row, block).start()
            item_row[first + block] = row
            item_block[first + block] = block
            return first

        lax.fori_loop(0, count, begin, items)
        items = items + count
    for at in range(GROUP - 1):
        item_row[items + at] = own_rows - 1
        item_block[items + at] = item_block[items - 1]
    groups = (items + GROUP - 1) // GROUP

    def members(group):
        return [
            (group * GROUP + at, item_row[group * GROUP + at], item_block[group * GROUP + at])
            for at in range(GROUP)
        ]

    highest[...] = jnp.full_like(highest, -jnp.inf)
    sums[...] = jnp.zeros_like(sums)
    summed[...] = jnp.zeros_like(summed)
    queries_copy.wait()
    column = lax.broadcasted_iota(jnp.int32, (heads, BLOCK), 1)

    def score(group, _):
        inside = members(group)
        for at, row, block in inside:
            pl.when(at < items)(lambda row=row, block=block: block_copy(row, block).wait())
        for at, row, block in inside:
            found = jnp.dot(
                queries[row], held[row, block], preferred_element_type=jnp.float32
            ) * QK ** (-0.5)
            found = jnp.where(column + block * BLOCK < length[row], found, -jnp.inf)
            scores[row, block] = found
            highest[row, block] = functools.reduce(jnp.maximum, lane_tiles(found))
        return 0

    lax.fori_loop(0, groups, score, 0)
    tops = [jnp.max(highest[row], axis=0) for row in range(own_rows)]
    for row in range(own_rows):
        top = jnp.max(tops[row], axis=1, keepdims=True)
        highest[row, 0] = jnp.broadcast_to(top, (heads, LANES))

    def lift(group, _):
        for at, row, block in members(group):
            top = highest[row, 0][:, :1]
            pl.when(at < items)(lambda row=row, block=block, top=top: lift_one(row, block, top))
        return 0

    def lift_one(row, block, top):
        weight = jnp.exp(scores[row, block] - top)
        scores[row, block] = weight
        sums[row, block] = sum(lane_tiles(weight))

    lax.fori_loop(0, groups, lift, 0)
    for row in range(own_rows):
        total = jnp.sum(jnp.sum(sums[row], axis=0), axis=1, keepdims=True)
        inverse[row] = jnp.broadcast_to(1.0 / total, (heads, LANES))

    def gather(group, _):
        terms = []
        for at, row, block in members(group):
            live = jnp.where(at < items, 1.0, 0.0)
            weight = scores[row, block] * (inverse[row][:, :1] * live)
            terms.append(
                lax.dot_general(
                    weight.astype(jnp.bfloat16),
                    held[row, block, :rank, :],
                    (((1,), (1,)), ((), ())),
                    preferred_element_type=jnp.float32,
                )
            )
        for (at, row, block), term in zip(members(group), terms):
            summed[row] += term
        return 0

    lax.fori_loop(0, groups, gather, 0)
    for row in range(own_rows):
        latent = summed[row]
        for device in range(devices):
            staged[device, row * own_heads : (row + 1) * own_heads, :] = latent[
                device * own_heads : (device + 1) * own_heads
            ]
    latent_ref[...] = staged[...].astype(latent_ref.dtype)


def attend(queries, cache, cache_len, devices, rank):
    own_rows, depth, heads = queries.shape
    blocks = cache.shape[2] // BLOCK
    packed = own_rows * heads // devices
    listed = own_rows * blocks + GROUP
    return pl.pallas_call(
        attend_kernel,
        out_shape=jax.ShapeDtypeStruct((devices, packed, rank), jnp.bfloat16),
        in_specs=[pl.BlockSpec(memory_space=pltpu.HBM)] * 3,
        out_specs=pl.BlockSpec(memory_space=pltpu.VMEM),
        scratch_shapes=[
            pltpu.SMEM((own_rows,), jnp.int32),
            pltpu.VMEM((own_rows, heads, depth), jnp.bfloat16),
            pltpu.VMEM((own_rows, blocks, depth, BLOCK), jnp.bfloat16),
            pltpu.VMEM((own_rows, blocks, heads, BLOCK), jnp.float32),
            pltpu.VMEM((own_rows, blocks, heads, LANES), jnp.float32),
            pltpu.VMEM((own_rows, blocks, heads, LANES), jnp.float32),
            pltpu.VMEM((own_rows, heads, LANES), jnp.float32),
            pltpu.VMEM((own_rows, heads, rank), jnp.float32),
            pltpu.VMEM((devices, packed, rank), jnp.float32),
            pltpu.SMEM((listed,), jnp.int32),
            pltpu.SMEM((listed,), jnp.int32),
            pltpu.SemaphoreType.DMA,
            pltpu.SemaphoreType.DMA,
            pltpu.SemaphoreType.DMA((own_rows, blocks)),
        ],
        compiler_params=pltpu.CompilerParams(vmem_limit_bytes=55 * MIB),
        cost_estimate=pl.CostEstimate(
            flops=own_rows * heads * cache.shape[2] * (depth + rank),
            bytes_accessed=cache.size,
            transcendentals=own_rows * heads * cache.shape[2],
        ),
        name="attend",
    )(cache_len, jnp.swapaxes(queries, 1, 2), cache)


def project_kernel(own_rows, far, here_ref, joined_ref, absorb_ref, w_ref, keep_ref, send_ref):
    own_heads = absorb_ref.shape[0]
    half, width = keep_ref.shape
    shape = (2 * half, joined_ref.shape[0])
    row = lax.broadcasted_iota(jnp.int32, shape, 0)
    place = lax.broadcasted_iota(jnp.int32, shape, 1)
    turn = own_rows.bit_length() - 1
    far_bits = far.bit_length() - 1
    request, slot = row & (own_rows - 1), row >> turn
    far_at, slot = slot & (far - 1), slot >> far_bits
    distance = (far_at << 3) + ((slot & 1) << 2) + ((slot >> 1 & 1) << 1) + (slot >> 2)
    device = distance ^ here_ref[0]
    values = []
    for head in range(own_heads):
        wanted = ((device << turn) + request) * own_heads + head
        choice = (place == wanted).astype(jnp.float32).astype(jnp.bfloat16)
        latent = jnp.dot(choice, joined_ref[...], preferred_element_type=jnp.float32)
        value = jnp.dot(
            latent.astype(jnp.bfloat16), absorb_ref[head], preferred_element_type=jnp.float32
        )
        values.append(value.astype(jnp.bfloat16))
    values = jnp.concatenate(values, axis=1)
    for at in range(0, width, TILE):
        term = jnp.dot(values, w_ref[:, at : at + TILE], preferred_element_type=jnp.float32)
        keep_ref[:, at : at + TILE] = term[:half]
        send_ref[:, at : at + TILE] = term[half:].astype(send_ref.dtype)


def project(here, joined, w_absorb, w_out, own_rows, rows, far):
    depth, width = w_out.shape
    return pl.pallas_call(
        functools.partial(project_kernel, own_rows, far),
        out_shape=(
            jax.ShapeDtypeStruct((rows // 2, width), jnp.float32),
            jax.ShapeDtypeStruct((rows // 2, width), jnp.bfloat16),
        ),
        in_specs=[pl.BlockSpec(memory_space=pltpu.SMEM)]
        + [pl.BlockSpec(memory_space=pltpu.VMEM)] * 3,
        out_specs=(pl.BlockSpec(memory_space=pltpu.VMEM),) * 2,
        compiler_params=pltpu.CompilerParams(vmem_limit_bytes=24 * MIB),
        cost_estimate=pl.CostEstimate(
            flops=2 * rows * depth * width, bytes_accessed=2 * depth * width, transcendentals=0
        ),
        name="project",
    )(here, joined, w_absorb, w_out)


def expert_kernel(own_ref, other_ref, gate_ref, up_ref, down_ref, keep_ref, send_ref):
    half, width = keep_ref.shape
    depth = width // 4
    gate, up = 0.0, 0.0
    for at in range(0, width, depth):
        tokens = jnp.concatenate(
            [own_ref[:, at : at + depth], other_ref[:, at : at + depth]], axis=0
        )
        gate = gate + jnp.dot(
            tokens, gate_ref[at : at + depth, :], preferred_element_type=jnp.float32
        )
        up = up + jnp.dot(
            tokens, up_ref[at : at + depth, :], preferred_element_type=jnp.float32
        )
    active = (gate / (1.0 + jnp.exp(-gate)) * up).astype(jnp.bfloat16)
    for at in range(0, width, TILE):
        term = jnp.dot(active, down_ref[:, at : at + TILE], preferred_element_type=jnp.float32)
        keep_ref[:, at : at + TILE] = term[:half]
        send_ref[:, at : at + TILE] = term[half:].astype(send_ref.dtype)


def run_expert(own, other, w_gate, w_up, w_down):
    half, width = own.shape
    hidden = w_gate.shape[1]
    return pl.pallas_call(
        expert_kernel,
        out_shape=(
            jax.ShapeDtypeStruct((half, width), jnp.float32),
            jax.ShapeDtypeStruct((half, width), jnp.bfloat16),
        ),
        in_specs=[pl.BlockSpec(memory_space=pltpu.VMEM)] * 5,
        out_specs=(pl.BlockSpec(memory_space=pltpu.VMEM),) * 2,
        compiler_params=pltpu.CompilerParams(vmem_limit_bytes=24 * MIB),
        cost_estimate=pl.CostEstimate(
            flops=12 * half * hidden * width,
            bytes_accessed=6 * hidden * width,
            transcendentals=2 * half * hidden,
        ),
        name="expert",
    )(own, other, w_gate, w_up, w_down)


def swap(array, distance):
    pairs = [(at, at ^ distance) for at in range(lax.axis_size("experts"))]
    return lax.ppermute(array, "experts", pairs)


def wide(array):
    return array.astype(jnp.float32)


def collect(keep, send):
    half = keep.shape[0]
    step = half // 4
    whole = keep + wide(swap(send, 1))
    parts = [whole[at : at + step] for at in range(0, half, step)]
    total = parts[0]
    for part, distance in ((3, 6), (1, 4), (2, 2)):
        total = total + wide(swap(parts[part].astype(jnp.bfloat16), distance))
    return total


def shards(
    queries,
    cache,
    cache_len,
    residual_in,
    w_absorb,
    w_out,
    norm_gain,
    expert_ids,
    route_gates,
    w_gate,
    w_up,
    w_down,
):
    devices = lax.axis_size("experts")
    rank_here = lax.axis_index("experts")
    own_rows = queries.shape[0]
    all_rows = expert_ids.shape[0]
    far = devices // 8
    split_ways = FF // w_gate.shape[1]
    assert split_ways == 8

    latent = attend(queries, cache, cache_len, devices, w_absorb.shape[1])
    joined = lax.all_to_all(latent, "experts", split_axis=0, concat_axis=0, tiled=True)
    joined = joined.reshape(-1, joined.shape[-1])
    here = rank_here.astype(jnp.int32)[None]
    keep, send = project(here, joined, w_absorb, w_out, own_rows, all_rows, far)

    total = collect(keep, send)
    total = jnp.concatenate([total[:own_rows] + wide(residual_in), total[own_rows:]])
    sent = total.astype(jnp.bfloat16)
    for at in range(1, far):
        block = swap(sent, 8 * at)
        total = total + wide(
            jnp.concatenate(
                [block[(to ^ at) * own_rows : ((to ^ at) + 1) * own_rows] for to in range(far)]
            )
        )
    stream = total.astype(jnp.bfloat16)
    attended = stream[:own_rows]
    widened = wide(stream)
    inverse = lax.rsqrt(jnp.mean(widened * widened, axis=-1, keepdims=True) + 1e-06)
    normed = (widened * inverse * norm_gain).astype(jnp.bfloat16)

    other = {distance: swap(normed, distance) for distance in (6, 4, 2)}
    own = jnp.concatenate([normed, other[4], other[2], other[6]])
    keep, send = run_expert(own, swap(own, 1), w_gate, w_up, w_down)

    total = collect(keep, send)
    own_ids = lax.dynamic_slice_in_dim(expert_ids, rank_here * own_rows, own_rows, 0)
    expert_out = 0.0
    for at in range(far):
        block = total[at * own_rows : (at + 1) * own_rows]
        block = wide(swap(block.astype(jnp.bfloat16), 8 * at)) if at else block
        expert = (rank_here ^ (8 * at)) // split_ways
        mixing = jnp.sum(
            route_gates * (own_ids == expert).astype(jnp.float32), axis=1, keepdims=True
        )
        expert_out = expert_out + mixing * block
    return (attended, expert_out.astype(jnp.bfloat16))


def solution(mesh):
    placed = (
        P(("groups", "experts"), None, None),
        P(("groups", "experts"), None, None),
        P(("groups", "experts")),
        P(("groups", "experts"), None),
        P("experts", None, None),
        P("experts", None),
        P(),
        P("groups", None),
        P(("groups", "experts"), None),
        P(None, "experts"),
        P(None, "experts"),
        P("experts", None),
    )
    return jax.shard_map(
        shards,
        mesh=mesh,
        in_specs=placed,
        out_specs=(P(("groups", "experts"), None), P(("groups", "experts"), None)),
        check_vma=False,
    )
```

time: 145 us -> 81.7 us (0.56)
  blocking collectives: 97.2 us -> 0 us
  waiting for transfers between devices: 0.01 us -> 39.3 us
  matrix products: 38 us -> 0 us
  starting transfers between devices: 3.63 us -> 20.9 us
  Pallas kernels: 0 us -> 15 us
  local copies, waits for them, and re-layouts: 2.21 us -> 3.88 us
    all_gather x2 -> x0, blocking collectives: 54.8 us -> none  [the longest x1 31.1 us: shards(): gates_all = lax.all_gather(route_gates, 'experts', axis=0, tiled=True)]
    all_to_all x2 -> x0, blocking collectives: 42.4 us -> none  [the longest x1 25.1 us: shards(): lax.all_to_all(sent, 'experts', split_axis=0, concat_axis=0, tiled=True)]
    ppermute x0 -> x14, waiting for transfers between devices: none -> 29.3 us  [swap(): return lax.ppermute(array, 'experts', pairs)]
    dot_general x5 -> x0, matrix products: 25.3 us -> none  [the longest x1 12.3 us: shards(): jnp.einsum('rhp,rcp->rhc', soft_w, cache[:, :latent_rank, :], preferred_e...]
    pallas_call x0 -> x3, Pallas kernels: none -> 15 us  [the longest x1 10.8 us: attend(): pl.pallas_call(attend_kernel, out_shape=jax.ShapeDtypeStruct((devices, pa...]
    ppermute x0 -> x14, starting transfers between devices: none -> 13.3 us  [swap(): return lax.ppermute(array, 'experts', pairs)]
    sub x1 -> x0, matrix products: 12.6 us -> none  [shards(): soft_w = jax.nn.softmax(scores, axis=-1).astype(jnp.bfloat16)]
    all_to_all x1, waiting for transfers between devices: 0.01 us -> 10 us  [shards(): lax.all_to_all(latent, 'experts', split_axis=0, concat_axis=0, tiled=True)]
  transfers between devices with their start and end apart: 1 -> 15, of which waited for: 0 -> 15; matrix products, arithmetic and copies ran while one was open for 0% -> 1% of each run, Pallas kernels for 0% -> 0%
where the time goes in v4:
time: 81.7 us; the launch traced here: 81.5 us
  waiting for transfers between devices  39.3 us (48%)
  starting transfers between devices  20.9 us (26%)
  Pallas kernels  15 us (18%)
  local copies, waits for them, and re-layouts  3.88 us (5%)
  other arithmetic  1.58 us (2%)
  between operations  0.83 us (1%)
    ppermute x14, waiting for transfers between devices, swap(): return lax.ppermute(array, 'experts', pairs)  29.3 us
    ppermute x14, starting transfers between devices, swap(): return lax.ppermute(array, 'experts', pairs)  13.3 us
    pallas_call x1, Pallas kernels, attend(): pl.pallas_call(attend_kernel, out_shape=jax.ShapeDtypeStruct((devices, pa...  10.8 us
    all_to_all x1, waiting for transfers between devices, shards(): lax.all_to_all(latent, 'experts', split_axis=0, concat_axis=0, tiled=True)  10 us
    all_to_all x1, starting transfers between devices, shards(): lax.all_to_all(latent, 'experts', split_axis=0, concat_axis=0, tiled=True)  7.67 us
    unnamed x18, local copies, waits for them, and re-layouts  3.13 us
    pallas_call x1, Pallas kernels, run_expert(): pl.pallas_call(expert_kernel, out_shape=(jax.ShapeDtypeStruct((half, widt...  2.1 us
    pallas_call x1, Pallas kernels, project(): pl.pallas_call(functools.partial(project_kernel, own_rows, far), out_shap...  2.09 us
  transfers between devices with their start and end apart: 15, of which 15 were waited for; matrix products, arithmetic and copies ran while one was open for 1% of the time, Pallas kernels for 0%

profile of v4, /device:TPU:0, one launch (start us, length us, event | category | flops | bytes accessed | tf_op | source)
XLA Modules:
  0.0 81.5 jit_solution(2042064493712003524)
XLA Ops:
  0.6 10.8 %attend.1 = bf16[16,16,512]{2,1,0:T(8,128)(2,1)} custom-call(s32[4]{0:T(128)} %len_ref.1, bf16[4,64,576]{2,1,0:T(8,128)(2,1)} %bitcast.4, bf16[4,576,4096]{2,1,0:T(8,128)(2,1)} %cache_ref.1), custom_call_target="tpu_custom_call" | custom-call | flops 1140850688 | bytes 9437184 | tf_op jit(solution)/shard_map/attend/pallas_call | solution.py:157
  11.4 7.7 %all-to-all-start = ((bf16[16,16,512]{2,1,0:T(8,128)(2,1)}), bf16[16,16,512]{2,1,0:T(8,128)(2,1)S(1)}, u32[]{:S(2)}, u32[]{:S(2)}) async-start(bf16[16,16,512]{2,1,0:T(8,128)(2,1)} %attend.1), calls=%async_computation | async-start | bytes 524288 | tf_op jit(solution)/shard_map/all_to_all | solution.py:320
  19.1 10.0 %all-to-all-done = bf16[16,16,512]{2,1,0:T(8,128)(2,1)S(1)} async-done(((bf16[16,16,512]{2,1,0:T(8,128)(2,1)}), bf16[16,16,512]{2,1,0:T(8,128)(2,1)S(1)}, u32[]{:S(2)}, u32[]{:S(2)}) %all-to-all-start) | async-done | bytes 262176 | tf_op jit(solution)/shard_map/all_to_all | solution.py:320
  29.1 3.1 %copy-done = bf16[512,7168]{1,0:T(8,128)(2,1)S(1)} copy-done((bf16[512,7168]{1,0:T(8,128)(2,1)S(1)}, bf16[512,7168]{1,0:T(8,128)(2,1)}, u32[]{:S(2)}) %copy-start) | copy-done | bytes 7340056
  32.2 2.1 %project.1 = (f32[32,7168]{1,0:T(8,128)S(1)}, bf16[32,7168]{1,0:T(8,128)(2,1)S(1)}) custom-call(s32[1]{0:T(128)} %bitcast.here_ref, bf16[256,512]{1,0:T(8,128)(2,1)S(1)} %bitcast.3, bf16[4,512,128]{2,1,0:T(8,128)(2,1)S(1)} %copy-done.4, bf16[512,7168]{1,0:T(8,128)(2,1)S(1)} %copy-done), custom_call_target="tpu_custom_call" | custom-call | flops 469762048 | bytes 7340032 | tf_op jit(solution)/shard_map/project/pallas_call | solution.py:218
  34.4 1.8 %collective-permute-done = bf16[32,7168]{1,0:T(8,128)(2,1)S(1)} collective-permute-done((bf16[32,7168]{1,0:T(8,128)(2,1)S(1)}, bf16[32,7168]{1,0:T(8,128)(2,1)S(1)}, u32[]{:S(2)}, u32[]{:S(2)}) %collective-permute-start) | collective-permute-done | bytes 458784 | tf_op jit(solution)/shard_map/ppermute | solution.py:279
  37.6 2.3 %collective-permute-start.1 = (bf16[8,7168]{1,0:T(8,128)(2,1)S(1)}, bf16[8,7168]{1,0:T(8,128)(2,1)S(1)}, u32[]{:S(2)}, u32[]{:S(2)}) collective-permute-start(bf16[8,7168]{1,0:T(8,128)(2,1)S(1)} %get-tuple-element.21), channel_id=1, source_target_pairs={{0,6},{1,7},{2,4},{3,5},{4,2},{5,3},{6,0},{7,1},{8,14},{9,15},{10,... | collective-permute-start | bytes 344072 | tf_op jit(solution)/shard_map/ppermute | solution.py:279
  39.9 1.7 %collective-permute-done.3 = bf16[8,7168]{1,0:T(8,128)(2,1)S(1)} collective-permute-done((bf16[8,7168]{1,0:T(8,128)(2,1)S(1)}, bf16[8,7168]{1,0:T(8,128)(2,1)S(1)}, u32[]{:S(2)}, u32[]{:S(2)}) %collective-permute-start.3) | collective-permute-done | bytes 114720 | tf_op jit(solution)/shard_map/ppermute | solution.py:279
  41.6 1.0 %collective-permute-done.2 = bf16[8,7168]{1,0:T(8,128)(2,1)S(1)} collective-permute-done((bf16[8,7168]{1,0:T(8,128)(2,1)S(1)}, bf16[8,7168]{1,0:T(8,128)(2,1)S(1)}, u32[]{:S(2)}, u32[]{:S(2)}) %collective-permute-start.2) | collective-permute-done | bytes 114720 | tf_op jit(solution)/shard_map/ppermute | solution.py:279
  42.6 2.7 %collective-permute-done.1 = bf16[8,7168]{1,0:T(8,128)(2,1)S(1)} collective-permute-done((bf16[8,7168]{1,0:T(8,128)(2,1)S(1)}, bf16[8,7168]{1,0:T(8,128)(2,1)S(1)}, u32[]{:S(2)}, u32[]{:S(2)}) %collective-permute-start.1) | collective-permute-done | bytes 114720 | tf_op jit(solution)/shard_map/ppermute | solution.py:279
  45.4 1.1 %collective-permute-start.4 = (bf16[8,7168]{1,0:T(8,128)(2,1)S(1)}, bf16[8,7168]{1,0:T(8,128)(2,1)S(1)}, u32[]{:S(2)}, u32[]{:S(2)}) collective-permute-start(bf16[8,7168]{1,0:T(8,128)(2,1)S(1)} %fusion.7), channel_id=1, source_target_pairs={{0,8},{1,9},{2,10},{3,11},{4,12},{5,13},{6,14},{7,15},{8,0},{9,1},... | collective-permute-start | bytes 344072 | tf_op jit(solution)/shard_map/ppermute | solution.py:279
  46.6 6.3 %collective-permute-done.4 = bf16[8,7168]{1,0:T(8,128)(2,1)S(1)} collective-permute-done((bf16[8,7168]{1,0:T(8,128)(2,1)S(1)}, bf16[8,7168]{1,0:T(8,128)(2,1)S(1)}, u32[]{:S(2)}, u32[]{:S(2)}) %collective-permute-start.4) | collective-permute-done | bytes 114720 | tf_op jit(solution)/shard_map/ppermute | solution.py:279
  54.1 2.8 %collective-permute-start.5 = (bf16[8,7168]{1,0:T(8,128)(2,1)S(1)}, bf16[8,7168]{1,0:T(8,128)(2,1)S(1)}, u32[]{:S(2)}, u32[]{:S(2)}) collective-permute-start(bf16[8,7168]{1,0:T(8,128)(2,1)S(1)} %fusion.2), channel_id=1, source_target_pairs={{0,4},{1,5},{2,6},{3,7},{4,0},{5,1},{6,2},{7,3},{8,12},{9,13},{10,... | collective-permute-start | bytes 344072 | tf_op jit(solution)/shard_map/ppermute | solution.py:279
  56.9 3.1 %collective-permute-done.7 = bf16[8,7168]{1,0:T(8,128)(2,1)S(1)} collective-permute-done((bf16[8,7168]{1,0:T(8,128)(2,1)S(1)}, bf16[8,7168]{1,0:T(8,128)(2,1)S(1)}, u32[]{:S(2)}, u32[]{:S(2)}) %collective-permute-start.7) | collective-permute-done | bytes 114720 | tf_op jit(solution)/shard_map/ppermute | solution.py:279
  60.7 1.8 %collective-permute-done.8.other_ref = bf16[32,7168]{1,0:T(8,128)(2,1)S(1)} collective-permute-done((bf16[32,7168]{1,0:T(8,128)(2,1)S(1)}, bf16[32,7168]{1,0:T(8,128)(2,1)S(1)}, u32[]{:S(2)}, u32[]{:S(2)}) %collective-permute-start.8) | collective-permute-done | bytes 458784 | tf_op jit(solution)/shard_map/ppermute | solution.py:279
  62.5 2.1 %expert.1 = (f32[32,7168]{1,0:T(8,128)S(1)}, bf16[32,7168]{1,0:T(8,128)(2,1)S(1)}) custom-call(bf16[32,7168]{1,0:T(8,128)(2,1)S(1)} %pad_maximum_fusion.own_ref, bf16[32,7168]{1,0:T(8,128)(2,1)S(1)} %collective-permute-done.8.other_ref, bf16[7168,256]{1,0:T(8,128)(2,1)S(1)} %copy-done.1, bf16[7168,256]{1,0:T(8,128)(2,1)S(1)} %copy-done.2, ...), custom_call_target="tpu_custom_call" | custom-call | flops 704643072 | bytes 11010048 | tf_op jit(solution)/shard_map/expert/pallas_call | solution.py:259
  64.8 1.7 %collective-permute-done.9 = bf16[32,7168]{1,0:T(8,128)(2,1)S(1)} collective-permute-done((bf16[32,7168]{1,0:T(8,128)(2,1)S(1)}, bf16[32,7168]{1,0:T(8,128)(2,1)S(1)}, u32[]{:S(2)}, u32[]{:S(2)}) %collective-permute-start.9) | collective-permute-done | bytes 458784 | tf_op jit(solution)/shard_map/ppermute | solution.py:279
  66.6 1.2 %collective-permute-start.12 = (bf16[8,7168]{1,0:T(8,128)(2,1)S(1)}, bf16[8,7168]{1,0:T(8,128)(2,1)S(1)}, u32[]{:S(2)}, u32[]{:S(2)}) collective-permute-start(bf16[8,7168]{1,0:T(8,128)(2,1)S(1)} %get-tuple-element.19), channel_id=1, source_target_pairs={{0,2},{1,3},{2,0},{3,1},{4,6},{5,7},{6,4},{7,5},{8,10},{9,11},{10,... | collective-permute-start | bytes 344072 | tf_op jit(solution)/shard_map/ppermute | solution.py:279
  68.4 1.7 %collective-permute-start.10 = (bf16[8,7168]{1,0:T(8,128)(2,1)S(1)}, bf16[8,7168]{1,0:T(8,128)(2,1)S(1)}, u32[]{:S(2)}, u32[]{:S(2)}) collective-permute-start(bf16[8,7168]{1,0:T(8,128)(2,1)S(1)} %get-tuple-element.18), channel_id=1, source_target_pairs={{0,6},{1,7},{2,4},{3,5},{4,2},{5,3},{6,0},{7,1},{8,14},{9,15},{10,... | collective-permute-start | bytes 344072 | tf_op jit(solution)/shard_map/ppermute | solution.py:279
  70.2 1.7 %collective-permute-done.12 = bf16[8,7168]{1,0:T(8,128)(2,1)S(1)} collective-permute-done((bf16[8,7168]{1,0:T(8,128)(2,1)S(1)}, bf16[8,7168]{1,0:T(8,128)(2,1)S(1)}, u32[]{:S(2)}, u32[]{:S(2)}) %collective-permute-start.12) | collective-permute-done | bytes 114720 | tf_op jit(solution)/shard_map/ppermute | solution.py:279
  71.9 2.0 %collective-permute-done.11 = bf16[8,7168]{1,0:T(8,128)(2,1)S(1)} collective-permute-done((bf16[8,7168]{1,0:T(8,128)(2,1)S(1)}, bf16[8,7168]{1,0:T(8,128)(2,1)S(1)}, u32[]{:S(2)}, u32[]{:S(2)}) %collective-permute-start.11) | collective-permute-done | bytes 114720 | tf_op jit(solution)/shard_map/ppermute | solution.py:279
  73.9 1.7 %collective-permute-done.10 = bf16[8,7168]{1,0:T(8,128)(2,1)S(1)} collective-permute-done((bf16[8,7168]{1,0:T(8,128)(2,1)S(1)}, bf16[8,7168]{1,0:T(8,128)(2,1)S(1)}, u32[]{:S(2)}, u32[]{:S(2)}) %collective-permute-start.10) | collective-permute-done | bytes 114720 | tf_op jit(solution)/shard_map/ppermute | solution.py:279
  75.6 1.1 %collective-permute-start.13 = (bf16[4,7168]{1,0:T(4,128)(2,1)S(1)}, bf16[4,7168]{1,0:T(4,128)(2,1)S(1)}, u32[]{:S(2)}, u32[]{:S(2)}) collective-permute-start(bf16[4,7168]{1,0:T(4,128)(2,1)S(1)} %slice.99), channel_id=1, source_target_pairs={{0,8},{1,9},{2,10},{3,11},{4,12},{5,13},{6,14},{7,15},{8,0},{9,1},... | collective-permute-start | bytes 172040 | tf_op jit(solution)/shard_map/ppermute | solution.py:279
  77.5 3.3 %collective-permute-done.13 = bf16[4,7168]{1,0:T(4,128)(2,1)S(1)} collective-permute-done((bf16[4,7168]{1,0:T(4,128)(2,1)S(1)}, bf16[4,7168]{1,0:T(4,128)(2,1)S(1)}, u32[]{:S(2)}, u32[]{:S(2)}) %collective-permute-start.13) | collective-permute-done | bytes 57376 | tf_op jit(solution)/shard_map/ppermute | solution.py:279
  (44 shorter events, 6.0 us)
Async XLA Ops:
  0.6 28.5 %copy-start.4 = (bf16[4,512,128]{2,1,0:T(8,128)(2,1)S(1)}, bf16[4,512,128]{2,1,0:T(8,128)(2,1)}, u32[]{:S(2)}) copy-start(bf16[4,512,128]{2,1,0:T(8,128)(2,1)} %absorb_ref.1) | copy-start | bytes 1572868
  11.4 17.7 %all-to-all-start = ((bf16[16,16,512]{2,1,0:T(8,128)(2,1)}), bf16[16,16,512]{2,1,0:T(8,128)(2,1)S(1)}, u32[]{:S(2)}, u32[]{:S(2)}) async-start(bf16[16,16,512]{2,1,0:T(8,128)(2,1)} %attend.1), calls=%async_computation | async-start | bytes 524288 | tf_op jit(solution)/shard_map/all_to_all | solution.py:320
  29.1 3.1 %copy-start = (bf16[512,7168]{1,0:T(8,128)(2,1)S(1)}, bf16[512,7168]{1,0:T(8,128)(2,1)}, u32[]{:S(2)}) copy-start(bf16[512,7168]{1,0:T(8,128)(2,1)} %w_ref.1) | copy-start | bytes 22020100
  32.2 30.2 %copy-start.2 = (bf16[7168,256]{1,0:T(8,128)(2,1)S(1)}, bf16[7168,256]{1,0:T(8,128)(2,1)}, u32[]{:S(2)}) copy-start(bf16[7168,256]{1,0:T(8,128)(2,1)} %up_ref.1) | copy-start | bytes 11010052
  32.2 30.2 %copy-start.3 = (bf16[256,7168]{1,0:T(8,128)(2,1)S(1)}, bf16[256,7168]{1,0:T(8,128)(2,1)}, u32[]{:S(2)}) copy-start(bf16[256,7168]{1,0:T(8,128)(2,1)} %down_ref.1) | copy-start | bytes 11010052
  34.3 11.0 %copy-start.5 = (bf16[4,7168]{1,0:T(4,128)(2,1)S(1)}, bf16[4,7168]{1,0:T(4,128)(2,1)}, u32[]{:S(2)}) copy-start(bf16[4,7168]{1,0:T(4,128)(2,1)} %param.15) | copy-start | bytes 172036
  34.3 18.9 %copy-start.6 = (f32[7168]{0:T(1024)S(1)}, f32[7168]{0:T(1024)}, u32[]{:S(2)}) copy-start(f32[7168]{0:T(1024)} %param.18) | copy-start | bytes 86020
  34.3 28.1 %copy-start.1 = (bf16[7168,256]{1,0:T(8,128)(2,1)S(1)}, bf16[7168,256]{1,0:T(8,128)(2,1)}, u32[]{:S(2)}) copy-start(bf16[7168,256]{1,0:T(8,128)(2,1)} %gate_ref.1) | copy-start | bytes 11010052
  34.4 1.9 %collective-permute-start = (bf16[32,7168]{1,0:T(8,128)(2,1)S(1)}, bf16[32,7168]{1,0:T(8,128)(2,1)S(1)}, u32[]{:S(2)}, u32[]{:S(2)}) collective-permute-start(bf16[32,7168]{1,0:T(8,128)(2,1)S(1)} %get-tuple-element.7), channel_id=1, source_target_pairs={{0,1},{1,0},{2,3},{3,2},{4,5},{5,4},{6,7},{7,6},{8,9},{9,8},{10,11... | collective-permute-start | bytes 1376264 | tf_op jit(solution)/shard_map/ppermute | solution.py:279
  36.4 5.3 %collective-permute-start.3 = (bf16[8,7168]{1,0:T(8,128)(2,1)S(1)}, bf16[8,7168]{1,0:T(8,128)(2,1)S(1)}, u32[]{:S(2)}, u32[]{:S(2)}) collective-permute-start(bf16[8,7168]{1,0:T(8,128)(2,1)S(1)} %get-tuple-element.22), channel_id=1, source_target_pairs={{0,2},{1,3},{2,0},{3,1},{4,6},{5,7},{6,4},{7,5},{8,10},{9,11},{10,... | collective-permute-start | bytes 344072 | tf_op jit(solution)/shard_map/ppermute | solution.py:279
  36.6 6.0 %collective-permute-start.2 = (bf16[8,7168]{1,0:T(8,128)(2,1)S(1)}, bf16[8,7168]{1,0:T(8,128)(2,1)S(1)}, u32[]{:S(2)}, u32[]{:S(2)}) collective-permute-start(bf16[8,7168]{1,0:T(8,128)(2,1)S(1)} %get-tuple-element.23), channel_id=1, source_target_pairs={{0,4},{1,5},{2,6},{3,7},{4,0},{5,1},{6,2},{7,3},{8,12},{9,13},{10,... | collective-permute-start | bytes 344072 | tf_op jit(solution)/shard_map/ppermute | solution.py:279
  37.6 7.7 %collective-permute-start.1 = (bf16[8,7168]{1,0:T(8,128)(2,1)S(1)}, bf16[8,7168]{1,0:T(8,128)(2,1)S(1)}, u32[]{:S(2)}, u32[]{:S(2)}) collective-permute-start(bf16[8,7168]{1,0:T(8,128)(2,1)S(1)} %get-tuple-element.21), channel_id=1, source_target_pairs={{0,6},{1,7},{2,4},{3,5},{4,2},{5,3},{6,0},{7,1},{8,14},{9,15},{10,... | collective-permute-start | bytes 344072 | tf_op jit(solution)/shard_map/ppermute | solution.py:279
  45.4 7.5 %collective-permute-start.4 = (bf16[8,7168]{1,0:T(8,128)(2,1)S(1)}, bf16[8,7168]{1,0:T(8,128)(2,1)S(1)}, u32[]{:S(2)}, u32[]{:S(2)}) collective-permute-start(bf16[8,7168]{1,0:T(8,128)(2,1)S(1)} %fusion.7), channel_id=1, source_target_pairs={{0,8},{1,9},{2,10},{3,11},{4,12},{5,13},{6,14},{7,15},{8,0},{9,1},... | collective-permute-start | bytes 344072 | tf_op jit(solution)/shard_map/ppermute | solution.py:279
  53.3 6.6 %collective-permute-start.7 = (bf16[8,7168]{1,0:T(8,128)(2,1)S(1)}, bf16[8,7168]{1,0:T(8,128)(2,1)S(1)}, u32[]{:S(2)}, u32[]{:S(2)}) collective-permute-start(bf16[8,7168]{1,0:T(8,128)(2,1)S(1)} %fusion.2), channel_id=1, source_target_pairs={{0,6},{1,7},{2,4},{3,5},{4,2},{5,3},{6,0},{7,1},{8,14},{9,15},{10,... | collective-permute-start | bytes 344072 | tf_op jit(solution)/shard_map/ppermute | solution.py:279
  53.4 6.9 %collective-permute-start.6 = (bf16[8,7168]{1,0:T(8,128)(2,1)S(1)}, bf16[8,7168]{1,0:T(8,128)(2,1)S(1)}, u32[]{:S(2)}, u32[]{:S(2)}) collective-permute-start(bf16[8,7168]{1,0:T(8,128)(2,1)S(1)} %fusion.2), channel_id=1, source_target_pairs={{0,2},{1,3},{2,0},{3,1},{4,6},{5,7},{6,4},{7,5},{8,10},{9,11},{10,... | collective-permute-start | bytes 344072 | tf_op jit(solution)/shard_map/ppermute | solution.py:279
  54.1 6.5 %collective-permute-start.5 = (bf16[8,7168]{1,0:T(8,128)(2,1)S(1)}, bf16[8,7168]{1,0:T(8,128)(2,1)S(1)}, u32[]{:S(2)}, u32[]{:S(2)}) collective-permute-start(bf16[8,7168]{1,0:T(8,128)(2,1)S(1)} %fusion.2), channel_id=1, source_target_pairs={{0,4},{1,5},{2,6},{3,7},{4,0},{5,1},{6,2},{7,3},{8,12},{9,13},{10,... | collective-permute-start | bytes 344072 | tf_op jit(solution)/shard_map/ppermute | solution.py:279
  60.6 1.9 %collective-permute-start.8 = (bf16[32,7168]{1,0:T(8,128)(2,1)S(1)}, bf16[32,7168]{1,0:T(8,128)(2,1)S(1)}, u32[]{:S(2)}, u32[]{:S(2)}) collective-permute-start(bf16[32,7168]{1,0:T(8,128)(2,1)S(1)} %pad_maximum_fusion.own_ref), channel_id=1, source_target_pairs={{0,1},{1,0},{2,3},{3,2},{4,5},{5,4},{6,7},{7,6},{8,9},{9,8},{10,11... | collective-permute-start | bytes 1376264 | tf_op jit(solution)/shard_map/ppermute | solution.py:279
  64.6 12.2 %copy-start.7 = (f32[4,2]{0,1:T(2,128)S(1)}, f32[4,2]{0,1:T(2,128)}, u32[]{:S(2)}) copy-start(f32[4,2]{0,1:T(2,128)} %param.20) | copy-start | bytes 100
  64.6 12.2 %copy-start.8 = (s32[64,2]{0,1:T(2,128)S(1)}, s32[64,2]{0,1:T(2,128)}, u32[]{:S(2)}) copy-start(s32[64,2]{0,1:T(2,128)} %param.19) | copy-start | bytes 1540
  64.6 1.9 %collective-permute-start.9 = (bf16[32,7168]{1,0:T(8,128)(2,1)S(1)}, bf16[32,7168]{1,0:T(8,128)(2,1)S(1)}, u32[]{:S(2)}, u32[]{:S(2)}) collective-permute-start(bf16[32,7168]{1,0:T(8,128)(2,1)S(1)} %get-tuple-element.9), channel_id=1, source_target_pairs={{0,1},{1,0},{2,3},{3,2},{4,5},{5,4},{6,7},{7,6},{8,9},{9,8},{10,11... | collective-permute-start | bytes 1376264 | tf_op jit(solution)/shard_map/ppermute | solution.py:279
  66.6 5.3 %collective-permute-start.12 = (bf16[8,7168]{1,0:T(8,128)(2,1)S(1)}, bf16[8,7168]{1,0:T(8,128)(2,1)S(1)}, u32[]{:S(2)}, u32[]{:S(2)}) collective-permute-start(bf16[8,7168]{1,0:T(8,128)(2,1)S(1)} %get-tuple-element.19), channel_id=1, source_target_pairs={{0,2},{1,3},{2,0},{3,1},{4,6},{5,7},{6,4},{7,5},{8,10},{9,11},{10,... | collective-permute-start | bytes 344072 | tf_op jit(solution)/shard_map/ppermute | solution.py:279
  67.8 6.0 %collective-permute-start.11 = (bf16[8,7168]{1,0:T(8,128)(2,1)S(1)}, bf16[8,7168]{1,0:T(8,128)(2,1)S(1)}, u32[]{:S(2)}, u32[]{:S(2)}) collective-permute-start(bf16[8,7168]{1,0:T(8,128)(2,1)S(1)} %get-tuple-element.20), channel_id=1, source_target_pairs={{0,4},{1,5},{2,6},{3,7},{4,0},{5,1},{6,2},{7,3},{8,12},{9,13},{10,... | collective-permute-start | bytes 344072 | tf_op jit(solution)/shard_map/ppermute | solution.py:279
  68.4 7.1 %collective-permute-start.10 = (bf16[8,7168]{1,0:T(8,128)(2,1)S(1)}, bf16[8,7168]{1,0:T(8,128)(2,1)S(1)}, u32[]{:S(2)}, u32[]{:S(2)}) collective-permute-start(bf16[8,7168]{1,0:T(8,128)(2,1)S(1)} %get-tuple-element.18), channel_id=1, source_target_pairs={{0,6},{1,7},{2,4},{3,5},{4,2},{5,3},{6,0},{7,1},{8,14},{9,15},{10,... | collective-permute-start | bytes 344072 | tf_op jit(solution)/shard_map/ppermute | solution.py:279
  75.6 5.2 %collective-permute-start.13 = (bf16[4,7168]{1,0:T(4,128)(2,1)S(1)}, bf16[4,7168]{1,0:T(4,128)(2,1)S(1)}, u32[]{:S(2)}, u32[]{:S(2)}) collective-permute-start(bf16[4,7168]{1,0:T(4,128)(2,1)S(1)} %slice.99), channel_id=1, source_target_pairs={{0,8},{1,9},{2,10},{3,11},{4,12},{5,13},{6,14},{7,15},{8,0},{9,1},... | collective-permute-start | bytes 172040 | tf_op jit(solution)/shard_map/ppermute | solution.py:279

commit v5 on v4

v5 whole, which is shorter than its diff:
```python
import functools

import jax
import jax.numpy as jnp
from jax import lax
from jax.experimental import pallas as pl
from jax.experimental.pallas import tpu as pltpu
from jax.sharding import PartitionSpec as P

QK = 192
FF = 2048
BLOCK = 512
GROUP = 4
LANES = 128
TILE = 256
PARTS = 4
MIB = 2**20


def lane_tiles(array):
    return [array[:, at : at + LANES] for at in range(0, array.shape[1], LANES)]


def attend_kernel(
    len_ref,
    queries_ref,
    cache_ref,
    latent_ref,
    length,
    queries,
    held,
    products,
    highest,
    sums,
    factors,
    staged,
    item_row,
    item_block,
    length_arrived,
    queries_arrived,
    arrived,
):
    own_rows, heads, _ = queries.shape
    devices, _, rank = staged.shape
    own_heads = heads // devices
    blocks = held.shape[1]

    length_copy = pltpu.make_async_copy(len_ref, length, length_arrived)
    length_copy.start()
    queries_copy = pltpu.make_async_copy(queries_ref, queries, queries_arrived)
    queries_copy.start()

    def block_copy(row, block):
        return pltpu.make_async_copy(
            cache_ref.at[row, :, pl.ds(pl.multiple_of(block * BLOCK, BLOCK), BLOCK)],
            held.at[row, block],
            arrived.at[row, block],
        )

    highest[...] = jnp.full_like(highest, -jnp.inf)
    sums[...] = jnp.zeros_like(sums)
    length_copy.wait()
    items = 0
    counts = []
    for row in range(own_rows):
        count = (length[row] + BLOCK - 1) // BLOCK

        def begin(block, first, row=row):
            block_copy(row, block).start()
            item_row[first + block] = row
            item_block[first + block] = block
            return first

        lax.fori_loop(0, count, begin, items)
        counts.append(count)
        items = items + count
    for at in range(GROUP - 1):
        item_row[items + at] = own_rows - 1
        item_block[items + at] = item_block[items - 1]
    groups = (items + GROUP - 1) // GROUP
    queries_copy.wait()
    column = lax.broadcasted_iota(jnp.int32, (heads, BLOCK), 1)

    def visit(group, _):
        inside = [
            (group * GROUP + at, item_row[group * GROUP + at], item_block[group * GROUP + at])
            for at in range(GROUP)
        ]
        for at, row, block in inside:
            pl.when(at < items)(lambda row=row, block=block: block_copy(row, block).wait())
        found = []
        for _, row, block in inside:
            score = jnp.dot(
                queries[row], held[row, block], preferred_element_type=jnp.float32
            ) * QK ** (-0.5)
            found.append(
                jnp.where(column + block * BLOCK < length[row], score, -jnp.inf)
            )
        tops = [
            jnp.max(functools.reduce(jnp.maximum, lane_tiles(score)), axis=1, keepdims=True)
            for score in found
        ]
        weights = [jnp.exp(score - top) for score, top in zip(found, tops)]
        for (_, row, block), top, weight in zip(inside, tops, weights):
            highest[row, block] = jnp.broadcast_to(top, (heads, LANES))
            sums[row, block] = sum(lane_tiles(weight))
            products[row, block] = lax.dot_general(
                weight.astype(jnp.bfloat16),
                held[row, block, :rank, :],
                (((1,), (1,)), ((), ())),
                preferred_element_type=jnp.float32,
            )
        return 0

    lax.fori_loop(0, groups, visit, 0)
    for row in range(own_rows):
        factor = jnp.exp(highest[row] - jnp.max(highest[row], axis=0, keepdims=True))
        total = jnp.sum(jnp.sum(sums[row] * factor, axis=0), axis=1, keepdims=True)
        factors[row] = factor * (1.0 / total)[None]
    for row in range(own_rows):

        def merge(block, latent, row=row):
            return latent + products[row, block] * factors[row, block][:, :1]

        latent = lax.fori_loop(
            0, counts[row], merge, jnp.zeros((heads, rank), jnp.float32)
        )
        for device in range(devices):
            staged[device, row * own_heads : (row + 1) * own_heads, :] = latent[
                device * own_heads : (device + 1) * own_heads
            ]
    latent_ref[...] = staged[...].astype(latent_ref.dtype)


def attend(queries, cache, cache_len, devices, rank):
    own_rows, depth, heads = queries.shape
    blocks = cache.shape[2] // BLOCK
    packed = own_rows * heads // devices
    listed = own_rows * blocks + GROUP
    return pl.pallas_call(
        attend_kernel,
        out_shape=jax.ShapeDtypeStruct((devices, packed, rank), jnp.bfloat16),
        in_specs=[pl.BlockSpec(memory_space=pl.ANY)] * 3,
        out_specs=pl.BlockSpec(memory_space=pltpu.VMEM),
        scratch_shapes=[
            pltpu.SMEM((own_rows,), jnp.int32),
            pltpu.VMEM((own_rows, heads, depth), jnp.bfloat16),
            pltpu.VMEM((own_rows, blocks, depth, BLOCK), jnp.bfloat16),
            pltpu.VMEM((own_rows, blocks, heads, rank), jnp.float32),
            pltpu.VMEM((own_rows, blocks, heads, LANES), jnp.float32),
            pltpu.VMEM((own_rows, blocks, heads, LANES), jnp.float32),
            pltpu.VMEM((own_rows, blocks, heads, LANES), jnp.float32),
            pltpu.VMEM((devices, packed, rank), jnp.float32),
            pltpu.SMEM((listed,), jnp.int32),
            pltpu.SMEM((listed,), jnp.int32),
            pltpu.SemaphoreType.DMA,
            pltpu.SemaphoreType.DMA,
            pltpu.SemaphoreType.DMA((own_rows, blocks)),
        ],
        compiler_params=pltpu.CompilerParams(vmem_limit_bytes=58 * MIB),
        cost_estimate=pl.CostEstimate(
            flops=own_rows * heads * cache.shape[2] * (depth + rank),
            bytes_accessed=cache.size,
            transcendentals=own_rows * heads * cache.shape[2],
        ),
        name="attend",
    )(cache_len, jnp.swapaxes(queries, 1, 2), cache)


def store_sides(term, at, keeps, sends):
    half, side = keeps[0].shape
    keep, send, at = keeps[at // side], sends[at // side], at % side
    keep[:, at : at + TILE] = term[:half]
    send[:, at : at + TILE] = term[half:].astype(send.dtype)


def side_shapes(half, width):
    return tuple(
        jax.ShapeDtypeStruct((half, width // 2), kind)
        for kind in (jnp.float32, jnp.bfloat16)
        for _ in range(2)
    )


def project_kernel(
    own_rows,
    far,
    here_ref,
    joined_ref,
    absorb_ref,
    residual_ref,
    w_ref,
    first_keep,
    second_keep,
    first_send,
    second_send,
    held,
    arrived,
):
    own_heads = absorb_ref.shape[0]
    half, side = first_keep.shape
    width = 2 * side
    part_width = width // PARTS
    copies = [
        pltpu.make_async_copy(
            w_ref.at[:, part * part_width : (part + 1) * part_width],
            held.at[:, part * part_width : (part + 1) * part_width],
            arrived.at[part],
        )
        for part in range(PARTS)
    ]
    for copy in copies:
        copy.start()
    shape = (2 * half, joined_ref.shape[0])
    row = lax.broadcasted_iota(jnp.int32, shape, 0)
    place = lax.broadcasted_iota(jnp.int32, shape, 1)
    turn = own_rows.bit_length() - 1
    far_bits = far.bit_length() - 1
    request, slot = row & (own_rows - 1), row >> turn
    far_at, slot = slot & (far - 1), slot >> far_bits
    distance = (far_at << 3) + ((slot & 1) << 2) + ((slot >> 1 & 1) << 1) + (slot >> 2)
    device = distance ^ here_ref[0]
    values = []
    for head in range(own_heads):
        wanted = ((device << turn) + request) * own_heads + head
        choice = (place == wanted).astype(jnp.float32).astype(jnp.bfloat16)
        latent = jnp.dot(choice, joined_ref[...], preferred_element_type=jnp.float32)
        value = jnp.dot(
            latent.astype(jnp.bfloat16), absorb_ref[head], preferred_element_type=jnp.float32
        )
        values.append(value.astype(jnp.bfloat16))
    values = jnp.concatenate(values, axis=1)
    for part in range(PARTS):
        copies[part].wait()
        for at in range(part * part_width, (part + 1) * part_width, TILE):
            term = jnp.dot(values, held[:, at : at + TILE], preferred_element_type=jnp.float32)
            store_sides(term, at, (first_keep, second_keep), (first_send, second_send))
    for at, keep in ((0, first_keep), (side, second_keep)):
        residual = residual_ref[:, at : at + side].astype(jnp.float32)
        keep[:own_rows, :] = keep[:own_rows, :] + residual


def project(here, joined, w_absorb, residual_in, w_out, rows, far):
    depth, width = w_out.shape
    own_rows = residual_in.shape[0]
    return pl.pallas_call(
        functools.partial(project_kernel, own_rows, far),
        out_shape=side_shapes(rows // 2, width),
        in_specs=[pl.BlockSpec(memory_space=pltpu.SMEM)]
        + [pl.BlockSpec(memory_space=pltpu.VMEM)] * 3
        + [pl.BlockSpec(memory_space=pl.ANY)],
        out_specs=(pl.BlockSpec(memory_space=pltpu.VMEM),) * 4,
        scratch_shapes=[
            pltpu.VMEM((depth, width), jnp.bfloat16),
            pltpu.SemaphoreType.DMA((PARTS,)),
        ],
        compiler_params=pltpu.CompilerParams(vmem_limit_bytes=55 * MIB),
        cost_estimate=pl.CostEstimate(
            flops=2 * rows * depth * width, bytes_accessed=2 * depth * width, transcendentals=0
        ),
        name="project",
    )(here, joined, w_absorb, residual_in, w_out)


def expert_kernel(
    first_own,
    first_other,
    second_own,
    second_other,
    gain_ref,
    gate_ref,
    up_ref,
    down_ref,
    first_keep,
    second_keep,
    first_send,
    second_send,
):
    half, side = first_own.shape
    width = 2 * side
    depth = width // PARTS
    streams = ((first_own, second_own), (first_other, second_other))
    inverses = []
    for stream in streams:
        squares = 0.0
        for ref in stream:
            for at in range(0, side, depth):
                piece = ref[:, at : at + depth].astype(jnp.float32)
                squares = squares + sum(lane_tiles(piece * piece))
        mean = jnp.sum(squares, axis=1, keepdims=True) / width
        inverses.append(lax.rsqrt(mean + 1e-06))
    gate, up = 0.0, 0.0
    for part in range(PARTS):
        at, place = part * depth, part * depth % side
        gain = gain_ref[:, at : at + depth]
        tokens = jnp.concatenate(
            [
                (
                    stream[at // side][:, place : place + depth].astype(jnp.float32)
                    * inverse
                    * gain
                ).astype(jnp.bfloat16)
                for stream, inverse in zip(streams, inverses)
            ],
            axis=0,
        )
        gate = gate + jnp.dot(
            tokens, gate_ref[at : at + depth, :], preferred_element_type=jnp.float32
        )
        up = up + jnp.dot(
            tokens, up_ref[at : at + depth, :], preferred_element_type=jnp.float32
        )
    active = (gate / (1.0 + jnp.exp(-gate)) * up).astype(jnp.bfloat16)
    for at in range(0, width, TILE):
        term = jnp.dot(active, down_ref[:, at : at + TILE], preferred_element_type=jnp.float32)
        store_sides(term, at, (first_keep, second_keep), (first_send, second_send))


def run_expert(streams, norm_gain, w_gate, w_up, w_down):
    half, side = streams[0].shape
    hidden = w_gate.shape[1]
    return pl.pallas_call(
        expert_kernel,
        out_shape=side_shapes(half, 2 * side),
        in_specs=[pl.BlockSpec(memory_space=pltpu.VMEM)] * 8,
        out_specs=(pl.BlockSpec(memory_space=pltpu.VMEM),) * 4,
        compiler_params=pltpu.CompilerParams(vmem_limit_bytes=24 * MIB),
        cost_estimate=pl.CostEstimate(
            flops=24 * half * hidden * side,
            bytes_accessed=12 * hidden * side,
            transcendentals=2 * half * hidden,
        ),
        name="expert",
    )(*streams, norm_gain[None], w_gate, w_up, w_down)


def swap(array, distance):
    pairs = [(at, at ^ distance) for at in range(lax.axis_size("experts"))]
    return lax.ppermute(array, "experts", pairs)


def wide(array):
    return array.astype(jnp.float32)


def collect(keep, send):
    half = keep.shape[0]
    step = half // 4
    whole = keep + wide(swap(send, 1))
    parts = [whole[at : at + step] for at in range(0, half, step)]
    total = parts[0]
    for part, distance in ((3, 6), (1, 4), (2, 2)):
        total = total + wide(swap(parts[part].astype(jnp.bfloat16), distance))
    return total


def exchange(total, far):
    own_rows = total.shape[0] // far
    sent = total.astype(jnp.bfloat16)
    for at in range(1, far):
        block = swap(sent, 8 * at)
        total = total + wide(
            jnp.concatenate(
                [block[(to ^ at) * own_rows : ((to ^ at) + 1) * own_rows] for to in range(far)]
            )
        )
    return total.astype(jnp.bfloat16)


def spread(stream):
    other = {distance: swap(stream, distance) for distance in (6, 4, 2)}
    own = jnp.concatenate([stream, other[4], other[2], other[6]])
    return own, swap(own, 1)


def shards(
    queries,
    cache,
    cache_len,
    residual_in,
    w_absorb,
    w_out,
    norm_gain,
    expert_ids,
    route_gates,
    w_gate,
    w_up,
    w_down,
):
    devices = lax.axis_size("experts")
    rank_here = lax.axis_index("experts")
    own_rows = queries.shape[0]
    all_rows = expert_ids.shape[0]
    far = devices // 8
    split_ways = FF // w_gate.shape[1]
    assert split_ways == 8

    latent = attend(queries, cache, cache_len, devices, w_absorb.shape[1])
    joined = lax.all_to_all(latent, "experts", split_axis=0, concat_axis=0, tiled=True)
    joined = joined.reshape(-1, joined.shape[-1])
    here = rank_here.astype(jnp.int32)[None]
    sides = project(here, joined, w_absorb, residual_in, w_out, all_rows, far)
    attended, streams = [], []
    for at in range(2):
        total = collect(sides[at], sides[at + 2])
        stream = exchange(total, far)
        attended.append(stream[:own_rows])
        streams.extend(spread(stream))
    attended = jnp.concatenate(attended, axis=1)

    sides = run_expert(streams, norm_gain, w_gate, w_up, w_down)
    own_ids = lax.dynamic_slice_in_dim(expert_ids, rank_here * own_rows, own_rows, 0)
    mixings = []
    for at in range(far):
        expert = (rank_here ^ (8 * at)) // split_ways
        mixings.append(
            jnp.sum(
                route_gates * (own_ids == expert).astype(jnp.float32), axis=1, keepdims=True
            )
        )
    expert_out = []
    for at in range(2):
        total = collect(sides[at], sides[at + 2])
        mixed = mixings[0] * total[:own_rows]
        for to in range(1, far):
            block = total[to * own_rows : (to + 1) * own_rows].astype(jnp.bfloat16)
            mixed = mixed + mixings[to] * wide(swap(block, 8 * to))
        expert_out.append(mixed.astype(jnp.bfloat16))
    return (attended, jnp.concatenate(expert_out, axis=1))


def solution(mesh):
    placed = (
        P(("groups", "experts"), None, None),
        P(("groups", "experts"), None, None),
        P(("groups", "experts")),
        P(("groups", "experts"), None),
        P("experts", None, None),
        P("experts", None),
        P(),
        P("groups", None),
        P(("groups", "experts"), None),
        P(None, "experts"),
        P(None, "experts"),
        P("experts", None),
    )
    return jax.shard_map(
        shards,
        mesh=mesh,
        in_specs=placed,
        out_specs=(P(("groups", "experts"), None), P(("groups", "experts"), None)),
        check_vma=False,
    )
```

time: 81.7 us -> 85.6 us (1.048); the launches traced: 81.5 us -> 84.1 us
  waiting for transfers between devices: 39.3 us -> 26.1 us
  starting transfers between devices: 20.9 us -> 33.6 us
  Pallas kernels: 15 us -> 18.6 us
  local copies, waits for them, and re-layouts: 3.88 us -> 0.88 us
  other arithmetic: 1.58 us -> 4.03 us
    ppermute x14 -> x28, starting transfers between devices: 13.3 us -> 27 us  [swap(): return lax.ppermute(array, 'experts', pairs)]
    ppermute x14 -> x28, waiting for transfers between devices: 29.3 us -> 16.1 us  [swap(): return lax.ppermute(array, 'experts', pairs)]
    pallas_call x1, Pallas kernels: 2.09 us -> 6.58 us  [project(): pl.pallas_call(functools.partial(project_kernel, own_rows, far), out_shap...]
    unnamed x18 -> x14, local copies, waits for them, and re-layouts: 3.13 us -> 0.73 us
    another operation x2 -> x4, other arithmetic: 0.19 us -> 2.25 us
    concatenate x1 -> x4, other arithmetic: 0.03 us -> 1.33 us  [the longest x1 0.65 us: shards(): return (attended, jnp.concatenate(expert_out, axis=1))]
    pallas_call x1, Pallas kernels: 10.8 us -> 9.63 us  [attend(): pl.pallas_call(attend_kernel, out_shape=jax.ShapeDtypeStruct((devices, pa...]
    all_to_all x1, starting transfers between devices: 7.67 us -> 6.57 us  [shards(): lax.all_to_all(latent, 'experts', split_axis=0, concat_axis=0, tiled=True)]
  transfers between devices with their start and end apart: 15 -> 29, of which waited for: 15 -> 14; matrix products, arithmetic and copies ran while one was open for 1% -> 4% of each run, Pallas kernels for 0% -> 0%
where the time goes in v5:
time: 85.6 us; the launch traced here: 84.1 us
  starting transfers between devices  33.6 us (39%)
  waiting for transfers between devices  26.1 us (30%)
  Pallas kernels  18.6 us (22%)
  other arithmetic  4.03 us (5%)
  between operations  0.89 us (1%)
  local copies, waits for them, and re-layouts  0.88 us (1%)
    ppermute x28, starting transfers between devices, swap(): return lax.ppermute(array, 'experts', pairs)  27 us
    ppermute x28, waiting for transfers between devices, swap(): return lax.ppermute(array, 'experts', pairs)  16.1 us
    all_to_all x1, waiting for transfers between devices, shards(): lax.all_to_all(latent, 'experts', split_axis=0, concat_axis=0, tiled=True)  10 us
    pallas_call x1, Pallas kernels, attend(): pl.pallas_call(attend_kernel, out_shape=jax.ShapeDtypeStruct((devices, pa...  9.63 us
    pallas_call x1, Pallas kernels, project(): pl.pallas_call(functools.partial(project_kernel, own_rows, far), out_shap...  6.58 us
    all_to_all x1, starting transfers between devices, shards(): lax.all_to_all(latent, 'experts', split_axis=0, concat_axis=0, tiled=True)  6.57 us
    pallas_call x1, Pallas kernels, run_expert(): pl.pallas_call(expert_kernel, out_shape=side_shapes(half, 2 * side), in_s...  2.34 us
    another operation x4, other arithmetic  2.25 us
  transfers between devices with their start and end apart: 29, of which 14 were waited for; matrix products, arithmetic and copies ran while one was open for 4% of the time, Pallas kernels for 0%

profile of v5, /device:TPU:0, one launch (start us, length us, event | category | flops | bytes accessed | tf_op | source)
XLA Modules:
  0.0 84.1 jit_solution(9781121460100639748)
XLA Ops:
  0.6 9.6 %attend.1 = bf16[16,16,512]{2,1,0:T(8,128)(2,1)} custom-call(s32[4]{0:T(128)} %len_ref.1, bf16[4,64,576]{2,1,0:T(8,128)(2,1)} %bitcast.6, bf16[4,576,4096]{2,1,0:T(8,128)(2,1)} %cache_ref.1), custom_call_target="tpu_custom_call" | custom-call | flops 1140850688 | bytes 9437184 | tf_op jit(solution)/shard_map/attend/pallas_call | solution.py:140
  10.3 6.6 %all-to-all-start = ((bf16[16,16,512]{2,1,0:T(8,128)(2,1)}), bf16[16,16,512]{2,1,0:T(8,128)(2,1)S(1)}, u32[]{:S(2)}, u32[]{:S(2)}) async-start(bf16[16,16,512]{2,1,0:T(8,128)(2,1)} %attend.1), calls=%async_computation | async-start | bytes 524288 | tf_op jit(solution)/shard_map/all_to_all | solution.py:399
  16.9 10.0 %all-to-all-done = bf16[16,16,512]{2,1,0:T(8,128)(2,1)S(1)} async-done(((bf16[16,16,512]{2,1,0:T(8,128)(2,1)}), bf16[16,16,512]{2,1,0:T(8,128)(2,1)S(1)}, u32[]{:S(2)}, u32[]{:S(2)}) %all-to-all-start) | async-done | bytes 262176 | tf_op jit(solution)/shard_map/all_to_all | solution.py:399
  27.6 6.6 %project.1 = (f32[32,3584]{1,0:T(8,128)}, f32[32,3584]{1,0:T(8,128)}, bf16[32,3584]{1,0:T(8,128)(2,1)}, bf16[32,3584]{1,0:T(8,128)(2,1)}) custom-call(s32[1]{0:T(128)} %bitcast.here_ref, bf16[256,512]{1,0:T(8,128)(2,1)} %bitcast.5, bf16[4,512,128]{2,1,0:T(8,128)(2,1)} %absorb_ref.1, bf16[4,7168]{1,0:T(4,128)(2,1)} %residual_ref.1, bf16[512,7168]{1,0:T(8,128)(2,1)} %w_ref.1), custom_call_target="tpu_custom_call" | custom-call | flops 469762048 | bytes 7340032 | tf_op jit(solution)/shard_map/project/pallas_call | solution.py:246
  34.8 1.2 %collective-permute-done = bf16[32,3584]{1,0:T(8,128)(2,1)S(1)} collective-permute-done((bf16[32,3584]{1,0:T(8,128)(2,1)}, bf16[32,3584]{1,0:T(8,128)(2,1)S(1)}, u32[]{:S(2)}, u32[]{:S(2)}) %collective-permute-start) | collective-permute-done | bytes 229408 | tf_op jit(solution)/shard_map/ppermute | solution.py:339
  38.3 2.3 %collective-permute-start.1 = (bf16[8,3584]{1,0:T(8,128)(2,1)S(1)}, bf16[8,3584]{1,0:T(8,128)(2,1)S(1)}, u32[]{:S(2)}, u32[]{:S(2)}) collective-permute-start(bf16[8,3584]{1,0:T(8,128)(2,1)S(1)} %get-tuple-element.34), channel_id=1, source_target_pairs={{0,6},{1,7},{2,4},{3,5},{4,2},{5,3},{6,0},{7,1},{8,14},{9,15},{10,... | collective-permute-start | bytes 172040 | tf_op jit(solution)/shard_map/ppermute | solution.py:339
  43.0 2.3 %collective-permute-start.6 = (bf16[8,3584]{1,0:T(8,128)(2,1)S(1)}, bf16[8,3584]{1,0:T(8,128)(2,1)S(1)}, u32[]{:S(2)}, u32[]{:S(2)}) collective-permute-start(bf16[8,3584]{1,0:T(8,128)(2,1)S(1)} %get-tuple-element.37), channel_id=1, source_target_pairs={{0,6},{1,7},{2,4},{3,5},{4,2},{5,3},{6,0},{7,1},{8,14},{9,15},{10,... | collective-permute-start | bytes 172040 | tf_op jit(solution)/shard_map/ppermute | solution.py:339
  45.3 1.1 %collective-permute-start.4 = (bf16[8,3584]{1,0:T(8,128)(2,1)S(1)}, bf16[8,3584]{1,0:T(8,128)(2,1)S(1)}, u32[]{:S(2)}, u32[]{:S(2)}) collective-permute-start(bf16[8,3584]{1,0:T(8,128)(2,1)S(1)} %fusion.12), channel_id=1, source_target_pairs={{0,8},{1,9},{2,10},{3,11},{4,12},{5,13},{6,14},{7,15},{8,0},{9,1},... | collective-permute-start | bytes 172040 | tf_op jit(solution)/shard_map/ppermute | solution.py:339
  46.6 2.1 %collective-permute-done.6 = bf16[8,3584]{1,0:T(8,128)(2,1)S(1)} collective-permute-done((bf16[8,3584]{1,0:T(8,128)(2,1)S(1)}, bf16[8,3584]{1,0:T(8,128)(2,1)S(1)}, u32[]{:S(2)}, u32[]{:S(2)}) %collective-permute-start.6) | collective-permute-done | bytes 57376 | tf_op jit(solution)/shard_map/ppermute | solution.py:339
  48.7 1.1 %collective-permute-start.9 = (bf16[8,3584]{1,0:T(8,128)(2,1)S(1)}, bf16[8,3584]{1,0:T(8,128)(2,1)S(1)}, u32[]{:S(2)}, u32[]{:S(2)}) collective-permute-start(bf16[8,3584]{1,0:T(8,128)(2,1)S(1)} %fusion.13), channel_id=1, source_target_pairs={{0,8},{1,9},{2,10},{3,11},{4,12},{5,13},{6,14},{7,15},{8,0},{9,1},... | collective-permute-start | bytes 172040 | tf_op jit(solution)/shard_map/ppermute | solution.py:339
  49.8 2.4 %collective-permute-done.4 = bf16[8,3584]{1,0:T(8,128)(2,1)S(1)} collective-permute-done((bf16[8,3584]{1,0:T(8,128)(2,1)S(1)}, bf16[8,3584]{1,0:T(8,128)(2,1)S(1)}, u32[]{:S(2)}, u32[]{:S(2)}) %collective-permute-start.4) | collective-permute-done | bytes 57376 | tf_op jit(solution)/shard_map/ppermute | solution.py:339
  52.9 2.9 %collective-permute-start.10 = (bf16[8,3584]{1,0:T(8,128)(2,1)S(1)}, bf16[8,3584]{1,0:T(8,128)(2,1)S(1)}, u32[]{:S(2)}, u32[]{:S(2)}) collective-permute-start(bf16[8,3584]{1,0:T(8,128)(2,1)S(1)} %add_convert_fusion.1), channel_id=1, source_target_pairs={{0,4},{1,5},{2,6},{3,7},{4,0},{5,1},{6,2},{7,3},{8,12},{9,13},{10,... | collective-permute-start | bytes 172040 | tf_op jit(solution)/shard_map/ppermute | solution.py:339
  56.3 1.1 %collective-permute-start.15 = (bf16[8,3584]{1,0:T(8,128)(2,1)S(1)}, bf16[8,3584]{1,0:T(8,128)(2,1)S(1)}, u32[]{:S(2)}, u32[]{:S(2)}) collective-permute-start(bf16[8,3584]{1,0:T(8,128)(2,1)S(1)} %add_convert_fusion), channel_id=1, source_target_pairs={{0,2},{1,3},{2,0},{3,1},{4,6},{5,7},{6,4},{7,5},{8,10},{9,11},{10,... | collective-permute-start | bytes 172040 | tf_op jit(solution)/shard_map/ppermute | solution.py:339
  57.6 1.9 %collective-permute-start.14 = (bf16[8,3584]{1,0:T(8,128)(2,1)S(1)}, bf16[8,3584]{1,0:T(8,128)(2,1)S(1)}, u32[]{:S(2)}, u32[]{:S(2)}) collective-permute-start(bf16[8,3584]{1,0:T(8,128)(2,1)S(1)} %add_convert_fusion), channel_id=1, source_target_pairs={{0,4},{1,5},{2,6},{3,7},{4,0},{5,1},{6,2},{7,3},{8,12},{9,13},{10,... | collective-permute-start | bytes 172040 | tf_op jit(solution)/shard_map/ppermute | solution.py:339
  59.6 1.5 %collective-permute-done.16 = bf16[8,3584]{1,0:T(8,128)(2,1)S(1)} collective-permute-done((bf16[8,3584]{1,0:T(8,128)(2,1)S(1)}, bf16[8,3584]{1,0:T(8,128)(2,1)S(1)}, u32[]{:S(2)}, u32[]{:S(2)}) %collective-permute-start.16) | collective-permute-done | bytes 57376 | tf_op jit(solution)/shard_map/ppermute | solution.py:339
  61.8 1.5 %collective-permute-done.17.second_other = bf16[32,3584]{1,0:T(8,128)(2,1)S(1)} collective-permute-done((bf16[32,3584]{1,0:T(8,128)(2,1)S(1)}, bf16[32,3584]{1,0:T(8,128)(2,1)S(1)}, u32[]{:S(2)}, u32[]{:S(2)}) %collective-permute-start.17) | collective-permute-done | bytes 229408 | tf_op jit(solution)/shard_map/ppermute | solution.py:339
  63.4 2.3 %expert.1 = (f32[32,3584]{1,0:T(8,128)S(1)}, f32[32,3584]{1,0:T(8,128)S(1)}, bf16[32,3584]{1,0:T(8,128)(2,1)S(1)}, bf16[32,3584]{1,0:T(8,128)(2,1)S(1)}) custom-call(bf16[32,3584]{1,0:T(8,128)(2,1)S(1)} %pad_maximum_fusion.first_own, bf16[32,3584]{1,0:T(8,128)(2,1)S(1)} %collective-permute-done.13.first_other, ...), custom_call_target="tpu_custom_call" | custom-call | flops 704643072 | bytes 11010048 | tf_op jit(solution)/shard_map/expert/pallas_call | solution.py:322
  68.2 1.2 %collective-permute-start.20 = (bf16[8,3584]{1,0:T(8,128)(2,1)S(1)}, bf16[8,3584]{1,0:T(8,128)(2,1)S(1)}, u32[]{:S(2)}, u32[]{:S(2)}) collective-permute-start(bf16[8,3584]{1,0:T(8,128)(2,1)S(1)} %get-tuple-element.30), channel_id=1, source_target_pairs={{0,4},{1,5},{2,6},{3,7},{4,0},{5,1},{6,2},{7,3},{8,12},{9,13},{10,... | collective-permute-start | bytes 172040 | tf_op jit(solution)/shard_map/ppermute | solution.py:339
  69.4 1.5 %collective-permute-start.19 = (bf16[8,3584]{1,0:T(8,128)(2,1)S(1)}, bf16[8,3584]{1,0:T(8,128)(2,1)S(1)}, u32[]{:S(2)}, u32[]{:S(2)}) collective-permute-start(bf16[8,3584]{1,0:T(8,128)(2,1)S(1)} %get-tuple-element.28), channel_id=1, source_target_pairs={{0,6},{1,7},{2,4},{3,5},{4,2},{5,3},{6,0},{7,1},{8,14},{9,15},{10,... | collective-permute-start | bytes 172040 | tf_op jit(solution)/shard_map/ppermute | solution.py:339
  71.8 1.2 %collective-permute-start.25 = (bf16[8,3584]{1,0:T(8,128)(2,1)S(1)}, bf16[8,3584]{1,0:T(8,128)(2,1)S(1)}, u32[]{:S(2)}, u32[]{:S(2)}) collective-permute-start(bf16[8,3584]{1,0:T(8,128)(2,1)S(1)} %get-tuple-element.33), channel_id=1, source_target_pairs={{0,4},{1,5},{2,6},{3,7},{4,0},{5,1},{6,2},{7,3},{8,12},{9,13},{10,... | collective-permute-start | bytes 172040 | tf_op jit(solution)/shard_map/ppermute | solution.py:339
  73.0 1.5 %collective-permute-start.24 = (bf16[8,3584]{1,0:T(8,128)(2,1)S(1)}, bf16[8,3584]{1,0:T(8,128)(2,1)S(1)}, u32[]{:S(2)}, u32[]{:S(2)}) collective-permute-start(bf16[8,3584]{1,0:T(8,128)(2,1)S(1)} %get-tuple-element.31), channel_id=1, source_target_pairs={{0,6},{1,7},{2,4},{3,5},{4,2},{5,3},{6,0},{7,1},{8,14},{9,15},{10,... | collective-permute-start | bytes 172040 | tf_op jit(solution)/shard_map/ppermute | solution.py:339
  74.8 1.3 %collective-permute-start.22 = (bf16[4,3584]{1,0:T(4,128)(2,1)S(1)}, bf16[4,3584]{1,0:T(4,128)(2,1)S(1)}, u32[]{:S(2)}, u32[]{:S(2)}) collective-permute-start(bf16[4,3584]{1,0:T(4,128)(2,1)S(1)} %slice.185), channel_id=1, source_target_pairs={{0,8},{1,9},{2,10},{3,11},{4,12},{5,13},{6,14},{7,15},{8,0},{9,1},... | collective-permute-start | bytes 86024 | tf_op jit(solution)/shard_map/ppermute | solution.py:339
  76.3 2.1 %collective-permute-done.24 = bf16[8,3584]{1,0:T(8,128)(2,1)S(1)} collective-permute-done((bf16[8,3584]{1,0:T(8,128)(2,1)S(1)}, bf16[8,3584]{1,0:T(8,128)(2,1)S(1)}, u32[]{:S(2)}, u32[]{:S(2)}) %collective-permute-start.24) | collective-permute-done | bytes 57376 | tf_op jit(solution)/shard_map/ppermute | solution.py:339
  80.0 3.3 %collective-permute-done.27 = bf16[4,3584]{1,0:T(4,128)(2,1)S(1)} collective-permute-done((bf16[4,3584]{1,0:T(4,128)(2,1)S(1)}, bf16[4,3584]{1,0:T(4,128)(2,1)S(1)}, u32[]{:S(2)}, u32[]{:S(2)}) %collective-permute-start.27) | collective-permute-done | bytes 28704 | tf_op jit(solution)/shard_map/ppermute | solution.py:339
  (77 shorter events, 14.4 us)
Async XLA Ops:
  10.3 16.6 %all-to-all-start = ((bf16[16,16,512]{2,1,0:T(8,128)(2,1)}), bf16[16,16,512]{2,1,0:T(8,128)(2,1)S(1)}, u32[]{:S(2)}, u32[]{:S(2)}) async-start(bf16[16,16,512]{2,1,0:T(8,128)(2,1)} %attend.1), calls=%async_computation | async-start | bytes 524288 | tf_op jit(solution)/shard_map/all_to_all | solution.py:399
  34.3 6.3 %collective-permute-start.5 = (bf16[32,3584]{1,0:T(8,128)(2,1)}, bf16[32,3584]{1,0:T(8,128)(2,1)S(1)}, u32[]{:S(2)}, u32[]{:S(2)}) collective-permute-start(bf16[32,3584]{1,0:T(8,128)(2,1)} %get-tuple-element.13), channel_id=1, source_target_pairs={{0,1},{1,0},{2,3},{3,2},{4,5},{5,4},{6,7},{7,6},{8,9},{9,8},{10,11... | collective-permute-start | bytes 688136 | tf_op jit(solution)/shard_map/ppermute | solution.py:339
  37.1 5.9 %collective-permute-start.3 = (bf16[8,3584]{1,0:T(8,128)(2,1)S(1)}, bf16[8,3584]{1,0:T(8,128)(2,1)S(1)}, u32[]{:S(2)}, u32[]{:S(2)}) collective-permute-start(bf16[8,3584]{1,0:T(8,128)(2,1)S(1)} %get-tuple-element.35), channel_id=1, source_target_pairs={{0,2},{1,3},{2,0},{3,1},{4,6},{5,7},{6,4},{7,5},{8,10},{9,11},{10,... | collective-permute-start | bytes 172040 | tf_op jit(solution)/shard_map/ppermute | solution.py:339
  37.3 8.0 %collective-permute-start.2 = (bf16[8,3584]{1,0:T(8,128)(2,1)S(1)}, bf16[8,3584]{1,0:T(8,128)(2,1)S(1)}, u32[]{:S(2)}, u32[]{:S(2)}) collective-permute-start(bf16[8,3584]{1,0:T(8,128)(2,1)S(1)} %get-tuple-element.36), channel_id=1, source_target_pairs={{0,4},{1,5},{2,6},{3,7},{4,0},{5,1},{6,2},{7,3},{8,12},{9,13},{10,... | collective-permute-start | bytes 172040 | tf_op jit(solution)/shard_map/ppermute | solution.py:339
  38.3 7.0 %collective-permute-start.1 = (bf16[8,3584]{1,0:T(8,128)(2,1)S(1)}, bf16[8,3584]{1,0:T(8,128)(2,1)S(1)}, u32[]{:S(2)}, u32[]{:S(2)}) collective-permute-start(bf16[8,3584]{1,0:T(8,128)(2,1)S(1)} %get-tuple-element.34), channel_id=1, source_target_pairs={{0,6},{1,7},{2,4},{3,5},{4,2},{5,3},{6,0},{7,1},{8,14},{9,15},{10,... | collective-permute-start | bytes 172040 | tf_op jit(solution)/shard_map/ppermute | solution.py:339
  41.7 4.9 %collective-permute-start.8 = (bf16[8,3584]{1,0:T(8,128)(2,1)S(1)}, bf16[8,3584]{1,0:T(8,128)(2,1)S(1)}, u32[]{:S(2)}, u32[]{:S(2)}) collective-permute-start(bf16[8,3584]{1,0:T(8,128)(2,1)S(1)} %get-tuple-element.38), channel_id=1, source_target_pairs={{0,2},{1,3},{2,0},{3,1},{4,6},{5,7},{6,4},{7,5},{8,10},{9,11},{10,... | collective-permute-start | bytes 172040 | tf_op jit(solution)/shard_map/ppermute | solution.py:339
  42.0 4.6 %collective-permute-start.7 = (bf16[8,3584]{1,0:T(8,128)(2,1)S(1)}, bf16[8,3584]{1,0:T(8,128)(2,1)S(1)}, u32[]{:S(2)}, u32[]{:S(2)}) collective-permute-start(bf16[8,3584]{1,0:T(8,128)(2,1)S(1)} %get-tuple-element.39), channel_id=1, source_target_pairs={{0,4},{1,5},{2,6},{3,7},{4,0},{5,1},{6,2},{7,3},{8,12},{9,13},{10,... | collective-permute-start | bytes 172040 | tf_op jit(solution)/shard_map/ppermute | solution.py:339
  43.0 5.7 %collective-permute-start.6 = (bf16[8,3584]{1,0:T(8,128)(2,1)S(1)}, bf16[8,3584]{1,0:T(8,128)(2,1)S(1)}, u32[]{:S(2)}, u32[]{:S(2)}) collective-permute-start(bf16[8,3584]{1,0:T(8,128)(2,1)S(1)} %get-tuple-element.37), channel_id=1, source_target_pairs={{0,6},{1,7},{2,4},{3,5},{4,2},{5,3},{6,0},{7,1},{8,14},{9,15},{10,... | collective-permute-start | bytes 172040 | tf_op jit(solution)/shard_map/ppermute | solution.py:339
  45.3 6.8 %collective-permute-start.4 = (bf16[8,3584]{1,0:T(8,128)(2,1)S(1)}, bf16[8,3584]{1,0:T(8,128)(2,1)S(1)}, u32[]{:S(2)}, u32[]{:S(2)}) collective-permute-start(bf16[8,3584]{1,0:T(8,128)(2,1)S(1)} %fusion.12), channel_id=1, source_target_pairs={{0,8},{1,9},{2,10},{3,11},{4,12},{5,13},{6,14},{7,15},{8,0},{9,1},... | collective-permute-start | bytes 172040 | tf_op jit(solution)/shard_map/ppermute | solution.py:339
  48.7 7.1 %collective-permute-start.9 = (bf16[8,3584]{1,0:T(8,128)(2,1)S(1)}, bf16[8,3584]{1,0:T(8,128)(2,1)S(1)}, u32[]{:S(2)}, u32[]{:S(2)}) collective-permute-start(bf16[8,3584]{1,0:T(8,128)(2,1)S(1)} %fusion.13), channel_id=1, source_target_pairs={{0,8},{1,9},{2,10},{3,11},{4,12},{5,13},{6,14},{7,15},{8,0},{9,1},... | collective-permute-start | bytes 172040 | tf_op jit(solution)/shard_map/ppermute | solution.py:339
  52.3 5.3 %collective-permute-start.12 = (bf16[8,3584]{1,0:T(8,128)(2,1)S(1)}, bf16[8,3584]{1,0:T(8,128)(2,1)S(1)}, u32[]{:S(2)}, u32[]{:S(2)}) collective-permute-start(bf16[8,3584]{1,0:T(8,128)(2,1)S(1)} %add_convert_fusion.1), channel_id=1, source_target_pairs={{0,6},{1,7},{2,4},{3,5},{4,2},{5,3},{6,0},{7,1},{8,14},{9,15},{10,... | collective-permute-start | bytes 172040 | tf_op jit(solution)/shard_map/ppermute | solution.py:339
  52.4 7.1 %collective-permute-start.11 = (bf16[8,3584]{1,0:T(8,128)(2,1)S(1)}, bf16[8,3584]{1,0:T(8,128)(2,1)S(1)}, u32[]{:S(2)}, u32[]{:S(2)}) collective-permute-start(bf16[8,3584]{1,0:T(8,128)(2,1)S(1)} %add_convert_fusion.1), channel_id=1, source_target_pairs={{0,2},{1,3},{2,0},{3,1},{4,6},{5,7},{6,4},{7,5},{8,10},{9,11},{10,... | collective-permute-start | bytes 172040 | tf_op jit(solution)/shard_map/ppermute | solution.py:339
  52.9 6.6 %collective-permute-start.10 = (bf16[8,3584]{1,0:T(8,128)(2,1)S(1)}, bf16[8,3584]{1,0:T(8,128)(2,1)S(1)}, u32[]{:S(2)}, u32[]{:S(2)}) collective-permute-start(bf16[8,3584]{1,0:T(8,128)(2,1)S(1)} %add_convert_fusion.1), channel_id=1, source_target_pairs={{0,4},{1,5},{2,6},{3,7},{4,0},{5,1},{6,2},{7,3},{8,12},{9,13},{10,... | collective-permute-start | bytes 172040 | tf_op jit(solution)/shard_map/ppermute | solution.py:339
  55.9 5.2 %collective-permute-start.16 = (bf16[8,3584]{1,0:T(8,128)(2,1)S(1)}, bf16[8,3584]{1,0:T(8,128)(2,1)S(1)}, u32[]{:S(2)}, u32[]{:S(2)}) collective-permute-start(bf16[8,3584]{1,0:T(8,128)(2,1)S(1)} %add_convert_fusion), channel_id=1, source_target_pairs={{0,6},{1,7},{2,4},{3,5},{4,2},{5,3},{6,0},{7,1},{8,14},{9,15},{10,... | collective-permute-start | bytes 172040 | tf_op jit(solution)/shard_map/ppermute | solution.py:339
  56.3 4.8 %collective-permute-start.15 = (bf16[8,3584]{1,0:T(8,128)(2,1)S(1)}, bf16[8,3584]{1,0:T(8,128)(2,1)S(1)}, u32[]{:S(2)}, u32[]{:S(2)}) collective-permute-start(bf16[8,3584]{1,0:T(8,128)(2,1)S(1)} %add_convert_fusion), channel_id=1, source_target_pairs={{0,2},{1,3},{2,0},{3,1},{4,6},{5,7},{6,4},{7,5},{8,10},{9,11},{10,... | collective-permute-start | bytes 172040 | tf_op jit(solution)/shard_map/ppermute | solution.py:339
  66.0 4.9 %collective-permute-start.23 = (bf16[32,3584]{1,0:T(8,128)(2,1)S(1)}, bf16[32,3584]{1,0:T(8,128)(2,1)S(1)}, u32[]{:S(2)}, u32[]{:S(2)}) collective-permute-start(bf16[32,3584]{1,0:T(8,128)(2,1)S(1)} %get-tuple-element.17), channel_id=1, source_target_pairs={{0,1},{1,0},{2,3},{3,2},{4,5},{5,4},{6,7},{7,6},{8,9},{9,8},{10,11... | collective-permute-start | bytes 688136 | tf_op jit(solution)/shard_map/ppermute | solution.py:339
  67.3 5.7 %collective-permute-start.21 = (bf16[8,3584]{1,0:T(8,128)(2,1)S(1)}, bf16[8,3584]{1,0:T(8,128)(2,1)S(1)}, u32[]{:S(2)}, u32[]{:S(2)}) collective-permute-start(bf16[8,3584]{1,0:T(8,128)(2,1)S(1)} %get-tuple-element.29), channel_id=1, source_target_pairs={{0,2},{1,3},{2,0},{3,1},{4,6},{5,7},{6,4},{7,5},{8,10},{9,11},{10,... | collective-permute-start | bytes 172040 | tf_op jit(solution)/shard_map/ppermute | solution.py:339
  68.2 6.3 %collective-permute-start.20 = (bf16[8,3584]{1,0:T(8,128)(2,1)S(1)}, bf16[8,3584]{1,0:T(8,128)(2,1)S(1)}, u32[]{:S(2)}, u32[]{:S(2)}) collective-permute-start(bf16[8,3584]{1,0:T(8,128)(2,1)S(1)} %get-tuple-element.30), channel_id=1, source_target_pairs={{0,4},{1,5},{2,6},{3,7},{4,0},{5,1},{6,2},{7,3},{8,12},{9,13},{10,... | collective-permute-start | bytes 172040 | tf_op jit(solution)/shard_map/ppermute | solution.py:339
  69.4 5.4 %collective-permute-start.19 = (bf16[8,3584]{1,0:T(8,128)(2,1)S(1)}, bf16[8,3584]{1,0:T(8,128)(2,1)S(1)}, u32[]{:S(2)}, u32[]{:S(2)}) collective-permute-start(bf16[8,3584]{1,0:T(8,128)(2,1)S(1)} %get-tuple-element.28), channel_id=1, source_target_pairs={{0,6},{1,7},{2,4},{3,5},{4,2},{5,3},{6,0},{7,1},{8,14},{9,15},{10,... | collective-permute-start | bytes 172040 | tf_op jit(solution)/shard_map/ppermute | solution.py:339
  71.0 5.2 %collective-permute-start.26 = (bf16[8,3584]{1,0:T(8,128)(2,1)S(1)}, bf16[8,3584]{1,0:T(8,128)(2,1)S(1)}, u32[]{:S(2)}, u32[]{:S(2)}) collective-permute-start(bf16[8,3584]{1,0:T(8,128)(2,1)S(1)} %get-tuple-element.32), channel_id=1, source_target_pairs={{0,2},{1,3},{2,0},{3,1},{4,6},{5,7},{6,4},{7,5},{8,10},{9,11},{10,... | collective-permute-start | bytes 172040 | tf_op jit(solution)/shard_map/ppermute | solution.py:339
  71.8 4.5 %collective-permute-start.25 = (bf16[8,3584]{1,0:T(8,128)(2,1)S(1)}, bf16[8,3584]{1,0:T(8,128)(2,1)S(1)}, u32[]{:S(2)}, u32[]{:S(2)}) collective-permute-start(bf16[8,3584]{1,0:T(8,128)(2,1)S(1)} %get-tuple-element.33), channel_id=1, source_target_pairs={{0,4},{1,5},{2,6},{3,7},{4,0},{5,1},{6,2},{7,3},{8,12},{9,13},{10,... | collective-permute-start | bytes 172040 | tf_op jit(solution)/shard_map/ppermute | solution.py:339
  73.0 5.4 %collective-permute-start.24 = (bf16[8,3584]{1,0:T(8,128)(2,1)S(1)}, bf16[8,3584]{1,0:T(8,128)(2,1)S(1)}, u32[]{:S(2)}, u32[]{:S(2)}) collective-permute-start(bf16[8,3584]{1,0:T(8,128)(2,1)S(1)} %get-tuple-element.31), channel_id=1, source_target_pairs={{0,6},{1,7},{2,4},{3,5},{4,2},{5,3},{6,0},{7,1},{8,14},{9,15},{10,... | collective-permute-start | bytes 172040 | tf_op jit(solution)/shard_map/ppermute | solution.py:339
  74.8 5.1 %collective-permute-start.22 = (bf16[4,3584]{1,0:T(4,128)(2,1)S(1)}, bf16[4,3584]{1,0:T(4,128)(2,1)S(1)}, u32[]{:S(2)}, u32[]{:S(2)}) collective-permute-start(bf16[4,3584]{1,0:T(4,128)(2,1)S(1)} %slice.185), channel_id=1, source_target_pairs={{0,8},{1,9},{2,10},{3,11},{4,12},{5,13},{6,14},{7,15},{8,0},{9,1},... | collective-permute-start | bytes 86024 | tf_op jit(solution)/shard_map/ppermute | solution.py:339
  78.4 4.8 %collective-permute-start.27 = (bf16[4,3584]{1,0:T(4,128)(2,1)S(1)}, bf16[4,3584]{1,0:T(4,128)(2,1)S(1)}, u32[]{:S(2)}, u32[]{:S(2)}) collective-permute-start(bf16[4,3584]{1,0:T(4,128)(2,1)S(1)} %slice.184), channel_id=1, source_target_pairs={{0,8},{1,9},{2,10},{3,11},{4,12},{5,13},{6,14},{7,15},{8,0},{9,1},... | collective-permute-start | bytes 86024 | tf_op jit(solution)/shard_map/ppermute | solution.py:339
  (12 other events, 146.9 us)

commit v6 on v5

--- a/solution.py
+++ b/solution.py
@@ -33,6 +33,8 @@
     highest,
     sums,
     factors,
+    even,
+    odd,
     staged,
     item_row,
     item_block,
@@ -81,26 +83,32 @@
     queries_copy.wait()
     column = lax.broadcasted_iota(jnp.int32, (heads, BLOCK), 1)
 
-    def visit(group, _):
-        inside = [
+    def members(group):
+        return [
             (group * GROUP + at, item_row[group * GROUP + at], item_block[group * GROUP + at])
             for at in range(GROUP)
         ]
-        for at, row, block in inside:
+
+    def wait(group):
+        for at, row, block in members(group):
             pl.when(at < items)(lambda row=row, block=block: block_copy(row, block).wait())
-        found = []
-        for _, row, block in inside:
-            score = jnp.dot(
+
+    def score(group, target):
+        for to, (_, row, block) in enumerate(members(group)):
+            found = jnp.dot(
                 queries[row], held[row, block], preferred_element_type=jnp.float32
             ) * QK ** (-0.5)
-            found.append(
-                jnp.where(column + block * BLOCK < length[row], score, -jnp.inf)
+            target[to] = jnp.where(column + block * BLOCK < length[row], found, -jnp.inf)
+
+    def weigh(group, source):
+        inside = members(group)
+        tops = [
+            jnp.max(
+                functools.reduce(jnp.maximum, lane_tiles(source[at])), axis=1, keepdims=True
             )
-        tops = [
-            jnp.max(functools.reduce(jnp.maximum, lane_tiles(score)), axis=1, keepdims=True)
-            for score in found
+            for at in range(GROUP)
         ]
-        weights = [jnp.exp(score - top) for score, top in zip(found, tops)]
+        weights = [jnp.exp(source[at] - top) for at, top in enumerate(tops)]
         for (_, row, block), top, weight in zip(inside, tops, weights):
             highest[row, block] = jnp.broadcast_to(top, (heads, LANES))
             sums[row, block] = sum(lane_tiles(weight))
@@ -110,9 +118,27 @@
                 (((1,), (1,)), ((), ())),
                 preferred_element_type=jnp.float32,
             )
+
+    def step(group, now, later):
+        @pl.when(group + 1 < groups)
+        def _():
+            wait(group + 1)
+            score(group + 1, later)
+            weigh(group, now)
+
+        @pl.when(group + 1 == groups)
+        def _():
+            weigh(group, now)
+
+    wait(0)
+    score(0, even)
+
+    def two_steps(pair, _):
+        step(2 * pair, even, odd)
+        step(2 * pair + 1, odd, even)
         return 0
 
-    lax.fori_loop(0, groups, visit, 0)
+    lax.fori_loop(0, (groups + 1) // 2, two_steps, 0)
     for row in range(own_rows):
         factor = jnp.exp(highest[row] - jnp.max(highest[row], axis=0, keepdims=True))
         total = jnp.sum(jnp.sum(sums[row] * factor, axis=0), axis=1, keepdims=True)
@@ -150,6 +176,8 @@
             pltpu.VMEM((own_rows, blocks, heads, LANES), jnp.float32),
             pltpu.VMEM((own_rows, blocks, heads, LANES), jnp.float32),
             pltpu.VMEM((own_rows, blocks, heads, LANES), jnp.float32),
+            pltpu.VMEM((GROUP, heads, BLOCK), jnp.float32),
+            pltpu.VMEM((GROUP, heads, BLOCK), jnp.float32),
             pltpu.VMEM((devices, packed, rank), jnp.float32),
             pltpu.SMEM((listed,), jnp.int32),
             pltpu.SMEM((listed,), jnp.int32),
@@ -157,7 +185,7 @@
             pltpu.SemaphoreType.DMA,
             pltpu.SemaphoreType.DMA((own_rows, blocks)),
         ],
-        compiler_params=pltpu.CompilerParams(vmem_limit_bytes=58 * MIB),
+        compiler_params=pltpu.CompilerParams(vmem_limit_bytes=52 * MIB),
         cost_estimate=pl.CostEstimate(
             flops=own_rows * heads * cache.shape[2] * (depth + rank),
             bytes_accessed=cache.size,
@@ -167,50 +195,21 @@
     )(cache_len, jnp.swapaxes(queries, 1, 2), cache)
 
 
-def store_sides(term, at, keeps, sends):
-    half, side = keeps[0].shape
-    keep, send, at = keeps[at // side], sends[at // side], at % side
-    keep[:, at : at + TILE] = term[:half]
-    send[:, at : at + TILE] = term[half:].astype(send.dtype)
-
-
-def side_shapes(half, width):
-    return tuple(
-        jax.ShapeDtypeStruct((half, width // 2), kind)
-        for kind in (jnp.float32, jnp.bfloat16)
-        for _ in range(2)
-    )
+def store_term(term, at, keep_ref, send_ref):
+    half = keep_ref.shape[0]
+    keep_ref[:, at : at + TILE] = term[:half]
+    send_ref[:, at : at + TILE] = term[half:].astype(send_ref.dtype)
+
+
+def term_shapes(half, width):
+    return tuple(jax.ShapeDtypeStruct((half, width), kind) for kind in (jnp.float32, jnp.bfloat16))
 
 
 def project_kernel(
-    own_rows,
-    far,
-    here_ref,
-    joined_ref,
-    absorb_ref,
-    residual_ref,
-    w_ref,
-    first_keep,
-    second_keep,
-    first_send,
-    second_send,
-    held,
-    arrived,
+    own_rows, far, here_ref, joined_ref, absorb_ref, residual_ref, w_ref, keep_ref, send_ref
 ):
     own_heads = absorb_ref.shape[0]
-    half, side = first_keep.shape
-    width = 2 * side
-    part_width = width // PARTS
-    copies = [
-        pltpu.make_async_copy(
-            w_ref.at[:, part * part_width : (part + 1) * part_width],
-            held.at[:, part * part_width : (part + 1) * part_width],
-            arrived.at[part],
-        )
-        for part in range(PARTS)
-    ]
-    for copy in copies:
-        copy.start()
+    half, width = keep_ref.shape
     shape = (2 * half, joined_ref.shape[0])
     row = lax.broadcasted_iota(jnp.int32, shape, 0)
     place = lax.broadcasted_iota(jnp.int32, shape, 1)
@@ -230,14 +229,10 @@
         )
         values.append(value.astype(jnp.bfloat16))
     values = jnp.concatenate(values, axis=1)
-    for part in range(PARTS):
-        copies[part].wait()
-        for at in range(part * part_width, (part + 1) * part_width, TILE):
-            term = jnp.dot(values, held[:, at : at + TILE], preferred_element_type=jnp.float32)
-            store_sides(term, at, (first_keep, second_keep), (first_send, second_send))
-    for at, keep in ((0, first_keep), (side, second_keep)):
-        residual = residual_ref[:, at : at + side].astype(jnp.float32)
-        keep[:own_rows, :] = keep[:own_rows, :] + residual
+    for at in range(0, width, TILE):
+        term = jnp.dot(values, w_ref[:, at : at + TILE], preferred_element_type=jnp.float32)
+        store_term(term, at, keep_ref, send_ref)
+    keep_ref[:own_rows, :] = keep_ref[:own_rows, :] + residual_ref[...].astype(jnp.float32)
 
 
 def project(here, joined, w_absorb, residual_in, w_out, rows, far):
@@ -245,16 +240,11 @@
     own_rows = residual_in.shape[0]
     return pl.pallas_call(
         functools.partial(project_kernel, own_rows, far),
-        out_shape=side_shapes(rows // 2, width),
+        out_shape=term_shapes(rows // 2, width),
         in_specs=[pl.BlockSpec(memory_space=pltpu.SMEM)]
-        + [pl.BlockSpec(memory_space=pltpu.VMEM)] * 3
-        + [pl.BlockSpec(memory_space=pl.ANY)],
-        out_specs=(pl.BlockSpec(memory_space=pltpu.VMEM),) * 4,
-        scratch_shapes=[
-            pltpu.VMEM((depth, width), jnp.bfloat16),
-            pltpu.SemaphoreType.DMA((PARTS,)),
-        ],
-        compiler_params=pltpu.CompilerParams(vmem_limit_bytes=55 * MIB),
+        + [pl.BlockSpec(memory_space=pltpu.VMEM)] * 4,
+        out_specs=(pl.BlockSpec(memory_space=pltpu.VMEM),) * 2,
+        compiler_params=pltpu.CompilerParams(vmem_limit_bytes=24 * MIB),
         cost_estimate=pl.CostEstimate(
             flops=2 * rows * depth * width, bytes_accessed=2 * depth * width, transcendentals=0
         ),
@@ -263,43 +253,27 @@
 
 
 def expert_kernel(
-    first_own,
-    first_other,
-    second_own,
-    second_other,
-    gain_ref,
-    gate_ref,
-    up_ref,
-    down_ref,
-    first_keep,
-    second_keep,
-    first_send,
-    second_send,
+    own_ref, other_ref, gain_ref, gate_ref, up_ref, down_ref, keep_ref, send_ref
 ):
-    half, side = first_own.shape
-    width = 2 * side
+    width = own_ref.shape[1]
     depth = width // PARTS
-    streams = ((first_own, second_own), (first_other, second_other))
+    streams = (own_ref, other_ref)
     inverses = []
     for stream in streams:
         squares = 0.0
-        for ref in stream:
-            for at in range(0, side, depth):
-                piece = ref[:, at : at + depth].astype(jnp.float32)
-                squares = squares + sum(lane_tiles(piece * piece))
+        for at in range(0, width, depth):
+            piece = stream[:, at : at + depth].astype(jnp.float32)
+            squares = squares + sum(lane_tiles(piece * piece))
         mean = jnp.sum(squares, axis=1, keepdims=True) / width
         inverses.append(lax.rsqrt(mean + 1e-06))
     gate, up = 0.0, 0.0
-    for part in range(PARTS):
-        at, place = part * depth, part * depth % side
+    for at in range(0, width, depth):
         gain = gain_ref[:, at : at + depth]
         tokens = jnp.concatenate(
             [
-                (
-                    stream[at // side][:, place : place + depth].astype(jnp.float32)
-                    * inverse
-                    * gain
-                ).astype(jnp.bfloat16)
+                (stream[:, at : at + depth].astype(jnp.float32) * inverse * gain).astype(
+                    jnp.bfloat16
+                )
                 for stream, inverse in zip(streams, inverses)
             ],
             axis=0,
@@ -313,25 +287,25 @@
     active = (gate / (1.0 + jnp.exp(-gate)) * up).astype(jnp.bfloat16)
     for at in range(0, width, TILE):
         term = jnp.dot(active, down_ref[:, at : at + TILE], preferred_element_type=jnp.float32)
-        store_sides(term, at, (first_keep, second_keep), (first_send, second_send))
-
-
-def run_expert(streams, norm_gain, w_gate, w_up, w_down):
-    half, side = streams[0].shape
+        store_term(term, at, keep_ref, send_ref)
+
+
+def run_expert(own, other, norm_gain, w_gate, w_up, w_down):
+    half, width = own.shape
     hidden = w_gate.shape[1]
     return pl.pallas_call(
         expert_kernel,
-        out_shape=side_shapes(half, 2 * side),
-        in_specs=[pl.BlockSpec(memory_space=pltpu.VMEM)] * 8,
-        out_specs=(pl.BlockSpec(memory_space=pltpu.VMEM),) * 4,
+        out_shape=term_shapes(half, width),
+        in_specs=[pl.BlockSpec(memory_space=pltpu.VMEM)] * 6,
+        out_specs=(pl.BlockSpec(memory_space=pltpu.VMEM),) * 2,
         compiler_params=pltpu.CompilerParams(vmem_limit_bytes=24 * MIB),
         cost_estimate=pl.CostEstimate(
-            flops=24 * half * hidden * side,
-            bytes_accessed=12 * hidden * side,
+            flops=12 * half * hidden * width,
+            bytes_accessed=6 * hidden * width,
             transcendentals=2 * half * hidden,
         ),
         name="expert",
-    )(*streams, norm_gain[None], w_gate, w_up, w_down)
+    )(own, other, norm_gain[None], w_gate, w_up, w_down)
 
 
 def swap(array, distance):
@@ -367,10 +341,13 @@
     return total.astype(jnp.bfloat16)
 
 
-def spread(stream):
-    other = {distance: swap(stream, distance) for distance in (6, 4, 2)}
-    own = jnp.concatenate([stream, other[4], other[2], other[6]])
-    return own, swap(own, 1)
+def squares():
+    devices = lax.axis_size("experts")
+    return [
+        [core + 2 * y + 4 * near + 8 * far for y in range(2) for near in range(2)]
+        for far in range(devices // 8)
+        for core in range(2)
+    ]
 
 
 def shards(
@@ -399,34 +376,34 @@
     joined = lax.all_to_all(latent, "experts", split_axis=0, concat_axis=0, tiled=True)
     joined = joined.reshape(-1, joined.shape[-1])
     here = rank_here.astype(jnp.int32)[None]
-    sides = project(here, joined, w_absorb, residual_in, w_out, all_rows, far)
-    attended, streams = [], []
-    for at in range(2):
-        total = collect(sides[at], sides[at + 2])
-        stream = exchange(total, far)
-        attended.append(stream[:own_rows])
-        streams.extend(spread(stream))
-    attended = jnp.concatenate(attended, axis=1)
-
-    sides = run_expert(streams, norm_gain, w_gate, w_up, w_down)
+    keep, send = project(here, joined, w_absorb, residual_in, w_out, all_rows, far)
+    stream = exchange(collect(keep, send), far)
+    attended = stream[:own_rows]
+
+    own = lax.all_gather(stream, "experts", axis=0, tiled=True, axis_index_groups=squares())
+    keep, send = run_expert(own, swap(own, 1), norm_gain, w_gate, w_up, w_down)
+
+    total = (keep + wide(swap(send, 1))).astype(jnp.bfloat16)
+    total = lax.all_to_all(
+        total.reshape(4, far * own_rows, -1),
+        "experts",
+        split_axis=0,
+        concat_axis=0,
+        axis_index_groups=squares(),
+        tiled=True,
+    )
+    total = jnp.sum(wide(total), axis=0)
     own_ids = lax.dynamic_slice_in_dim(expert_ids, rank_here * own_rows, own_rows, 0)
-    mixings = []
+    expert_out = 0.0
     for at in range(far):
+        block = total[at * own_rows : (at + 1) * own_rows]
+        block = wide(swap(block.astype(jnp.bfloat16), 8 * at)) if at else block
         expert = (rank_here ^ (8 * at)) // split_ways
-        mixings.append(
-            jnp.sum(
-                route_gates * (own_ids == expert).astype(jnp.float32), axis=1, keepdims=True
-            )
-        )
-    expert_out = []
-    for at in range(2):
-        total = collect(sides[at], sides[at + 2])
-        mixed = mixings[0] * total[:own_rows]
-        for to in range(1, far):
-            block = total[to * own_rows : (to + 1) * own_rows].astype(jnp.bfloat16)
-            mixed = mixed + mixings[to] * wide(swap(block, 8 * to))
-        expert_out.append(mixed.astype(jnp.bfloat16))
-    return (attended, jnp.concatenate(expert_out, axis=1))
+        mixing = jnp.sum(
+            route_gates * (own_ids == expert).astype(jnp.float32), axis=1, keepdims=True
+        )
+        expert_out = expert_out + mixing * block
+    return (attended, expert_out.astype(jnp.bfloat16))
 
 
 def solution(mesh):

time: 85.6 us -> 91.9 us (1.074); the launches traced: 84.1 us -> 91.6 us
  starting transfers between devices: 33.6 us -> 15 us
  blocking collectives: 0 us -> 14 us
  waiting for transfers between devices: 26.1 us -> 39.9 us
  local copies, waits for them, and re-layouts: 0.88 us -> 5.48 us
  Pallas kernels: 18.6 us -> 14.4 us
  other arithmetic: 4.03 us -> 2 us
    ppermute x28 -> x8, starting transfers between devices: 27 us -> 5.01 us  [swap(): return lax.ppermute(array, 'experts', pairs)]
    all_gather x0 -> x1, blocking collectives: none -> 14 us  [shards(): lax.all_gather(stream, 'experts', axis=0, tiled=True, axis_index_groups=s...]
    all_to_all x0 -> x1, waiting for transfers between devices: none -> 7.83 us  [shards(): lax.all_to_all(total.reshape(4, far * own_rows, -1), 'experts', split_axi...]
    ppermute x28 -> x8, waiting for transfers between devices: 16.1 us -> 22 us  [swap(): return lax.ppermute(array, 'experts', pairs)]
    pallas_call x1, Pallas kernels: 6.58 us -> 2.1 us  [project(): pl.pallas_call(functools.partial(project_kernel, own_rows, far), out_shap...]
    unnamed x14 -> x22, local copies, waits for them, and re-layouts: 0.73 us -> 4.74 us
    all_to_all x0 -> x1, starting transfers between devices: none -> 3.46 us  [shards(): lax.all_to_all(total.reshape(4, far * own_rows, -1), 'experts', split_axi...]
    another operation x4 -> x1, other arithmetic: 2.25 us -> 0.09 us
  transfers between devices with their start and end apart: 29 -> 10, of which waited for: 14 -> 10; matrix products, arithmetic and copies ran while one was open for 4% -> 1% of each run, Pallas kernels for 0% -> 0%
where the time goes in v6:
time: 91.9 us; the launch traced here: 91.6 us
  waiting for transfers between devices  39.9 us (43%)
  starting transfers between devices  15 us (16%)
  Pallas kernels  14.4 us (16%)
  blocking collectives  14 us (15%)
  local copies, waits for them, and re-layouts  5.48 us (6%)
  other arithmetic  2 us (2%)
    ppermute x8, waiting for transfers between devices, swap(): return lax.ppermute(array, 'experts', pairs)  22 us
    all_gather x1, blocking collectives, shards(): lax.all_gather(stream, 'experts', axis=0, tiled=True, axis_index_groups=s...  14 us
    all_to_all x1, waiting for transfers between devices, shards(): lax.all_to_all(latent, 'experts', split_axis=0, concat_axis=0, tiled=True)  10 us
    pallas_call x1, Pallas kernels, attend(): pl.pallas_call(attend_kernel, out_shape=jax.ShapeDtypeStruct((devices, pa...  9.95 us
    all_to_all x1, waiting for transfers between devices, shards(): lax.all_to_all(total.reshape(4, far * own_rows, -1), 'experts', split_axi...  7.83 us
    all_to_all x1, starting transfers between devices, shards(): lax.all_to_all(latent, 'experts', split_axis=0, concat_axis=0, tiled=True)  6.53 us
    ppermute x8, starting transfers between devices, swap(): return lax.ppermute(array, 'experts', pairs)  5.01 us
    unnamed x22, local copies, waits for them, and re-layouts  4.74 us
  transfers between devices with their start and end apart: 10, of which 10 were waited for; matrix products, arithmetic and copies ran while one was open for 1% of the time, Pallas kernels for 0%

profile of v6, /device:TPU:0, one launch (start us, length us, event | category | flops | bytes accessed | tf_op | source)
XLA Modules:
  0.0 91.6 jit_solution(9904705596558814431)
XLA Ops:
  0.6 1.0 %copy-done.5 = bf16[4,576,64]{1,2,0:T(8,128)(2,1)S(1)} copy-done((bf16[4,576,64]{1,2,0:T(8,128)(2,1)S(1)}, bf16[4,576,64]{1,2,0:T(8,128)(2,1)}, u32[]{:S(2)}) %copy-start.5) | copy-done | bytes 294936
  1.6 0.7 copy-done.8
  2.3 9.9 %attend.1 = bf16[16,16,512]{2,1,0:T(8,128)(2,1)} custom-call(s32[4]{0:T(128)S(1)} %copy-done.8, bf16[4,64,576]{2,1,0:T(8,128)(2,1)S(1)} %bitcast.7, bf16[4,576,4096]{2,1,0:T(8,128)(2,1)} %cache_ref.1), custom_call_target="tpu_custom_call" | custom-call | flops 1140850688 | bytes 9437184 | tf_op jit(solution)/shard_map/attend/pallas_call | solution.py:166
  12.2 6.5 %all-to-all-start = ((bf16[16,16,512]{2,1,0:T(8,128)(2,1)}), bf16[16,16,512]{2,1,0:T(8,128)(2,1)S(1)}, u32[]{:S(2)}, u32[]{:S(2)}) async-start(bf16[16,16,512]{2,1,0:T(8,128)(2,1)} %attend.1), calls=%async_computation | async-start | bytes 524288 | tf_op jit(solution)/shard_map/all_to_all | solution.py:376
  18.8 10.0 %all-to-all-done = bf16[16,16,512]{2,1,0:T(8,128)(2,1)S(1)} async-done(((bf16[16,16,512]{2,1,0:T(8,128)(2,1)}), bf16[16,16,512]{2,1,0:T(8,128)(2,1)S(1)}, u32[]{:S(2)}, u32[]{:S(2)}) %all-to-all-start) | async-done | bytes 262176 | tf_op jit(solution)/shard_map/all_to_all | solution.py:376
  28.8 3.1 %copy-done = bf16[512,7168]{1,0:T(8,128)(2,1)S(1)} copy-done((bf16[512,7168]{1,0:T(8,128)(2,1)S(1)}, bf16[512,7168]{1,0:T(8,128)(2,1)}, u32[]{:S(2)}) %copy-start) | copy-done | bytes 7340056
  31.9 2.1 %project.1 = (f32[32,7168]{1,0:T(8,128)S(1)}, bf16[32,7168]{1,0:T(8,128)(2,1)S(1)}) custom-call(s32[1]{0:T(128)} %bitcast.here_ref, bf16[256,512]{1,0:T(8,128)(2,1)S(1)} %bitcast.6, bf16[4,512,128]{2,1,0:T(8,128)(2,1)S(1)} %copy-done.4, bf16[4,7168]{1,0:T(4,128)(2,1)S(1)} %copy-done.6, bf16[512,7168]{1,0:T(8,128)(2,1)S(1)} %copy-done), custom_call_target="tpu_custom_call" | custom-call | flops 469762048 | bytes 7340032 | tf_op jit(solution)/shard_map/project/pallas_call | solution.py:241
  34.1 1.8 %collective-permute-done = bf16[32,7168]{1,0:T(8,128)(2,1)S(1)} collective-permute-done((bf16[32,7168]{1,0:T(8,128)(2,1)S(1)}, bf16[32,7168]{1,0:T(8,128)(2,1)S(1)}, u32[]{:S(2)}, u32[]{:S(2)}) %collective-permute-start) | collective-permute-done | bytes 458784 | tf_op jit(solution)/shard_map/ppermute | solution.py:313
  36.0 0.7 collective-permute-start.1
  36.7 1.0 %collective-permute-start.2 = (bf16[8,7168]{1,0:T(8,128)(2,1)S(1)}, bf16[8,7168]{1,0:T(8,128)(2,1)S(1)}, u32[]{:S(2)}, u32[]{:S(2)}) collective-permute-start(bf16[8,7168]{1,0:T(8,128)(2,1)S(1)} %get-tuple-element.16), channel_id=1, source_target_pairs={{0,4},{1,5},{2,6},{3,7},{4,0},{5,1},{6,2},{7,3},{8,12},{9,13},{10,... | collective-permute-start | bytes 344072 | tf_op jit(solution)/shard_map/ppermute | solution.py:313
  37.7 1.9 %collective-permute-start.3 = (bf16[8,7168]{1,0:T(8,128)(2,1)S(1)}, bf16[8,7168]{1,0:T(8,128)(2,1)S(1)}, u32[]{:S(2)}, u32[]{:S(2)}) collective-permute-start(bf16[8,7168]{1,0:T(8,128)(2,1)S(1)} %get-tuple-element.15), channel_id=1, source_target_pairs={{0,2},{1,3},{2,0},{3,1},{4,6},{5,7},{6,4},{7,5},{8,10},{9,11},{10,... | collective-permute-start | bytes 344072 | tf_op jit(solution)/shard_map/ppermute | solution.py:313
  39.6 3.4 %collective-permute-done.1 = bf16[8,7168]{1,0:T(8,128)(2,1)S(1)} collective-permute-done((bf16[8,7168]{1,0:T(8,128)(2,1)S(1)}, bf16[8,7168]{1,0:T(8,128)(2,1)S(1)}, u32[]{:S(2)}, u32[]{:S(2)}) %collective-permute-start.1) | collective-permute-done | bytes 114720 | tf_op jit(solution)/shard_map/ppermute | solution.py:313
  43.6 1.1 %collective-permute-done.3 = bf16[8,7168]{1,0:T(8,128)(2,1)S(1)} collective-permute-done((bf16[8,7168]{1,0:T(8,128)(2,1)S(1)}, bf16[8,7168]{1,0:T(8,128)(2,1)S(1)}, u32[]{:S(2)}, u32[]{:S(2)}) %collective-permute-start.3) | collective-permute-done | bytes 114720 | tf_op jit(solution)/shard_map/ppermute | solution.py:313
  44.7 1.1 %collective-permute-start.4 = (bf16[8,7168]{1,0:T(8,128)(2,1)S(1)}, bf16[8,7168]{1,0:T(8,128)(2,1)S(1)}, u32[]{:S(2)}, u32[]{:S(2)}) collective-permute-start(bf16[8,7168]{1,0:T(8,128)(2,1)S(1)} %fusion.5), channel_id=1, source_target_pairs={{0,8},{1,9},{2,10},{3,11},{4,12},{5,13},{6,14},{7,15},{8,0},{9,1},... | collective-permute-start | bytes 344072 | tf_op jit(solution)/shard_map/ppermute | solution.py:313
  45.8 7.4 %collective-permute-done.4 = bf16[8,7168]{1,0:T(8,128)(2,1)S(1)} collective-permute-done((bf16[8,7168]{1,0:T(8,128)(2,1)S(1)}, bf16[8,7168]{1,0:T(8,128)(2,1)S(1)}, u32[]{:S(2)}, u32[]{:S(2)}) %collective-permute-start.4) | collective-permute-done | bytes 114720 | tf_op jit(solution)/shard_map/ppermute | solution.py:313
  53.4 14.0 %all_gather.3.own_ref = bf16[32,7168]{1,0:T(8,128)(2,1)S(1)} all-gather(bf16[8,7168]{1,0:T(8,128)(2,1)S(1)} %add_convert_fusion.1), channel_id=1, replica_groups={{0,4,2,6},{1,5,3,7},{8,12,10,14},{9,13,11,15},{16,20,18,22},{17,21,19,2..., dimensions={0}, use_global_device_ids=true | all-gather | bytes 573440 | tf_op jit(solution)/shard_map/all_gather | solution.py:383
  67.4 1.8 %collective-permute-done.5.other_ref = bf16[32,7168]{1,0:T(8,128)(2,1)S(1)} collective-permute-done((bf16[32,7168]{1,0:T(8,128)(2,1)S(1)}, bf16[32,7168]{1,0:T(8,128)(2,1)S(1)}, u32[]{:S(2)}, u32[]{:S(2)}) %collective-permute-start.5) | collective-permute-done | bytes 458784 | tf_op jit(solution)/shard_map/ppermute | solution.py:313
  69.2 2.4 %expert.1 = (f32[32,7168]{1,0:T(8,128)S(1)}, bf16[32,7168]{1,0:T(8,128)(2,1)S(1)}) custom-call(bf16[32,7168]{1,0:T(8,128)(2,1)S(1)} %all_gather.3.own_ref, bf16[32,7168]{1,0:T(8,128)(2,1)S(1)} %collective-permute-done.5.other_ref, f32[1,7168]{1,0:T(1,128)S(1)} %bitcast.8, bf16[7168,256]{1,0:T(8,128)(2,1)S(1)} %copy-done.1, bf16[7168,256]{1,0:T(8,128)(2,1)S(1)} %copy-done.2, ...), custom_call_target="tpu_custom_call" | custom-call | flops 704643072 | bytes 11010048 | tf_op jit(solution)/shard_map/expert/pallas_call | solution.py:296
  71.8 1.7 %collective-permute-done.6 = bf16[32,7168]{1,0:T(8,128)(2,1)S(1)} collective-permute-done((bf16[32,7168]{1,0:T(8,128)(2,1)S(1)}, bf16[32,7168]{1,0:T(8,128)(2,1)S(1)}, u32[]{:S(2)}, u32[]{:S(2)}) %collective-permute-start.6) | collective-permute-done | bytes 458784 | tf_op jit(solution)/shard_map/ppermute | solution.py:313
  73.5 0.8 fusion
  74.3 3.5 %all-to-all-start.1 = ((bf16[4,8,7168]{2,1,0:T(8,128)(2,1)}), bf16[4,8,7168]{2,1,0:T(8,128)(2,1)S(1)}, u32[]{:S(2)}, u32[]{:S(2)}) async-start(bf16[4,8,7168]{2,1,0:T(8,128)(2,1)} %fusion), calls=%async_computation.1 | async-start | bytes 917504 | tf_op jit(solution)/shard_map/all_to_all | solution.py:387
  77.8 7.8 %all-to-all-done.1 = bf16[4,8,7168]{2,1,0:T(8,128)(2,1)S(1)} async-done(((bf16[4,8,7168]{2,1,0:T(8,128)(2,1)}), bf16[4,8,7168]{2,1,0:T(8,128)(2,1)S(1)}, u32[]{:S(2)}, u32[]{:S(2)}) %all-to-all-start.1) | async-done | bytes 458784 | tf_op jit(solution)/shard_map/all_to_all | solution.py:387
  86.6 4.3 %collective-permute-done.7 = bf16[4,7168]{1,0:T(4,128)(2,1)S(1)} collective-permute-done((bf16[4,7168]{1,0:T(4,128)(2,1)S(1)}, bf16[4,7168]{1,0:T(4,128)(2,1)S(1)}, u32[]{:S(2)}, u32[]{:S(2)}) %collective-permute-start.7) | collective-permute-done | bytes 57376 | tf_op jit(solution)/shard_map/ppermute | solution.py:313
  90.9 0.7 fusion.4
  (33 shorter events, 2.1 us)
Async XLA Ops:
  0.6 1.0 %copy-start.5 = (bf16[4,576,64]{1,2,0:T(8,128)(2,1)S(1)}, bf16[4,576,64]{1,2,0:T(8,128)(2,1)}, u32[]{:S(2)}) copy-start(bf16[4,576,64]{1,2,0:T(8,128)(2,1)} %param.12) | copy-start | bytes 884740
  1.6 0.7 copy-start.8
  2.3 26.5 %copy-start.4 = (bf16[4,512,128]{2,1,0:T(8,128)(2,1)S(1)}, bf16[4,512,128]{2,1,0:T(8,128)(2,1)}, u32[]{:S(2)}) copy-start(bf16[4,512,128]{2,1,0:T(8,128)(2,1)} %absorb_ref.1) | copy-start | bytes 1572868
  2.3 26.5 %copy-start.6 = (bf16[4,7168]{1,0:T(4,128)(2,1)S(1)}, bf16[4,7168]{1,0:T(4,128)(2,1)}, u32[]{:S(2)}) copy-start(bf16[4,7168]{1,0:T(4,128)(2,1)} %residual_ref.1) | copy-start | bytes 172036
  12.2 16.6 %all-to-all-start = ((bf16[16,16,512]{2,1,0:T(8,128)(2,1)}), bf16[16,16,512]{2,1,0:T(8,128)(2,1)S(1)}, u32[]{:S(2)}, u32[]{:S(2)}) async-start(bf16[16,16,512]{2,1,0:T(8,128)(2,1)} %attend.1), calls=%async_computation | async-start | bytes 524288 | tf_op jit(solution)/shard_map/all_to_all | solution.py:376
  28.8 3.1 %copy-start = (bf16[512,7168]{1,0:T(8,128)(2,1)S(1)}, bf16[512,7168]{1,0:T(8,128)(2,1)}, u32[]{:S(2)}) copy-start(bf16[512,7168]{1,0:T(8,128)(2,1)} %w_ref.1) | copy-start | bytes 22020100
  31.9 37.3 %copy-start.2 = (bf16[7168,256]{1,0:T(8,128)(2,1)S(1)}, bf16[7168,256]{1,0:T(8,128)(2,1)}, u32[]{:S(2)}) copy-start(bf16[7168,256]{1,0:T(8,128)(2,1)} %up_ref.1) | copy-start | bytes 11010052
  31.9 37.3 %copy-start.3 = (bf16[256,7168]{1,0:T(8,128)(2,1)S(1)}, bf16[256,7168]{1,0:T(8,128)(2,1)}, u32[]{:S(2)}) copy-start(bf16[256,7168]{1,0:T(8,128)(2,1)} %down_ref.1) | copy-start | bytes 11010052
  34.0 35.2 %copy-start.1 = (bf16[7168,256]{1,0:T(8,128)(2,1)S(1)}, bf16[7168,256]{1,0:T(8,128)(2,1)}, u32[]{:S(2)}) copy-start(bf16[7168,256]{1,0:T(8,128)(2,1)} %gate_ref.1) | copy-start | bytes 11010052
  34.0 35.2 %copy-start.7 = (f32[7168]{0:T(1024)S(1)}, f32[7168]{0:T(1024)}, u32[]{:S(2)}) copy-start(f32[7168]{0:T(1024)} %param.18) | copy-start | bytes 86020
  34.0 1.9 %collective-permute-start = (bf16[32,7168]{1,0:T(8,128)(2,1)S(1)}, bf16[32,7168]{1,0:T(8,128)(2,1)S(1)}, u32[]{:S(2)}, u32[]{:S(2)}) collective-permute-start(bf16[32,7168]{1,0:T(8,128)(2,1)S(1)} %get-tuple-element.7), channel_id=1, source_target_pairs={{0,1},{1,0},{2,3},{3,2},{4,5},{5,4},{6,7},{7,6},{8,9},{9,8},{10,11... | collective-permute-start | bytes 1376264 | tf_op jit(solution)/shard_map/ppermute | solution.py:313
  36.0 7.0 %collective-permute-start.1 = (bf16[8,7168]{1,0:T(8,128)(2,1)S(1)}, bf16[8,7168]{1,0:T(8,128)(2,1)S(1)}, u32[]{:S(2)}, u32[]{:S(2)}) collective-permute-start(bf16[8,7168]{1,0:T(8,128)(2,1)S(1)} %get-tuple-element.14), channel_id=1, source_target_pairs={{0,6},{1,7},{2,4},{3,5},{4,2},{5,3},{6,0},{7,1},{8,14},{9,15},{10,... | collective-permute-start | bytes 344072 | tf_op jit(solution)/shard_map/ppermute | solution.py:313
  36.7 6.9 %collective-permute-start.2 = (bf16[8,7168]{1,0:T(8,128)(2,1)S(1)}, bf16[8,7168]{1,0:T(8,128)(2,1)S(1)}, u32[]{:S(2)}, u32[]{:S(2)}) collective-permute-start(bf16[8,7168]{1,0:T(8,128)(2,1)S(1)} %get-tuple-element.16), channel_id=1, source_target_pairs={{0,4},{1,5},{2,6},{3,7},{4,0},{5,1},{6,2},{7,3},{8,12},{9,13},{10,... | collective-permute-start | bytes 344072 | tf_op jit(solution)/shard_map/ppermute | solution.py:313
  37.7 6.9 %collective-permute-start.3 = (bf16[8,7168]{1,0:T(8,128)(2,1)S(1)}, bf16[8,7168]{1,0:T(8,128)(2,1)S(1)}, u32[]{:S(2)}, u32[]{:S(2)}) collective-permute-start(bf16[8,7168]{1,0:T(8,128)(2,1)S(1)} %get-tuple-element.15), channel_id=1, source_target_pairs={{0,2},{1,3},{2,0},{3,1},{4,6},{5,7},{6,4},{7,5},{8,10},{9,11},{10,... | collective-permute-start | bytes 344072 | tf_op jit(solution)/shard_map/ppermute | solution.py:313
  44.7 8.5 %collective-permute-start.4 = (bf16[8,7168]{1,0:T(8,128)(2,1)S(1)}, bf16[8,7168]{1,0:T(8,128)(2,1)S(1)}, u32[]{:S(2)}, u32[]{:S(2)}) collective-permute-start(bf16[8,7168]{1,0:T(8,128)(2,1)S(1)} %fusion.5), channel_id=1, source_target_pairs={{0,8},{1,9},{2,10},{3,11},{4,12},{5,13},{6,14},{7,15},{8,0},{9,1},... | collective-permute-start | bytes 344072 | tf_op jit(solution)/shard_map/ppermute | solution.py:313
  67.4 1.8 %collective-permute-start.5 = (bf16[32,7168]{1,0:T(8,128)(2,1)S(1)}, bf16[32,7168]{1,0:T(8,128)(2,1)S(1)}, u32[]{:S(2)}, u32[]{:S(2)}) collective-permute-start(bf16[32,7168]{1,0:T(8,128)(2,1)S(1)} %all_gather.3.own_ref), channel_id=1, source_target_pairs={{0,1},{1,0},{2,3},{3,2},{4,5},{5,4},{6,7},{7,6},{8,9},{9,8},{10,11... | collective-permute-start | bytes 1376264 | tf_op jit(solution)/shard_map/ppermute | solution.py:313
  69.2 16.6 %copy-start.9 = (f32[4,2]{0,1:T(2,128)S(1)}, f32[4,2]{0,1:T(2,128)}, u32[]{:S(2)}) copy-start(f32[4,2]{0,1:T(2,128)} %param.20) | copy-start | bytes 100
  69.2 16.6 %copy-start.10 = (s32[64,2]{0,1:T(2,128)S(1)}, s32[64,2]{0,1:T(2,128)}, u32[]{:S(2)}) copy-start(s32[64,2]{0,1:T(2,128)} %param.19) | copy-start | bytes 1540
  71.6 1.9 %collective-permute-start.6 = (bf16[32,7168]{1,0:T(8,128)(2,1)S(1)}, bf16[32,7168]{1,0:T(8,128)(2,1)S(1)}, u32[]{:S(2)}, u32[]{:S(2)}) collective-permute-start(bf16[32,7168]{1,0:T(8,128)(2,1)S(1)} %get-tuple-element.9), channel_id=1, source_target_pairs={{0,1},{1,0},{2,3},{3,2},{4,5},{5,4},{6,7},{7,6},{8,9},{9,8},{10,11... | collective-permute-start | bytes 1376264 | tf_op jit(solution)/shard_map/ppermute | solution.py:313
  74.3 11.3 %all-to-all-start.1 = ((bf16[4,8,7168]{2,1,0:T(8,128)(2,1)}), bf16[4,8,7168]{2,1,0:T(8,128)(2,1)S(1)}, u32[]{:S(2)}, u32[]{:S(2)}) async-start(bf16[4,8,7168]{2,1,0:T(8,128)(2,1)} %fusion), calls=%async_computation.1 | async-start | bytes 917504 | tf_op jit(solution)/shard_map/all_to_all | solution.py:387
  85.7 5.1 %collective-permute-start.7 = (bf16[4,7168]{1,0:T(4,128)(2,1)S(1)}, bf16[4,7168]{1,0:T(4,128)(2,1)S(1)}, u32[]{:S(2)}, u32[]{:S(2)}) collective-permute-start(bf16[4,7168]{1,0:T(4,128)(2,1)S(1)} %slice.64), channel_id=1, source_target_pairs={{0,8},{1,9},{2,10},{3,11},{4,12},{5,13},{6,14},{7,15},{8,0},{9,1},... | collective-permute-start | bytes 172040 | tf_op jit(solution)/shard_map/ppermute | solution.py:313

commit v7 on v6

v7 whole, which is shorter than its diff:
```python
import functools

import jax
import jax.numpy as jnp
from jax import lax
from jax.experimental import pallas as pl
from jax.experimental.pallas import tpu as pltpu
from jax.sharding import PartitionSpec as P

QK = 192
FF = 2048
BLOCK = 512
GROUP = 4
LANES = 128
TILE = 256
PARTS = 4
SQUARE = (0, 4, 2, 6)
PIECES = len(SQUARE)
MIB = 2**20


def lane_tiles(array):
    return [array[:, at : at + LANES] for at in range(0, array.shape[1], LANES)]


def attend_kernel(
    len_ref,
    queries_ref,
    cache_ref,
    latent_ref,
    length,
    queries,
    held,
    products,
    highest,
    sums,
    factors,
    staged,
    item_row,
    item_block,
    length_arrived,
    queries_arrived,
    arrived,
):
    own_rows, heads, _ = queries.shape
    devices, _, rank = staged.shape
    own_heads = heads // devices
    blocks = held.shape[1]

    length_copy = pltpu.make_async_copy(len_ref, length, length_arrived)
    length_copy.start()
    queries_copy = pltpu.make_async_copy(queries_ref, queries, queries_arrived)
    queries_copy.start()

    def block_copy(row, block):
        return pltpu.make_async_copy(
            cache_ref.at[row, :, pl.ds(pl.multiple_of(block * BLOCK, BLOCK), BLOCK)],
            held.at[row, block],
            arrived.at[row, block],
        )

    for row in range(own_rows):
        block_copy(row, 0).start()
        item_row[row] = row
        item_block[row] = 0
    highest[...] = jnp.full_like(highest, -jnp.inf)
    sums[...] = jnp.zeros_like(sums)
    length_copy.wait()
    items = own_rows
    counts = []
    for row in range(own_rows):
        count = (length[row] + BLOCK - 1) // BLOCK

        def begin(block, first, row=row):
            block_copy(row, block).start()
            item_row[first + block] = row
            item_block[first + block] = block
            return first

        lax.fori_loop(1, count, begin, items - 1)
        counts.append(count)
        items = items + count - 1
    queries_copy.wait()
    column = lax.broadcasted_iota(jnp.int32, (heads, BLOCK), 1)

    def visit(first, many):
        inside = [(item_row[first + at], item_block[first + at]) for at in range(many)]
        for row, block in inside:
            block_copy(row, block).wait()
        found = []
        for row, block in inside:
            score = jnp.dot(
                queries[row], held[row, block], preferred_element_type=jnp.float32
            ) * QK ** (-0.5)
            found.append(
                jnp.where(column + block * BLOCK < length[row], score, -jnp.inf)
            )
        tops = [
            jnp.max(functools.reduce(jnp.maximum, lane_tiles(score)), axis=1, keepdims=True)
            for score in found
        ]
        weights = [jnp.exp(score - top) for score, top in zip(found, tops)]
        for (row, block), top, weight in zip(inside, tops, weights):
            highest[row, block] = jnp.broadcast_to(top, (heads, LANES))
            sums[row, block] = sum(lane_tiles(weight))
            products[row, block] = lax.dot_general(
                weight.astype(jnp.bfloat16),
                held[row, block, :rank, :],
                (((1,), (1,)), ((), ())),
                preferred_element_type=jnp.float32,
            )

    def visit_group(group, _):
        visit(group * GROUP, GROUP)
        return 0

    whole = items // GROUP
    lax.fori_loop(0, whole, visit_group, 0)
    pl.when((items & 2) != 0)(lambda: visit(whole * GROUP, 2))
    pl.when((items & 1) != 0)(lambda: visit(items - 1, 1))
    for row in range(own_rows):
        factor = jnp.exp(highest[row] - jnp.max(highest[row], axis=0, keepdims=True))
        total = jnp.sum(jnp.sum(sums[row] * factor, axis=0), axis=1, keepdims=True)
        factors[row] = factor * (1.0 / total)[None]
    for row in range(own_rows):

        def merge(block, latent, row=row):
            return latent + products[row, block] * factors[row, block][:, :1]

        latent = lax.fori_loop(
            0, counts[row], merge, jnp.zeros((heads, rank), jnp.float32)
        )
        for device in range(devices):
            staged[device, row * own_heads : (row + 1) * own_heads, :] = latent[
                device * own_heads : (device + 1) * own_heads
            ]
    latent_ref[...] = staged[...].astype(latent_ref.dtype)


def attend(queries, cache, cache_len, devices, rank):
    own_rows, depth, heads = queries.shape
    blocks = cache.shape[2] // BLOCK
    packed = own_rows * heads // devices
    listed = own_rows * blocks
    return pl.pallas_call(
        attend_kernel,
        out_shape=jax.ShapeDtypeStruct((devices, packed, rank), jnp.bfloat16),
        in_specs=[pl.BlockSpec(memory_space=pl.ANY)] * 3,
        out_specs=pl.BlockSpec(memory_space=pltpu.VMEM),
        scratch_shapes=[
            pltpu.SMEM((own_rows,), jnp.int32),
            pltpu.VMEM((own_rows, heads, depth), jnp.bfloat16),
            pltpu.VMEM((own_rows, blocks, depth, BLOCK), jnp.bfloat16),
            pltpu.VMEM((own_rows, blocks, heads, rank), jnp.float32),
            pltpu.VMEM((own_rows, blocks, heads, LANES), jnp.float32),
            pltpu.VMEM((own_rows, blocks, heads, LANES), jnp.float32),
            pltpu.VMEM((own_rows, blocks, heads, LANES), jnp.float32),
            pltpu.VMEM((devices, packed, rank), jnp.float32),
            pltpu.SMEM((listed,), jnp.int32),
            pltpu.SMEM((listed,), jnp.int32),
            pltpu.SemaphoreType.DMA,
            pltpu.SemaphoreType.DMA,
            pltpu.SemaphoreType.DMA((own_rows, blocks)),
        ],
        compiler_params=pltpu.CompilerParams(vmem_limit_bytes=55 * MIB),
        cost_estimate=pl.CostEstimate(
            flops=own_rows * heads * cache.shape[2] * (depth + rank),
            bytes_accessed=cache.size,
            transcendentals=own_rows * heads * cache.shape[2],
        ),
        name="attend",
    )(cache_len, jnp.swapaxes(queries, 1, 2), cache)


def store_term(term, at, refs):
    rows = term.shape[0] // len(refs)
    for piece, ref in enumerate(refs):
        ref[:, at : at + TILE] = term[piece * rows : (piece + 1) * rows].astype(ref.dtype)


def term_shapes(rows, width):
    return tuple(
        jax.ShapeDtypeStruct((rows, width), kind)
        for kind in (jnp.float32, jnp.bfloat16)
        for _ in range(PIECES)
    )


def project_kernel(own_rows, far, joined_ref, residual_ref, absorb_ref, w_ref, *pieces):
    own_heads = absorb_ref.shape[0]
    width = w_ref.shape[1]
    shape = (len(pieces) * pieces[0].shape[0], joined_ref.shape[0])
    row = lax.broadcasted_iota(jnp.int32, shape, 0)
    place = lax.broadcasted_iota(jnp.int32, shape, 1)
    turn = own_rows.bit_length() - 1
    far_bits = far.bit_length() - 1
    request, slot = row & (own_rows - 1), row >> turn
    far_at, slot = slot & (far - 1), slot >> far_bits
    distance = (far_at << 3) + ((slot & 1) << 2) + ((slot >> 1 & 1) << 1) + (slot >> 2)
    device = distance ^ lax.axis_index("experts")
    values = []
    for head in range(own_heads):
        wanted = ((device << turn) + request) * own_heads + head
        choice = (place == wanted).astype(jnp.float32).astype(jnp.bfloat16)
        latent = jnp.dot(choice, joined_ref[...], preferred_element_type=jnp.float32)
        value = jnp.dot(
            latent.astype(jnp.bfloat16), absorb_ref[head], preferred_element_type=jnp.float32
        )
        values.append(value.astype(jnp.bfloat16))
    values = jnp.concatenate(values, axis=1)
    for at in range(0, width, TILE):
        term = jnp.dot(values, w_ref[:, at : at + TILE], preferred_element_type=jnp.float32)
        store_term(term, at, pieces)
    residual = residual_ref[...].astype(jnp.float32)
    pieces[0][:own_rows, :] = pieces[0][:own_rows, :] + residual


def project(joined, w_absorb, residual_in, w_out, rows, far):
    depth, width = w_out.shape
    own_rows = residual_in.shape[0]
    return pl.pallas_call(
        functools.partial(project_kernel, own_rows, far),
        out_shape=term_shapes(rows // (2 * PIECES), width),
        in_specs=[pl.BlockSpec(memory_space=pltpu.VMEM)] * 4,
        out_specs=(pl.BlockSpec(memory_space=pltpu.VMEM),) * (2 * PIECES),
        compiler_params=pltpu.CompilerParams(vmem_limit_bytes=24 * MIB),
        cost_estimate=pl.CostEstimate(
            flops=2 * rows * depth * width, bytes_accessed=2 * depth * width, transcendentals=0
        ),
        name="project",
    )(joined, residual_in, w_absorb, w_out)


def expert_kernel(*refs):
    streams, (gain_ref, gate_ref, up_ref, down_ref), pieces = refs[:8], refs[8:12], refs[12:]
    width = gain_ref.shape[1]
    depth = width // PARTS
    inverses = []
    for stream in streams:
        squares = 0.0
        for at in range(0, width, depth):
            piece = stream[:, at : at + depth].astype(jnp.float32)
            squares = squares + sum(lane_tiles(piece * piece))
        mean = jnp.sum(squares, axis=1, keepdims=True) / width
        inverses.append(lax.rsqrt(mean + 1e-06))
    gate, up = 0.0, 0.0
    for at in range(0, width, depth):
        gain = gain_ref[:, at : at + depth]
        tokens = jnp.concatenate(
            [
                stream[:, at : at + depth].astype(jnp.float32) * inverse * gain
                for stream, inverse in zip(streams, inverses)
            ],
            axis=0,
        ).astype(jnp.bfloat16)
        gate = gate + jnp.dot(
            tokens, gate_ref[at : at + depth, :], preferred_element_type=jnp.float32
        )
        up = up + jnp.dot(
            tokens, up_ref[at : at + depth, :], preferred_element_type=jnp.float32
        )
    active = (gate / (1.0 + jnp.exp(-gate)) * up).astype(jnp.bfloat16)
    for at in range(0, width, TILE):
        term = jnp.dot(active, down_ref[:, at : at + TILE], preferred_element_type=jnp.float32)
        store_term(term, at, pieces)


def run_expert(streams, norm_gain, w_gate, w_up, w_down):
    rows, width = streams[0].shape
    hidden = w_gate.shape[1]
    return pl.pallas_call(
        expert_kernel,
        out_shape=term_shapes(rows, width),
        in_specs=[pl.BlockSpec(memory_space=pltpu.VMEM)] * (2 * PIECES + 4),
        out_specs=(pl.BlockSpec(memory_space=pltpu.VMEM),) * (2 * PIECES),
        compiler_params=pltpu.CompilerParams(vmem_limit_bytes=24 * MIB),
        cost_estimate=pl.CostEstimate(
            flops=12 * PIECES * rows * hidden * width,
            bytes_accessed=6 * hidden * width,
            transcendentals=2 * PIECES * rows * hidden,
        ),
        name="expert",
    )(*streams, norm_gain[None], w_gate, w_up, w_down)


def swap(array, distance):
    pairs = [(at, at ^ distance) for at in range(lax.axis_size("experts"))]
    return lax.ppermute(array, "experts", pairs)


def wide(array):
    return array.astype(jnp.float32)


def collect(terms):
    keeps, sends = terms[:PIECES], terms[PIECES:]
    total = 0.0
    for piece in (3, 1, 2, 0):
        part = keeps[piece] + wide(swap(sends[piece], 1))
        if piece:
            part = wide(swap(part.astype(jnp.bfloat16), SQUARE[piece]))
        total = total + part
    return total


def exchange(total, far):
    own_rows = total.shape[0] // far
    sent = total.astype(jnp.bfloat16)
    for at in range(1, far):
        block = swap(sent, 8 * at)
        total = total + wide(
            jnp.concatenate(
                [block[(to ^ at) * own_rows : ((to ^ at) + 1) * own_rows] for to in range(far)]
            )
        )
    return total.astype(jnp.bfloat16)


def spread(stream):
    own = [swap(stream, distance) if distance else stream for distance in SQUARE]
    return own + [swap(piece, 1) for piece in own]


def shards(
    queries,
    cache,
    cache_len,
    residual_in,
    w_absorb,
    w_out,
    norm_gain,
    expert_ids,
    route_gates,
    w_gate,
    w_up,
    w_down,
):
    devices = lax.axis_size("experts")
    rank_here = lax.axis_index("experts")
    own_rows = queries.shape[0]
    all_rows = expert_ids.shape[0]
    far = devices // 8
    split_ways = FF // w_gate.shape[1]
    assert split_ways == 8

    latent = attend(queries, cache, cache_len, devices, w_absorb.shape[1])
    joined = lax.all_to_all(latent, "experts", split_axis=0, concat_axis=0, tiled=True)
    joined = joined.reshape(-1, joined.shape[-1])
    terms = project(joined, w_absorb, residual_in, w_out, all_rows, far)
    stream = exchange(collect(terms), far)
    attended = stream[:own_rows]

    total = collect(run_expert(spread(stream), norm_gain, w_gate, w_up, w_down))
    own_ids = lax.dynamic_slice_in_dim(expert_ids, rank_here * own_rows, own_rows, 0)
    expert_out = 0.0
    for at in range(far):
        block = total[at * own_rows : (at + 1) * own_rows]
        block = wide(swap(block.astype(jnp.bfloat16), 8 * at)) if at else block
        expert = (rank_here ^ (8 * at)) // split_ways
        mixing = jnp.sum(
            route_gates * (own_ids == expert).astype(jnp.float32), axis=1, keepdims=True
        )
        expert_out = expert_out + mixing * block
    return (attended, expert_out.astype(jnp.bfloat16))


def solution(mesh):
    placed = (
        P(("groups", "experts"), None, None),
        P(("groups", "experts"), None, None),
        P(("groups", "experts")),
        P(("groups", "experts"), None),
        P("experts", None, None),
        P("experts", None),
        P(),
        P("groups", None),
        P(("groups", "experts"), None),
        P(None, "experts"),
        P(None, "experts"),
        P("experts", None),
    )
    return jax.shard_map(
        shards,
        mesh=mesh,
        in_specs=placed,
        out_specs=(P(("groups", "experts"), None), P(("groups", "experts"), None)),
        check_vma=False,
    )
```

time: 91.9 us -> 78.3 us (0.85); the launches traced: 91.6 us -> 79.6 us
  waiting for transfers between devices: 39.9 us -> 27.3 us
  blocking collectives: 14 us -> 21.2 us
  local copies, waits for them, and re-layouts: 5.48 us -> 0.77 us
  Pallas kernels: 14.4 us -> 12.3 us
  starting transfers between devices: 15 us -> 16 us
    all_to_all x0 -> x1, blocking collectives: none -> 21.2 us  [shards(): lax.all_to_all(latent, 'experts', split_axis=0, concat_axis=0, tiled=True)]
    all_to_all x2 -> x0, waiting for transfers between devices: 17.9 us -> none  [the longest x1 10 us: shards(): lax.all_to_all(latent, 'experts', split_axis=0, concat_axis=0, tiled=True)]
    all_gather x1 -> x0, blocking collectives: 14 us -> none  [shards(): lax.all_gather(stream, 'experts', axis=0, tiled=True, axis_index_groups=s...]
    ppermute x8 -> x23, starting transfers between devices: 5.01 us -> 16 us  [swap(): return lax.ppermute(array, 'experts', pairs)]
    all_to_all x2 -> x0, starting transfers between devices: 9.99 us -> none  [the longest x1 6.53 us: shards(): lax.all_to_all(latent, 'experts', split_axis=0, concat_axis=0, tiled=True)]
    ppermute x8 -> x23, waiting for transfers between devices: 22 us -> 27.3 us  [swap(): return lax.ppermute(array, 'experts', pairs)]
    unnamed x22 -> x20, local copies, waits for them, and re-layouts: 4.74 us -> 0.06 us
    pallas_call x1, Pallas kernels: 9.95 us -> 7.84 us  [attend(): pl.pallas_call(attend_kernel, out_shape=jax.ShapeDtypeStruct((devices, pa...]
  transfers between devices with their start and end apart: 10 -> 23, of which waited for: 10 -> 14; matrix products, arithmetic and copies ran while one was open for 1% -> 1% of each run, Pallas kernels for 0% -> 0%
where the time goes in v7:
time: 78.3 us; the launch traced here: 79.6 us
  waiting for transfers between devices  27.3 us (35%)
  blocking collectives  21.2 us (27%)
  starting transfers between devices  16 us (20%)
  Pallas kernels  12.3 us (16%)
  other arithmetic  1.27 us (2%)
  between operations  0.85 us (1%)
    ppermute x23, waiting for transfers between devices, swap(): return lax.ppermute(array, 'experts', pairs)  27.3 us
    all_to_all x1, blocking collectives, shards(): lax.all_to_all(latent, 'experts', split_axis=0, concat_axis=0, tiled=True)  21.2 us
    ppermute x23, starting transfers between devices, swap(): return lax.ppermute(array, 'experts', pairs)  16 us
    pallas_call x1, Pallas kernels, attend(): pl.pallas_call(attend_kernel, out_shape=jax.ShapeDtypeStruct((devices, pa...  7.84 us
    pallas_call x1, Pallas kernels, run_expert(): pl.pallas_call(expert_kernel, out_shape=term_shapes(rows, width), in_spec...  2.34 us
    pallas_call x1, Pallas kernels, project(): pl.pallas_call(functools.partial(project_kernel, own_rows, far), out_shap...  2.11 us
  transfers between devices with their start and end apart: 23, of which 14 were waited for; matrix products, arithmetic and copies ran while one was open for 1% of the time, Pallas kernels for 0%

profile of v7, /device:TPU:0, one launch (start us, length us, event | category | flops | bytes accessed | tf_op | source)
XLA Modules:
  0.0 79.6 jit_solution(5408424148961749028)
XLA Ops:
  0.7 7.8 %attend.1 = bf16[16,16,512]{2,1,0:T(8,128)(2,1)} custom-call(s32[4]{0:T(128)} %len_ref.1, bf16[4,64,576]{2,1,0:T(8,128)(2,1)} %bitcast.7, bf16[4,576,4096]{2,1,0:T(8,128)(2,1)} %cache_ref.1), custom_call_target="tpu_custom_call" | custom-call | flops 1140850688 | bytes 9437184 | tf_op jit(solution)/shard_map/attend/pallas_call | solution.py:145
  8.5 21.2 %all_to_all.5 = bf16[16,16,512]{2,1,0:T(8,128)(2,1)S(1)} all-to-all(bf16[16,16,512]{2,1,0:T(8,128)(2,1)} %attend.1), channel_id=1, replica_groups=mesh['groups'=2,'experts'=16] {'experts'}, dimensions={0} | all-to-all | bytes 524288 | tf_op jit(solution)/shard_map/all_to_all | solution.py:347
  29.8 2.1 %project.1 = (f32[8,7168]{1,0:T(8,128)S(1)}, f32[8,7168]{1,0:T(8,128)S(1)}, f32[8,7168]{1,0:T(8,128)S(1)}, f32[8,7168]{1,0:T(8,128)S(1)}, bf16[8,7168]{1,0:T(8,1...) custom-call(bf16[256,512]{1,0:T(8,128)(2,1)S(1)} %bitcast.5, ...), custom_call_target="tpu_custom_call" | custom-call | flops 469762048 | bytes 7340032 | tf_op jit(solution)/shard_map/project/pallas_call | solution.py:221
  33.3 0.7 collective-permute-start.1
  34.0 1.1 %collective-permute-start.3 = (bf16[8,7168]{1,0:T(8,128)(2,1)S(1)}, bf16[8,7168]{1,0:T(8,128)(2,1)S(1)}, u32[]{:S(2)}, u32[]{:S(2)}) collective-permute-start(bf16[8,7168]{1,0:T(8,128)(2,1)S(1)} %add_convert_fusion.5), channel_id=1, source_target_pairs={{0,4},{1,5},{2,6},{3,7},{4,0},{5,1},{6,2},{7,3},{8,12},{9,13},{10,... | collective-permute-start | bytes 344072 | tf_op jit(solution)/shard_map/ppermute | solution.py:288
  35.2 1.9 %collective-permute-start.5 = (bf16[8,7168]{1,0:T(8,128)(2,1)S(1)}, bf16[8,7168]{1,0:T(8,128)(2,1)S(1)}, u32[]{:S(2)}, u32[]{:S(2)}) collective-permute-start(bf16[8,7168]{1,0:T(8,128)(2,1)S(1)} %add_convert_fusion.4), channel_id=1, source_target_pairs={{0,2},{1,3},{2,0},{3,1},{4,6},{5,7},{6,4},{7,5},{8,10},{9,11},{10,... | collective-permute-start | bytes 344072 | tf_op jit(solution)/shard_map/ppermute | solution.py:288
  37.1 3.2 %collective-permute-done.1 = bf16[8,7168]{1,0:T(8,128)(2,1)S(1)} collective-permute-done((bf16[8,7168]{1,0:T(8,128)(2,1)S(1)}, bf16[8,7168]{1,0:T(8,128)(2,1)S(1)}, u32[]{:S(2)}, u32[]{:S(2)}) %collective-permute-start.1) | collective-permute-done | bytes 114720 | tf_op jit(solution)/shard_map/ppermute | solution.py:288
  40.8 1.1 %collective-permute-done.5 = bf16[8,7168]{1,0:T(8,128)(2,1)S(1)} collective-permute-done((bf16[8,7168]{1,0:T(8,128)(2,1)S(1)}, bf16[8,7168]{1,0:T(8,128)(2,1)S(1)}, u32[]{:S(2)}, u32[]{:S(2)}) %collective-permute-start.5) | collective-permute-done | bytes 114720 | tf_op jit(solution)/shard_map/ppermute | solution.py:288
  42.0 1.1 %collective-permute-start.7 = (bf16[8,7168]{1,0:T(8,128)(2,1)S(1)}, bf16[8,7168]{1,0:T(8,128)(2,1)S(1)}, u32[]{:S(2)}, u32[]{:S(2)}) collective-permute-start(bf16[8,7168]{1,0:T(8,128)(2,1)S(1)} %fusion.4), channel_id=1, source_target_pairs={{0,8},{1,9},{2,10},{3,11},{4,12},{5,13},{6,14},{7,15},{8,0},{9,1},... | collective-permute-start | bytes 344072 | tf_op jit(solution)/shard_map/ppermute | solution.py:288
  43.1 7.3 %collective-permute-done.7 = bf16[8,7168]{1,0:T(8,128)(2,1)S(1)} collective-permute-done((bf16[8,7168]{1,0:T(8,128)(2,1)S(1)}, bf16[8,7168]{1,0:T(8,128)(2,1)S(1)}, u32[]{:S(2)}, u32[]{:S(2)}) %collective-permute-start.7) | collective-permute-done | bytes 114720 | tf_op jit(solution)/shard_map/ppermute | solution.py:288
  50.8 3.4 %collective-permute-start.10 = (bf16[8,7168]{1,0:T(8,128)(2,1)S(1)}, bf16[8,7168]{1,0:T(8,128)(2,1)S(1)}, u32[]{:S(2)}, u32[]{:S(2)}) collective-permute-start(bf16[8,7168]{1,0:T(8,128)(2,1)S(1)} %add_convert_fusion.3.refs_0_), channel_id=1, source_target_pairs={{0,6},{1,7},{2,4},{3,5},{4,2},{5,3},{6,0},{7,1},{8,14},{9,15},{10,... | collective-permute-start | bytes 344072 | tf_op jit(solution)/shard_map/ppermute | solution.py:288
  54.2 2.5 %collective-permute-done.8.refs_1_ = bf16[8,7168]{1,0:T(8,128)(2,1)S(1)} collective-permute-done((bf16[8,7168]{1,0:T(8,128)(2,1)S(1)}, bf16[8,7168]{1,0:T(8,128)(2,1)S(1)}, u32[]{:S(2)}, u32[]{:S(2)}) %collective-permute-start.8) | collective-permute-done | bytes 114720 | tf_op jit(solution)/shard_map/ppermute | solution.py:288
  56.7 1.6 %collective-permute-done.9.refs_2_ = bf16[8,7168]{1,0:T(8,128)(2,1)S(1)} collective-permute-done((bf16[8,7168]{1,0:T(8,128)(2,1)S(1)}, bf16[8,7168]{1,0:T(8,128)(2,1)S(1)}, u32[]{:S(2)}, u32[]{:S(2)}) %collective-permute-start.9) | collective-permute-done | bytes 114720 | tf_op jit(solution)/shard_map/ppermute | solution.py:288
  58.8 0.8 %collective-permute-done.13.refs_6_ = bf16[8,7168]{1,0:T(8,128)(2,1)S(1)} collective-permute-done((bf16[8,7168]{1,0:T(8,128)(2,1)S(1)}, bf16[8,7168]{1,0:T(8,128)(2,1)S(1)}, u32[]{:S(2)}, u32[]{:S(2)}) %collective-permute-start.13) | collective-permute-done | bytes 114720 | tf_op jit(solution)/shard_map/ppermute | solution.py:288
  59.8 2.3 %expert.1 = (f32[8,7168]{1,0:T(8,128)S(1)}, f32[8,7168]{1,0:T(8,128)S(1)}, f32[8,7168]{1,0:T(8,128)S(1)}, f32[8,7168]{1,0:T(8,128)S(1)}, bf16[8,7168]{1,0:T(8,12...) custom-call(bf16[8,7168]{1,0:T(8,128)(2,1)S(1)} %add_convert_fusion.3.refs_0_, ...), custom_call_target="tpu_custom_call" | custom-call | flops 704643072 | bytes 11010048 | tf_op jit(solution)/shard_map/expert/pallas_call | solution.py:271
  63.6 1.5 %collective-permute-start.16 = (bf16[8,7168]{1,0:T(8,128)(2,1)S(1)}, bf16[8,7168]{1,0:T(8,128)(2,1)S(1)}, u32[]{:S(2)}, u32[]{:S(2)}) collective-permute-start(bf16[8,7168]{1,0:T(8,128)(2,1)S(1)} %add_convert_fusion.2), channel_id=1, source_target_pairs={{0,6},{1,7},{2,4},{3,5},{4,2},{5,3},{6,0},{7,1},{8,14},{9,15},{10,... | collective-permute-start | bytes 344072 | tf_op jit(solution)/shard_map/ppermute | solution.py:288
  65.1 1.3 %collective-permute-start.18 = (bf16[8,7168]{1,0:T(8,128)(2,1)S(1)}, bf16[8,7168]{1,0:T(8,128)(2,1)S(1)}, u32[]{:S(2)}, u32[]{:S(2)}) collective-permute-start(bf16[8,7168]{1,0:T(8,128)(2,1)S(1)} %add_convert_fusion.1), channel_id=1, source_target_pairs={{0,4},{1,5},{2,6},{3,7},{4,0},{5,1},{6,2},{7,3},{8,12},{9,13},{10,... | collective-permute-start | bytes 344072 | tf_op jit(solution)/shard_map/ppermute | solution.py:288
  66.5 0.9 %collective-permute-start.20 = (bf16[8,7168]{1,0:T(8,128)(2,1)S(1)}, bf16[8,7168]{1,0:T(8,128)(2,1)S(1)}, u32[]{:S(2)}, u32[]{:S(2)}) collective-permute-start(bf16[8,7168]{1,0:T(8,128)(2,1)S(1)} %add_convert_fusion), channel_id=1, source_target_pairs={{0,2},{1,3},{2,0},{3,1},{4,6},{5,7},{6,4},{7,5},{8,10},{9,11},{10,... | collective-permute-start | bytes 344072 | tf_op jit(solution)/shard_map/ppermute | solution.py:288
  67.4 3.2 %collective-permute-done.16 = bf16[8,7168]{1,0:T(8,128)(2,1)S(1)} collective-permute-done((bf16[8,7168]{1,0:T(8,128)(2,1)S(1)}, bf16[8,7168]{1,0:T(8,128)(2,1)S(1)}, u32[]{:S(2)}, u32[]{:S(2)}) %collective-permute-start.16) | collective-permute-done | bytes 114720 | tf_op jit(solution)/shard_map/ppermute | solution.py:288
  70.5 1.4 %collective-permute-done.18 = bf16[8,7168]{1,0:T(8,128)(2,1)S(1)} collective-permute-done((bf16[8,7168]{1,0:T(8,128)(2,1)S(1)}, bf16[8,7168]{1,0:T(8,128)(2,1)S(1)}, u32[]{:S(2)}, u32[]{:S(2)}) %collective-permute-start.18) | collective-permute-done | bytes 114720 | tf_op jit(solution)/shard_map/ppermute | solution.py:288
  72.5 1.3 %collective-permute-start.22 = (bf16[4,7168]{1,0:T(4,128)(2,1)S(1)}, bf16[4,7168]{1,0:T(4,128)(2,1)S(1)}, u32[]{:S(2)}, u32[]{:S(2)}) collective-permute-start(bf16[4,7168]{1,0:T(4,128)(2,1)S(1)} %slice.32), channel_id=1, source_target_pairs={{0,8},{1,9},{2,10},{3,11},{4,12},{5,13},{6,14},{7,15},{8,0},{9,1},... | collective-permute-start | bytes 172040 | tf_op jit(solution)/shard_map/ppermute | solution.py:288
  73.9 0.6 slice.23
  74.6 4.3 %collective-permute-done.22 = bf16[4,7168]{1,0:T(4,128)(2,1)S(1)} collective-permute-done((bf16[4,7168]{1,0:T(4,128)(2,1)S(1)}, bf16[4,7168]{1,0:T(4,128)(2,1)S(1)}, u32[]{:S(2)}, u32[]{:S(2)}) %collective-permute-start.22) | collective-permute-done | bytes 57376 | tf_op jit(solution)/shard_map/ppermute | solution.py:288
  78.9 0.7 fusion.1
  (61 shorter events, 5.3 us)
Async XLA Ops:
  29.7 30.1 %copy-start = (bf16[7168,256]{1,0:T(8,128)(2,1)S(1)}, bf16[7168,256]{1,0:T(8,128)(2,1)}, u32[]{:S(2)}) copy-start(bf16[7168,256]{1,0:T(8,128)(2,1)} %refs_9_.1) | copy-start | bytes 11010052
  31.9 1.4 %collective-permute-start = (bf16[8,7168]{1,0:T(8,128)(2,1)S(1)}, bf16[8,7168]{1,0:T(8,128)(2,1)S(1)}, u32[]{:S(2)}, u32[]{:S(2)}) collective-permute-start(bf16[8,7168]{1,0:T(8,128)(2,1)S(1)} %get-tuple-element.19), channel_id=1, source_target_pairs={{0,1},{1,0},{2,3},{3,2},{4,5},{5,4},{6,7},{7,6},{8,9},{9,8},{10,11... | collective-permute-start | bytes 344072 | tf_op jit(solution)/shard_map/ppermute | solution.py:288
  32.0 2.0 %collective-permute-start.2 = (bf16[8,7168]{1,0:T(8,128)(2,1)S(1)}, bf16[8,7168]{1,0:T(8,128)(2,1)S(1)}, u32[]{:S(2)}, u32[]{:S(2)}) collective-permute-start(bf16[8,7168]{1,0:T(8,128)(2,1)S(1)} %get-tuple-element.21), channel_id=1, source_target_pairs={{0,1},{1,0},{2,3},{3,2},{4,5},{5,4},{6,7},{7,6},{8,9},{9,8},{10,11... | collective-permute-start | bytes 344072 | tf_op jit(solution)/shard_map/ppermute | solution.py:288
  32.5 2.7 %collective-permute-start.4 = (bf16[8,7168]{1,0:T(8,128)(2,1)S(1)}, bf16[8,7168]{1,0:T(8,128)(2,1)S(1)}, u32[]{:S(2)}, u32[]{:S(2)}) collective-permute-start(bf16[8,7168]{1,0:T(8,128)(2,1)S(1)} %get-tuple-element.23), channel_id=1, source_target_pairs={{0,1},{1,0},{2,3},{3,2},{4,5},{5,4},{6,7},{7,6},{8,9},{9,8},{10,11... | collective-permute-start | bytes 344072 | tf_op jit(solution)/shard_map/ppermute | solution.py:288
  32.5 4.5 %collective-permute-start.6 = (bf16[8,7168]{1,0:T(8,128)(2,1)S(1)}, bf16[8,7168]{1,0:T(8,128)(2,1)S(1)}, u32[]{:S(2)}, u32[]{:S(2)}) collective-permute-start(bf16[8,7168]{1,0:T(8,128)(2,1)S(1)} %get-tuple-element.25), channel_id=1, source_target_pairs={{0,1},{1,0},{2,3},{3,2},{4,5},{5,4},{6,7},{7,6},{8,9},{9,8},{10,11... | collective-permute-start | bytes 344072 | tf_op jit(solution)/shard_map/ppermute | solution.py:288
  33.3 7.0 %collective-permute-start.1 = (bf16[8,7168]{1,0:T(8,128)(2,1)S(1)}, bf16[8,7168]{1,0:T(8,128)(2,1)S(1)}, u32[]{:S(2)}, u32[]{:S(2)}) collective-permute-start(bf16[8,7168]{1,0:T(8,128)(2,1)S(1)} %add_convert_fusion.6), channel_id=1, source_target_pairs={{0,6},{1,7},{2,4},{3,5},{4,2},{5,3},{6,0},{7,1},{8,14},{9,15},{10,... | collective-permute-start | bytes 344072 | tf_op jit(solution)/shard_map/ppermute | solution.py:288
  34.0 6.9 %collective-permute-start.3 = (bf16[8,7168]{1,0:T(8,128)(2,1)S(1)}, bf16[8,7168]{1,0:T(8,128)(2,1)S(1)}, u32[]{:S(2)}, u32[]{:S(2)}) collective-permute-start(bf16[8,7168]{1,0:T(8,128)(2,1)S(1)} %add_convert_fusion.5), channel_id=1, source_target_pairs={{0,4},{1,5},{2,6},{3,7},{4,0},{5,1},{6,2},{7,3},{8,12},{9,13},{10,... | collective-permute-start | bytes 344072 | tf_op jit(solution)/shard_map/ppermute | solution.py:288
  35.2 6.8 %collective-permute-start.5 = (bf16[8,7168]{1,0:T(8,128)(2,1)S(1)}, bf16[8,7168]{1,0:T(8,128)(2,1)S(1)}, u32[]{:S(2)}, u32[]{:S(2)}) collective-permute-start(bf16[8,7168]{1,0:T(8,128)(2,1)S(1)} %add_convert_fusion.4), channel_id=1, source_target_pairs={{0,2},{1,3},{2,0},{3,1},{4,6},{5,7},{6,4},{7,5},{8,10},{9,11},{10,... | collective-permute-start | bytes 344072 | tf_op jit(solution)/shard_map/ppermute | solution.py:288
  42.0 8.4 %collective-permute-start.7 = (bf16[8,7168]{1,0:T(8,128)(2,1)S(1)}, bf16[8,7168]{1,0:T(8,128)(2,1)S(1)}, u32[]{:S(2)}, u32[]{:S(2)}) collective-permute-start(bf16[8,7168]{1,0:T(8,128)(2,1)S(1)} %fusion.4), channel_id=1, source_target_pairs={{0,8},{1,9},{2,10},{3,11},{4,12},{5,13},{6,14},{7,15},{8,0},{9,1},... | collective-permute-start | bytes 344072 | tf_op jit(solution)/shard_map/ppermute | solution.py:288
  50.6 6.1 %collective-permute-start.8 = (bf16[8,7168]{1,0:T(8,128)(2,1)S(1)}, bf16[8,7168]{1,0:T(8,128)(2,1)S(1)}, u32[]{:S(2)}, u32[]{:S(2)}) collective-permute-start(bf16[8,7168]{1,0:T(8,128)(2,1)S(1)} %add_convert_fusion.3.refs_0_), channel_id=1, source_target_pairs={{0,4},{1,5},{2,6},{3,7},{4,0},{5,1},{6,2},{7,3},{8,12},{9,13},{10,... | collective-permute-start | bytes 344072 | tf_op jit(solution)/shard_map/ppermute | solution.py:288
  50.7 7.6 %collective-permute-start.9 = (bf16[8,7168]{1,0:T(8,128)(2,1)S(1)}, bf16[8,7168]{1,0:T(8,128)(2,1)S(1)}, u32[]{:S(2)}, u32[]{:S(2)}) collective-permute-start(bf16[8,7168]{1,0:T(8,128)(2,1)S(1)} %add_convert_fusion.3.refs_0_), channel_id=1, source_target_pairs={{0,2},{1,3},{2,0},{3,1},{4,6},{5,7},{6,4},{7,5},{8,10},{9,11},{10,... | collective-permute-start | bytes 344072 | tf_op jit(solution)/shard_map/ppermute | solution.py:288
  50.8 7.5 %collective-permute-start.10 = (bf16[8,7168]{1,0:T(8,128)(2,1)S(1)}, bf16[8,7168]{1,0:T(8,128)(2,1)S(1)}, u32[]{:S(2)}, u32[]{:S(2)}) collective-permute-start(bf16[8,7168]{1,0:T(8,128)(2,1)S(1)} %add_convert_fusion.3.refs_0_), channel_id=1, source_target_pairs={{0,6},{1,7},{2,4},{3,5},{4,2},{5,3},{6,0},{7,1},{8,14},{9,15},{10,... | collective-permute-start | bytes 344072 | tf_op jit(solution)/shard_map/ppermute | solution.py:288
  54.2 4.6 %collective-permute-start.11 = (bf16[8,7168]{1,0:T(8,128)(2,1)S(1)}, bf16[8,7168]{1,0:T(8,128)(2,1)S(1)}, u32[]{:S(2)}, u32[]{:S(2)}) collective-permute-start(bf16[8,7168]{1,0:T(8,128)(2,1)S(1)} %add_convert_fusion.3.refs_0_), channel_id=1, source_target_pairs={{0,1},{1,0},{2,3},{3,2},{4,5},{5,4},{6,7},{7,6},{8,9},{9,8},{10,11... | collective-permute-start | bytes 344072 | tf_op jit(solution)/shard_map/ppermute | solution.py:288
  56.7 2.1 %collective-permute-start.12 = (bf16[8,7168]{1,0:T(8,128)(2,1)S(1)}, bf16[8,7168]{1,0:T(8,128)(2,1)S(1)}, u32[]{:S(2)}, u32[]{:S(2)}) collective-permute-start(bf16[8,7168]{1,0:T(8,128)(2,1)S(1)} %collective-permute-done.8.refs_1_), channel_id=1, source_target_pairs={{0,1},{1,0},{2,3},{3,2},{4,5},{5,4},{6,7},{7,6},{8,9},{9,8},{10,11... | collective-permute-start | bytes 344072 | tf_op jit(solution)/shard_map/ppermute | solution.py:288
  58.3 1.3 %collective-permute-start.13 = (bf16[8,7168]{1,0:T(8,128)(2,1)S(1)}, bf16[8,7168]{1,0:T(8,128)(2,1)S(1)}, u32[]{:S(2)}, u32[]{:S(2)}) collective-permute-start(bf16[8,7168]{1,0:T(8,128)(2,1)S(1)} %collective-permute-done.9.refs_2_), channel_id=1, source_target_pairs={{0,1},{1,0},{2,3},{3,2},{4,5},{5,4},{6,7},{7,6},{8,9},{9,8},{10,11... | collective-permute-start | bytes 344072 | tf_op jit(solution)/shard_map/ppermute | solution.py:288
  58.3 1.5 %collective-permute-start.14 = (bf16[8,7168]{1,0:T(8,128)(2,1)S(1)}, bf16[8,7168]{1,0:T(8,128)(2,1)S(1)}, u32[]{:S(2)}, u32[]{:S(2)}) collective-permute-start(bf16[8,7168]{1,0:T(8,128)(2,1)S(1)} %collective-permute-done.10.refs_3_), channel_id=1, source_target_pairs={{0,1},{1,0},{2,3},{3,2},{4,5},{5,4},{6,7},{7,6},{8,9},{9,8},{10,11... | collective-permute-start | bytes 344072 | tf_op jit(solution)/shard_map/ppermute | solution.py:288
  62.2 1.4 %collective-permute-start.15 = (bf16[8,7168]{1,0:T(8,128)(2,1)S(1)}, bf16[8,7168]{1,0:T(8,128)(2,1)S(1)}, u32[]{:S(2)}, u32[]{:S(2)}) collective-permute-start(bf16[8,7168]{1,0:T(8,128)(2,1)S(1)} %get-tuple-element.27), channel_id=1, source_target_pairs={{0,1},{1,0},{2,3},{3,2},{4,5},{5,4},{6,7},{7,6},{8,9},{9,8},{10,11... | collective-permute-start | bytes 344072 | tf_op jit(solution)/shard_map/ppermute | solution.py:288
  62.6 2.5 %collective-permute-start.17 = (bf16[8,7168]{1,0:T(8,128)(2,1)S(1)}, bf16[8,7168]{1,0:T(8,128)(2,1)S(1)}, u32[]{:S(2)}, u32[]{:S(2)}) collective-permute-start(bf16[8,7168]{1,0:T(8,128)(2,1)S(1)} %get-tuple-element.29), channel_id=1, source_target_pairs={{0,1},{1,0},{2,3},{3,2},{4,5},{5,4},{6,7},{7,6},{8,9},{9,8},{10,11... | collective-permute-start | bytes 344072 | tf_op jit(solution)/shard_map/ppermute | solution.py:288
  62.8 3.7 %collective-permute-start.19 = (bf16[8,7168]{1,0:T(8,128)(2,1)S(1)}, bf16[8,7168]{1,0:T(8,128)(2,1)S(1)}, u32[]{:S(2)}, u32[]{:S(2)}) collective-permute-start(bf16[8,7168]{1,0:T(8,128)(2,1)S(1)} %get-tuple-element.31), channel_id=1, source_target_pairs={{0,1},{1,0},{2,3},{3,2},{4,5},{5,4},{6,7},{7,6},{8,9},{9,8},{10,11... | collective-permute-start | bytes 344072 | tf_op jit(solution)/shard_map/ppermute | solution.py:288
  63.1 4.2 %collective-permute-start.21 = (bf16[8,7168]{1,0:T(8,128)(2,1)S(1)}, bf16[8,7168]{1,0:T(8,128)(2,1)S(1)}, u32[]{:S(2)}, u32[]{:S(2)}) collective-permute-start(bf16[8,7168]{1,0:T(8,128)(2,1)S(1)} %get-tuple-element.33), channel_id=1, source_target_pairs={{0,1},{1,0},{2,3},{3,2},{4,5},{5,4},{6,7},{7,6},{8,9},{9,8},{10,11... | collective-permute-start | bytes 344072 | tf_op jit(solution)/shard_map/ppermute | solution.py:288
  63.6 6.9 %collective-permute-start.16 = (bf16[8,7168]{1,0:T(8,128)(2,1)S(1)}, bf16[8,7168]{1,0:T(8,128)(2,1)S(1)}, u32[]{:S(2)}, u32[]{:S(2)}) collective-permute-start(bf16[8,7168]{1,0:T(8,128)(2,1)S(1)} %add_convert_fusion.2), channel_id=1, source_target_pairs={{0,6},{1,7},{2,4},{3,5},{4,2},{5,3},{6,0},{7,1},{8,14},{9,15},{10,... | collective-permute-start | bytes 344072 | tf_op jit(solution)/shard_map/ppermute | solution.py:288
  65.1 6.9 %collective-permute-start.18 = (bf16[8,7168]{1,0:T(8,128)(2,1)S(1)}, bf16[8,7168]{1,0:T(8,128)(2,1)S(1)}, u32[]{:S(2)}, u32[]{:S(2)}) collective-permute-start(bf16[8,7168]{1,0:T(8,128)(2,1)S(1)} %add_convert_fusion.1), channel_id=1, source_target_pairs={{0,4},{1,5},{2,6},{3,7},{4,0},{5,1},{6,2},{7,3},{8,12},{9,13},{10,... | collective-permute-start | bytes 344072 | tf_op jit(solution)/shard_map/ppermute | solution.py:288
  66.5 6.0 %collective-permute-start.20 = (bf16[8,7168]{1,0:T(8,128)(2,1)S(1)}, bf16[8,7168]{1,0:T(8,128)(2,1)S(1)}, u32[]{:S(2)}, u32[]{:S(2)}) collective-permute-start(bf16[8,7168]{1,0:T(8,128)(2,1)S(1)} %add_convert_fusion), channel_id=1, source_target_pairs={{0,2},{1,3},{2,0},{3,1},{4,6},{5,7},{6,4},{7,5},{8,10},{9,11},{10,... | collective-permute-start | bytes 344072 | tf_op jit(solution)/shard_map/ppermute | solution.py:288
  72.5 6.4 %collective-permute-start.22 = (bf16[4,7168]{1,0:T(4,128)(2,1)S(1)}, bf16[4,7168]{1,0:T(4,128)(2,1)S(1)}, u32[]{:S(2)}, u32[]{:S(2)}) collective-permute-start(bf16[4,7168]{1,0:T(4,128)(2,1)S(1)} %slice.32), channel_id=1, source_target_pairs={{0,8},{1,9},{2,10},{3,11},{4,12},{5,13},{6,14},{7,15},{8,0},{9,1},... | collective-permute-start | bytes 172040 | tf_op jit(solution)/shard_map/ppermute | solution.py:288
  (9 other events, 234.4 us)

commit v8 on v7

--- a/solution.py
+++ b/solution.py
@@ -14,7 +14,7 @@
 LANES = 128
 TILE = 256
 PARTS = 4
-SQUARE = (0, 4, 2, 6)
+SQUARE = (0, 6, 4, 2)
 PIECES = len(SQUARE)
 MIB = 2**20
 
@@ -27,7 +27,8 @@
     len_ref,
     queries_ref,
     cache_ref,
-    latent_ref,
+    near_ref,
+    across_ref,
     length,
     queries,
     held,
@@ -124,17 +125,28 @@
         factors[row] = factor * (1.0 / total)[None]
     for row in range(own_rows):
 
-        def merge(block, latent, row=row):
-            return latent + products[row, block] * factors[row, block][:, :1]
-
-        latent = lax.fori_loop(
-            0, counts[row], merge, jnp.zeros((heads, rank), jnp.float32)
-        )
+        def merge(block, tiles, row=row):
+            factor = factors[row, block]
+            return tuple(
+                tile + product * factor
+                for tile, product in zip(tiles, lane_tiles(products[row, block]))
+            )
+
+        tiles = lax.fori_loop(
+            0,
+            counts[row],
+            merge,
+            (jnp.zeros((heads, LANES), jnp.float32),) * (rank // LANES),
+        )
+        latent = jnp.concatenate(tiles, axis=1)
         for device in range(devices):
             staged[device, row * own_heads : (row + 1) * own_heads, :] = latent[
                 device * own_heads : (device + 1) * own_heads
             ]
-    latent_ref[...] = staged[...].astype(latent_ref.dtype)
+    core = lax.axis_index("experts") & 1
+    for chip in range(devices // 2):
+        near_ref[chip] = staged[2 * chip + core].astype(near_ref.dtype)
+        across_ref[chip] = staged[2 * chip + 1 - core].astype(across_ref.dtype)
 
 
 def attend(queries, cache, cache_len, devices, rank):
@@ -144,9 +156,9 @@
     listed = own_rows * blocks
     return pl.pallas_call(
         attend_kernel,
-        out_shape=jax.ShapeDtypeStruct((devices, packed, rank), jnp.bfloat16),
+        out_shape=(jax.ShapeDtypeStruct((devices // 2, packed, rank), jnp.bfloat16),) * 2,
         in_specs=[pl.BlockSpec(memory_space=pl.ANY)] * 3,
-        out_specs=pl.BlockSpec(memory_space=pltpu.VMEM),
+        out_specs=(pl.BlockSpec(memory_space=pltpu.VMEM),) * 2,
         scratch_shapes=[
             pltpu.SMEM((own_rows,), jnp.int32),
             pltpu.VMEM((own_rows, heads, depth), jnp.bfloat16),
@@ -196,8 +208,9 @@
     far_bits = far.bit_length() - 1
     request, slot = row & (own_rows - 1), row >> turn
     far_at, slot = slot & (far - 1), slot >> far_bits
-    distance = (far_at << 3) + ((slot & 1) << 2) + ((slot >> 1 & 1) << 1) + (slot >> 2)
+    distance = (far_at << 3) + ((4 - (slot & 3) & 3) << 1) + (slot >> 2)
     device = distance ^ lax.axis_index("experts")
+    device = (device & ~1) + (distance & 1)
     values = []
     for head in range(own_heads):
         wanted = ((device << turn) + request) * own_heads + head
@@ -295,7 +308,7 @@
 def collect(terms):
     keeps, sends = terms[:PIECES], terms[PIECES:]
     total = 0.0
-    for piece in (3, 1, 2, 0):
+    for piece in (1, 2, 3, 0):
         part = keeps[piece] + wide(swap(sends[piece], 1))
         if piece:
             part = wide(swap(part.astype(jnp.bfloat16), SQUARE[piece]))
@@ -343,8 +356,16 @@
     split_ways = FF // w_gate.shape[1]
     assert split_ways == 8
 
-    latent = attend(queries, cache, cache_len, devices, w_absorb.shape[1])
-    joined = lax.all_to_all(latent, "experts", split_axis=0, concat_axis=0, tiled=True)
+    near, across = attend(queries, cache, cache_len, devices, w_absorb.shape[1])
+    same_core = [[2 * chip + core for chip in range(devices // 2)] for core in range(2)]
+    joined = lax.all_to_all(
+        jnp.concatenate([near, swap(across, 1)], axis=1),
+        "experts",
+        split_axis=0,
+        concat_axis=0,
+        axis_index_groups=same_core,
+        tiled=True,
+    )
     joined = joined.reshape(-1, joined.shape[-1])
     terms = project(joined, w_absorb, residual_in, w_out, all_rows, far)
     stream = exchange(collect(terms), far)

time: 78.3 us -> 76.8 us (0.981); the launches traced: 79.6 us -> 76.9 us
  Pallas kernels: 12.3 us -> 9.03 us
  other arithmetic: 1.27 us -> 2.16 us
    pallas_call x1, Pallas kernels: 7.84 us -> 4.57 us  [attend(): pl.pallas_call(attend_kernel, out_shape=(jax.ShapeDtypeStruct((devices //...]
    concatenate x0 -> x1, other arithmetic: none -> 0.92 us  [shards(): jnp.concatenate([near, swap(across, 1)], axis=1)]
    ppermute x23 -> x24, waiting for transfers between devices: 27.3 us -> 27.7 us  [swap(): return lax.ppermute(array, 'experts', pairs)]
    ppermute x23 -> x24, starting transfers between devices: 16 us -> 15.8 us  [swap(): return lax.ppermute(array, 'experts', pairs)]
  transfers between devices with their start and end apart: 23 -> 24, of which waited for: 14 -> 15; matrix products, arithmetic and copies ran while one was open for 1% -> 1% of each run, Pallas kernels for 0% -> 0%
where the time goes in v8:
time: 76.8 us; the launch traced here: 76.9 us
  waiting for transfers between devices  27.7 us (36%)
  blocking collectives  20.6 us (27%)
  starting transfers between devices  15.8 us (21%)
  Pallas kernels  9.03 us (12%)
  other arithmetic  2.16 us (3%)
  between operations  0.84 us (1%)
  local copies, waits for them, and re-layouts  0.77 us (1%)
    ppermute x24, waiting for transfers between devices, swap(): return lax.ppermute(array, 'experts', pairs)  27.7 us
    all_to_all x1, blocking collectives, shards(): lax.all_to_all(jnp.concatenate([near, swap(across, 1)], axis=1), 'experts...  20.6 us
    ppermute x24, starting transfers between devices, swap(): return lax.ppermute(array, 'experts', pairs)  15.8 us
    pallas_call x1, Pallas kernels, attend(): pl.pallas_call(attend_kernel, out_shape=(jax.ShapeDtypeStruct((devices //...  4.57 us
    pallas_call x1, Pallas kernels, run_expert(): pl.pallas_call(expert_kernel, out_shape=term_shapes(rows, width), in_spec...  2.36 us
    pallas_call x1, Pallas kernels, project(): pl.pallas_call(functools.partial(project_kernel, own_rows, far), out_shap...  2.1 us
  transfers between devices with their start and end apart: 24, of which 15 were waited for; matrix products, arithmetic and copies ran while one was open for 1% of the time, Pallas kernels for 0%

profile of v8, /device:TPU:0, one launch (start us, length us, event | category | flops | bytes accessed | tf_op | source)
XLA Modules:
  0.0 76.9 jit_solution(2769694543050695311)
XLA Ops:
  0.7 4.6 %attend.1 = (bf16[8,16,512]{2,1,0:T(8,128)(2,1)}, bf16[8,16,512]{2,1,0:T(8,128)(2,1)}) custom-call(s32[4]{0:T(128)} %len_ref.1, bf16[4,64,576]{2,1,0:T(8,128)(2,1)} %bitcast.7, bf16[4,576,4096]{2,1,0:T(8,128)(2,1)} %cache_ref.1), custom_call_target="tpu_custom_call" | custom-call | flops 1140850688 | bytes 9437184 | tf_op jit(solution)/shard_map/attend/pallas_call | solution.py:157
  5.8 1.2 %collective-permute-done = bf16[8,16,512]{2,1,0:T(8,128)(2,1)S(1)} collective-permute-done((bf16[8,16,512]{2,1,0:T(8,128)(2,1)}, bf16[8,16,512]{2,1,0:T(8,128)(2,1)S(1)}, u32[]{:S(2)}, u32[]{:S(2)}) %collective-permute-start) | collective-permute-done | bytes 131104 | tf_op jit(solution)/shard_map/ppermute | solution.py:301
  7.0 0.9 %pad_maximum_fusion = bf16[8,32,512]{2,1,0:T(8,128)(2,1)S(1)} fusion(bf16[8,16,512]{2,1,0:T(8,128)(2,1)S(1)} %collective-permute-done, bf16[8,16,512]{2,1,0:T(8,128)(2,1)} %get-tuple-element.20), kind=kLoop, calls=%fused_computation | loop fusion | flops 524288 | bytes 524288 | tf_op jit(solution)/shard_map/concatenate | solution.py:362
  7.9 20.6 %all_to_all.5 = bf16[8,32,512]{2,1,0:T(8,128)(2,1)S(1)} all-to-all(bf16[8,32,512]{2,1,0:T(8,128)(2,1)S(1)} %pad_maximum_fusion), channel_id=1, replica_groups={{0,2,4,6,8,10,12,14},{1,3,5,7,9,11,13,15},{16,18,20,22,24,26,28,30},{17..., dimensions={0} | all-to-all | bytes 524288 | tf_op jit(solution)/shard_map/all_to_all | solution.py:361
  28.5 2.1 %project.1 = (f32[8,7168]{1,0:T(8,128)S(1)}, f32[8,7168]{1,0:T(8,128)S(1)}, f32[8,7168]{1,0:T(8,128)S(1)}, f32[8,7168]{1,0:T(8,128)S(1)}, bf16[8,7168]{1,0:T(8,1...) custom-call(bf16[256,512]{1,0:T(8,128)(2,1)S(1)} %bitcast.5, ...), custom_call_target="tpu_custom_call" | custom-call | flops 469762048 | bytes 7340032 | tf_op jit(solution)/shard_map/project/pallas_call | solution.py:234
  32.0 1.0 %collective-permute-start.2 = (bf16[8,7168]{1,0:T(8,128)(2,1)S(1)}, bf16[8,7168]{1,0:T(8,128)(2,1)S(1)}, u32[]{:S(2)}, u32[]{:S(2)}) collective-permute-start(bf16[8,7168]{1,0:T(8,128)(2,1)S(1)} %add_convert_fusion.6), channel_id=1, source_target_pairs={{0,6},{1,7},{2,4},{3,5},{4,2},{5,3},{6,0},{7,1},{8,14},{9,15},{10,... | collective-permute-start | bytes 344072 | tf_op jit(solution)/shard_map/ppermute | solution.py:301
  33.1 2.0 %collective-permute-start.4 = (bf16[8,7168]{1,0:T(8,128)(2,1)S(1)}, bf16[8,7168]{1,0:T(8,128)(2,1)S(1)}, u32[]{:S(2)}, u32[]{:S(2)}) collective-permute-start(bf16[8,7168]{1,0:T(8,128)(2,1)S(1)} %add_convert_fusion.5), channel_id=1, source_target_pairs={{0,4},{1,5},{2,6},{3,7},{4,0},{5,1},{6,2},{7,3},{8,12},{9,13},{10,... | collective-permute-start | bytes 344072 | tf_op jit(solution)/shard_map/ppermute | solution.py:301
  35.8 3.2 %collective-permute-done.2 = bf16[8,7168]{1,0:T(8,128)(2,1)S(1)} collective-permute-done((bf16[8,7168]{1,0:T(8,128)(2,1)S(1)}, bf16[8,7168]{1,0:T(8,128)(2,1)S(1)}, u32[]{:S(2)}, u32[]{:S(2)}) %collective-permute-start.2) | collective-permute-done | bytes 114720 | tf_op jit(solution)/shard_map/ppermute | solution.py:301
  39.0 1.6 %collective-permute-done.4 = bf16[8,7168]{1,0:T(8,128)(2,1)S(1)} collective-permute-done((bf16[8,7168]{1,0:T(8,128)(2,1)S(1)}, bf16[8,7168]{1,0:T(8,128)(2,1)S(1)}, u32[]{:S(2)}, u32[]{:S(2)}) %collective-permute-start.4) | collective-permute-done | bytes 114720 | tf_op jit(solution)/shard_map/ppermute | solution.py:301
  40.7 1.0 %collective-permute-start.8 = (bf16[8,7168]{1,0:T(8,128)(2,1)S(1)}, bf16[8,7168]{1,0:T(8,128)(2,1)S(1)}, u32[]{:S(2)}, u32[]{:S(2)}) collective-permute-start(bf16[8,7168]{1,0:T(8,128)(2,1)S(1)} %fusion.4), channel_id=1, source_target_pairs={{0,8},{1,9},{2,10},{3,11},{4,12},{5,13},{6,14},{7,15},{8,0},{9,1},... | collective-permute-start | bytes 344072 | tf_op jit(solution)/shard_map/ppermute | solution.py:301
  41.7 6.9 %collective-permute-done.8 = bf16[8,7168]{1,0:T(8,128)(2,1)S(1)} collective-permute-done((bf16[8,7168]{1,0:T(8,128)(2,1)S(1)}, bf16[8,7168]{1,0:T(8,128)(2,1)S(1)}, u32[]{:S(2)}, u32[]{:S(2)}) %collective-permute-start.8) | collective-permute-done | bytes 114720 | tf_op jit(solution)/shard_map/ppermute | solution.py:301
  48.9 2.4 %collective-permute-start.10 = (bf16[8,7168]{1,0:T(8,128)(2,1)S(1)}, bf16[8,7168]{1,0:T(8,128)(2,1)S(1)}, u32[]{:S(2)}, u32[]{:S(2)}) collective-permute-start(bf16[8,7168]{1,0:T(8,128)(2,1)S(1)} %add_convert_fusion.3.refs_0_), channel_id=1, source_target_pairs={{0,4},{1,5},{2,6},{3,7},{4,0},{5,1},{6,2},{7,3},{8,12},{9,13},{10,... | collective-permute-start | bytes 344072 | tf_op jit(solution)/shard_map/ppermute | solution.py:301
  51.3 1.0 %collective-permute-start.11 = (bf16[8,7168]{1,0:T(8,128)(2,1)S(1)}, bf16[8,7168]{1,0:T(8,128)(2,1)S(1)}, u32[]{:S(2)}, u32[]{:S(2)}) collective-permute-start(bf16[8,7168]{1,0:T(8,128)(2,1)S(1)} %add_convert_fusion.3.refs_0_), channel_id=1, source_target_pairs={{0,2},{1,3},{2,0},{3,1},{4,6},{5,7},{6,4},{7,5},{8,10},{9,11},{10,... | collective-permute-start | bytes 344072 | tf_op jit(solution)/shard_map/ppermute | solution.py:301
  52.4 2.7 %collective-permute-done.9.refs_1_ = bf16[8,7168]{1,0:T(8,128)(2,1)S(1)} collective-permute-done((bf16[8,7168]{1,0:T(8,128)(2,1)S(1)}, bf16[8,7168]{1,0:T(8,128)(2,1)S(1)}, u32[]{:S(2)}, u32[]{:S(2)}) %collective-permute-start.9) | collective-permute-done | bytes 114720 | tf_op jit(solution)/shard_map/ppermute | solution.py:301
  55.1 1.4 %collective-permute-done.10.refs_2_ = bf16[8,7168]{1,0:T(8,128)(2,1)S(1)} collective-permute-done((bf16[8,7168]{1,0:T(8,128)(2,1)S(1)}, bf16[8,7168]{1,0:T(8,128)(2,1)S(1)}, u32[]{:S(2)}, u32[]{:S(2)}) %collective-permute-start.10) | collective-permute-done | bytes 114720 | tf_op jit(solution)/shard_map/ppermute | solution.py:301
  57.0 0.8 %collective-permute-done.14.refs_6_ = bf16[8,7168]{1,0:T(8,128)(2,1)S(1)} collective-permute-done((bf16[8,7168]{1,0:T(8,128)(2,1)S(1)}, bf16[8,7168]{1,0:T(8,128)(2,1)S(1)}, u32[]{:S(2)}, u32[]{:S(2)}) %collective-permute-start.14) | collective-permute-done | bytes 114720 | tf_op jit(solution)/shard_map/ppermute | solution.py:301
  58.1 2.4 %expert.1 = (f32[8,7168]{1,0:T(8,128)S(1)}, f32[8,7168]{1,0:T(8,128)S(1)}, f32[8,7168]{1,0:T(8,128)S(1)}, f32[8,7168]{1,0:T(8,128)S(1)}, bf16[8,7168]{1,0:T(8,12...) custom-call(bf16[8,7168]{1,0:T(8,128)(2,1)S(1)} %add_convert_fusion.3.refs_0_, ...), custom_call_target="tpu_custom_call" | custom-call | flops 704643072 | bytes 11010048 | tf_op jit(solution)/shard_map/expert/pallas_call | solution.py:284
  62.3 2.4 %collective-permute-start.19 = (bf16[8,7168]{1,0:T(8,128)(2,1)S(1)}, bf16[8,7168]{1,0:T(8,128)(2,1)S(1)}, u32[]{:S(2)}, u32[]{:S(2)}) collective-permute-start(bf16[8,7168]{1,0:T(8,128)(2,1)S(1)} %add_convert_fusion.1), channel_id=1, source_target_pairs={{0,4},{1,5},{2,6},{3,7},{4,0},{5,1},{6,2},{7,3},{8,12},{9,13},{10,... | collective-permute-start | bytes 344072 | tf_op jit(solution)/shard_map/ppermute | solution.py:301
  64.8 0.9 %collective-permute-start.21 = (bf16[8,7168]{1,0:T(8,128)(2,1)S(1)}, bf16[8,7168]{1,0:T(8,128)(2,1)S(1)}, u32[]{:S(2)}, u32[]{:S(2)}) collective-permute-start(bf16[8,7168]{1,0:T(8,128)(2,1)S(1)} %add_convert_fusion), channel_id=1, source_target_pairs={{0,2},{1,3},{2,0},{3,1},{4,6},{5,7},{6,4},{7,5},{8,10},{9,11},{10,... | collective-permute-start | bytes 344072 | tf_op jit(solution)/shard_map/ppermute | solution.py:301
  65.6 3.2 %collective-permute-done.17 = bf16[8,7168]{1,0:T(8,128)(2,1)S(1)} collective-permute-done((bf16[8,7168]{1,0:T(8,128)(2,1)S(1)}, bf16[8,7168]{1,0:T(8,128)(2,1)S(1)}, u32[]{:S(2)}, u32[]{:S(2)}) %collective-permute-start.17) | collective-permute-done | bytes 114720 | tf_op jit(solution)/shard_map/ppermute | solution.py:301
  68.8 1.4 %collective-permute-done.19 = bf16[8,7168]{1,0:T(8,128)(2,1)S(1)} collective-permute-done((bf16[8,7168]{1,0:T(8,128)(2,1)S(1)}, bf16[8,7168]{1,0:T(8,128)(2,1)S(1)}, u32[]{:S(2)}, u32[]{:S(2)}) %collective-permute-start.19) | collective-permute-done | bytes 114720 | tf_op jit(solution)/shard_map/ppermute | solution.py:301
  70.7 0.9 %collective-permute-start.23 = (bf16[4,7168]{1,0:T(4,128)(2,1)S(1)}, bf16[4,7168]{1,0:T(4,128)(2,1)S(1)}, u32[]{:S(2)}, u32[]{:S(2)}) collective-permute-start(bf16[4,7168]{1,0:T(4,128)(2,1)S(1)} %slice.32), channel_id=1, source_target_pairs={{0,8},{1,9},{2,10},{3,11},{4,12},{5,13},{6,14},{7,15},{8,0},{9,1},... | collective-permute-start | bytes 172040 | tf_op jit(solution)/shard_map/ppermute | solution.py:301
  72.4 3.8 %collective-permute-done.23 = bf16[4,7168]{1,0:T(4,128)(2,1)S(1)} collective-permute-done((bf16[4,7168]{1,0:T(4,128)(2,1)S(1)}, bf16[4,7168]{1,0:T(4,128)(2,1)S(1)}, u32[]{:S(2)}, u32[]{:S(2)}) %collective-permute-start.23) | collective-permute-done | bytes 57376 | tf_op jit(solution)/shard_map/ppermute | solution.py:301
  76.2 0.7 fusion.1
  (64 shorter events, 6.9 us)
Async XLA Ops:
  5.2 1.7 %collective-permute-start = (bf16[8,16,512]{2,1,0:T(8,128)(2,1)}, bf16[8,16,512]{2,1,0:T(8,128)(2,1)S(1)}, u32[]{:S(2)}, u32[]{:S(2)}) collective-permute-start(bf16[8,16,512]{2,1,0:T(8,128)(2,1)} %get-tuple-element.21), channel_id=1, source_target_pairs={{0,1},{1,0},{2,3},{3,2},{4,5},{5,4},{6,7},{7,6},{8,9},{9,8},{10,11... | collective-permute-start | bytes 393224 | tf_op jit(solution)/shard_map/ppermute | solution.py:301
  30.6 1.4 %collective-permute-start.1 = (bf16[8,7168]{1,0:T(8,128)(2,1)S(1)}, bf16[8,7168]{1,0:T(8,128)(2,1)S(1)}, u32[]{:S(2)}, u32[]{:S(2)}) collective-permute-start(bf16[8,7168]{1,0:T(8,128)(2,1)S(1)} %get-tuple-element.23), channel_id=1, source_target_pairs={{0,1},{1,0},{2,3},{3,2},{4,5},{5,4},{6,7},{7,6},{8,9},{9,8},{10,11... | collective-permute-start | bytes 344072 | tf_op jit(solution)/shard_map/ppermute | solution.py:301
  30.7 2.3 %collective-permute-start.3 = (bf16[8,7168]{1,0:T(8,128)(2,1)S(1)}, bf16[8,7168]{1,0:T(8,128)(2,1)S(1)}, u32[]{:S(2)}, u32[]{:S(2)}) collective-permute-start(bf16[8,7168]{1,0:T(8,128)(2,1)S(1)} %get-tuple-element.25), channel_id=1, source_target_pairs={{0,1},{1,0},{2,3},{3,2},{4,5},{5,4},{6,7},{7,6},{8,9},{9,8},{10,11... | collective-permute-start | bytes 344072 | tf_op jit(solution)/shard_map/ppermute | solution.py:301
  31.2 3.9 %collective-permute-start.5 = (bf16[8,7168]{1,0:T(8,128)(2,1)S(1)}, bf16[8,7168]{1,0:T(8,128)(2,1)S(1)}, u32[]{:S(2)}, u32[]{:S(2)}) collective-permute-start(bf16[8,7168]{1,0:T(8,128)(2,1)S(1)} %get-tuple-element.27), channel_id=1, source_target_pairs={{0,1},{1,0},{2,3},{3,2},{4,5},{5,4},{6,7},{7,6},{8,9},{9,8},{10,11... | collective-permute-start | bytes 344072 | tf_op jit(solution)/shard_map/ppermute | solution.py:301
  31.3 4.5 %collective-permute-start.7 = (bf16[8,7168]{1,0:T(8,128)(2,1)S(1)}, bf16[8,7168]{1,0:T(8,128)(2,1)S(1)}, u32[]{:S(2)}, u32[]{:S(2)}) collective-permute-start(bf16[8,7168]{1,0:T(8,128)(2,1)S(1)} %get-tuple-element.29), channel_id=1, source_target_pairs={{0,1},{1,0},{2,3},{3,2},{4,5},{5,4},{6,7},{7,6},{8,9},{9,8},{10,11... | collective-permute-start | bytes 344072 | tf_op jit(solution)/shard_map/ppermute | solution.py:301
  32.0 7.0 %collective-permute-start.2 = (bf16[8,7168]{1,0:T(8,128)(2,1)S(1)}, bf16[8,7168]{1,0:T(8,128)(2,1)S(1)}, u32[]{:S(2)}, u32[]{:S(2)}) collective-permute-start(bf16[8,7168]{1,0:T(8,128)(2,1)S(1)} %add_convert_fusion.6), channel_id=1, source_target_pairs={{0,6},{1,7},{2,4},{3,5},{4,2},{5,3},{6,0},{7,1},{8,14},{9,15},{10,... | collective-permute-start | bytes 344072 | tf_op jit(solution)/shard_map/ppermute | solution.py:301
  33.1 7.6 %collective-permute-start.4 = (bf16[8,7168]{1,0:T(8,128)(2,1)S(1)}, bf16[8,7168]{1,0:T(8,128)(2,1)S(1)}, u32[]{:S(2)}, u32[]{:S(2)}) collective-permute-start(bf16[8,7168]{1,0:T(8,128)(2,1)S(1)} %add_convert_fusion.5), channel_id=1, source_target_pairs={{0,4},{1,5},{2,6},{3,7},{4,0},{5,1},{6,2},{7,3},{8,12},{9,13},{10,... | collective-permute-start | bytes 344072 | tf_op jit(solution)/shard_map/ppermute | solution.py:301
  35.1 5.6 %collective-permute-start.6 = (bf16[8,7168]{1,0:T(8,128)(2,1)S(1)}, bf16[8,7168]{1,0:T(8,128)(2,1)S(1)}, u32[]{:S(2)}, u32[]{:S(2)}) collective-permute-start(bf16[8,7168]{1,0:T(8,128)(2,1)S(1)} %add_convert_fusion.4), channel_id=1, source_target_pairs={{0,2},{1,3},{2,0},{3,1},{4,6},{5,7},{6,4},{7,5},{8,10},{9,11},{10,... | collective-permute-start | bytes 344072 | tf_op jit(solution)/shard_map/ppermute | solution.py:301
  40.7 7.9 %collective-permute-start.8 = (bf16[8,7168]{1,0:T(8,128)(2,1)S(1)}, bf16[8,7168]{1,0:T(8,128)(2,1)S(1)}, u32[]{:S(2)}, u32[]{:S(2)}) collective-permute-start(bf16[8,7168]{1,0:T(8,128)(2,1)S(1)} %fusion.4), channel_id=1, source_target_pairs={{0,8},{1,9},{2,10},{3,11},{4,12},{5,13},{6,14},{7,15},{8,0},{9,1},... | collective-permute-start | bytes 344072 | tf_op jit(solution)/shard_map/ppermute | solution.py:301
  48.8 6.2 %collective-permute-start.9 = (bf16[8,7168]{1,0:T(8,128)(2,1)S(1)}, bf16[8,7168]{1,0:T(8,128)(2,1)S(1)}, u32[]{:S(2)}, u32[]{:S(2)}) collective-permute-start(bf16[8,7168]{1,0:T(8,128)(2,1)S(1)} %add_convert_fusion.3.refs_0_), channel_id=1, source_target_pairs={{0,6},{1,7},{2,4},{3,5},{4,2},{5,3},{6,0},{7,1},{8,14},{9,15},{10,... | collective-permute-start | bytes 344072 | tf_op jit(solution)/shard_map/ppermute | solution.py:301
  48.9 7.6 %collective-permute-start.10 = (bf16[8,7168]{1,0:T(8,128)(2,1)S(1)}, bf16[8,7168]{1,0:T(8,128)(2,1)S(1)}, u32[]{:S(2)}, u32[]{:S(2)}) collective-permute-start(bf16[8,7168]{1,0:T(8,128)(2,1)S(1)} %add_convert_fusion.3.refs_0_), channel_id=1, source_target_pairs={{0,4},{1,5},{2,6},{3,7},{4,0},{5,1},{6,2},{7,3},{8,12},{9,13},{10,... | collective-permute-start | bytes 344072 | tf_op jit(solution)/shard_map/ppermute | solution.py:301
  51.3 5.4 %collective-permute-start.11 = (bf16[8,7168]{1,0:T(8,128)(2,1)S(1)}, bf16[8,7168]{1,0:T(8,128)(2,1)S(1)}, u32[]{:S(2)}, u32[]{:S(2)}) collective-permute-start(bf16[8,7168]{1,0:T(8,128)(2,1)S(1)} %add_convert_fusion.3.refs_0_), channel_id=1, source_target_pairs={{0,2},{1,3},{2,0},{3,1},{4,6},{5,7},{6,4},{7,5},{8,10},{9,11},{10,... | collective-permute-start | bytes 344072 | tf_op jit(solution)/shard_map/ppermute | solution.py:301
  52.4 4.6 %collective-permute-start.12 = (bf16[8,7168]{1,0:T(8,128)(2,1)S(1)}, bf16[8,7168]{1,0:T(8,128)(2,1)S(1)}, u32[]{:S(2)}, u32[]{:S(2)}) collective-permute-start(bf16[8,7168]{1,0:T(8,128)(2,1)S(1)} %add_convert_fusion.3.refs_0_), channel_id=1, source_target_pairs={{0,1},{1,0},{2,3},{3,2},{4,5},{5,4},{6,7},{7,6},{8,9},{9,8},{10,11... | collective-permute-start | bytes 344072 | tf_op jit(solution)/shard_map/ppermute | solution.py:301
  55.1 1.9 %collective-permute-start.13 = (bf16[8,7168]{1,0:T(8,128)(2,1)S(1)}, bf16[8,7168]{1,0:T(8,128)(2,1)S(1)}, u32[]{:S(2)}, u32[]{:S(2)}) collective-permute-start(bf16[8,7168]{1,0:T(8,128)(2,1)S(1)} %collective-permute-done.9.refs_1_), channel_id=1, source_target_pairs={{0,1},{1,0},{2,3},{3,2},{4,5},{5,4},{6,7},{7,6},{8,9},{9,8},{10,11... | collective-permute-start | bytes 344072 | tf_op jit(solution)/shard_map/ppermute | solution.py:301
  56.5 1.3 %collective-permute-start.14 = (bf16[8,7168]{1,0:T(8,128)(2,1)S(1)}, bf16[8,7168]{1,0:T(8,128)(2,1)S(1)}, u32[]{:S(2)}, u32[]{:S(2)}) collective-permute-start(bf16[8,7168]{1,0:T(8,128)(2,1)S(1)} %collective-permute-done.10.refs_2_), channel_id=1, source_target_pairs={{0,1},{1,0},{2,3},{3,2},{4,5},{5,4},{6,7},{7,6},{8,9},{9,8},{10,11... | collective-permute-start | bytes 344072 | tf_op jit(solution)/shard_map/ppermute | solution.py:301
  56.7 1.3 %collective-permute-start.15 = (bf16[8,7168]{1,0:T(8,128)(2,1)S(1)}, bf16[8,7168]{1,0:T(8,128)(2,1)S(1)}, u32[]{:S(2)}, u32[]{:S(2)}) collective-permute-start(bf16[8,7168]{1,0:T(8,128)(2,1)S(1)} %collective-permute-done.11.refs_3_), channel_id=1, source_target_pairs={{0,1},{1,0},{2,3},{3,2},{4,5},{5,4},{6,7},{7,6},{8,9},{9,8},{10,11... | collective-permute-start | bytes 344072 | tf_op jit(solution)/shard_map/ppermute | solution.py:301
  60.5 1.4 %collective-permute-start.16 = (bf16[8,7168]{1,0:T(8,128)(2,1)S(1)}, bf16[8,7168]{1,0:T(8,128)(2,1)S(1)}, u32[]{:S(2)}, u32[]{:S(2)}) collective-permute-start(bf16[8,7168]{1,0:T(8,128)(2,1)S(1)} %get-tuple-element.31), channel_id=1, source_target_pairs={{0,1},{1,0},{2,3},{3,2},{4,5},{5,4},{6,7},{7,6},{8,9},{9,8},{10,11... | collective-permute-start | bytes 344072 | tf_op jit(solution)/shard_map/ppermute | solution.py:301
  60.8 1.5 %collective-permute-start.18 = (bf16[8,7168]{1,0:T(8,128)(2,1)S(1)}, bf16[8,7168]{1,0:T(8,128)(2,1)S(1)}, u32[]{:S(2)}, u32[]{:S(2)}) collective-permute-start(bf16[8,7168]{1,0:T(8,128)(2,1)S(1)} %get-tuple-element.33), channel_id=1, source_target_pairs={{0,1},{1,0},{2,3},{3,2},{4,5},{5,4},{6,7},{7,6},{8,9},{9,8},{10,11... | collective-permute-start | bytes 344072 | tf_op jit(solution)/shard_map/ppermute | solution.py:301
  61.0 3.7 %collective-permute-start.20 = (bf16[8,7168]{1,0:T(8,128)(2,1)S(1)}, bf16[8,7168]{1,0:T(8,128)(2,1)S(1)}, u32[]{:S(2)}, u32[]{:S(2)}) collective-permute-start(bf16[8,7168]{1,0:T(8,128)(2,1)S(1)} %get-tuple-element.35), channel_id=1, source_target_pairs={{0,1},{1,0},{2,3},{3,2},{4,5},{5,4},{6,7},{7,6},{8,9},{9,8},{10,11... | collective-permute-start | bytes 344072 | tf_op jit(solution)/shard_map/ppermute | solution.py:301
  61.3 4.3 %collective-permute-start.22 = (bf16[8,7168]{1,0:T(8,128)(2,1)S(1)}, bf16[8,7168]{1,0:T(8,128)(2,1)S(1)}, u32[]{:S(2)}, u32[]{:S(2)}) collective-permute-start(bf16[8,7168]{1,0:T(8,128)(2,1)S(1)} %get-tuple-element.37), channel_id=1, source_target_pairs={{0,1},{1,0},{2,3},{3,2},{4,5},{5,4},{6,7},{7,6},{8,9},{9,8},{10,11... | collective-permute-start | bytes 344072 | tf_op jit(solution)/shard_map/ppermute | solution.py:301
  61.9 6.9 %collective-permute-start.17 = (bf16[8,7168]{1,0:T(8,128)(2,1)S(1)}, bf16[8,7168]{1,0:T(8,128)(2,1)S(1)}, u32[]{:S(2)}, u32[]{:S(2)}) collective-permute-start(bf16[8,7168]{1,0:T(8,128)(2,1)S(1)} %add_convert_fusion.2), channel_id=1, source_target_pairs={{0,6},{1,7},{2,4},{3,5},{4,2},{5,3},{6,0},{7,1},{8,14},{9,15},{10,... | collective-permute-start | bytes 344072 | tf_op jit(solution)/shard_map/ppermute | solution.py:301
  62.3 8.0 %collective-permute-start.19 = (bf16[8,7168]{1,0:T(8,128)(2,1)S(1)}, bf16[8,7168]{1,0:T(8,128)(2,1)S(1)}, u32[]{:S(2)}, u32[]{:S(2)}) collective-permute-start(bf16[8,7168]{1,0:T(8,128)(2,1)S(1)} %add_convert_fusion.1), channel_id=1, source_target_pairs={{0,4},{1,5},{2,6},{3,7},{4,0},{5,1},{6,2},{7,3},{8,12},{9,13},{10,... | collective-permute-start | bytes 344072 | tf_op jit(solution)/shard_map/ppermute | solution.py:301
  64.8 5.9 %collective-permute-start.21 = (bf16[8,7168]{1,0:T(8,128)(2,1)S(1)}, bf16[8,7168]{1,0:T(8,128)(2,1)S(1)}, u32[]{:S(2)}, u32[]{:S(2)}) collective-permute-start(bf16[8,7168]{1,0:T(8,128)(2,1)S(1)} %add_convert_fusion), channel_id=1, source_target_pairs={{0,2},{1,3},{2,0},{3,1},{4,6},{5,7},{6,4},{7,5},{8,10},{9,11},{10,... | collective-permute-start | bytes 344072 | tf_op jit(solution)/shard_map/ppermute | solution.py:301
  70.7 5.5 %collective-permute-start.23 = (bf16[4,7168]{1,0:T(4,128)(2,1)S(1)}, bf16[4,7168]{1,0:T(4,128)(2,1)S(1)}, u32[]{:S(2)}, u32[]{:S(2)}) collective-permute-start(bf16[4,7168]{1,0:T(4,128)(2,1)S(1)} %slice.32), channel_id=1, source_target_pairs={{0,8},{1,9},{2,10},{3,11},{4,12},{5,13},{6,14},{7,15},{8,0},{9,1},... | collective-permute-start | bytes 172040 | tf_op jit(solution)/shard_map/ppermute | solution.py:301
  (10 other events, 256.6 us)

commit v9 on v7

--- a/solution.py
+++ b/solution.py
@@ -14,7 +14,7 @@
 LANES = 128
 TILE = 256
 PARTS = 4
-SQUARE = (0, 4, 2, 6)
+SQUARE = (0, 6, 4, 2)
 PIECES = len(SQUARE)
 MIB = 2**20
 
@@ -124,12 +124,20 @@
         factors[row] = factor * (1.0 / total)[None]
     for row in range(own_rows):
 
-        def merge(block, latent, row=row):
-            return latent + products[row, block] * factors[row, block][:, :1]
-
-        latent = lax.fori_loop(
-            0, counts[row], merge, jnp.zeros((heads, rank), jnp.float32)
-        )
+        def merge(block, tiles, row=row):
+            factor = factors[row, block]
+            return tuple(
+                tile + product * factor
+                for tile, product in zip(tiles, lane_tiles(products[row, block]))
+            )
+
+        tiles = lax.fori_loop(
+            0,
+            counts[row],
+            merge,
+            (jnp.zeros((heads, LANES), jnp.float32),) * (rank // LANES),
+        )
+        latent = jnp.concatenate(tiles, axis=1)
         for device in range(devices):
             staged[device, row * own_heads : (row + 1) * own_heads, :] = latent[
                 device * own_heads : (device + 1) * own_heads
@@ -196,7 +204,7 @@
     far_bits = far.bit_length() - 1
     request, slot = row & (own_rows - 1), row >> turn
     far_at, slot = slot & (far - 1), slot >> far_bits
-    distance = (far_at << 3) + ((slot & 1) << 2) + ((slot >> 1 & 1) << 1) + (slot >> 2)
+    distance = (far_at << 3) + ((4 - (slot & 3) & 3) << 1) + (slot >> 2)
     device = distance ^ lax.axis_index("experts")
     values = []
     for head in range(own_heads):
@@ -295,7 +303,7 @@
 def collect(terms):
     keeps, sends = terms[:PIECES], terms[PIECES:]
     total = 0.0
-    for piece in (3, 1, 2, 0):
+    for piece in (1, 2, 3, 0):
         part = keeps[piece] + wide(swap(sends[piece], 1))
         if piece:
             part = wide(swap(part.astype(jnp.bfloat16), SQUARE[piece]))
@@ -350,17 +358,31 @@
     stream = exchange(collect(terms), far)
     attended = stream[:own_rows]
 
-    total = collect(run_expert(spread(stream), norm_gain, w_gate, w_up, w_down))
+    terms = run_expert(spread(stream), norm_gain, w_gate, w_up, w_down)
+    parts = [
+        keep + wide(swap(send, 1)) for keep, send in zip(terms[:PIECES], terms[PIECES:])
+    ]
     own_ids = lax.dynamic_slice_in_dim(expert_ids, rank_here * own_rows, own_rows, 0)
+    sent = {
+        distance + 8 * at: part[at * own_rows : (at + 1) * own_rows].astype(jnp.bfloat16)
+        for at in reversed(range(far))
+        for part, distance in zip(parts, SQUARE)
+        if distance + at
+    }
+    order = list(reversed(sent))
+    for earlier, later in zip(order, order[1:]):
+        sent[later], sent[earlier] = lax.optimization_barrier((sent[later], sent[earlier]))
     expert_out = 0.0
-    for at in range(far):
-        block = total[at * own_rows : (at + 1) * own_rows]
-        block = wide(swap(block.astype(jnp.bfloat16), 8 * at)) if at else block
+    for at in reversed(range(far)):
         expert = (rank_here ^ (8 * at)) // split_ways
         mixing = jnp.sum(
             route_gates * (own_ids == expert).astype(jnp.float32), axis=1, keepdims=True
         )
-        expert_out = expert_out + mixing * block
+        for part, distance in zip(parts, SQUARE):
+            block = part[at * own_rows : (at + 1) * own_rows]
+            if distance + at:
+                block = wide(swap(sent[distance + 8 * at], distance + 8 * at))
+            expert_out = expert_out + mixing * block
     return (attended, expert_out.astype(jnp.bfloat16))
 
 

time: 78.3 us -> 77.2 us (0.986); the launches traced: 79.6 us -> 77.2 us
  starting transfers between devices: 16 us -> 20 us
  waiting for transfers between devices: 27.3 us -> 23.5 us
  blocking collectives: 21.2 us -> 19 us
    ppermute x23 -> x26, starting transfers between devices: 16 us -> 20 us  [swap(): return lax.ppermute(array, 'experts', pairs)]
    ppermute x23 -> x26, waiting for transfers between devices: 27.3 us -> 23.5 us  [swap(): return lax.ppermute(array, 'experts', pairs)]
    all_to_all x1, blocking collectives: 21.2 us -> 19 us  [shards(): lax.all_to_all(latent, 'experts', split_axis=0, concat_axis=0, tiled=True)]
  transfers between devices with their start and end apart: 23 -> 26, of which waited for: 14 -> 15; matrix products, arithmetic and copies ran while one was open for 1% -> 1% of each run, Pallas kernels for 0% -> 0%
where the time goes in v9:
time: 77.2 us
  waiting for transfers between devices  23.5 us (30%)
  starting transfers between devices  20 us (26%)
  blocking collectives  19 us (25%)
  Pallas kernels  11.6 us (15%)
  other arithmetic  1.3 us (2%)
  local copies, waits for them, and re-layouts  0.89 us (1%)
  between operations  0.88 us (1%)
    ppermute x26, waiting for transfers between devices, swap(): return lax.ppermute(array, 'experts', pairs)  23.5 us
    ppermute x26, starting transfers between devices, swap(): return lax.ppermute(array, 'experts', pairs)  20 us
    all_to_all x1, blocking collectives, shards(): lax.all_to_all(latent, 'experts', split_axis=0, concat_axis=0, tiled=True)  19 us
    pallas_call x1, Pallas kernels, attend(): pl.pallas_call(attend_kernel, out_shape=jax.ShapeDtypeStruct((devices, pa...  7.15 us
    pallas_call x1, Pallas kernels, run_expert(): pl.pallas_call(expert_kernel, out_shape=term_shapes(rows, width), in_spec...  2.34 us
    pallas_call x1, Pallas kernels, project(): pl.pallas_call(functools.partial(project_kernel, own_rows, far), out_shap...  2.11 us
  transfers between devices with their start and end apart: 26, of which 15 were waited for; matrix products, arithmetic and copies ran while one was open for 1% of the time, Pallas kernels for 0%

profile of v9, /device:TPU:0, one launch (start us, length us, event | category | flops | bytes accessed | tf_op | source)
XLA Modules:
  0.0 77.2 jit_solution(2606970558007830808)
XLA Ops:
  0.7 7.2 %attend.1 = bf16[16,16,512]{2,1,0:T(8,128)(2,1)} custom-call(s32[4]{0:T(128)} %len_ref.1, bf16[4,64,576]{2,1,0:T(8,128)(2,1)} %bitcast.7, bf16[4,576,4096]{2,1,0:T(8,128)(2,1)} %cache_ref.1), custom_call_target="tpu_custom_call" | custom-call | flops 1140850688 | bytes 9437184 | tf_op jit(solution)/shard_map/attend/pallas_call | solution.py:153
  7.8 19.0 %all_to_all.5 = bf16[16,16,512]{2,1,0:T(8,128)(2,1)S(1)} all-to-all(bf16[16,16,512]{2,1,0:T(8,128)(2,1)} %attend.1), channel_id=1, replica_groups=mesh['groups'=2,'experts'=16] {'experts'}, dimensions={0} | all-to-all | bytes 524288 | tf_op jit(solution)/shard_map/all_to_all | solution.py:355
  26.9 2.1 %project.1 = (f32[8,7168]{1,0:T(8,128)S(1)}, f32[8,7168]{1,0:T(8,128)S(1)}, f32[8,7168]{1,0:T(8,128)S(1)}, f32[8,7168]{1,0:T(8,128)S(1)}, bf16[8,7168]{1,0:T(8,1...) custom-call(bf16[256,512]{1,0:T(8,128)(2,1)S(1)} %bitcast.5, ...), custom_call_target="tpu_custom_call" | custom-call | flops 469762048 | bytes 7340032 | tf_op jit(solution)/shard_map/project/pallas_call | solution.py:229
  30.4 0.7 collective-permute-start.1
  31.1 1.1 %collective-permute-start.3 = (bf16[8,7168]{1,0:T(8,128)(2,1)S(1)}, bf16[8,7168]{1,0:T(8,128)(2,1)S(1)}, u32[]{:S(2)}, u32[]{:S(2)}) collective-permute-start(bf16[8,7168]{1,0:T(8,128)(2,1)S(1)} %add_convert_fusion.5), channel_id=1, source_target_pairs={{0,4},{1,5},{2,6},{3,7},{4,0},{5,1},{6,2},{7,3},{8,12},{9,13},{10,... | collective-permute-start | bytes 344072 | tf_op jit(solution)/shard_map/ppermute | solution.py:296
  32.3 1.9 %collective-permute-start.5 = (bf16[8,7168]{1,0:T(8,128)(2,1)S(1)}, bf16[8,7168]{1,0:T(8,128)(2,1)S(1)}, u32[]{:S(2)}, u32[]{:S(2)}) collective-permute-start(bf16[8,7168]{1,0:T(8,128)(2,1)S(1)} %add_convert_fusion.4), channel_id=1, source_target_pairs={{0,2},{1,3},{2,0},{3,1},{4,6},{5,7},{6,4},{7,5},{8,10},{9,11},{10,... | collective-permute-start | bytes 344072 | tf_op jit(solution)/shard_map/ppermute | solution.py:296
  34.2 3.2 %collective-permute-done.1 = bf16[8,7168]{1,0:T(8,128)(2,1)S(1)} collective-permute-done((bf16[8,7168]{1,0:T(8,128)(2,1)S(1)}, bf16[8,7168]{1,0:T(8,128)(2,1)S(1)}, u32[]{:S(2)}, u32[]{:S(2)}) %collective-permute-start.1) | collective-permute-done | bytes 114720 | tf_op jit(solution)/shard_map/ppermute | solution.py:296
  38.0 1.1 %collective-permute-done.5 = bf16[8,7168]{1,0:T(8,128)(2,1)S(1)} collective-permute-done((bf16[8,7168]{1,0:T(8,128)(2,1)S(1)}, bf16[8,7168]{1,0:T(8,128)(2,1)S(1)}, u32[]{:S(2)}, u32[]{:S(2)}) %collective-permute-start.5) | collective-permute-done | bytes 114720 | tf_op jit(solution)/shard_map/ppermute | solution.py:296
  39.1 1.1 %collective-permute-start.7 = (bf16[8,7168]{1,0:T(8,128)(2,1)S(1)}, bf16[8,7168]{1,0:T(8,128)(2,1)S(1)}, u32[]{:S(2)}, u32[]{:S(2)}) collective-permute-start(bf16[8,7168]{1,0:T(8,128)(2,1)S(1)} %fusion.7), channel_id=1, source_target_pairs={{0,8},{1,9},{2,10},{3,11},{4,12},{5,13},{6,14},{7,15},{8,0},{9,1},... | collective-permute-start | bytes 344072 | tf_op jit(solution)/shard_map/ppermute | solution.py:296
  40.3 7.3 %collective-permute-done.7 = bf16[8,7168]{1,0:T(8,128)(2,1)S(1)} collective-permute-done((bf16[8,7168]{1,0:T(8,128)(2,1)S(1)}, bf16[8,7168]{1,0:T(8,128)(2,1)S(1)}, u32[]{:S(2)}, u32[]{:S(2)}) %collective-permute-start.7) | collective-permute-done | bytes 114720 | tf_op jit(solution)/shard_map/ppermute | solution.py:296
  47.8 1.4 %collective-permute-start.9 = (bf16[8,7168]{1,0:T(8,128)(2,1)S(1)}, bf16[8,7168]{1,0:T(8,128)(2,1)S(1)}, u32[]{:S(2)}, u32[]{:S(2)}) collective-permute-start(bf16[8,7168]{1,0:T(8,128)(2,1)S(1)} %add_convert_fusion.3.refs_0_), channel_id=1, source_target_pairs={{0,4},{1,5},{2,6},{3,7},{4,0},{5,1},{6,2},{7,3},{8,12},{9,13},{10,... | collective-permute-start | bytes 344072 | tf_op jit(solution)/shard_map/ppermute | solution.py:296
  49.2 2.1 %collective-permute-start.10 = (bf16[8,7168]{1,0:T(8,128)(2,1)S(1)}, bf16[8,7168]{1,0:T(8,128)(2,1)S(1)}, u32[]{:S(2)}, u32[]{:S(2)}) collective-permute-start(bf16[8,7168]{1,0:T(8,128)(2,1)S(1)} %add_convert_fusion.3.refs_0_), channel_id=1, source_target_pairs={{0,2},{1,3},{2,0},{3,1},{4,6},{5,7},{6,4},{7,5},{8,10},{9,11},{10,... | collective-permute-start | bytes 344072 | tf_op jit(solution)/shard_map/ppermute | solution.py:296
  51.3 3.4 %collective-permute-done.8.refs_1_ = bf16[8,7168]{1,0:T(8,128)(2,1)S(1)} collective-permute-done((bf16[8,7168]{1,0:T(8,128)(2,1)S(1)}, bf16[8,7168]{1,0:T(8,128)(2,1)S(1)}, u32[]{:S(2)}, u32[]{:S(2)}) %collective-permute-start.8) | collective-permute-done | bytes 114720 | tf_op jit(solution)/shard_map/ppermute | solution.py:296
  55.3 1.0 %collective-permute-done.10.refs_3_ = bf16[8,7168]{1,0:T(8,128)(2,1)S(1)} collective-permute-done((bf16[8,7168]{1,0:T(8,128)(2,1)S(1)}, bf16[8,7168]{1,0:T(8,128)(2,1)S(1)}, u32[]{:S(2)}, u32[]{:S(2)}) %collective-permute-start.10) | collective-permute-done | bytes 114720 | tf_op jit(solution)/shard_map/ppermute | solution.py:296
  56.3 1.3 %collective-permute-done.14.refs_7_ = bf16[8,7168]{1,0:T(8,128)(2,1)S(1)} collective-permute-done((bf16[8,7168]{1,0:T(8,128)(2,1)S(1)}, bf16[8,7168]{1,0:T(8,128)(2,1)S(1)}, u32[]{:S(2)}, u32[]{:S(2)}) %collective-permute-start.14) | collective-permute-done | bytes 114720 | tf_op jit(solution)/shard_map/ppermute | solution.py:296
  57.6 2.3 %expert.1 = (f32[8,7168]{1,0:T(8,128)S(1)}, f32[8,7168]{1,0:T(8,128)S(1)}, f32[8,7168]{1,0:T(8,128)S(1)}, f32[8,7168]{1,0:T(8,128)S(1)}, bf16[8,7168]{1,0:T(8,12...) custom-call(bf16[8,7168]{1,0:T(8,128)(2,1)S(1)} %add_convert_fusion.3.refs_0_, ...), custom_call_target="tpu_custom_call" | custom-call | flops 704643072 | bytes 11010048 | tf_op jit(solution)/shard_map/expert/pallas_call | solution.py:279
  62.2 2.6 %collective-permute-start.20 = (bf16[4,7168]{1,0:T(4,128)(2,1)S(1)}, bf16[4,7168]{1,0:T(4,128)(2,1)S(1)}, u32[]{:S(2)}, u32[]{:S(2)}) collective-permute-start(bf16[4,7168]{1,0:T(4,128)(2,1)S(1)} %get-tuple-element.52), channel_id=1, source_target_pairs={{0,14},{1,15},{2,12},{3,13},{4,10},{5,11},{6,8},{7,9},{8,6},{9,7},... | collective-permute-start | bytes 172040 | tf_op jit(solution)/shard_map/ppermute | solution.py:296
  64.8 1.6 %collective-permute-start.21 = (bf16[4,7168]{1,0:T(4,128)(2,1)S(1)}, bf16[4,7168]{1,0:T(4,128)(2,1)S(1)}, u32[]{:S(2)}, u32[]{:S(2)}) collective-permute-start(bf16[4,7168]{1,0:T(4,128)(2,1)S(1)} %get-tuple-element.53), channel_id=1, source_target_pairs={{0,12},{1,13},{2,14},{3,15},{4,8},{5,9},{6,10},{7,11},{8,4},{9,5},... | collective-permute-start | bytes 172040 | tf_op jit(solution)/shard_map/ppermute | solution.py:296
  66.4 1.6 %collective-permute-start.22 = (bf16[4,7168]{1,0:T(4,128)(2,1)S(1)}, bf16[4,7168]{1,0:T(4,128)(2,1)S(1)}, u32[]{:S(2)}, u32[]{:S(2)}) collective-permute-start(bf16[4,7168]{1,0:T(4,128)(2,1)S(1)} %get-tuple-element.54), channel_id=1, source_target_pairs={{0,10},{1,11},{2,8},{3,9},{4,14},{5,15},{6,12},{7,13},{8,2},{9,3},... | collective-permute-start | bytes 172040 | tf_op jit(solution)/shard_map/ppermute | solution.py:296
  68.0 2.1 %collective-permute-start.23 = (bf16[4,7168]{1,0:T(4,128)(2,1)S(1)}, bf16[4,7168]{1,0:T(4,128)(2,1)S(1)}, u32[]{:S(2)}, u32[]{:S(2)}) collective-permute-start(bf16[4,7168]{1,0:T(4,128)(2,1)S(1)} %get-tuple-element.55), channel_id=1, source_target_pairs={{0,6},{1,7},{2,4},{3,5},{4,2},{5,3},{6,0},{7,1},{8,14},{9,15},{10,... | collective-permute-start | bytes 172040 | tf_op jit(solution)/shard_map/ppermute | solution.py:296
  70.1 1.4 %collective-permute-done.19 = bf16[4,7168]{1,0:T(4,128)(2,1)S(1)} collective-permute-done((bf16[4,7168]{1,0:T(4,128)(2,1)S(1)}, bf16[4,7168]{1,0:T(4,128)(2,1)S(1)}, u32[]{:S(2)}, u32[]{:S(2)}) %collective-permute-start.19) | collective-permute-done | bytes 57376 | tf_op jit(solution)/shard_map/ppermute | solution.py:296
  71.6 1.0 %collective-permute-start.25 = (bf16[4,7168]{1,0:T(4,128)(2,1)S(1)}, bf16[4,7168]{1,0:T(4,128)(2,1)S(1)}, u32[]{:S(2)}, u32[]{:S(2)}) collective-permute-start(bf16[4,7168]{1,0:T(4,128)(2,1)S(1)} %get-tuple-element.57), channel_id=1, source_target_pairs={{0,2},{1,3},{2,0},{3,1},{4,6},{5,7},{6,4},{7,5},{8,10},{9,11},{10,... | collective-permute-start | bytes 172040 | tf_op jit(solution)/shard_map/ppermute | solution.py:296
  73.3 2.6 %collective-permute-done.22 = bf16[4,7168]{1,0:T(4,128)(2,1)S(1)} collective-permute-done((bf16[4,7168]{1,0:T(4,128)(2,1)S(1)}, bf16[4,7168]{1,0:T(4,128)(2,1)S(1)}, u32[]{:S(2)}, u32[]{:S(2)}) %collective-permute-start.22) | collective-permute-done | bytes 57376 | tf_op jit(solution)/shard_map/ppermute | solution.py:296
  76.4 0.8 %fusion.4 = bf16[4,7168]{1,0:T(4,128)(2,1)} fusion(f32[8,7168]{1,0:T(8,128)S(1)} %convert_add_fusion, bf16[4,7168]{1,0:T(4,128)(2,1)S(1)} %collective-permute-done.25, bf16[4,7168]{1,0:T(4,128)(2,1)S(1)} %collective-permute-done.24, bf16[4,7168]{1,0:T(4,128)(2,1)S(1)} %collective-permute-done.23, bf16[4,7168]{1,0:T(4,128)(2,1)S(1)} %collective-permute-done.22, ...), kind=kLoop, calls=%fused_computation.14 | loop fusion | flops 573440 | bytes 573472 | tf_op jit(solution)/shard_map/convert_element_type | solution.py:386
  (70 shorter events, 6.4 us)
Async XLA Ops:
  29.0 1.4 %collective-permute-start = (bf16[8,7168]{1,0:T(8,128)(2,1)S(1)}, bf16[8,7168]{1,0:T(8,128)(2,1)S(1)}, u32[]{:S(2)}, u32[]{:S(2)}) collective-permute-start(bf16[8,7168]{1,0:T(8,128)(2,1)S(1)} %get-tuple-element.31), channel_id=1, source_target_pairs={{0,1},{1,0},{2,3},{3,2},{4,5},{5,4},{6,7},{7,6},{8,9},{9,8},{10,11... | collective-permute-start | bytes 344072 | tf_op jit(solution)/shard_map/ppermute | solution.py:296
  29.1 2.0 %collective-permute-start.2 = (bf16[8,7168]{1,0:T(8,128)(2,1)S(1)}, bf16[8,7168]{1,0:T(8,128)(2,1)S(1)}, u32[]{:S(2)}, u32[]{:S(2)}) collective-permute-start(bf16[8,7168]{1,0:T(8,128)(2,1)S(1)} %get-tuple-element.33), channel_id=1, source_target_pairs={{0,1},{1,0},{2,3},{3,2},{4,5},{5,4},{6,7},{7,6},{8,9},{9,8},{10,11... | collective-permute-start | bytes 344072 | tf_op jit(solution)/shard_map/ppermute | solution.py:296
  29.6 2.7 %collective-permute-start.4 = (bf16[8,7168]{1,0:T(8,128)(2,1)S(1)}, bf16[8,7168]{1,0:T(8,128)(2,1)S(1)}, u32[]{:S(2)}, u32[]{:S(2)}) collective-permute-start(bf16[8,7168]{1,0:T(8,128)(2,1)S(1)} %get-tuple-element.35), channel_id=1, source_target_pairs={{0,1},{1,0},{2,3},{3,2},{4,5},{5,4},{6,7},{7,6},{8,9},{9,8},{10,11... | collective-permute-start | bytes 344072 | tf_op jit(solution)/shard_map/ppermute | solution.py:296
  29.7 4.5 %collective-permute-start.6 = (bf16[8,7168]{1,0:T(8,128)(2,1)S(1)}, bf16[8,7168]{1,0:T(8,128)(2,1)S(1)}, u32[]{:S(2)}, u32[]{:S(2)}) collective-permute-start(bf16[8,7168]{1,0:T(8,128)(2,1)S(1)} %get-tuple-element.37), channel_id=1, source_target_pairs={{0,1},{1,0},{2,3},{3,2},{4,5},{5,4},{6,7},{7,6},{8,9},{9,8},{10,11... | collective-permute-start | bytes 344072 | tf_op jit(solution)/shard_map/ppermute | solution.py:296
  30.4 7.0 %collective-permute-start.1 = (bf16[8,7168]{1,0:T(8,128)(2,1)S(1)}, bf16[8,7168]{1,0:T(8,128)(2,1)S(1)}, u32[]{:S(2)}, u32[]{:S(2)}) collective-permute-start(bf16[8,7168]{1,0:T(8,128)(2,1)S(1)} %add_convert_fusion.6), channel_id=1, source_target_pairs={{0,6},{1,7},{2,4},{3,5},{4,2},{5,3},{6,0},{7,1},{8,14},{9,15},{10,... | collective-permute-start | bytes 344072 | tf_op jit(solution)/shard_map/ppermute | solution.py:296
  31.1 6.9 %collective-permute-start.3 = (bf16[8,7168]{1,0:T(8,128)(2,1)S(1)}, bf16[8,7168]{1,0:T(8,128)(2,1)S(1)}, u32[]{:S(2)}, u32[]{:S(2)}) collective-permute-start(bf16[8,7168]{1,0:T(8,128)(2,1)S(1)} %add_convert_fusion.5), channel_id=1, source_target_pairs={{0,4},{1,5},{2,6},{3,7},{4,0},{5,1},{6,2},{7,3},{8,12},{9,13},{10,... | collective-permute-start | bytes 344072 | tf_op jit(solution)/shard_map/ppermute | solution.py:296
  32.3 6.8 %collective-permute-start.5 = (bf16[8,7168]{1,0:T(8,128)(2,1)S(1)}, bf16[8,7168]{1,0:T(8,128)(2,1)S(1)}, u32[]{:S(2)}, u32[]{:S(2)}) collective-permute-start(bf16[8,7168]{1,0:T(8,128)(2,1)S(1)} %add_convert_fusion.4), channel_id=1, source_target_pairs={{0,2},{1,3},{2,0},{3,1},{4,6},{5,7},{6,4},{7,5},{8,10},{9,11},{10,... | collective-permute-start | bytes 344072 | tf_op jit(solution)/shard_map/ppermute | solution.py:296
  39.1 8.4 %collective-permute-start.7 = (bf16[8,7168]{1,0:T(8,128)(2,1)S(1)}, bf16[8,7168]{1,0:T(8,128)(2,1)S(1)}, u32[]{:S(2)}, u32[]{:S(2)}) collective-permute-start(bf16[8,7168]{1,0:T(8,128)(2,1)S(1)} %fusion.7), channel_id=1, source_target_pairs={{0,8},{1,9},{2,10},{3,11},{4,12},{5,13},{6,14},{7,15},{8,0},{9,1},... | collective-permute-start | bytes 344072 | tf_op jit(solution)/shard_map/ppermute | solution.py:296
  47.8 7.0 %collective-permute-start.8 = (bf16[8,7168]{1,0:T(8,128)(2,1)S(1)}, bf16[8,7168]{1,0:T(8,128)(2,1)S(1)}, u32[]{:S(2)}, u32[]{:S(2)}) collective-permute-start(bf16[8,7168]{1,0:T(8,128)(2,1)S(1)} %add_convert_fusion.3.refs_0_), channel_id=1, source_target_pairs={{0,6},{1,7},{2,4},{3,5},{4,2},{5,3},{6,0},{7,1},{8,14},{9,15},{10,... | collective-permute-start | bytes 344072 | tf_op jit(solution)/shard_map/ppermute | solution.py:296
  47.8 6.9 %collective-permute-start.9 = (bf16[8,7168]{1,0:T(8,128)(2,1)S(1)}, bf16[8,7168]{1,0:T(8,128)(2,1)S(1)}, u32[]{:S(2)}, u32[]{:S(2)}) collective-permute-start(bf16[8,7168]{1,0:T(8,128)(2,1)S(1)} %add_convert_fusion.3.refs_0_), channel_id=1, source_target_pairs={{0,4},{1,5},{2,6},{3,7},{4,0},{5,1},{6,2},{7,3},{8,12},{9,13},{10,... | collective-permute-start | bytes 344072 | tf_op jit(solution)/shard_map/ppermute | solution.py:296
  49.2 7.0 %collective-permute-start.10 = (bf16[8,7168]{1,0:T(8,128)(2,1)S(1)}, bf16[8,7168]{1,0:T(8,128)(2,1)S(1)}, u32[]{:S(2)}, u32[]{:S(2)}) collective-permute-start(bf16[8,7168]{1,0:T(8,128)(2,1)S(1)} %add_convert_fusion.3.refs_0_), channel_id=1, source_target_pairs={{0,2},{1,3},{2,0},{3,1},{4,6},{5,7},{6,4},{7,5},{8,10},{9,11},{10,... | collective-permute-start | bytes 344072 | tf_op jit(solution)/shard_map/ppermute | solution.py:296
  51.3 5.0 %collective-permute-start.11 = (bf16[8,7168]{1,0:T(8,128)(2,1)S(1)}, bf16[8,7168]{1,0:T(8,128)(2,1)S(1)}, u32[]{:S(2)}, u32[]{:S(2)}) collective-permute-start(bf16[8,7168]{1,0:T(8,128)(2,1)S(1)} %add_convert_fusion.3.refs_0_), channel_id=1, source_target_pairs={{0,1},{1,0},{2,3},{3,2},{4,5},{5,4},{6,7},{7,6},{8,9},{9,8},{10,11... | collective-permute-start | bytes 344072 | tf_op jit(solution)/shard_map/ppermute | solution.py:296
  54.7 1.5 %collective-permute-start.12 = (bf16[8,7168]{1,0:T(8,128)(2,1)S(1)}, bf16[8,7168]{1,0:T(8,128)(2,1)S(1)}, u32[]{:S(2)}, u32[]{:S(2)}) collective-permute-start(bf16[8,7168]{1,0:T(8,128)(2,1)S(1)} %collective-permute-done.8.refs_1_), channel_id=1, source_target_pairs={{0,1},{1,0},{2,3},{3,2},{4,5},{5,4},{6,7},{7,6},{8,9},{9,8},{10,11... | collective-permute-start | bytes 344072 | tf_op jit(solution)/shard_map/ppermute | solution.py:296
  54.7 1.5 %collective-permute-start.13 = (bf16[8,7168]{1,0:T(8,128)(2,1)S(1)}, bf16[8,7168]{1,0:T(8,128)(2,1)S(1)}, u32[]{:S(2)}, u32[]{:S(2)}) collective-permute-start(bf16[8,7168]{1,0:T(8,128)(2,1)S(1)} %collective-permute-done.9.refs_2_), channel_id=1, source_target_pairs={{0,1},{1,0},{2,3},{3,2},{4,5},{5,4},{6,7},{7,6},{8,9},{9,8},{10,11... | collective-permute-start | bytes 344072 | tf_op jit(solution)/shard_map/ppermute | solution.py:296
  60.0 1.4 %collective-permute-start.16 = (bf16[8,7168]{1,0:T(8,128)(2,1)S(1)}, bf16[8,7168]{1,0:T(8,128)(2,1)S(1)}, u32[]{:S(2)}, u32[]{:S(2)}) collective-permute-start(bf16[8,7168]{1,0:T(8,128)(2,1)S(1)} %get-tuple-element.41), channel_id=1, source_target_pairs={{0,1},{1,0},{2,3},{3,2},{4,5},{5,4},{6,7},{7,6},{8,9},{9,8},{10,11... | collective-permute-start | bytes 344072 | tf_op jit(solution)/shard_map/ppermute | solution.py:296
  60.2 1.3 %collective-permute-start.18 = (bf16[8,7168]{1,0:T(8,128)(2,1)S(1)}, bf16[8,7168]{1,0:T(8,128)(2,1)S(1)}, u32[]{:S(2)}, u32[]{:S(2)}) collective-permute-start(bf16[8,7168]{1,0:T(8,128)(2,1)S(1)} %get-tuple-element.45), channel_id=1, source_target_pairs={{0,1},{1,0},{2,3},{3,2},{4,5},{5,4},{6,7},{7,6},{8,9},{9,8},{10,11... | collective-permute-start | bytes 344072 | tf_op jit(solution)/shard_map/ppermute | solution.py:296
  60.7 1.3 %collective-permute-start.15 = (bf16[8,7168]{1,0:T(8,128)(2,1)S(1)}, bf16[8,7168]{1,0:T(8,128)(2,1)S(1)}, u32[]{:S(2)}, u32[]{:S(2)}) collective-permute-start(bf16[8,7168]{1,0:T(8,128)(2,1)S(1)} %get-tuple-element.39), channel_id=1, source_target_pairs={{0,1},{1,0},{2,3},{3,2},{4,5},{5,4},{6,7},{7,6},{8,9},{9,8},{10,11... | collective-permute-start | bytes 344072 | tf_op jit(solution)/shard_map/ppermute | solution.py:296
  62.1 9.4 %collective-permute-start.19 = (bf16[4,7168]{1,0:T(4,128)(2,1)S(1)}, bf16[4,7168]{1,0:T(4,128)(2,1)S(1)}, u32[]{:S(2)}, u32[]{:S(2)}) collective-permute-start(bf16[4,7168]{1,0:T(4,128)(2,1)S(1)} %slice.74), channel_id=1, source_target_pairs={{0,8},{1,9},{2,10},{3,11},{4,12},{5,13},{6,14},{7,15},{8,0},{9,1},... | collective-permute-start | bytes 172040 | tf_op jit(solution)/shard_map/ppermute | solution.py:296
  62.2 9.4 %collective-permute-start.20 = (bf16[4,7168]{1,0:T(4,128)(2,1)S(1)}, bf16[4,7168]{1,0:T(4,128)(2,1)S(1)}, u32[]{:S(2)}, u32[]{:S(2)}) collective-permute-start(bf16[4,7168]{1,0:T(4,128)(2,1)S(1)} %get-tuple-element.52), channel_id=1, source_target_pairs={{0,14},{1,15},{2,12},{3,13},{4,10},{5,11},{6,8},{7,9},{8,6},{9,7},... | collective-permute-start | bytes 172040 | tf_op jit(solution)/shard_map/ppermute | solution.py:296
  64.8 8.4 %collective-permute-start.21 = (bf16[4,7168]{1,0:T(4,128)(2,1)S(1)}, bf16[4,7168]{1,0:T(4,128)(2,1)S(1)}, u32[]{:S(2)}, u32[]{:S(2)}) collective-permute-start(bf16[4,7168]{1,0:T(4,128)(2,1)S(1)} %get-tuple-element.53), channel_id=1, source_target_pairs={{0,12},{1,13},{2,14},{3,15},{4,8},{5,9},{6,10},{7,11},{8,4},{9,5},... | collective-permute-start | bytes 172040 | tf_op jit(solution)/shard_map/ppermute | solution.py:296
  66.4 9.4 %collective-permute-start.22 = (bf16[4,7168]{1,0:T(4,128)(2,1)S(1)}, bf16[4,7168]{1,0:T(4,128)(2,1)S(1)}, u32[]{:S(2)}, u32[]{:S(2)}) collective-permute-start(bf16[4,7168]{1,0:T(4,128)(2,1)S(1)} %get-tuple-element.54), channel_id=1, source_target_pairs={{0,10},{1,11},{2,8},{3,9},{4,14},{5,15},{6,12},{7,13},{8,2},{9,3},... | collective-permute-start | bytes 172040 | tf_op jit(solution)/shard_map/ppermute | solution.py:296
  68.0 7.8 %collective-permute-start.23 = (bf16[4,7168]{1,0:T(4,128)(2,1)S(1)}, bf16[4,7168]{1,0:T(4,128)(2,1)S(1)}, u32[]{:S(2)}, u32[]{:S(2)}) collective-permute-start(bf16[4,7168]{1,0:T(4,128)(2,1)S(1)} %get-tuple-element.55), channel_id=1, source_target_pairs={{0,6},{1,7},{2,4},{3,5},{4,2},{5,3},{6,0},{7,1},{8,14},{9,15},{10,... | collective-permute-start | bytes 172040 | tf_op jit(solution)/shard_map/ppermute | solution.py:296
  71.6 4.3 %collective-permute-start.24 = (bf16[4,7168]{1,0:T(4,128)(2,1)S(1)}, bf16[4,7168]{1,0:T(4,128)(2,1)S(1)}, u32[]{:S(2)}, u32[]{:S(2)}) collective-permute-start(bf16[4,7168]{1,0:T(4,128)(2,1)S(1)} %get-tuple-element.56), channel_id=1, source_target_pairs={{0,4},{1,5},{2,6},{3,7},{4,0},{5,1},{6,2},{7,3},{8,12},{9,13},{10,... | collective-permute-start | bytes 172040 | tf_op jit(solution)/shard_map/ppermute | solution.py:296
  71.6 4.8 %collective-permute-start.25 = (bf16[4,7168]{1,0:T(4,128)(2,1)S(1)}, bf16[4,7168]{1,0:T(4,128)(2,1)S(1)}, u32[]{:S(2)}, u32[]{:S(2)}) collective-permute-start(bf16[4,7168]{1,0:T(4,128)(2,1)S(1)} %get-tuple-element.57), channel_id=1, source_target_pairs={{0,2},{1,3},{2,0},{3,1},{4,6},{5,7},{6,4},{7,5},{8,10},{9,11},{10,... | collective-permute-start | bytes 172040 | tf_op jit(solution)/shard_map/ppermute | solution.py:296
  (12 other events, 260.1 us)

commit v10 on v7

--- a/solution.py
+++ b/solution.py
@@ -10,11 +10,12 @@
 QK = 192
 FF = 2048
 BLOCK = 512
+LOWEST = -3e38
 GROUP = 4
 LANES = 128
 TILE = 256
 PARTS = 4
-SQUARE = (0, 4, 2, 6)
+SQUARE = (0, 6, 4, 2)
 PIECES = len(SQUARE)
 MIB = 2**20
 
@@ -31,10 +32,9 @@
     length,
     queries,
     held,
-    products,
+    summed,
     highest,
     sums,
-    factors,
     staged,
     item_row,
     item_block,
@@ -63,11 +63,11 @@
         block_copy(row, 0).start()
         item_row[row] = row
         item_block[row] = 0
-    highest[...] = jnp.full_like(highest, -jnp.inf)
+    highest[...] = jnp.full_like(highest, LOWEST)
     sums[...] = jnp.zeros_like(sums)
+    summed[...] = jnp.zeros_like(summed)
     length_copy.wait()
     items = own_rows
-    counts = []
     for row in range(own_rows):
         count = (length[row] + BLOCK - 1) // BLOCK
 
@@ -78,7 +78,6 @@
             return first
 
         lax.fori_loop(1, count, begin, items - 1)
-        counts.append(count)
         items = items + count - 1
     queries_copy.wait()
     column = lax.broadcasted_iota(jnp.int32, (heads, BLOCK), 1)
@@ -100,15 +99,25 @@
             for score in found
         ]
         weights = [jnp.exp(score - top) for score, top in zip(found, tops)]
-        for (row, block), top, weight in zip(inside, tops, weights):
-            highest[row, block] = jnp.broadcast_to(top, (heads, LANES))
-            sums[row, block] = sum(lane_tiles(weight))
-            products[row, block] = lax.dot_general(
+        terms = [
+            lax.dot_general(
                 weight.astype(jnp.bfloat16),
                 held[row, block, :rank, :],
                 (((1,), (1,)), ((), ())),
                 preferred_element_type=jnp.float32,
             )
+            for (row, block), weight in zip(inside, weights)
+        ]
+        for (row, _), top, weight, term in zip(inside, tops, weights, terms):
+            before = highest[row]
+            after = jnp.maximum(before, top)
+            old, new = jnp.exp(before - after), jnp.exp(top - after)
+            highest[row] = after
+            sums[row] = sums[row] * old + sum(lane_tiles(weight)) * new
+            for at in range(0, rank, LANES):
+                summed[row, :, at : at + LANES] = (
+                    summed[row, :, at : at + LANES] * old + term[:, at : at + LANES] * new
+                )
 
     def visit_group(group, _):
         visit(group * GROUP, GROUP)
@@ -119,17 +128,7 @@
     pl.when((items & 2) != 0)(lambda: visit(whole * GROUP, 2))
     pl.when((items & 1) != 0)(lambda: visit(items - 1, 1))
     for row in range(own_rows):
-        factor = jnp.exp(highest[row] - jnp.max(highest[row], axis=0, keepdims=True))
-        total = jnp.sum(jnp.sum(sums[row] * factor, axis=0), axis=1, keepdims=True)
-        factors[row] = factor * (1.0 / total)[None]
-    for row in range(own_rows):
-
-        def merge(block, latent, row=row):
-            return latent + products[row, block] * factors[row, block][:, :1]
-
-        latent = lax.fori_loop(
-            0, counts[row], merge, jnp.zeros((heads, rank), jnp.float32)
-        )
+        latent = summed[row] * (1.0 / jnp.sum(sums[row], axis=1, keepdims=True))
         for device in range(devices):
             staged[device, row * own_heads : (row + 1) * own_heads, :] = latent[
                 device * own_heads : (device + 1) * own_heads
@@ -151,10 +150,9 @@
             pltpu.SMEM((own_rows,), jnp.int32),
             pltpu.VMEM((own_rows, heads, depth), jnp.bfloat16),
             pltpu.VMEM((own_rows, blocks, depth, BLOCK), jnp.bfloat16),
-            pltpu.VMEM((own_rows, blocks, heads, rank), jnp.float32),
-            pltpu.VMEM((own_rows, blocks, heads, LANES), jnp.float32),
-            pltpu.VMEM((own_rows, blocks, heads, LANES), jnp.float32),
-            pltpu.VMEM((own_rows, blocks, heads, LANES), jnp.float32),
+            pltpu.VMEM((own_rows, heads, rank), jnp.float32),
+            pltpu.VMEM((own_rows, heads, LANES), jnp.float32),
+            pltpu.VMEM((own_rows, heads, LANES), jnp.float32),
             pltpu.VMEM((devices, packed, rank), jnp.float32),
             pltpu.SMEM((listed,), jnp.int32),
             pltpu.SMEM((listed,), jnp.int32),
@@ -196,7 +194,7 @@
     far_bits = far.bit_length() - 1
     request, slot = row & (own_rows - 1), row >> turn
     far_at, slot = slot & (far - 1), slot >> far_bits
-    distance = (far_at << 3) + ((slot & 1) << 2) + ((slot >> 1 & 1) << 1) + (slot >> 2)
+    distance = (far_at << 3) + ((4 - (slot & 3) & 3) << 1) + (slot >> 2)
     device = distance ^ lax.axis_index("experts")
     values = []
     for head in range(own_heads):
@@ -295,7 +293,7 @@
 def collect(terms):
     keeps, sends = terms[:PIECES], terms[PIECES:]
     total = 0.0
-    for piece in (3, 1, 2, 0):
+    for piece in (1, 2, 3, 0):
         part = keeps[piece] + wide(swap(sends[piece], 1))
         if piece:
             part = wide(swap(part.astype(jnp.bfloat16), SQUARE[piece]))

time: 78.3 us -> 74.7 us (0.954)
  blocking collectives: 21.2 us -> 16.8 us
  starting transfers between devices: 16 us -> 14.8 us
    all_to_all x1, blocking collectives: 21.2 us -> 16.8 us  [shards(): lax.all_to_all(latent, 'experts', split_axis=0, concat_axis=0, tiled=True)]
    ppermute x23, starting transfers between devices: 16 us -> 14.8 us  [swap(): return lax.ppermute(array, 'experts', pairs)]
  transfers between devices with their start and end apart: 23 -> 23, of which waited for: 14 -> 13; matrix products, arithmetic and copies ran while one was open for 1% -> 1% of each run, Pallas kernels for 0% -> 0%
where the time goes in v10:
time: 74.7 us; the launch traced here: 75.3 us
  waiting for transfers between devices  27.8 us (37%)
  blocking collectives  16.8 us (22%)
  starting transfers between devices  14.8 us (20%)
  Pallas kernels  13 us (17%)
  other arithmetic  1.27 us (2%)
  between operations  0.87 us (1%)
  local copies, waits for them, and re-layouts  0.76 us (1%)
    ppermute x23, waiting for transfers between devices, swap(): return lax.ppermute(array, 'experts', pairs)  27.8 us
    all_to_all x1, blocking collectives, shards(): lax.all_to_all(latent, 'experts', split_axis=0, concat_axis=0, tiled=True)  16.8 us
    ppermute x23, starting transfers between devices, swap(): return lax.ppermute(array, 'experts', pairs)  14.8 us
    pallas_call x1, Pallas kernels, attend(): pl.pallas_call(attend_kernel, out_shape=jax.ShapeDtypeStruct((devices, pa...  8.58 us
    pallas_call x1, Pallas kernels, run_expert(): pl.pallas_call(expert_kernel, out_shape=term_shapes(rows, width), in_spec...  2.34 us
    pallas_call x1, Pallas kernels, project(): pl.pallas_call(functools.partial(project_kernel, own_rows, far), out_shap...  2.11 us
  transfers between devices with their start and end apart: 23, of which 13 were waited for; matrix products, arithmetic and copies ran while one was open for 1% of the time, Pallas kernels for 0%

profile of v10, /device:TPU:0, one launch (start us, length us, event | category | flops | bytes accessed | tf_op | source)
XLA Modules:
  0.0 75.3 jit_solution(1880911812408040920)
XLA Ops:
  0.7 8.6 %attend.1 = bf16[16,16,512]{2,1,0:T(8,128)(2,1)} custom-call(s32[4]{0:T(128)} %len_ref.1, bf16[4,64,576]{2,1,0:T(8,128)(2,1)} %bitcast.7, bf16[4,576,4096]{2,1,0:T(8,128)(2,1)} %cache_ref.1), custom_call_target="tpu_custom_call" | custom-call | flops 1140850688 | bytes 9437184 | tf_op jit(solution)/shard_map/attend/pallas_call | solution.py:144
  9.3 16.8 %all_to_all.5 = bf16[16,16,512]{2,1,0:T(8,128)(2,1)S(1)} all-to-all(bf16[16,16,512]{2,1,0:T(8,128)(2,1)} %attend.1), channel_id=1, replica_groups=mesh['groups'=2,'experts'=16] {'experts'}, dimensions={0} | all-to-all | bytes 524288 | tf_op jit(solution)/shard_map/all_to_all | solution.py:345
  26.1 2.1 %project.1 = (f32[8,7168]{1,0:T(8,128)S(1)}, f32[8,7168]{1,0:T(8,128)S(1)}, f32[8,7168]{1,0:T(8,128)S(1)}, f32[8,7168]{1,0:T(8,128)S(1)}, bf16[8,7168]{1,0:T(8,1...) custom-call(bf16[256,512]{1,0:T(8,128)(2,1)S(1)} %bitcast.5, ...), custom_call_target="tpu_custom_call" | custom-call | flops 469762048 | bytes 7340032 | tf_op jit(solution)/shard_map/project/pallas_call | solution.py:219
  29.6 0.7 collective-permute-start.1
  30.3 1.1 %collective-permute-start.3 = (bf16[8,7168]{1,0:T(8,128)(2,1)S(1)}, bf16[8,7168]{1,0:T(8,128)(2,1)S(1)}, u32[]{:S(2)}, u32[]{:S(2)}) collective-permute-start(bf16[8,7168]{1,0:T(8,128)(2,1)S(1)} %add_convert_fusion.5), channel_id=1, source_target_pairs={{0,4},{1,5},{2,6},{3,7},{4,0},{5,1},{6,2},{7,3},{8,12},{9,13},{10,... | collective-permute-start | bytes 344072 | tf_op jit(solution)/shard_map/ppermute | solution.py:286
  31.5 1.9 %collective-permute-start.5 = (bf16[8,7168]{1,0:T(8,128)(2,1)S(1)}, bf16[8,7168]{1,0:T(8,128)(2,1)S(1)}, u32[]{:S(2)}, u32[]{:S(2)}) collective-permute-start(bf16[8,7168]{1,0:T(8,128)(2,1)S(1)} %add_convert_fusion.4), channel_id=1, source_target_pairs={{0,2},{1,3},{2,0},{3,1},{4,6},{5,7},{6,4},{7,5},{8,10},{9,11},{10,... | collective-permute-start | bytes 344072 | tf_op jit(solution)/shard_map/ppermute | solution.py:286
  33.4 3.2 %collective-permute-done.1 = bf16[8,7168]{1,0:T(8,128)(2,1)S(1)} collective-permute-done((bf16[8,7168]{1,0:T(8,128)(2,1)S(1)}, bf16[8,7168]{1,0:T(8,128)(2,1)S(1)}, u32[]{:S(2)}, u32[]{:S(2)}) %collective-permute-start.1) | collective-permute-done | bytes 114720 | tf_op jit(solution)/shard_map/ppermute | solution.py:286
  36.6 0.6 collective-permute-done.3
  37.2 1.1 %collective-permute-done.5 = bf16[8,7168]{1,0:T(8,128)(2,1)S(1)} collective-permute-done((bf16[8,7168]{1,0:T(8,128)(2,1)S(1)}, bf16[8,7168]{1,0:T(8,128)(2,1)S(1)}, u32[]{:S(2)}, u32[]{:S(2)}) %collective-permute-start.5) | collective-permute-done | bytes 114720 | tf_op jit(solution)/shard_map/ppermute | solution.py:286
  38.3 1.1 %collective-permute-start.7 = (bf16[8,7168]{1,0:T(8,128)(2,1)S(1)}, bf16[8,7168]{1,0:T(8,128)(2,1)S(1)}, u32[]{:S(2)}, u32[]{:S(2)}) collective-permute-start(bf16[8,7168]{1,0:T(8,128)(2,1)S(1)} %fusion.4), channel_id=1, source_target_pairs={{0,8},{1,9},{2,10},{3,11},{4,12},{5,13},{6,14},{7,15},{8,0},{9,1},... | collective-permute-start | bytes 344072 | tf_op jit(solution)/shard_map/ppermute | solution.py:286
  39.5 7.3 %collective-permute-done.7 = bf16[8,7168]{1,0:T(8,128)(2,1)S(1)} collective-permute-done((bf16[8,7168]{1,0:T(8,128)(2,1)S(1)}, bf16[8,7168]{1,0:T(8,128)(2,1)S(1)}, u32[]{:S(2)}, u32[]{:S(2)}) %collective-permute-start.7) | collective-permute-done | bytes 114720 | tf_op jit(solution)/shard_map/ppermute | solution.py:286
  47.0 1.4 %collective-permute-start.9 = (bf16[8,7168]{1,0:T(8,128)(2,1)S(1)}, bf16[8,7168]{1,0:T(8,128)(2,1)S(1)}, u32[]{:S(2)}, u32[]{:S(2)}) collective-permute-start(bf16[8,7168]{1,0:T(8,128)(2,1)S(1)} %add_convert_fusion.3.refs_0_), channel_id=1, source_target_pairs={{0,4},{1,5},{2,6},{3,7},{4,0},{5,1},{6,2},{7,3},{8,12},{9,13},{10,... | collective-permute-start | bytes 344072 | tf_op jit(solution)/shard_map/ppermute | solution.py:286
  48.4 2.1 %collective-permute-start.10 = (bf16[8,7168]{1,0:T(8,128)(2,1)S(1)}, bf16[8,7168]{1,0:T(8,128)(2,1)S(1)}, u32[]{:S(2)}, u32[]{:S(2)}) collective-permute-start(bf16[8,7168]{1,0:T(8,128)(2,1)S(1)} %add_convert_fusion.3.refs_0_), channel_id=1, source_target_pairs={{0,2},{1,3},{2,0},{3,1},{4,6},{5,7},{6,4},{7,5},{8,10},{9,11},{10,... | collective-permute-start | bytes 344072 | tf_op jit(solution)/shard_map/ppermute | solution.py:286
  50.5 3.4 %collective-permute-done.8.refs_1_ = bf16[8,7168]{1,0:T(8,128)(2,1)S(1)} collective-permute-done((bf16[8,7168]{1,0:T(8,128)(2,1)S(1)}, bf16[8,7168]{1,0:T(8,128)(2,1)S(1)}, u32[]{:S(2)}, u32[]{:S(2)}) %collective-permute-start.8) | collective-permute-done | bytes 114720 | tf_op jit(solution)/shard_map/ppermute | solution.py:286
  54.5 1.0 %collective-permute-done.10.refs_3_ = bf16[8,7168]{1,0:T(8,128)(2,1)S(1)} collective-permute-done((bf16[8,7168]{1,0:T(8,128)(2,1)S(1)}, bf16[8,7168]{1,0:T(8,128)(2,1)S(1)}, u32[]{:S(2)}, u32[]{:S(2)}) %collective-permute-start.10) | collective-permute-done | bytes 114720 | tf_op jit(solution)/shard_map/ppermute | solution.py:286
  55.5 1.3 %collective-permute-done.14.refs_7_ = bf16[8,7168]{1,0:T(8,128)(2,1)S(1)} collective-permute-done((bf16[8,7168]{1,0:T(8,128)(2,1)S(1)}, bf16[8,7168]{1,0:T(8,128)(2,1)S(1)}, u32[]{:S(2)}, u32[]{:S(2)}) %collective-permute-start.14) | collective-permute-done | bytes 114720 | tf_op jit(solution)/shard_map/ppermute | solution.py:286
  56.8 2.3 %expert.1 = (f32[8,7168]{1,0:T(8,128)S(1)}, f32[8,7168]{1,0:T(8,128)S(1)}, f32[8,7168]{1,0:T(8,128)S(1)}, f32[8,7168]{1,0:T(8,128)S(1)}, bf16[8,7168]{1,0:T(8,12...) custom-call(bf16[8,7168]{1,0:T(8,128)(2,1)S(1)} %add_convert_fusion.3.refs_0_, ...), custom_call_target="tpu_custom_call" | custom-call | flops 704643072 | bytes 11010048 | tf_op jit(solution)/shard_map/expert/pallas_call | solution.py:269
  61.0 2.0 %collective-permute-start.18 = (bf16[8,7168]{1,0:T(8,128)(2,1)S(1)}, bf16[8,7168]{1,0:T(8,128)(2,1)S(1)}, u32[]{:S(2)}, u32[]{:S(2)}) collective-permute-start(bf16[8,7168]{1,0:T(8,128)(2,1)S(1)} %add_convert_fusion.1), channel_id=1, source_target_pairs={{0,4},{1,5},{2,6},{3,7},{4,0},{5,1},{6,2},{7,3},{8,12},{9,13},{10,... | collective-permute-start | bytes 344072 | tf_op jit(solution)/shard_map/ppermute | solution.py:286
  63.0 1.4 %collective-permute-start.20 = (bf16[8,7168]{1,0:T(8,128)(2,1)S(1)}, bf16[8,7168]{1,0:T(8,128)(2,1)S(1)}, u32[]{:S(2)}, u32[]{:S(2)}) collective-permute-start(bf16[8,7168]{1,0:T(8,128)(2,1)S(1)} %add_convert_fusion), channel_id=1, source_target_pairs={{0,2},{1,3},{2,0},{3,1},{4,6},{5,7},{6,4},{7,5},{8,10},{9,11},{10,... | collective-permute-start | bytes 344072 | tf_op jit(solution)/shard_map/ppermute | solution.py:286
  64.4 3.2 %collective-permute-done.16 = bf16[8,7168]{1,0:T(8,128)(2,1)S(1)} collective-permute-done((bf16[8,7168]{1,0:T(8,128)(2,1)S(1)}, bf16[8,7168]{1,0:T(8,128)(2,1)S(1)}, u32[]{:S(2)}, u32[]{:S(2)}) %collective-permute-start.16) | collective-permute-done | bytes 114720 | tf_op jit(solution)/shard_map/ppermute | solution.py:286
  67.6 1.1 %collective-permute-done.18 = bf16[8,7168]{1,0:T(8,128)(2,1)S(1)} collective-permute-done((bf16[8,7168]{1,0:T(8,128)(2,1)S(1)}, bf16[8,7168]{1,0:T(8,128)(2,1)S(1)}, u32[]{:S(2)}, u32[]{:S(2)}) %collective-permute-start.18) | collective-permute-done | bytes 114720 | tf_op jit(solution)/shard_map/ppermute | solution.py:286
  69.5 0.6 slice.23
  70.2 4.4 %collective-permute-done.22 = bf16[4,7168]{1,0:T(4,128)(2,1)S(1)} collective-permute-done((bf16[4,7168]{1,0:T(4,128)(2,1)S(1)}, bf16[4,7168]{1,0:T(4,128)(2,1)S(1)}, u32[]{:S(2)}, u32[]{:S(2)}) %collective-permute-start.22) | collective-permute-done | bytes 57376 | tf_op jit(solution)/shard_map/ppermute | solution.py:286
  74.5 0.7 fusion.1
  (61 shorter events, 5.0 us)
Async XLA Ops:
  26.1 30.7 %copy-start = (bf16[7168,256]{1,0:T(8,128)(2,1)S(1)}, bf16[7168,256]{1,0:T(8,128)(2,1)}, u32[]{:S(2)}) copy-start(bf16[7168,256]{1,0:T(8,128)(2,1)} %refs_9_.1) | copy-start | bytes 11010052
  28.2 1.4 %collective-permute-start = (bf16[8,7168]{1,0:T(8,128)(2,1)S(1)}, bf16[8,7168]{1,0:T(8,128)(2,1)S(1)}, u32[]{:S(2)}, u32[]{:S(2)}) collective-permute-start(bf16[8,7168]{1,0:T(8,128)(2,1)S(1)} %get-tuple-element.19), channel_id=1, source_target_pairs={{0,1},{1,0},{2,3},{3,2},{4,5},{5,4},{6,7},{7,6},{8,9},{9,8},{10,11... | collective-permute-start | bytes 344072 | tf_op jit(solution)/shard_map/ppermute | solution.py:286
  28.3 2.0 %collective-permute-start.2 = (bf16[8,7168]{1,0:T(8,128)(2,1)S(1)}, bf16[8,7168]{1,0:T(8,128)(2,1)S(1)}, u32[]{:S(2)}, u32[]{:S(2)}) collective-permute-start(bf16[8,7168]{1,0:T(8,128)(2,1)S(1)} %get-tuple-element.21), channel_id=1, source_target_pairs={{0,1},{1,0},{2,3},{3,2},{4,5},{5,4},{6,7},{7,6},{8,9},{9,8},{10,11... | collective-permute-start | bytes 344072 | tf_op jit(solution)/shard_map/ppermute | solution.py:286
  28.8 2.7 %collective-permute-start.4 = (bf16[8,7168]{1,0:T(8,128)(2,1)S(1)}, bf16[8,7168]{1,0:T(8,128)(2,1)S(1)}, u32[]{:S(2)}, u32[]{:S(2)}) collective-permute-start(bf16[8,7168]{1,0:T(8,128)(2,1)S(1)} %get-tuple-element.23), channel_id=1, source_target_pairs={{0,1},{1,0},{2,3},{3,2},{4,5},{5,4},{6,7},{7,6},{8,9},{9,8},{10,11... | collective-permute-start | bytes 344072 | tf_op jit(solution)/shard_map/ppermute | solution.py:286
  28.9 4.5 %collective-permute-start.6 = (bf16[8,7168]{1,0:T(8,128)(2,1)S(1)}, bf16[8,7168]{1,0:T(8,128)(2,1)S(1)}, u32[]{:S(2)}, u32[]{:S(2)}) collective-permute-start(bf16[8,7168]{1,0:T(8,128)(2,1)S(1)} %get-tuple-element.25), channel_id=1, source_target_pairs={{0,1},{1,0},{2,3},{3,2},{4,5},{5,4},{6,7},{7,6},{8,9},{9,8},{10,11... | collective-permute-start | bytes 344072 | tf_op jit(solution)/shard_map/ppermute | solution.py:286
  29.6 7.0 %collective-permute-start.1 = (bf16[8,7168]{1,0:T(8,128)(2,1)S(1)}, bf16[8,7168]{1,0:T(8,128)(2,1)S(1)}, u32[]{:S(2)}, u32[]{:S(2)}) collective-permute-start(bf16[8,7168]{1,0:T(8,128)(2,1)S(1)} %add_convert_fusion.6), channel_id=1, source_target_pairs={{0,6},{1,7},{2,4},{3,5},{4,2},{5,3},{6,0},{7,1},{8,14},{9,15},{10,... | collective-permute-start | bytes 344072 | tf_op jit(solution)/shard_map/ppermute | solution.py:286
  30.3 6.9 %collective-permute-start.3 = (bf16[8,7168]{1,0:T(8,128)(2,1)S(1)}, bf16[8,7168]{1,0:T(8,128)(2,1)S(1)}, u32[]{:S(2)}, u32[]{:S(2)}) collective-permute-start(bf16[8,7168]{1,0:T(8,128)(2,1)S(1)} %add_convert_fusion.5), channel_id=1, source_target_pairs={{0,4},{1,5},{2,6},{3,7},{4,0},{5,1},{6,2},{7,3},{8,12},{9,13},{10,... | collective-permute-start | bytes 344072 | tf_op jit(solution)/shard_map/ppermute | solution.py:286
  31.5 6.8 %collective-permute-start.5 = (bf16[8,7168]{1,0:T(8,128)(2,1)S(1)}, bf16[8,7168]{1,0:T(8,128)(2,1)S(1)}, u32[]{:S(2)}, u32[]{:S(2)}) collective-permute-start(bf16[8,7168]{1,0:T(8,128)(2,1)S(1)} %add_convert_fusion.4), channel_id=1, source_target_pairs={{0,2},{1,3},{2,0},{3,1},{4,6},{5,7},{6,4},{7,5},{8,10},{9,11},{10,... | collective-permute-start | bytes 344072 | tf_op jit(solution)/shard_map/ppermute | solution.py:286
  38.3 8.4 %collective-permute-start.7 = (bf16[8,7168]{1,0:T(8,128)(2,1)S(1)}, bf16[8,7168]{1,0:T(8,128)(2,1)S(1)}, u32[]{:S(2)}, u32[]{:S(2)}) collective-permute-start(bf16[8,7168]{1,0:T(8,128)(2,1)S(1)} %fusion.4), channel_id=1, source_target_pairs={{0,8},{1,9},{2,10},{3,11},{4,12},{5,13},{6,14},{7,15},{8,0},{9,1},... | collective-permute-start | bytes 344072 | tf_op jit(solution)/shard_map/ppermute | solution.py:286
  47.0 7.0 %collective-permute-start.8 = (bf16[8,7168]{1,0:T(8,128)(2,1)S(1)}, bf16[8,7168]{1,0:T(8,128)(2,1)S(1)}, u32[]{:S(2)}, u32[]{:S(2)}) collective-permute-start(bf16[8,7168]{1,0:T(8,128)(2,1)S(1)} %add_convert_fusion.3.refs_0_), channel_id=1, source_target_pairs={{0,6},{1,7},{2,4},{3,5},{4,2},{5,3},{6,0},{7,1},{8,14},{9,15},{10,... | collective-permute-start | bytes 344072 | tf_op jit(solution)/shard_map/ppermute | solution.py:286
  47.0 6.9 %collective-permute-start.9 = (bf16[8,7168]{1,0:T(8,128)(2,1)S(1)}, bf16[8,7168]{1,0:T(8,128)(2,1)S(1)}, u32[]{:S(2)}, u32[]{:S(2)}) collective-permute-start(bf16[8,7168]{1,0:T(8,128)(2,1)S(1)} %add_convert_fusion.3.refs_0_), channel_id=1, source_target_pairs={{0,4},{1,5},{2,6},{3,7},{4,0},{5,1},{6,2},{7,3},{8,12},{9,13},{10,... | collective-permute-start | bytes 344072 | tf_op jit(solution)/shard_map/ppermute | solution.py:286
  48.4 7.0 %collective-permute-start.10 = (bf16[8,7168]{1,0:T(8,128)(2,1)S(1)}, bf16[8,7168]{1,0:T(8,128)(2,1)S(1)}, u32[]{:S(2)}, u32[]{:S(2)}) collective-permute-start(bf16[8,7168]{1,0:T(8,128)(2,1)S(1)} %add_convert_fusion.3.refs_0_), channel_id=1, source_target_pairs={{0,2},{1,3},{2,0},{3,1},{4,6},{5,7},{6,4},{7,5},{8,10},{9,11},{10,... | collective-permute-start | bytes 344072 | tf_op jit(solution)/shard_map/ppermute | solution.py:286
  50.5 5.0 %collective-permute-start.11 = (bf16[8,7168]{1,0:T(8,128)(2,1)S(1)}, bf16[8,7168]{1,0:T(8,128)(2,1)S(1)}, u32[]{:S(2)}, u32[]{:S(2)}) collective-permute-start(bf16[8,7168]{1,0:T(8,128)(2,1)S(1)} %add_convert_fusion.3.refs_0_), channel_id=1, source_target_pairs={{0,1},{1,0},{2,3},{3,2},{4,5},{5,4},{6,7},{7,6},{8,9},{9,8},{10,11... | collective-permute-start | bytes 344072 | tf_op jit(solution)/shard_map/ppermute | solution.py:286
  53.9 1.5 %collective-permute-start.12 = (bf16[8,7168]{1,0:T(8,128)(2,1)S(1)}, bf16[8,7168]{1,0:T(8,128)(2,1)S(1)}, u32[]{:S(2)}, u32[]{:S(2)}) collective-permute-start(bf16[8,7168]{1,0:T(8,128)(2,1)S(1)} %collective-permute-done.8.refs_1_), channel_id=1, source_target_pairs={{0,1},{1,0},{2,3},{3,2},{4,5},{5,4},{6,7},{7,6},{8,9},{9,8},{10,11... | collective-permute-start | bytes 344072 | tf_op jit(solution)/shard_map/ppermute | solution.py:286
  53.9 1.5 %collective-permute-start.13 = (bf16[8,7168]{1,0:T(8,128)(2,1)S(1)}, bf16[8,7168]{1,0:T(8,128)(2,1)S(1)}, u32[]{:S(2)}, u32[]{:S(2)}) collective-permute-start(bf16[8,7168]{1,0:T(8,128)(2,1)S(1)} %collective-permute-done.9.refs_2_), channel_id=1, source_target_pairs={{0,1},{1,0},{2,3},{3,2},{4,5},{5,4},{6,7},{7,6},{8,9},{9,8},{10,11... | collective-permute-start | bytes 344072 | tf_op jit(solution)/shard_map/ppermute | solution.py:286
  55.5 1.3 %collective-permute-start.14 = (bf16[8,7168]{1,0:T(8,128)(2,1)S(1)}, bf16[8,7168]{1,0:T(8,128)(2,1)S(1)}, u32[]{:S(2)}, u32[]{:S(2)}) collective-permute-start(bf16[8,7168]{1,0:T(8,128)(2,1)S(1)} %collective-permute-done.10.refs_3_), channel_id=1, source_target_pairs={{0,1},{1,0},{2,3},{3,2},{4,5},{5,4},{6,7},{7,6},{8,9},{9,8},{10,11... | collective-permute-start | bytes 344072 | tf_op jit(solution)/shard_map/ppermute | solution.py:286
  59.2 1.4 %collective-permute-start.15 = (bf16[8,7168]{1,0:T(8,128)(2,1)S(1)}, bf16[8,7168]{1,0:T(8,128)(2,1)S(1)}, u32[]{:S(2)}, u32[]{:S(2)}) collective-permute-start(bf16[8,7168]{1,0:T(8,128)(2,1)S(1)} %get-tuple-element.27), channel_id=1, source_target_pairs={{0,1},{1,0},{2,3},{3,2},{4,5},{5,4},{6,7},{7,6},{8,9},{9,8},{10,11... | collective-permute-start | bytes 344072 | tf_op jit(solution)/shard_map/ppermute | solution.py:286
  59.4 1.6 %collective-permute-start.17 = (bf16[8,7168]{1,0:T(8,128)(2,1)S(1)}, bf16[8,7168]{1,0:T(8,128)(2,1)S(1)}, u32[]{:S(2)}, u32[]{:S(2)}) collective-permute-start(bf16[8,7168]{1,0:T(8,128)(2,1)S(1)} %get-tuple-element.29), channel_id=1, source_target_pairs={{0,1},{1,0},{2,3},{3,2},{4,5},{5,4},{6,7},{7,6},{8,9},{9,8},{10,11... | collective-permute-start | bytes 344072 | tf_op jit(solution)/shard_map/ppermute | solution.py:286
  59.8 3.2 %collective-permute-start.19 = (bf16[8,7168]{1,0:T(8,128)(2,1)S(1)}, bf16[8,7168]{1,0:T(8,128)(2,1)S(1)}, u32[]{:S(2)}, u32[]{:S(2)}) collective-permute-start(bf16[8,7168]{1,0:T(8,128)(2,1)S(1)} %get-tuple-element.31), channel_id=1, source_target_pairs={{0,1},{1,0},{2,3},{3,2},{4,5},{5,4},{6,7},{7,6},{8,9},{9,8},{10,11... | collective-permute-start | bytes 344072 | tf_op jit(solution)/shard_map/ppermute | solution.py:286
  59.9 4.4 %collective-permute-start.21 = (bf16[8,7168]{1,0:T(8,128)(2,1)S(1)}, bf16[8,7168]{1,0:T(8,128)(2,1)S(1)}, u32[]{:S(2)}, u32[]{:S(2)}) collective-permute-start(bf16[8,7168]{1,0:T(8,128)(2,1)S(1)} %get-tuple-element.33), channel_id=1, source_target_pairs={{0,1},{1,0},{2,3},{3,2},{4,5},{5,4},{6,7},{7,6},{8,9},{9,8},{10,11... | collective-permute-start | bytes 344072 | tf_op jit(solution)/shard_map/ppermute | solution.py:286
  60.6 7.0 %collective-permute-start.16 = (bf16[8,7168]{1,0:T(8,128)(2,1)S(1)}, bf16[8,7168]{1,0:T(8,128)(2,1)S(1)}, u32[]{:S(2)}, u32[]{:S(2)}) collective-permute-start(bf16[8,7168]{1,0:T(8,128)(2,1)S(1)} %add_convert_fusion.2), channel_id=1, source_target_pairs={{0,6},{1,7},{2,4},{3,5},{4,2},{5,3},{6,0},{7,1},{8,14},{9,15},{10,... | collective-permute-start | bytes 344072 | tf_op jit(solution)/shard_map/ppermute | solution.py:286
  61.0 7.7 %collective-permute-start.18 = (bf16[8,7168]{1,0:T(8,128)(2,1)S(1)}, bf16[8,7168]{1,0:T(8,128)(2,1)S(1)}, u32[]{:S(2)}, u32[]{:S(2)}) collective-permute-start(bf16[8,7168]{1,0:T(8,128)(2,1)S(1)} %add_convert_fusion.1), channel_id=1, source_target_pairs={{0,4},{1,5},{2,6},{3,7},{4,0},{5,1},{6,2},{7,3},{8,12},{9,13},{10,... | collective-permute-start | bytes 344072 | tf_op jit(solution)/shard_map/ppermute | solution.py:286
  63.0 6.2 %collective-permute-start.20 = (bf16[8,7168]{1,0:T(8,128)(2,1)S(1)}, bf16[8,7168]{1,0:T(8,128)(2,1)S(1)}, u32[]{:S(2)}, u32[]{:S(2)}) collective-permute-start(bf16[8,7168]{1,0:T(8,128)(2,1)S(1)} %add_convert_fusion), channel_id=1, source_target_pairs={{0,2},{1,3},{2,0},{3,1},{4,6},{5,7},{6,4},{7,5},{8,10},{9,11},{10,... | collective-permute-start | bytes 344072 | tf_op jit(solution)/shard_map/ppermute | solution.py:286
  69.3 5.2 %collective-permute-start.22 = (bf16[4,7168]{1,0:T(4,128)(2,1)S(1)}, bf16[4,7168]{1,0:T(4,128)(2,1)S(1)}, u32[]{:S(2)}, u32[]{:S(2)}) collective-permute-start(bf16[4,7168]{1,0:T(4,128)(2,1)S(1)} %slice.32), channel_id=1, source_target_pairs={{0,8},{1,9},{2,10},{3,11},{4,12},{5,13},{6,14},{7,15},{8,0},{9,1},... | collective-permute-start | bytes 172040 | tf_op jit(solution)/shard_map/ppermute | solution.py:286
  (9 other events, 218.9 us)

commit v11 on v10

--- a/solution.py
+++ b/solution.py
@@ -17,6 +17,7 @@
 PARTS = 4
 SQUARE = (0, 6, 4, 2)
 PIECES = len(SQUARE)
+SIDES = 2
 MIB = 2**20
 
 
@@ -196,15 +197,23 @@
     far_at, slot = slot & (far - 1), slot >> far_bits
     distance = (far_at << 3) + ((4 - (slot & 3) & 3) << 1) + (slot >> 2)
     device = distance ^ lax.axis_index("experts")
-    values = []
+    choices = []
     for head in range(own_heads):
         wanted = ((device << turn) + request) * own_heads + head
-        choice = (place == wanted).astype(jnp.float32).astype(jnp.bfloat16)
-        latent = jnp.dot(choice, joined_ref[...], preferred_element_type=jnp.float32)
-        value = jnp.dot(
-            latent.astype(jnp.bfloat16), absorb_ref[head], preferred_element_type=jnp.float32
-        )
-        values.append(value.astype(jnp.bfloat16))
+        choices.append((place == wanted).astype(jnp.float32))
+    latents = jnp.dot(
+        jnp.concatenate(choices, axis=0).astype(jnp.bfloat16),
+        joined_ref[...],
+        preferred_element_type=jnp.float32,
+    ).astype(jnp.bfloat16)
+    values = [
+        jnp.dot(
+            latents[head * shape[0] : (head + 1) * shape[0]],
+            absorb_ref[head],
+            preferred_element_type=jnp.float32,
+        ).astype(jnp.bfloat16)
+        for head in range(own_heads)
+    ]
     values = jnp.concatenate(values, axis=1)
     for at in range(0, width, TILE):
         term = jnp.dot(values, w_ref[:, at : at + TILE], preferred_element_type=jnp.float32)
@@ -230,23 +239,31 @@
 
 
 def expert_kernel(*refs):
-    streams, (gain_ref, gate_ref, up_ref, down_ref), pieces = refs[:8], refs[8:12], refs[12:]
+    count = 2 * PIECES * SIDES
+    streams, (gain_ref, gate_ref, up_ref, down_ref) = refs[:count], refs[count : count + 4]
+    pieces = refs[count + 4 :]
+    streams = [streams[at :: 2 * PIECES] for at in range(2 * PIECES)]
     width = gain_ref.shape[1]
+    side = width // SIDES
     depth = width // PARTS
     inverses = []
     for stream in streams:
         squares = 0.0
-        for at in range(0, width, depth):
-            piece = stream[:, at : at + depth].astype(jnp.float32)
-            squares = squares + sum(lane_tiles(piece * piece))
+        for ref in stream:
+            for at in range(0, side, depth):
+                piece = ref[:, at : at + depth].astype(jnp.float32)
+                squares = squares + sum(lane_tiles(piece * piece))
         mean = jnp.sum(squares, axis=1, keepdims=True) / width
         inverses.append(lax.rsqrt(mean + 1e-06))
     gate, up = 0.0, 0.0
     for at in range(0, width, depth):
         gain = gain_ref[:, at : at + depth]
+        place = at % side
         tokens = jnp.concatenate(
             [
-                stream[:, at : at + depth].astype(jnp.float32) * inverse * gain
+                stream[at // side][:, place : place + depth].astype(jnp.float32)
+                * inverse
+                * gain
                 for stream, inverse in zip(streams, inverses)
             ],
             axis=0,
@@ -264,12 +281,12 @@
 
 
 def run_expert(streams, norm_gain, w_gate, w_up, w_down):
-    rows, width = streams[0].shape
-    hidden = w_gate.shape[1]
+    rows = streams[0].shape[0]
+    width, hidden = w_gate.shape
     return pl.pallas_call(
         expert_kernel,
         out_shape=term_shapes(rows, width),
-        in_specs=[pl.BlockSpec(memory_space=pltpu.VMEM)] * (2 * PIECES + 4),
+        in_specs=[pl.BlockSpec(memory_space=pltpu.VMEM)] * (2 * PIECES * SIDES + 4),
         out_specs=(pl.BlockSpec(memory_space=pltpu.VMEM),) * (2 * PIECES),
         compiler_params=pltpu.CompilerParams(vmem_limit_bytes=24 * MIB),
         cost_estimate=pl.CostEstimate(
@@ -345,10 +362,19 @@
     joined = lax.all_to_all(latent, "experts", split_axis=0, concat_axis=0, tiled=True)
     joined = joined.reshape(-1, joined.shape[-1])
     terms = project(joined, w_absorb, residual_in, w_out, all_rows, far)
-    stream = exchange(collect(terms), far)
-    attended = stream[:own_rows]
-
-    total = collect(run_expert(spread(stream), norm_gain, w_gate, w_up, w_down))
+    total = collect(terms)
+    side = total.shape[1] // SIDES
+    totals = lax.optimization_barrier(
+        [total[:, at * side : (at + 1) * side] for at in range(SIDES)]
+    )
+    attended, streams = [], []
+    for total in totals:
+        stream = exchange(total, far)
+        attended.append(stream[:own_rows])
+        streams.extend(spread(stream))
+    attended = jnp.concatenate(attended, axis=1)
+
+    total = collect(run_expert(streams, norm_gain, w_gate, w_up, w_down))
     own_ids = lax.dynamic_slice_in_dim(expert_ids, rank_here * own_rows, own_rows, 0)
     expert_out = 0.0
     for at in range(far):

time: 74.7 us -> 76.7 us (1.027)
  starting transfers between devices: 14.8 us -> 20.8 us
  waiting for transfers between devices: 27.8 us -> 23.5 us
  Pallas kernels: 13 us -> 10.7 us
  blocking collectives: 16.8 us -> 18.8 us
    ppermute x23 -> x31, starting transfers between devices: 14.8 us -> 20.8 us  [swap(): return lax.ppermute(array, 'experts', pairs)]
    ppermute x23 -> x31, waiting for transfers between devices: 27.8 us -> 23.5 us  [swap(): return lax.ppermute(array, 'experts', pairs)]
    all_to_all x1, blocking collectives: 16.8 us -> 18.8 us  [shards(): lax.all_to_all(latent, 'experts', split_axis=0, concat_axis=0, tiled=True)]
    pallas_call x1, Pallas kernels: 8.58 us -> 6.66 us  [attend(): pl.pallas_call(attend_kernel, out_shape=jax.ShapeDtypeStruct((devices, pa...]
  transfers between devices with their start and end apart: 23 -> 31, of which waited for: 13 -> 16; matrix products, arithmetic and copies ran while one was open for 1% -> 1% of each run, Pallas kernels for 0% -> 0%
where the time goes in v11:
time: 76.7 us
  waiting for transfers between devices  23.5 us (31%)
  starting transfers between devices  20.8 us (27%)
  blocking collectives  18.8 us (25%)
  Pallas kernels  10.7 us (14%)
  other arithmetic  1.88 us (2%)
  between operations  0.9 us (1%)
    ppermute x31, waiting for transfers between devices, swap(): return lax.ppermute(array, 'experts', pairs)  23.5 us
    ppermute x31, starting transfers between devices, swap(): return lax.ppermute(array, 'experts', pairs)  20.8 us
    all_to_all x1, blocking collectives, shards(): lax.all_to_all(latent, 'experts', split_axis=0, concat_axis=0, tiled=True)  18.8 us
    pallas_call x1, Pallas kernels, attend(): pl.pallas_call(attend_kernel, out_shape=jax.ShapeDtypeStruct((devices, pa...  6.66 us
    pallas_call x1, Pallas kernels, run_expert(): pl.pallas_call(expert_kernel, out_shape=term_shapes(rows, width), in_spec...  2.36 us
    pallas_call x1, Pallas kernels, project(): pl.pallas_call(functools.partial(project_kernel, own_rows, far), out_shap...  1.68 us
  transfers between devices with their start and end apart: 31, of which 16 were waited for; matrix products, arithmetic and copies ran while one was open for 1% of the time, Pallas kernels for 0%

profile of v11, /device:TPU:0, one launch (start us, length us, event | category | flops | bytes accessed | tf_op | source)
XLA Modules:
  0.0 76.7 jit_solution(8311846362088578724)
XLA Ops:
  0.7 6.7 %attend.1 = bf16[16,16,512]{2,1,0:T(8,128)(2,1)} custom-call(s32[4]{0:T(128)} %len_ref.1, bf16[4,64,576]{2,1,0:T(8,128)(2,1)} %bitcast.7, bf16[4,576,4096]{2,1,0:T(8,128)(2,1)} %cache_ref.1), custom_call_target="tpu_custom_call" | custom-call | flops 1140850688 | bytes 9437184 | tf_op jit(solution)/shard_map/attend/pallas_call | solution.py:145
  7.3 18.8 %all_to_all.5 = bf16[16,16,512]{2,1,0:T(8,128)(2,1)S(1)} all-to-all(bf16[16,16,512]{2,1,0:T(8,128)(2,1)} %attend.1), channel_id=1, replica_groups=mesh['groups'=2,'experts'=16] {'experts'}, dimensions={0} | all-to-all | bytes 524288 | tf_op jit(solution)/shard_map/all_to_all | solution.py:362
  26.2 1.7 %project.1 = (f32[8,7168]{1,0:T(8,128)S(1)}, f32[8,7168]{1,0:T(8,128)S(1)}, f32[8,7168]{1,0:T(8,128)S(1)}, f32[8,7168]{1,0:T(8,128)S(1)}, bf16[8,7168]{1,0:T(8,1...) custom-call(bf16[256,512]{1,0:T(8,128)(2,1)S(1)} %bitcast.5, ...), custom_call_target="tpu_custom_call" | custom-call | flops 469762048 | bytes 7340032 | tf_op jit(solution)/shard_map/project/pallas_call | solution.py:228
  30.0 1.1 %collective-permute-start.3 = (bf16[8,7168]{1,0:T(8,128)(2,1)S(1)}, bf16[8,7168]{1,0:T(8,128)(2,1)S(1)}, u32[]{:S(2)}, u32[]{:S(2)}) collective-permute-start(bf16[8,7168]{1,0:T(8,128)(2,1)S(1)} %add_convert_fusion.4), channel_id=1, source_target_pairs={{0,4},{1,5},{2,6},{3,7},{4,0},{5,1},{6,2},{7,3},{8,12},{9,13},{10,... | collective-permute-start | bytes 344072 | tf_op jit(solution)/shard_map/ppermute | solution.py:303
  31.2 1.9 %collective-permute-start.5 = (bf16[8,7168]{1,0:T(8,128)(2,1)S(1)}, bf16[8,7168]{1,0:T(8,128)(2,1)S(1)}, u32[]{:S(2)}, u32[]{:S(2)}) collective-permute-start(bf16[8,7168]{1,0:T(8,128)(2,1)S(1)} %add_convert_fusion.3), channel_id=1, source_target_pairs={{0,2},{1,3},{2,0},{3,1},{4,6},{5,7},{6,4},{7,5},{8,10},{9,11},{10,... | collective-permute-start | bytes 344072 | tf_op jit(solution)/shard_map/ppermute | solution.py:303
  33.1 3.2 %collective-permute-done.1 = bf16[8,7168]{1,0:T(8,128)(2,1)S(1)} collective-permute-done((bf16[8,7168]{1,0:T(8,128)(2,1)S(1)}, bf16[8,7168]{1,0:T(8,128)(2,1)S(1)}, u32[]{:S(2)}, u32[]{:S(2)}) %collective-permute-start.1) | collective-permute-done | bytes 114720 | tf_op jit(solution)/shard_map/ppermute | solution.py:303
  36.9 1.1 %collective-permute-done.5 = bf16[8,7168]{1,0:T(8,128)(2,1)S(1)} collective-permute-done((bf16[8,7168]{1,0:T(8,128)(2,1)S(1)}, bf16[8,7168]{1,0:T(8,128)(2,1)S(1)}, u32[]{:S(2)}, u32[]{:S(2)}) %collective-permute-start.5) | collective-permute-done | bytes 114720 | tf_op jit(solution)/shard_map/ppermute | solution.py:303
  38.1 1.1 %collective-permute-start.7 = (bf16[8,3584]{1,0:T(8,128)(2,1)S(1)}, bf16[8,3584]{1,0:T(8,128)(2,1)S(1)}, u32[]{:S(2)}, u32[]{:S(2)}) collective-permute-start(bf16[8,3584]{1,0:T(8,128)(2,1)S(1)} %convert_element_type.97), channel_id=1, source_target_pairs={{0,8},{1,9},{2,10},{3,11},{4,12},{5,13},{6,14},{7,15},{8,0},{9,1},... | collective-permute-start | bytes 172040 | tf_op jit(solution)/shard_map/ppermute | solution.py:303
  39.2 1.9 %collective-permute-start.8 = (bf16[8,3584]{1,0:T(8,128)(2,1)S(1)}, bf16[8,3584]{1,0:T(8,128)(2,1)S(1)}, u32[]{:S(2)}, u32[]{:S(2)}) collective-permute-start(bf16[8,3584]{1,0:T(8,128)(2,1)S(1)} %convert_element_type.100), channel_id=1, source_target_pairs={{0,8},{1,9},{2,10},{3,11},{4,12},{5,13},{6,14},{7,15},{8,0},{9,1},... | collective-permute-start | bytes 172040 | tf_op jit(solution)/shard_map/ppermute | solution.py:303
  41.1 4.4 %collective-permute-done.7 = bf16[8,3584]{1,0:T(8,128)(2,1)S(1)} collective-permute-done((bf16[8,3584]{1,0:T(8,128)(2,1)S(1)}, bf16[8,3584]{1,0:T(8,128)(2,1)S(1)}, u32[]{:S(2)}, u32[]{:S(2)}) %collective-permute-start.7) | collective-permute-done | bytes 57376 | tf_op jit(solution)/shard_map/ppermute | solution.py:303
  45.7 1.7 %collective-permute-start.10 = (bf16[8,3584]{1,0:T(8,128)(2,1)S(1)}, bf16[8,3584]{1,0:T(8,128)(2,1)S(1)}, u32[]{:S(2)}, u32[]{:S(2)}) collective-permute-start(bf16[8,3584]{1,0:T(8,128)(2,1)S(1)} %add_convert_fusion.7.refs_0_), channel_id=1, source_target_pairs={{0,4},{1,5},{2,6},{3,7},{4,0},{5,1},{6,2},{7,3},{8,12},{9,13},{10,... | collective-permute-start | bytes 172040 | tf_op jit(solution)/shard_map/ppermute | solution.py:303
  47.4 1.8 %collective-permute-start.11 = (bf16[8,3584]{1,0:T(8,128)(2,1)S(1)}, bf16[8,3584]{1,0:T(8,128)(2,1)S(1)}, u32[]{:S(2)}, u32[]{:S(2)}) collective-permute-start(bf16[8,3584]{1,0:T(8,128)(2,1)S(1)} %add_convert_fusion.7.refs_0_), channel_id=1, source_target_pairs={{0,2},{1,3},{2,0},{3,1},{4,6},{5,7},{6,4},{7,5},{8,10},{9,11},{10,... | collective-permute-start | bytes 172040 | tf_op jit(solution)/shard_map/ppermute | solution.py:303
  49.4 1.4 %collective-permute-done.9.refs_1_ = bf16[8,3584]{1,0:T(8,128)(2,1)S(1)} collective-permute-done((bf16[8,3584]{1,0:T(8,128)(2,1)S(1)}, bf16[8,3584]{1,0:T(8,128)(2,1)S(1)}, u32[]{:S(2)}, u32[]{:S(2)}) %collective-permute-start.9) | collective-permute-done | bytes 57376 | tf_op jit(solution)/shard_map/ppermute | solution.py:303
  51.1 1.8 %collective-permute-start.18 = (bf16[8,3584]{1,0:T(8,128)(2,1)S(1)}, bf16[8,3584]{1,0:T(8,128)(2,1)S(1)}, u32[]{:S(2)}, u32[]{:S(2)}) collective-permute-start(bf16[8,3584]{1,0:T(8,128)(2,1)S(1)} %add_convert_fusion.6.refs_8_), channel_id=1, source_target_pairs={{0,2},{1,3},{2,0},{3,1},{4,6},{5,7},{6,4},{7,5},{8,10},{9,11},{10,... | collective-permute-start | bytes 172040 | tf_op jit(solution)/shard_map/ppermute | solution.py:303
  53.4 1.6 %collective-permute-done.16.refs_9_ = bf16[8,3584]{1,0:T(8,128)(2,1)S(1)} collective-permute-done((bf16[8,3584]{1,0:T(8,128)(2,1)S(1)}, bf16[8,3584]{1,0:T(8,128)(2,1)S(1)}, u32[]{:S(2)}, u32[]{:S(2)}) %collective-permute-start.16) | collective-permute-done | bytes 57376 | tf_op jit(solution)/shard_map/ppermute | solution.py:303
  57.6 2.4 %expert.1 = (f32[8,7168]{1,0:T(8,128)S(1)}, f32[8,7168]{1,0:T(8,128)S(1)}, f32[8,7168]{1,0:T(8,128)S(1)}, f32[8,7168]{1,0:T(8,128)S(1)}, bf16[8,7168]{1,0:T(8,12...) custom-call(bf16[8,3584]{1,0:T(8,128)(2,1)S(1)} %add_convert_fusion.7.refs_0_, ...), custom_call_target="tpu_custom_call" | custom-call | flops 704643072 | bytes 11010048 | tf_op jit(solution)/shard_map/expert/pallas_call | solution.py:286
  61.4 1.3 %collective-permute-start.24 = (bf16[8,7168]{1,0:T(8,128)(2,1)S(1)}, bf16[8,7168]{1,0:T(8,128)(2,1)S(1)}, u32[]{:S(2)}, u32[]{:S(2)}) collective-permute-start(bf16[8,7168]{1,0:T(8,128)(2,1)S(1)} %add_convert_fusion.2), channel_id=1, source_target_pairs={{0,6},{1,7},{2,4},{3,5},{4,2},{5,3},{6,0},{7,1},{8,14},{9,15},{10,... | collective-permute-start | bytes 344072 | tf_op jit(solution)/shard_map/ppermute | solution.py:303
  62.7 1.6 %collective-permute-start.26 = (bf16[8,7168]{1,0:T(8,128)(2,1)S(1)}, bf16[8,7168]{1,0:T(8,128)(2,1)S(1)}, u32[]{:S(2)}, u32[]{:S(2)}) collective-permute-start(bf16[8,7168]{1,0:T(8,128)(2,1)S(1)} %add_convert_fusion.1), channel_id=1, source_target_pairs={{0,4},{1,5},{2,6},{3,7},{4,0},{5,1},{6,2},{7,3},{8,12},{9,13},{10,... | collective-permute-start | bytes 344072 | tf_op jit(solution)/shard_map/ppermute | solution.py:303
  64.3 0.9 %collective-permute-start.28 = (bf16[8,7168]{1,0:T(8,128)(2,1)S(1)}, bf16[8,7168]{1,0:T(8,128)(2,1)S(1)}, u32[]{:S(2)}, u32[]{:S(2)}) collective-permute-start(bf16[8,7168]{1,0:T(8,128)(2,1)S(1)} %add_convert_fusion), channel_id=1, source_target_pairs={{0,2},{1,3},{2,0},{3,1},{4,6},{5,7},{6,4},{7,5},{8,10},{9,11},{10,... | collective-permute-start | bytes 344072 | tf_op jit(solution)/shard_map/ppermute | solution.py:303
  65.3 3.1 %collective-permute-done.24 = bf16[8,7168]{1,0:T(8,128)(2,1)S(1)} collective-permute-done((bf16[8,7168]{1,0:T(8,128)(2,1)S(1)}, bf16[8,7168]{1,0:T(8,128)(2,1)S(1)}, u32[]{:S(2)}, u32[]{:S(2)}) %collective-permute-start.24) | collective-permute-done | bytes 114720 | tf_op jit(solution)/shard_map/ppermute | solution.py:303
  68.3 1.4 %collective-permute-done.26 = bf16[8,7168]{1,0:T(8,128)(2,1)S(1)} collective-permute-done((bf16[8,7168]{1,0:T(8,128)(2,1)S(1)}, bf16[8,7168]{1,0:T(8,128)(2,1)S(1)}, u32[]{:S(2)}, u32[]{:S(2)}) %collective-permute-start.26) | collective-permute-done | bytes 114720 | tf_op jit(solution)/shard_map/ppermute | solution.py:303
  70.1 0.8 %collective-permute-start.30 = (bf16[4,7168]{1,0:T(4,128)(2,1)S(1)}, bf16[4,7168]{1,0:T(4,128)(2,1)S(1)}, u32[]{:S(2)}, u32[]{:S(2)}) collective-permute-start(bf16[4,7168]{1,0:T(4,128)(2,1)S(1)} %slice.57), channel_id=1, source_target_pairs={{0,8},{1,9},{2,10},{3,11},{4,12},{5,13},{6,14},{7,15},{8,0},{9,1},... | collective-permute-start | bytes 172040 | tf_op jit(solution)/shard_map/ppermute | solution.py:303
  71.6 4.4 %collective-permute-done.30 = bf16[4,7168]{1,0:T(4,128)(2,1)S(1)} collective-permute-done((bf16[4,7168]{1,0:T(4,128)(2,1)S(1)}, bf16[4,7168]{1,0:T(4,128)(2,1)S(1)}, u32[]{:S(2)}, u32[]{:S(2)}) %collective-permute-start.30) | collective-permute-done | bytes 57376 | tf_op jit(solution)/shard_map/ppermute | solution.py:303
  76.0 0.7 fusion.1
  (84 shorter events, 9.2 us)
Async XLA Ops:
  28.0 2.0 %collective-permute-start.2 = (bf16[8,7168]{1,0:T(8,128)(2,1)S(1)}, bf16[8,7168]{1,0:T(8,128)(2,1)S(1)}, u32[]{:S(2)}, u32[]{:S(2)}) collective-permute-start(bf16[8,7168]{1,0:T(8,128)(2,1)S(1)} %get-tuple-element.23), channel_id=1, source_target_pairs={{0,1},{1,0},{2,3},{3,2},{4,5},{5,4},{6,7},{7,6},{8,9},{9,8},{10,11... | collective-permute-start | bytes 344072 | tf_op jit(solution)/shard_map/ppermute | solution.py:303
  28.5 2.7 %collective-permute-start.4 = (bf16[8,7168]{1,0:T(8,128)(2,1)S(1)}, bf16[8,7168]{1,0:T(8,128)(2,1)S(1)}, u32[]{:S(2)}, u32[]{:S(2)}) collective-permute-start(bf16[8,7168]{1,0:T(8,128)(2,1)S(1)} %get-tuple-element.25), channel_id=1, source_target_pairs={{0,1},{1,0},{2,3},{3,2},{4,5},{5,4},{6,7},{7,6},{8,9},{9,8},{10,11... | collective-permute-start | bytes 344072 | tf_op jit(solution)/shard_map/ppermute | solution.py:303
  28.6 4.5 %collective-permute-start.6 = (bf16[8,7168]{1,0:T(8,128)(2,1)S(1)}, bf16[8,7168]{1,0:T(8,128)(2,1)S(1)}, u32[]{:S(2)}, u32[]{:S(2)}) collective-permute-start(bf16[8,7168]{1,0:T(8,128)(2,1)S(1)} %get-tuple-element.27), channel_id=1, source_target_pairs={{0,1},{1,0},{2,3},{3,2},{4,5},{5,4},{6,7},{7,6},{8,9},{9,8},{10,11... | collective-permute-start | bytes 344072 | tf_op jit(solution)/shard_map/ppermute | solution.py:303
  29.3 7.0 %collective-permute-start.1 = (bf16[8,7168]{1,0:T(8,128)(2,1)S(1)}, bf16[8,7168]{1,0:T(8,128)(2,1)S(1)}, u32[]{:S(2)}, u32[]{:S(2)}) collective-permute-start(bf16[8,7168]{1,0:T(8,128)(2,1)S(1)} %add_convert_fusion.5), channel_id=1, source_target_pairs={{0,6},{1,7},{2,4},{3,5},{4,2},{5,3},{6,0},{7,1},{8,14},{9,15},{10,... | collective-permute-start | bytes 344072 | tf_op jit(solution)/shard_map/ppermute | solution.py:303
  30.0 6.9 %collective-permute-start.3 = (bf16[8,7168]{1,0:T(8,128)(2,1)S(1)}, bf16[8,7168]{1,0:T(8,128)(2,1)S(1)}, u32[]{:S(2)}, u32[]{:S(2)}) collective-permute-start(bf16[8,7168]{1,0:T(8,128)(2,1)S(1)} %add_convert_fusion.4), channel_id=1, source_target_pairs={{0,4},{1,5},{2,6},{3,7},{4,0},{5,1},{6,2},{7,3},{8,12},{9,13},{10,... | collective-permute-start | bytes 344072 | tf_op jit(solution)/shard_map/ppermute | solution.py:303
  31.2 6.8 %collective-permute-start.5 = (bf16[8,7168]{1,0:T(8,128)(2,1)S(1)}, bf16[8,7168]{1,0:T(8,128)(2,1)S(1)}, u32[]{:S(2)}, u32[]{:S(2)}) collective-permute-start(bf16[8,7168]{1,0:T(8,128)(2,1)S(1)} %add_convert_fusion.3), channel_id=1, source_target_pairs={{0,2},{1,3},{2,0},{3,1},{4,6},{5,7},{6,4},{7,5},{8,10},{9,11},{10,... | collective-permute-start | bytes 344072 | tf_op jit(solution)/shard_map/ppermute | solution.py:303
  38.1 7.5 %collective-permute-start.7 = (bf16[8,3584]{1,0:T(8,128)(2,1)S(1)}, bf16[8,3584]{1,0:T(8,128)(2,1)S(1)}, u32[]{:S(2)}, u32[]{:S(2)}) collective-permute-start(bf16[8,3584]{1,0:T(8,128)(2,1)S(1)} %convert_element_type.97), channel_id=1, source_target_pairs={{0,8},{1,9},{2,10},{3,11},{4,12},{5,13},{6,14},{7,15},{8,0},{9,1},... | collective-permute-start | bytes 172040 | tf_op jit(solution)/shard_map/ppermute | solution.py:303
  39.2 10.0 %collective-permute-start.8 = (bf16[8,3584]{1,0:T(8,128)(2,1)S(1)}, bf16[8,3584]{1,0:T(8,128)(2,1)S(1)}, u32[]{:S(2)}, u32[]{:S(2)}) collective-permute-start(bf16[8,3584]{1,0:T(8,128)(2,1)S(1)} %convert_element_type.100), channel_id=1, source_target_pairs={{0,8},{1,9},{2,10},{3,11},{4,12},{5,13},{6,14},{7,15},{8,0},{9,1},... | collective-permute-start | bytes 172040 | tf_op jit(solution)/shard_map/ppermute | solution.py:303
  45.6 5.1 %collective-permute-start.9 = (bf16[8,3584]{1,0:T(8,128)(2,1)S(1)}, bf16[8,3584]{1,0:T(8,128)(2,1)S(1)}, u32[]{:S(2)}, u32[]{:S(2)}) collective-permute-start(bf16[8,3584]{1,0:T(8,128)(2,1)S(1)} %add_convert_fusion.7.refs_0_), channel_id=1, source_target_pairs={{0,6},{1,7},{2,4},{3,5},{4,2},{5,3},{6,0},{7,1},{8,14},{9,15},{10,... | collective-permute-start | bytes 172040 | tf_op jit(solution)/shard_map/ppermute | solution.py:303
  45.7 5.3 %collective-permute-start.10 = (bf16[8,3584]{1,0:T(8,128)(2,1)S(1)}, bf16[8,3584]{1,0:T(8,128)(2,1)S(1)}, u32[]{:S(2)}, u32[]{:S(2)}) collective-permute-start(bf16[8,3584]{1,0:T(8,128)(2,1)S(1)} %add_convert_fusion.7.refs_0_), channel_id=1, source_target_pairs={{0,4},{1,5},{2,6},{3,7},{4,0},{5,1},{6,2},{7,3},{8,12},{9,13},{10,... | collective-permute-start | bytes 172040 | tf_op jit(solution)/shard_map/ppermute | solution.py:303
  47.4 5.4 %collective-permute-start.11 = (bf16[8,3584]{1,0:T(8,128)(2,1)S(1)}, bf16[8,3584]{1,0:T(8,128)(2,1)S(1)}, u32[]{:S(2)}, u32[]{:S(2)}) collective-permute-start(bf16[8,3584]{1,0:T(8,128)(2,1)S(1)} %add_convert_fusion.7.refs_0_), channel_id=1, source_target_pairs={{0,2},{1,3},{2,0},{3,1},{4,6},{5,7},{6,4},{7,5},{8,10},{9,11},{10,... | collective-permute-start | bytes 172040 | tf_op jit(solution)/shard_map/ppermute | solution.py:303
  49.2 3.7 %collective-permute-start.12 = (bf16[8,3584]{1,0:T(8,128)(2,1)S(1)}, bf16[8,3584]{1,0:T(8,128)(2,1)S(1)}, u32[]{:S(2)}, u32[]{:S(2)}) collective-permute-start(bf16[8,3584]{1,0:T(8,128)(2,1)S(1)} %add_convert_fusion.7.refs_0_), channel_id=1, source_target_pairs={{0,1},{1,0},{2,3},{3,2},{4,5},{5,4},{6,7},{7,6},{8,9},{9,8},{10,11... | collective-permute-start | bytes 172040 | tf_op jit(solution)/shard_map/ppermute | solution.py:303
  49.3 5.7 %collective-permute-start.16 = (bf16[8,3584]{1,0:T(8,128)(2,1)S(1)}, bf16[8,3584]{1,0:T(8,128)(2,1)S(1)}, u32[]{:S(2)}, u32[]{:S(2)}) collective-permute-start(bf16[8,3584]{1,0:T(8,128)(2,1)S(1)} %add_convert_fusion.6.refs_8_), channel_id=1, source_target_pairs={{0,6},{1,7},{2,4},{3,5},{4,2},{5,3},{6,0},{7,1},{8,14},{9,15},{10,... | collective-permute-start | bytes 172040 | tf_op jit(solution)/shard_map/ppermute | solution.py:303
  50.8 4.2 %collective-permute-start.17 = (bf16[8,3584]{1,0:T(8,128)(2,1)S(1)}, bf16[8,3584]{1,0:T(8,128)(2,1)S(1)}, u32[]{:S(2)}, u32[]{:S(2)}) collective-permute-start(bf16[8,3584]{1,0:T(8,128)(2,1)S(1)} %add_convert_fusion.6.refs_8_), channel_id=1, source_target_pairs={{0,4},{1,5},{2,6},{3,7},{4,0},{5,1},{6,2},{7,3},{8,12},{9,13},{10,... | collective-permute-start | bytes 172040 | tf_op jit(solution)/shard_map/ppermute | solution.py:303
  51.1 4.7 %collective-permute-start.18 = (bf16[8,3584]{1,0:T(8,128)(2,1)S(1)}, bf16[8,3584]{1,0:T(8,128)(2,1)S(1)}, u32[]{:S(2)}, u32[]{:S(2)}) collective-permute-start(bf16[8,3584]{1,0:T(8,128)(2,1)S(1)} %add_convert_fusion.6.refs_8_), channel_id=1, source_target_pairs={{0,2},{1,3},{2,0},{3,1},{4,6},{5,7},{6,4},{7,5},{8,10},{9,11},{10,... | collective-permute-start | bytes 172040 | tf_op jit(solution)/shard_map/ppermute | solution.py:303
  52.8 3.0 %collective-permute-start.19 = (bf16[8,3584]{1,0:T(8,128)(2,1)S(1)}, bf16[8,3584]{1,0:T(8,128)(2,1)S(1)}, u32[]{:S(2)}, u32[]{:S(2)}) collective-permute-start(bf16[8,3584]{1,0:T(8,128)(2,1)S(1)} %add_convert_fusion.6.refs_8_), channel_id=1, source_target_pairs={{0,1},{1,0},{2,3},{3,2},{4,5},{5,4},{6,7},{7,6},{8,9},{9,8},{10,11... | collective-permute-start | bytes 172040 | tf_op jit(solution)/shard_map/ppermute | solution.py:303
  52.9 3.5 %collective-permute-start.13 = (bf16[8,3584]{1,0:T(8,128)(2,1)S(1)}, bf16[8,3584]{1,0:T(8,128)(2,1)S(1)}, u32[]{:S(2)}, u32[]{:S(2)}) collective-permute-start(bf16[8,3584]{1,0:T(8,128)(2,1)S(1)} %collective-permute-done.9.refs_1_), channel_id=1, source_target_pairs={{0,1},{1,0},{2,3},{3,2},{4,5},{5,4},{6,7},{7,6},{8,9},{9,8},{10,11... | collective-permute-start | bytes 172040 | tf_op jit(solution)/shard_map/ppermute | solution.py:303
  60.2 2.5 %collective-permute-start.25 = (bf16[8,7168]{1,0:T(8,128)(2,1)S(1)}, bf16[8,7168]{1,0:T(8,128)(2,1)S(1)}, u32[]{:S(2)}, u32[]{:S(2)}) collective-permute-start(bf16[8,7168]{1,0:T(8,128)(2,1)S(1)} %get-tuple-element.33), channel_id=1, source_target_pairs={{0,1},{1,0},{2,3},{3,2},{4,5},{5,4},{6,7},{7,6},{8,9},{9,8},{10,11... | collective-permute-start | bytes 344072 | tf_op jit(solution)/shard_map/ppermute | solution.py:303
  60.5 3.7 %collective-permute-start.27 = (bf16[8,7168]{1,0:T(8,128)(2,1)S(1)}, bf16[8,7168]{1,0:T(8,128)(2,1)S(1)}, u32[]{:S(2)}, u32[]{:S(2)}) collective-permute-start(bf16[8,7168]{1,0:T(8,128)(2,1)S(1)} %get-tuple-element.35), channel_id=1, source_target_pairs={{0,1},{1,0},{2,3},{3,2},{4,5},{5,4},{6,7},{7,6},{8,9},{9,8},{10,11... | collective-permute-start | bytes 344072 | tf_op jit(solution)/shard_map/ppermute | solution.py:303
  60.7 4.6 %collective-permute-start.29 = (bf16[8,7168]{1,0:T(8,128)(2,1)S(1)}, bf16[8,7168]{1,0:T(8,128)(2,1)S(1)}, u32[]{:S(2)}, u32[]{:S(2)}) collective-permute-start(bf16[8,7168]{1,0:T(8,128)(2,1)S(1)} %get-tuple-element.37), channel_id=1, source_target_pairs={{0,1},{1,0},{2,3},{3,2},{4,5},{5,4},{6,7},{7,6},{8,9},{9,8},{10,11... | collective-permute-start | bytes 344072 | tf_op jit(solution)/shard_map/ppermute | solution.py:303
  61.4 7.0 %collective-permute-start.24 = (bf16[8,7168]{1,0:T(8,128)(2,1)S(1)}, bf16[8,7168]{1,0:T(8,128)(2,1)S(1)}, u32[]{:S(2)}, u32[]{:S(2)}) collective-permute-start(bf16[8,7168]{1,0:T(8,128)(2,1)S(1)} %add_convert_fusion.2), channel_id=1, source_target_pairs={{0,6},{1,7},{2,4},{3,5},{4,2},{5,3},{6,0},{7,1},{8,14},{9,15},{10,... | collective-permute-start | bytes 344072 | tf_op jit(solution)/shard_map/ppermute | solution.py:303
  62.7 7.1 %collective-permute-start.26 = (bf16[8,7168]{1,0:T(8,128)(2,1)S(1)}, bf16[8,7168]{1,0:T(8,128)(2,1)S(1)}, u32[]{:S(2)}, u32[]{:S(2)}) collective-permute-start(bf16[8,7168]{1,0:T(8,128)(2,1)S(1)} %add_convert_fusion.1), channel_id=1, source_target_pairs={{0,4},{1,5},{2,6},{3,7},{4,0},{5,1},{6,2},{7,3},{8,12},{9,13},{10,... | collective-permute-start | bytes 344072 | tf_op jit(solution)/shard_map/ppermute | solution.py:303
  64.3 5.7 %collective-permute-start.28 = (bf16[8,7168]{1,0:T(8,128)(2,1)S(1)}, bf16[8,7168]{1,0:T(8,128)(2,1)S(1)}, u32[]{:S(2)}, u32[]{:S(2)}) collective-permute-start(bf16[8,7168]{1,0:T(8,128)(2,1)S(1)} %add_convert_fusion), channel_id=1, source_target_pairs={{0,2},{1,3},{2,0},{3,1},{4,6},{5,7},{6,4},{7,5},{8,10},{9,11},{10,... | collective-permute-start | bytes 344072 | tf_op jit(solution)/shard_map/ppermute | solution.py:303
  70.1 5.9 %collective-permute-start.30 = (bf16[4,7168]{1,0:T(4,128)(2,1)S(1)}, bf16[4,7168]{1,0:T(4,128)(2,1)S(1)}, u32[]{:S(2)}, u32[]{:S(2)}) collective-permute-start(bf16[4,7168]{1,0:T(4,128)(2,1)S(1)} %slice.57), channel_id=1, source_target_pairs={{0,8},{1,9},{2,10},{3,11},{4,12},{5,13},{6,14},{7,15},{8,0},{9,1},... | collective-permute-start | bytes 172040 | tf_op jit(solution)/shard_map/ppermute | solution.py:303
  (17 other events, 248.8 us)

commit v12 on v10

--- a/solution.py
+++ b/solution.py
@@ -10,7 +10,6 @@
 QK = 192
 FF = 2048
 BLOCK = 512
-LOWEST = -3e38
 GROUP = 4
 LANES = 128
 TILE = 256
@@ -63,9 +62,6 @@
         block_copy(row, 0).start()
         item_row[row] = row
         item_block[row] = 0
-    highest[...] = jnp.full_like(highest, LOWEST)
-    sums[...] = jnp.zeros_like(sums)
-    summed[...] = jnp.zeros_like(summed)
     length_copy.wait()
     items = own_rows
     for row in range(own_rows):
@@ -82,12 +78,11 @@
     queries_copy.wait()
     column = lax.broadcasted_iota(jnp.int32, (heads, BLOCK), 1)
 
-    def visit(first, many):
-        inside = [(item_row[first + at], item_block[first + at]) for at in range(many)]
-        for row, block in inside:
-            block_copy(row, block).wait()
+    def visit(inside, new):
         found = []
         for row, block in inside:
+            if new:
+                block_copy(row, block).wait()
             score = jnp.dot(
                 queries[row], held[row, block], preferred_element_type=jnp.float32
             ) * QK ** (-0.5)
@@ -109,24 +104,38 @@
             for (row, block), weight in zip(inside, weights)
         ]
         for (row, _), top, weight, term in zip(inside, tops, weights, terms):
+            if new:
+                highest[row] = jnp.broadcast_to(top, (heads, LANES))
+                sums[row] = sum(lane_tiles(weight))
+                summed[row] = term
+                continue
             before = highest[row]
             after = jnp.maximum(before, top)
-            old, new = jnp.exp(before - after), jnp.exp(top - after)
+            ours, theirs = jnp.exp(before - after), jnp.exp(top - after)
             highest[row] = after
-            sums[row] = sums[row] * old + sum(lane_tiles(weight)) * new
+            sums[row] = sums[row] * ours + sum(lane_tiles(weight)) * theirs
             for at in range(0, rank, LANES):
                 summed[row, :, at : at + LANES] = (
-                    summed[row, :, at : at + LANES] * old + term[:, at : at + LANES] * new
+                    summed[row, :, at : at + LANES] * ours
+                    + term[:, at : at + LANES] * theirs
                 )
 
+    def visit_items(first, many):
+        inside = [(item_row[first + at], item_block[first + at]) for at in range(many)]
+        for row, block in inside:
+            block_copy(row, block).wait()
+        visit(inside, False)
+
     def visit_group(group, _):
-        visit(group * GROUP, GROUP)
+        visit_items(own_rows + group * GROUP, GROUP)
         return 0
 
-    whole = items // GROUP
+    visit([(row, 0) for row in range(own_rows)], True)
+    rest = items - own_rows
+    whole = rest // GROUP
     lax.fori_loop(0, whole, visit_group, 0)
-    pl.when((items & 2) != 0)(lambda: visit(whole * GROUP, 2))
-    pl.when((items & 1) != 0)(lambda: visit(items - 1, 1))
+    pl.when((rest & 2) != 0)(lambda: visit_items(own_rows + whole * GROUP, 2))
+    pl.when((rest & 1) != 0)(lambda: visit_items(items - 1, 1))
     for row in range(own_rows):
         latent = summed[row] * (1.0 / jnp.sum(sums[row], axis=1, keepdims=True))
         for device in range(devices):
@@ -196,15 +205,23 @@
     far_at, slot = slot & (far - 1), slot >> far_bits
     distance = (far_at << 3) + ((4 - (slot & 3) & 3) << 1) + (slot >> 2)
     device = distance ^ lax.axis_index("experts")
-    values = []
+    choices = []
     for head in range(own_heads):
         wanted = ((device << turn) + request) * own_heads + head
-        choice = (place == wanted).astype(jnp.float32).astype(jnp.bfloat16)
-        latent = jnp.dot(choice, joined_ref[...], preferred_element_type=jnp.float32)
-        value = jnp.dot(
-            latent.astype(jnp.bfloat16), absorb_ref[head], preferred_element_type=jnp.float32
-        )
-        values.append(value.astype(jnp.bfloat16))
+        choices.append((place == wanted).astype(jnp.float32))
+    latents = jnp.dot(
+        jnp.concatenate(choices, axis=0).astype(jnp.bfloat16),
+        joined_ref[...],
+        preferred_element_type=jnp.float32,
+    ).astype(jnp.bfloat16)
+    values = [
+        jnp.dot(
+            latents[head * shape[0] : (head + 1) * shape[0]],
+            absorb_ref[head],
+            preferred_element_type=jnp.float32,
+        ).astype(jnp.bfloat16)
+        for head in range(own_heads)
+    ]
     values = jnp.concatenate(values, axis=1)
     for at in range(0, width, TILE):
         term = jnp.dot(values, w_ref[:, at : at + TILE], preferred_element_type=jnp.float32)

time: 74.7 us -> 74.3 us (level); the launches traced: 75.3 us -> 74.1 us
  Pallas kernels: 13 us -> 9.71 us
  blocking collectives: 16.8 us -> 18.9 us
    pallas_call x1, Pallas kernels: 8.58 us -> 5.68 us  [attend(): pl.pallas_call(attend_kernel, out_shape=jax.ShapeDtypeStruct((devices, pa...]
    all_to_all x1, blocking collectives: 16.8 us -> 18.9 us  [shards(): lax.all_to_all(latent, 'experts', split_axis=0, concat_axis=0, tiled=True)]
where the time goes in v12:
time: 74.3 us; the launch traced here: 74.1 us
  waiting for transfers between devices  27.8 us (37%)
  blocking collectives  18.9 us (25%)
  starting transfers between devices  14.8 us (20%)
  Pallas kernels  9.71 us (13%)
  other arithmetic  1.27 us (2%)
  between operations  0.87 us (1%)
  local copies, waits for them, and re-layouts  0.76 us (1%)
    ppermute x23, waiting for transfers between devices, swap(): return lax.ppermute(array, 'experts', pairs)  27.8 us
    all_to_all x1, blocking collectives, shards(): lax.all_to_all(latent, 'experts', split_axis=0, concat_axis=0, tiled=True)  18.9 us
    ppermute x23, starting transfers between devices, swap(): return lax.ppermute(array, 'experts', pairs)  14.8 us
    pallas_call x1, Pallas kernels, attend(): pl.pallas_call(attend_kernel, out_shape=jax.ShapeDtypeStruct((devices, pa...  5.68 us
    pallas_call x1, Pallas kernels, run_expert(): pl.pallas_call(expert_kernel, out_shape=term_shapes(rows, width), in_spec...  2.34 us
    pallas_call x1, Pallas kernels, project(): pl.pallas_call(functools.partial(project_kernel, own_rows, far), out_shap...  1.69 us
  transfers between devices with their start and end apart: 23, of which 13 were waited for; matrix products, arithmetic and copies ran while one was open for 1% of the time, Pallas kernels for 0%

profile of v12, /device:TPU:0, one launch (start us, length us, event | category | flops | bytes accessed | tf_op | source)
XLA Modules:
  0.0 74.1 jit_solution(11866343823832110767)
XLA Ops:
  0.7 5.7 %attend.1 = bf16[16,16,512]{2,1,0:T(8,128)(2,1)} custom-call(s32[4]{0:T(128)} %len_ref.1, bf16[4,64,576]{2,1,0:T(8,128)(2,1)} %bitcast.7, bf16[4,576,4096]{2,1,0:T(8,128)(2,1)} %cache_ref.1), custom_call_target="tpu_custom_call" | custom-call | flops 1140850688 | bytes 9437184 | tf_op jit(solution)/shard_map/attend/pallas_call | solution.py:153
  6.4 18.9 %all_to_all.5 = bf16[16,16,512]{2,1,0:T(8,128)(2,1)S(1)} all-to-all(bf16[16,16,512]{2,1,0:T(8,128)(2,1)} %attend.1), channel_id=1, replica_groups=mesh['groups'=2,'experts'=16] {'experts'}, dimensions={0} | all-to-all | bytes 524288 | tf_op jit(solution)/shard_map/all_to_all | solution.py:362
  25.4 1.7 %project.1 = (f32[8,7168]{1,0:T(8,128)S(1)}, f32[8,7168]{1,0:T(8,128)S(1)}, f32[8,7168]{1,0:T(8,128)S(1)}, f32[8,7168]{1,0:T(8,128)S(1)}, bf16[8,7168]{1,0:T(8,1...) custom-call(bf16[256,512]{1,0:T(8,128)(2,1)S(1)} %bitcast.5, ...), custom_call_target="tpu_custom_call" | custom-call | flops 469762048 | bytes 7340032 | tf_op jit(solution)/shard_map/project/pallas_call | solution.py:236
  28.5 0.7 collective-permute-start.1
  29.2 1.1 %collective-permute-start.3 = (bf16[8,7168]{1,0:T(8,128)(2,1)S(1)}, bf16[8,7168]{1,0:T(8,128)(2,1)S(1)}, u32[]{:S(2)}, u32[]{:S(2)}) collective-permute-start(bf16[8,7168]{1,0:T(8,128)(2,1)S(1)} %add_convert_fusion.5), channel_id=1, source_target_pairs={{0,4},{1,5},{2,6},{3,7},{4,0},{5,1},{6,2},{7,3},{8,12},{9,13},{10,... | collective-permute-start | bytes 344072 | tf_op jit(solution)/shard_map/ppermute | solution.py:303
  30.3 1.9 %collective-permute-start.5 = (bf16[8,7168]{1,0:T(8,128)(2,1)S(1)}, bf16[8,7168]{1,0:T(8,128)(2,1)S(1)}, u32[]{:S(2)}, u32[]{:S(2)}) collective-permute-start(bf16[8,7168]{1,0:T(8,128)(2,1)S(1)} %add_convert_fusion.4), channel_id=1, source_target_pairs={{0,2},{1,3},{2,0},{3,1},{4,6},{5,7},{6,4},{7,5},{8,10},{9,11},{10,... | collective-permute-start | bytes 344072 | tf_op jit(solution)/shard_map/ppermute | solution.py:303
  32.3 3.2 %collective-permute-done.1 = bf16[8,7168]{1,0:T(8,128)(2,1)S(1)} collective-permute-done((bf16[8,7168]{1,0:T(8,128)(2,1)S(1)}, bf16[8,7168]{1,0:T(8,128)(2,1)S(1)}, u32[]{:S(2)}, u32[]{:S(2)}) %collective-permute-start.1) | collective-permute-done | bytes 114720 | tf_op jit(solution)/shard_map/ppermute | solution.py:303
  35.5 0.6 collective-permute-done.3
  36.0 1.1 %collective-permute-done.5 = bf16[8,7168]{1,0:T(8,128)(2,1)S(1)} collective-permute-done((bf16[8,7168]{1,0:T(8,128)(2,1)S(1)}, bf16[8,7168]{1,0:T(8,128)(2,1)S(1)}, u32[]{:S(2)}, u32[]{:S(2)}) %collective-permute-start.5) | collective-permute-done | bytes 114720 | tf_op jit(solution)/shard_map/ppermute | solution.py:303
  37.2 1.1 %collective-permute-start.7 = (bf16[8,7168]{1,0:T(8,128)(2,1)S(1)}, bf16[8,7168]{1,0:T(8,128)(2,1)S(1)}, u32[]{:S(2)}, u32[]{:S(2)}) collective-permute-start(bf16[8,7168]{1,0:T(8,128)(2,1)S(1)} %fusion.4), channel_id=1, source_target_pairs={{0,8},{1,9},{2,10},{3,11},{4,12},{5,13},{6,14},{7,15},{8,0},{9,1},... | collective-permute-start | bytes 344072 | tf_op jit(solution)/shard_map/ppermute | solution.py:303
  38.3 7.3 %collective-permute-done.7 = bf16[8,7168]{1,0:T(8,128)(2,1)S(1)} collective-permute-done((bf16[8,7168]{1,0:T(8,128)(2,1)S(1)}, bf16[8,7168]{1,0:T(8,128)(2,1)S(1)}, u32[]{:S(2)}, u32[]{:S(2)}) %collective-permute-start.7) | collective-permute-done | bytes 114720 | tf_op jit(solution)/shard_map/ppermute | solution.py:303
  45.9 1.4 %collective-permute-start.9 = (bf16[8,7168]{1,0:T(8,128)(2,1)S(1)}, bf16[8,7168]{1,0:T(8,128)(2,1)S(1)}, u32[]{:S(2)}, u32[]{:S(2)}) collective-permute-start(bf16[8,7168]{1,0:T(8,128)(2,1)S(1)} %add_convert_fusion.3.refs_0_), channel_id=1, source_target_pairs={{0,4},{1,5},{2,6},{3,7},{4,0},{5,1},{6,2},{7,3},{8,12},{9,13},{10,... | collective-permute-start | bytes 344072 | tf_op jit(solution)/shard_map/ppermute | solution.py:303
  47.3 2.1 %collective-permute-start.10 = (bf16[8,7168]{1,0:T(8,128)(2,1)S(1)}, bf16[8,7168]{1,0:T(8,128)(2,1)S(1)}, u32[]{:S(2)}, u32[]{:S(2)}) collective-permute-start(bf16[8,7168]{1,0:T(8,128)(2,1)S(1)} %add_convert_fusion.3.refs_0_), channel_id=1, source_target_pairs={{0,2},{1,3},{2,0},{3,1},{4,6},{5,7},{6,4},{7,5},{8,10},{9,11},{10,... | collective-permute-start | bytes 344072 | tf_op jit(solution)/shard_map/ppermute | solution.py:303
  49.4 3.4 %collective-permute-done.8.refs_1_ = bf16[8,7168]{1,0:T(8,128)(2,1)S(1)} collective-permute-done((bf16[8,7168]{1,0:T(8,128)(2,1)S(1)}, bf16[8,7168]{1,0:T(8,128)(2,1)S(1)}, u32[]{:S(2)}, u32[]{:S(2)}) %collective-permute-start.8) | collective-permute-done | bytes 114720 | tf_op jit(solution)/shard_map/ppermute | solution.py:303
  53.3 1.0 %collective-permute-done.10.refs_3_ = bf16[8,7168]{1,0:T(8,128)(2,1)S(1)} collective-permute-done((bf16[8,7168]{1,0:T(8,128)(2,1)S(1)}, bf16[8,7168]{1,0:T(8,128)(2,1)S(1)}, u32[]{:S(2)}, u32[]{:S(2)}) %collective-permute-start.10) | collective-permute-done | bytes 114720 | tf_op jit(solution)/shard_map/ppermute | solution.py:303
  54.3 1.3 %collective-permute-done.14.refs_7_ = bf16[8,7168]{1,0:T(8,128)(2,1)S(1)} collective-permute-done((bf16[8,7168]{1,0:T(8,128)(2,1)S(1)}, bf16[8,7168]{1,0:T(8,128)(2,1)S(1)}, u32[]{:S(2)}, u32[]{:S(2)}) %collective-permute-start.14) | collective-permute-done | bytes 114720 | tf_op jit(solution)/shard_map/ppermute | solution.py:303
  55.7 2.3 %expert.1 = (f32[8,7168]{1,0:T(8,128)S(1)}, f32[8,7168]{1,0:T(8,128)S(1)}, f32[8,7168]{1,0:T(8,128)S(1)}, f32[8,7168]{1,0:T(8,128)S(1)}, bf16[8,7168]{1,0:T(8,12...) custom-call(bf16[8,7168]{1,0:T(8,128)(2,1)S(1)} %add_convert_fusion.3.refs_0_, ...), custom_call_target="tpu_custom_call" | custom-call | flops 704643072 | bytes 11010048 | tf_op jit(solution)/shard_map/expert/pallas_call | solution.py:286
  59.8 2.0 %collective-permute-start.18 = (bf16[8,7168]{1,0:T(8,128)(2,1)S(1)}, bf16[8,7168]{1,0:T(8,128)(2,1)S(1)}, u32[]{:S(2)}, u32[]{:S(2)}) collective-permute-start(bf16[8,7168]{1,0:T(8,128)(2,1)S(1)} %add_convert_fusion.1), channel_id=1, source_target_pairs={{0,4},{1,5},{2,6},{3,7},{4,0},{5,1},{6,2},{7,3},{8,12},{9,13},{10,... | collective-permute-start | bytes 344072 | tf_op jit(solution)/shard_map/ppermute | solution.py:303
  61.8 1.4 %collective-permute-start.20 = (bf16[8,7168]{1,0:T(8,128)(2,1)S(1)}, bf16[8,7168]{1,0:T(8,128)(2,1)S(1)}, u32[]{:S(2)}, u32[]{:S(2)}) collective-permute-start(bf16[8,7168]{1,0:T(8,128)(2,1)S(1)} %add_convert_fusion), channel_id=1, source_target_pairs={{0,2},{1,3},{2,0},{3,1},{4,6},{5,7},{6,4},{7,5},{8,10},{9,11},{10,... | collective-permute-start | bytes 344072 | tf_op jit(solution)/shard_map/ppermute | solution.py:303
  63.2 3.2 %collective-permute-done.16 = bf16[8,7168]{1,0:T(8,128)(2,1)S(1)} collective-permute-done((bf16[8,7168]{1,0:T(8,128)(2,1)S(1)}, bf16[8,7168]{1,0:T(8,128)(2,1)S(1)}, u32[]{:S(2)}, u32[]{:S(2)}) %collective-permute-start.16) | collective-permute-done | bytes 114720 | tf_op jit(solution)/shard_map/ppermute | solution.py:303
  66.4 1.1 %collective-permute-done.18 = bf16[8,7168]{1,0:T(8,128)(2,1)S(1)} collective-permute-done((bf16[8,7168]{1,0:T(8,128)(2,1)S(1)}, bf16[8,7168]{1,0:T(8,128)(2,1)S(1)}, u32[]{:S(2)}, u32[]{:S(2)}) %collective-permute-start.18) | collective-permute-done | bytes 114720 | tf_op jit(solution)/shard_map/ppermute | solution.py:303
  68.4 0.6 slice.23
  69.0 4.4 %collective-permute-done.22 = bf16[4,7168]{1,0:T(4,128)(2,1)S(1)} collective-permute-done((bf16[4,7168]{1,0:T(4,128)(2,1)S(1)}, bf16[4,7168]{1,0:T(4,128)(2,1)S(1)}, u32[]{:S(2)}, u32[]{:S(2)}) %collective-permute-start.22) | collective-permute-done | bytes 57376 | tf_op jit(solution)/shard_map/ppermute | solution.py:303
  73.4 0.7 fusion.1
  (61 shorter events, 5.0 us)
Async XLA Ops:
  25.3 30.3 %copy-start = (bf16[7168,256]{1,0:T(8,128)(2,1)S(1)}, bf16[7168,256]{1,0:T(8,128)(2,1)}, u32[]{:S(2)}) copy-start(bf16[7168,256]{1,0:T(8,128)(2,1)} %refs_9_.1) | copy-start | bytes 11010052
  27.1 1.4 %collective-permute-start = (bf16[8,7168]{1,0:T(8,128)(2,1)S(1)}, bf16[8,7168]{1,0:T(8,128)(2,1)S(1)}, u32[]{:S(2)}, u32[]{:S(2)}) collective-permute-start(bf16[8,7168]{1,0:T(8,128)(2,1)S(1)} %get-tuple-element.19), channel_id=1, source_target_pairs={{0,1},{1,0},{2,3},{3,2},{4,5},{5,4},{6,7},{7,6},{8,9},{9,8},{10,11... | collective-permute-start | bytes 344072 | tf_op jit(solution)/shard_map/ppermute | solution.py:303
  27.1 2.0 %collective-permute-start.2 = (bf16[8,7168]{1,0:T(8,128)(2,1)S(1)}, bf16[8,7168]{1,0:T(8,128)(2,1)S(1)}, u32[]{:S(2)}, u32[]{:S(2)}) collective-permute-start(bf16[8,7168]{1,0:T(8,128)(2,1)S(1)} %get-tuple-element.21), channel_id=1, source_target_pairs={{0,1},{1,0},{2,3},{3,2},{4,5},{5,4},{6,7},{7,6},{8,9},{9,8},{10,11... | collective-permute-start | bytes 344072 | tf_op jit(solution)/shard_map/ppermute | solution.py:303
  27.6 2.7 %collective-permute-start.4 = (bf16[8,7168]{1,0:T(8,128)(2,1)S(1)}, bf16[8,7168]{1,0:T(8,128)(2,1)S(1)}, u32[]{:S(2)}, u32[]{:S(2)}) collective-permute-start(bf16[8,7168]{1,0:T(8,128)(2,1)S(1)} %get-tuple-element.23), channel_id=1, source_target_pairs={{0,1},{1,0},{2,3},{3,2},{4,5},{5,4},{6,7},{7,6},{8,9},{9,8},{10,11... | collective-permute-start | bytes 344072 | tf_op jit(solution)/shard_map/ppermute | solution.py:303
  27.7 4.5 %collective-permute-start.6 = (bf16[8,7168]{1,0:T(8,128)(2,1)S(1)}, bf16[8,7168]{1,0:T(8,128)(2,1)S(1)}, u32[]{:S(2)}, u32[]{:S(2)}) collective-permute-start(bf16[8,7168]{1,0:T(8,128)(2,1)S(1)} %get-tuple-element.25), channel_id=1, source_target_pairs={{0,1},{1,0},{2,3},{3,2},{4,5},{5,4},{6,7},{7,6},{8,9},{9,8},{10,11... | collective-permute-start | bytes 344072 | tf_op jit(solution)/shard_map/ppermute | solution.py:303
  28.5 7.0 %collective-permute-start.1 = (bf16[8,7168]{1,0:T(8,128)(2,1)S(1)}, bf16[8,7168]{1,0:T(8,128)(2,1)S(1)}, u32[]{:S(2)}, u32[]{:S(2)}) collective-permute-start(bf16[8,7168]{1,0:T(8,128)(2,1)S(1)} %add_convert_fusion.6), channel_id=1, source_target_pairs={{0,6},{1,7},{2,4},{3,5},{4,2},{5,3},{6,0},{7,1},{8,14},{9,15},{10,... | collective-permute-start | bytes 344072 | tf_op jit(solution)/shard_map/ppermute | solution.py:303
  29.2 6.9 %collective-permute-start.3 = (bf16[8,7168]{1,0:T(8,128)(2,1)S(1)}, bf16[8,7168]{1,0:T(8,128)(2,1)S(1)}, u32[]{:S(2)}, u32[]{:S(2)}) collective-permute-start(bf16[8,7168]{1,0:T(8,128)(2,1)S(1)} %add_convert_fusion.5), channel_id=1, source_target_pairs={{0,4},{1,5},{2,6},{3,7},{4,0},{5,1},{6,2},{7,3},{8,12},{9,13},{10,... | collective-permute-start | bytes 344072 | tf_op jit(solution)/shard_map/ppermute | solution.py:303
  30.3 6.8 %collective-permute-start.5 = (bf16[8,7168]{1,0:T(8,128)(2,1)S(1)}, bf16[8,7168]{1,0:T(8,128)(2,1)S(1)}, u32[]{:S(2)}, u32[]{:S(2)}) collective-permute-start(bf16[8,7168]{1,0:T(8,128)(2,1)S(1)} %add_convert_fusion.4), channel_id=1, source_target_pairs={{0,2},{1,3},{2,0},{3,1},{4,6},{5,7},{6,4},{7,5},{8,10},{9,11},{10,... | collective-permute-start | bytes 344072 | tf_op jit(solution)/shard_map/ppermute | solution.py:303
  37.2 8.4 %collective-permute-start.7 = (bf16[8,7168]{1,0:T(8,128)(2,1)S(1)}, bf16[8,7168]{1,0:T(8,128)(2,1)S(1)}, u32[]{:S(2)}, u32[]{:S(2)}) collective-permute-start(bf16[8,7168]{1,0:T(8,128)(2,1)S(1)} %fusion.4), channel_id=1, source_target_pairs={{0,8},{1,9},{2,10},{3,11},{4,12},{5,13},{6,14},{7,15},{8,0},{9,1},... | collective-permute-start | bytes 344072 | tf_op jit(solution)/shard_map/ppermute | solution.py:303
  45.8 7.0 %collective-permute-start.8 = (bf16[8,7168]{1,0:T(8,128)(2,1)S(1)}, bf16[8,7168]{1,0:T(8,128)(2,1)S(1)}, u32[]{:S(2)}, u32[]{:S(2)}) collective-permute-start(bf16[8,7168]{1,0:T(8,128)(2,1)S(1)} %add_convert_fusion.3.refs_0_), channel_id=1, source_target_pairs={{0,6},{1,7},{2,4},{3,5},{4,2},{5,3},{6,0},{7,1},{8,14},{9,15},{10,... | collective-permute-start | bytes 344072 | tf_op jit(solution)/shard_map/ppermute | solution.py:303
  45.9 6.9 %collective-permute-start.9 = (bf16[8,7168]{1,0:T(8,128)(2,1)S(1)}, bf16[8,7168]{1,0:T(8,128)(2,1)S(1)}, u32[]{:S(2)}, u32[]{:S(2)}) collective-permute-start(bf16[8,7168]{1,0:T(8,128)(2,1)S(1)} %add_convert_fusion.3.refs_0_), channel_id=1, source_target_pairs={{0,4},{1,5},{2,6},{3,7},{4,0},{5,1},{6,2},{7,3},{8,12},{9,13},{10,... | collective-permute-start | bytes 344072 | tf_op jit(solution)/shard_map/ppermute | solution.py:303
  47.3 7.0 %collective-permute-start.10 = (bf16[8,7168]{1,0:T(8,128)(2,1)S(1)}, bf16[8,7168]{1,0:T(8,128)(2,1)S(1)}, u32[]{:S(2)}, u32[]{:S(2)}) collective-permute-start(bf16[8,7168]{1,0:T(8,128)(2,1)S(1)} %add_convert_fusion.3.refs_0_), channel_id=1, source_target_pairs={{0,2},{1,3},{2,0},{3,1},{4,6},{5,7},{6,4},{7,5},{8,10},{9,11},{10,... | collective-permute-start | bytes 344072 | tf_op jit(solution)/shard_map/ppermute | solution.py:303
  49.4 5.0 %collective-permute-start.11 = (bf16[8,7168]{1,0:T(8,128)(2,1)S(1)}, bf16[8,7168]{1,0:T(8,128)(2,1)S(1)}, u32[]{:S(2)}, u32[]{:S(2)}) collective-permute-start(bf16[8,7168]{1,0:T(8,128)(2,1)S(1)} %add_convert_fusion.3.refs_0_), channel_id=1, source_target_pairs={{0,1},{1,0},{2,3},{3,2},{4,5},{5,4},{6,7},{7,6},{8,9},{9,8},{10,11... | collective-permute-start | bytes 344072 | tf_op jit(solution)/shard_map/ppermute | solution.py:303
  52.8 1.5 %collective-permute-start.12 = (bf16[8,7168]{1,0:T(8,128)(2,1)S(1)}, bf16[8,7168]{1,0:T(8,128)(2,1)S(1)}, u32[]{:S(2)}, u32[]{:S(2)}) collective-permute-start(bf16[8,7168]{1,0:T(8,128)(2,1)S(1)} %collective-permute-done.8.refs_1_), channel_id=1, source_target_pairs={{0,1},{1,0},{2,3},{3,2},{4,5},{5,4},{6,7},{7,6},{8,9},{9,8},{10,11... | collective-permute-start | bytes 344072 | tf_op jit(solution)/shard_map/ppermute | solution.py:303
  52.8 1.5 %collective-permute-start.13 = (bf16[8,7168]{1,0:T(8,128)(2,1)S(1)}, bf16[8,7168]{1,0:T(8,128)(2,1)S(1)}, u32[]{:S(2)}, u32[]{:S(2)}) collective-permute-start(bf16[8,7168]{1,0:T(8,128)(2,1)S(1)} %collective-permute-done.9.refs_2_), channel_id=1, source_target_pairs={{0,1},{1,0},{2,3},{3,2},{4,5},{5,4},{6,7},{7,6},{8,9},{9,8},{10,11... | collective-permute-start | bytes 344072 | tf_op jit(solution)/shard_map/ppermute | solution.py:303
  54.3 1.3 %collective-permute-start.14 = (bf16[8,7168]{1,0:T(8,128)(2,1)S(1)}, bf16[8,7168]{1,0:T(8,128)(2,1)S(1)}, u32[]{:S(2)}, u32[]{:S(2)}) collective-permute-start(bf16[8,7168]{1,0:T(8,128)(2,1)S(1)} %collective-permute-done.10.refs_3_), channel_id=1, source_target_pairs={{0,1},{1,0},{2,3},{3,2},{4,5},{5,4},{6,7},{7,6},{8,9},{9,8},{10,11... | collective-permute-start | bytes 344072 | tf_op jit(solution)/shard_map/ppermute | solution.py:303
  58.0 1.4 %collective-permute-start.15 = (bf16[8,7168]{1,0:T(8,128)(2,1)S(1)}, bf16[8,7168]{1,0:T(8,128)(2,1)S(1)}, u32[]{:S(2)}, u32[]{:S(2)}) collective-permute-start(bf16[8,7168]{1,0:T(8,128)(2,1)S(1)} %get-tuple-element.27), channel_id=1, source_target_pairs={{0,1},{1,0},{2,3},{3,2},{4,5},{5,4},{6,7},{7,6},{8,9},{9,8},{10,11... | collective-permute-start | bytes 344072 | tf_op jit(solution)/shard_map/ppermute | solution.py:303
  58.2 1.6 %collective-permute-start.17 = (bf16[8,7168]{1,0:T(8,128)(2,1)S(1)}, bf16[8,7168]{1,0:T(8,128)(2,1)S(1)}, u32[]{:S(2)}, u32[]{:S(2)}) collective-permute-start(bf16[8,7168]{1,0:T(8,128)(2,1)S(1)} %get-tuple-element.29), channel_id=1, source_target_pairs={{0,1},{1,0},{2,3},{3,2},{4,5},{5,4},{6,7},{7,6},{8,9},{9,8},{10,11... | collective-permute-start | bytes 344072 | tf_op jit(solution)/shard_map/ppermute | solution.py:303
  58.6 3.2 %collective-permute-start.19 = (bf16[8,7168]{1,0:T(8,128)(2,1)S(1)}, bf16[8,7168]{1,0:T(8,128)(2,1)S(1)}, u32[]{:S(2)}, u32[]{:S(2)}) collective-permute-start(bf16[8,7168]{1,0:T(8,128)(2,1)S(1)} %get-tuple-element.31), channel_id=1, source_target_pairs={{0,1},{1,0},{2,3},{3,2},{4,5},{5,4},{6,7},{7,6},{8,9},{9,8},{10,11... | collective-permute-start | bytes 344072 | tf_op jit(solution)/shard_map/ppermute | solution.py:303
  58.8 4.4 %collective-permute-start.21 = (bf16[8,7168]{1,0:T(8,128)(2,1)S(1)}, bf16[8,7168]{1,0:T(8,128)(2,1)S(1)}, u32[]{:S(2)}, u32[]{:S(2)}) collective-permute-start(bf16[8,7168]{1,0:T(8,128)(2,1)S(1)} %get-tuple-element.33), channel_id=1, source_target_pairs={{0,1},{1,0},{2,3},{3,2},{4,5},{5,4},{6,7},{7,6},{8,9},{9,8},{10,11... | collective-permute-start | bytes 344072 | tf_op jit(solution)/shard_map/ppermute | solution.py:303
  59.5 7.0 %collective-permute-start.16 = (bf16[8,7168]{1,0:T(8,128)(2,1)S(1)}, bf16[8,7168]{1,0:T(8,128)(2,1)S(1)}, u32[]{:S(2)}, u32[]{:S(2)}) collective-permute-start(bf16[8,7168]{1,0:T(8,128)(2,1)S(1)} %add_convert_fusion.2), channel_id=1, source_target_pairs={{0,6},{1,7},{2,4},{3,5},{4,2},{5,3},{6,0},{7,1},{8,14},{9,15},{10,... | collective-permute-start | bytes 344072 | tf_op jit(solution)/shard_map/ppermute | solution.py:303
  59.8 7.7 %collective-permute-start.18 = (bf16[8,7168]{1,0:T(8,128)(2,1)S(1)}, bf16[8,7168]{1,0:T(8,128)(2,1)S(1)}, u32[]{:S(2)}, u32[]{:S(2)}) collective-permute-start(bf16[8,7168]{1,0:T(8,128)(2,1)S(1)} %add_convert_fusion.1), channel_id=1, source_target_pairs={{0,4},{1,5},{2,6},{3,7},{4,0},{5,1},{6,2},{7,3},{8,12},{9,13},{10,... | collective-permute-start | bytes 344072 | tf_op jit(solution)/shard_map/ppermute | solution.py:303
  61.8 6.2 %collective-permute-start.20 = (bf16[8,7168]{1,0:T(8,128)(2,1)S(1)}, bf16[8,7168]{1,0:T(8,128)(2,1)S(1)}, u32[]{:S(2)}, u32[]{:S(2)}) collective-permute-start(bf16[8,7168]{1,0:T(8,128)(2,1)S(1)} %add_convert_fusion), channel_id=1, source_target_pairs={{0,2},{1,3},{2,0},{3,1},{4,6},{5,7},{6,4},{7,5},{8,10},{9,11},{10,... | collective-permute-start | bytes 344072 | tf_op jit(solution)/shard_map/ppermute | solution.py:303
  68.2 5.2 %collective-permute-start.22 = (bf16[4,7168]{1,0:T(4,128)(2,1)S(1)}, bf16[4,7168]{1,0:T(4,128)(2,1)S(1)}, u32[]{:S(2)}, u32[]{:S(2)}) collective-permute-start(bf16[4,7168]{1,0:T(4,128)(2,1)S(1)} %slice.32), channel_id=1, source_target_pairs={{0,8},{1,9},{2,10},{3,11},{4,12},{5,13},{6,14},{7,15},{8,0},{9,1},... | collective-permute-start | bytes 172040 | tf_op jit(solution)/shard_map/ppermute | solution.py:303
  (9 other events, 214.7 us)

commit v13 on v10

--- a/solution.py
+++ b/solution.py
@@ -15,7 +15,7 @@
 LANES = 128
 TILE = 256
 PARTS = 4
-SQUARE = (0, 6, 4, 2)
+SQUARE = (6, 4, 2, 0)
 PIECES = len(SQUARE)
 MIB = 2**20
 
@@ -171,46 +171,55 @@
 
 
 def store_term(term, at, refs):
-    rows = term.shape[0] // len(refs)
-    for piece, ref in enumerate(refs):
-        ref[:, at : at + TILE] = term[piece * rows : (piece + 1) * rows].astype(ref.dtype)
+    first = 0
+    for ref in refs:
+        rows = ref.shape[0]
+        ref[:, at : at + TILE] = term[first : first + rows].astype(ref.dtype)
+        first += rows
 
 
 def term_shapes(rows, width):
-    return tuple(
-        jax.ShapeDtypeStruct((rows, width), kind)
-        for kind in (jnp.float32, jnp.bfloat16)
-        for _ in range(PIECES)
-    )
+    kept = [jax.ShapeDtypeStruct((rows, width), jnp.float32)] * PIECES
+    sent = [jax.ShapeDtypeStruct((many * rows, width), jnp.bfloat16) for many in (1, PIECES - 1)]
+    return kept + sent
 
 
 def project_kernel(own_rows, far, joined_ref, residual_ref, absorb_ref, w_ref, *pieces):
     own_heads = absorb_ref.shape[0]
     width = w_ref.shape[1]
-    shape = (len(pieces) * pieces[0].shape[0], joined_ref.shape[0])
+    shape = (2 * PIECES * pieces[0].shape[0], joined_ref.shape[0])
     row = lax.broadcasted_iota(jnp.int32, shape, 0)
     place = lax.broadcasted_iota(jnp.int32, shape, 1)
     turn = own_rows.bit_length() - 1
     far_bits = far.bit_length() - 1
     request, slot = row & (own_rows - 1), row >> turn
     far_at, slot = slot & (far - 1), slot >> far_bits
-    distance = (far_at << 3) + ((4 - (slot & 3) & 3) << 1) + (slot >> 2)
+    distance = (far_at << 3) + ((3 - (slot & 3)) << 1) + (slot >> 2)
     device = distance ^ lax.axis_index("experts")
-    values = []
+    choices = []
     for head in range(own_heads):
         wanted = ((device << turn) + request) * own_heads + head
-        choice = (place == wanted).astype(jnp.float32).astype(jnp.bfloat16)
-        latent = jnp.dot(choice, joined_ref[...], preferred_element_type=jnp.float32)
-        value = jnp.dot(
-            latent.astype(jnp.bfloat16), absorb_ref[head], preferred_element_type=jnp.float32
-        )
-        values.append(value.astype(jnp.bfloat16))
+        choices.append((place == wanted).astype(jnp.float32))
+    latents = jnp.dot(
+        jnp.concatenate(choices, axis=0).astype(jnp.bfloat16),
+        joined_ref[...],
+        preferred_element_type=jnp.float32,
+    ).astype(jnp.bfloat16)
+    values = [
+        jnp.dot(
+            latents[head * shape[0] : (head + 1) * shape[0]],
+            absorb_ref[head],
+            preferred_element_type=jnp.float32,
+        ).astype(jnp.bfloat16)
+        for head in range(own_heads)
+    ]
     values = jnp.concatenate(values, axis=1)
     for at in range(0, width, TILE):
         term = jnp.dot(values, w_ref[:, at : at + TILE], preferred_element_type=jnp.float32)
         store_term(term, at, pieces)
     residual = residual_ref[...].astype(jnp.float32)
-    pieces[0][:own_rows, :] = pieces[0][:own_rows, :] + residual
+    stays = pieces[PIECES - 1]
+    stays[:own_rows, :] = stays[:own_rows, :] + residual
 
 
 def project(joined, w_absorb, residual_in, w_out, rows, far):
@@ -220,7 +229,7 @@
         functools.partial(project_kernel, own_rows, far),
         out_shape=term_shapes(rows // (2 * PIECES), width),
         in_specs=[pl.BlockSpec(memory_space=pltpu.VMEM)] * 4,
-        out_specs=(pl.BlockSpec(memory_space=pltpu.VMEM),) * (2 * PIECES),
+        out_specs=[pl.BlockSpec(memory_space=pltpu.VMEM)] * (PIECES + 2),
         compiler_params=pltpu.CompilerParams(vmem_limit_bytes=24 * MIB),
         cost_estimate=pl.CostEstimate(
             flops=2 * rows * depth * width, bytes_accessed=2 * depth * width, transcendentals=0
@@ -230,7 +239,10 @@
 
 
 def expert_kernel(*refs):
-    streams, (gain_ref, gate_ref, up_ref, down_ref), pieces = refs[:8], refs[8:12], refs[12:]
+    count = 2 * PIECES
+    streams, (gain_ref, gate_ref, up_ref, down_ref) = refs[:count], refs[count : count + 4]
+    pieces = refs[count + 4 :]
+    streams = streams[1:PIECES] + streams[:1] + streams[PIECES + 1 :] + streams[PIECES : PIECES + 1]
     width = gain_ref.shape[1]
     depth = width // PARTS
     inverses = []
@@ -270,7 +282,7 @@
         expert_kernel,
         out_shape=term_shapes(rows, width),
         in_specs=[pl.BlockSpec(memory_space=pltpu.VMEM)] * (2 * PIECES + 4),
-        out_specs=(pl.BlockSpec(memory_space=pltpu.VMEM),) * (2 * PIECES),
+        out_specs=[pl.BlockSpec(memory_space=pltpu.VMEM)] * (PIECES + 2),
         compiler_params=pltpu.CompilerParams(vmem_limit_bytes=24 * MIB),
         cost_estimate=pl.CostEstimate(
             flops=12 * PIECES * rows * hidden * width,
@@ -291,12 +303,17 @@
 
 
 def collect(terms):
-    keeps, sends = terms[:PIECES], terms[PIECES:]
+    *keeps, first, rest = terms
+    rows = first.shape[0]
+    rest = swap(rest, 1)
+    others = [swap(first, 1)] + [
+        rest[at * rows : (at + 1) * rows] for at in range(PIECES - 1)
+    ]
     total = 0.0
-    for piece in (1, 2, 3, 0):
-        part = keeps[piece] + wide(swap(sends[piece], 1))
-        if piece:
-            part = wide(swap(part.astype(jnp.bfloat16), SQUARE[piece]))
+    for keep, other, distance in zip(keeps, others, SQUARE):
+        part = keep + wide(other)
+        if distance:
+            part = wide(swap(part.astype(jnp.bfloat16), distance))
         total = total + part
     return total
 
@@ -315,7 +332,7 @@
 
 
 def spread(stream):
-    own = [swap(stream, distance) if distance else stream for distance in SQUARE]
+    own = [stream] + [swap(stream, distance) for distance in SQUARE if distance]
     return own + [swap(piece, 1) for piece in own]
 
 
@@ -350,15 +367,18 @@
 
     total = collect(run_expert(spread(stream), norm_gain, w_gate, w_up, w_down))
     own_ids = lax.dynamic_slice_in_dim(expert_ids, rank_here * own_rows, own_rows, 0)
-    expert_out = 0.0
+    mixings = []
     for at in range(far):
-        block = total[at * own_rows : (at + 1) * own_rows]
-        block = wide(swap(block.astype(jnp.bfloat16), 8 * at)) if at else block
         expert = (rank_here ^ (8 * at)) // split_ways
-        mixing = jnp.sum(
-            route_gates * (own_ids == expert).astype(jnp.float32), axis=1, keepdims=True
+        mixings.append(
+            jnp.sum(
+                route_gates * (own_ids == expert).astype(jnp.float32), axis=1, keepdims=True
+            )
         )
-        expert_out = expert_out + mixing * block
+    expert_out = lax.optimization_barrier(mixings[0] * total[:own_rows])
+    for at in range(1, far):
+        block = total[at * own_rows : (at + 1) * own_rows].astype(jnp.bfloat16)
+        expert_out = expert_out + mixings[at] * wide(swap(block, 8 * at))
     return (attended, expert_out.astype(jnp.bfloat16))
 
 

time: 74.7 us -> 75.3 us (level); the launches traced: 75.3 us -> 75.1 us
  Pallas kernels: 13 us -> 10.7 us
  blocking collectives: 16.8 us -> 18.9 us
  starting transfers between devices: 14.8 us -> 13.5 us
  waiting for transfers between devices: 27.8 us -> 29 us
    all_to_all x1, blocking collectives: 16.8 us -> 18.9 us  [shards(): lax.all_to_all(latent, 'experts', split_axis=0, concat_axis=0, tiled=True)]
    pallas_call x1, Pallas kernels: 8.58 us -> 6.66 us  [attend(): pl.pallas_call(attend_kernel, out_shape=jax.ShapeDtypeStruct((devices, pa...]
    ppermute x23 -> x19, waiting for transfers between devices: 27.8 us -> 29 us  [swap(): return lax.ppermute(array, 'experts', pairs)]
    ppermute x23 -> x19, starting transfers between devices: 14.8 us -> 13.5 us  [swap(): return lax.ppermute(array, 'experts', pairs)]
  transfers between devices with their start and end apart: 23 -> 19, of which waited for: 13 -> 14; matrix products, arithmetic and copies ran while one was open for 1% -> 1% of each run, Pallas kernels for 0% -> 0%
where the time goes in v13:
time: 75.3 us; the launch traced here: 75.1 us
  waiting for transfers between devices  29 us (39%)
  blocking collectives  18.9 us (25%)
  starting transfers between devices  13.5 us (18%)
  Pallas kernels  10.7 us (14%)
  other arithmetic  1.33 us (2%)
  between operations  0.85 us (1%)
  local copies, waits for them, and re-layouts  0.77 us (1%)
    ppermute x19, waiting for transfers between devices, swap(): return lax.ppermute(array, 'experts', pairs)  29 us
    all_to_all x1, blocking collectives, shards(): lax.all_to_all(latent, 'experts', split_axis=0, concat_axis=0, tiled=True)  18.9 us
    ppermute x19, starting transfers between devices, swap(): return lax.ppermute(array, 'experts', pairs)  13.5 us
    pallas_call x1, Pallas kernels, attend(): pl.pallas_call(attend_kernel, out_shape=jax.ShapeDtypeStruct((devices, pa...  6.66 us
    pallas_call x1, Pallas kernels, run_expert(): pl.pallas_call(expert_kernel, out_shape=term_shapes(rows, width), in_spec...  2.35 us
    pallas_call x1, Pallas kernels, project(): pl.pallas_call(functools.partial(project_kernel, own_rows, far), out_shap...  1.69 us
  transfers between devices with their start and end apart: 19, of which 14 were waited for; matrix products, arithmetic and copies ran while one was open for 1% of the time, Pallas kernels for 0%

profile of v13, /device:TPU:0, one launch (start us, length us, event | category | flops | bytes accessed | tf_op | source)
XLA Modules:
  0.0 75.1 jit_solution(3991604775893165571)
XLA Ops:
  0.7 6.7 %attend.1 = bf16[16,16,512]{2,1,0:T(8,128)(2,1)} custom-call(s32[4]{0:T(128)} %len_ref.1, bf16[4,64,576]{2,1,0:T(8,128)(2,1)} %bitcast.7, bf16[4,576,4096]{2,1,0:T(8,128)(2,1)} %cache_ref.1), custom_call_target="tpu_custom_call" | custom-call | flops 1140850688 | bytes 9437184 | tf_op jit(solution)/shard_map/attend/pallas_call | solution.py:144
  7.3 18.9 %all_to_all.5 = bf16[16,16,512]{2,1,0:T(8,128)(2,1)S(1)} all-to-all(bf16[16,16,512]{2,1,0:T(8,128)(2,1)} %attend.1), channel_id=1, replica_groups=mesh['groups'=2,'experts'=16] {'experts'}, dimensions={0} | all-to-all | bytes 524288 | tf_op jit(solution)/shard_map/all_to_all | solution.py:362
  26.3 1.7 %project.1 = (f32[8,7168]{1,0:T(8,128)S(1)}, f32[8,7168]{1,0:T(8,128)S(1)}, f32[8,7168]{1,0:T(8,128)S(1)}, f32[8,7168]{1,0:T(8,128)S(1)}, bf16[8,7168]{1,0:T(8,128)(2,1)S(1)}, /*index=5*/bf16[24,7168]{1,0:T(8,128)(2,1)S(1)}) custom-call(bf16[256,512]{1,0:T(8,128)(2,1)S(1)} %bitcast.5, bf16[4,7168]{1,0:T(4,128)(2,1)S(1)} %copy-done.4, ...), custom_call_target="tpu_custom_call" | custom-call | flops 469762048 | bytes 7340032 | tf_op jit(solution)/shard_map/project/pallas_call | solution.py:228
  28.6 0.8 %collective-permute-done = bf16[8,7168]{1,0:T(8,128)(2,1)S(1)} collective-permute-done((bf16[8,7168]{1,0:T(8,128)(2,1)S(1)}, bf16[8,7168]{1,0:T(8,128)(2,1)S(1)}, u32[]{:S(2)}, u32[]{:S(2)}) %collective-permute-start) | collective-permute-done | bytes 114720 | tf_op jit(solution)/shard_map/ppermute | solution.py:298
  29.4 0.6 collective-permute-start.1
  30.1 1.1 %collective-permute-start.3 = (bf16[8,7168]{1,0:T(8,128)(2,1)S(1)}, bf16[8,7168]{1,0:T(8,128)(2,1)S(1)}, u32[]{:S(2)}, u32[]{:S(2)}) collective-permute-start(bf16[8,7168]{1,0:T(8,128)(2,1)S(1)} %get-tuple-element.30), channel_id=1, source_target_pairs={{0,4},{1,5},{2,6},{3,7},{4,0},{5,1},{6,2},{7,3},{8,12},{9,13},{10,... | collective-permute-start | bytes 344072 | tf_op jit(solution)/shard_map/ppermute | solution.py:298
  31.2 1.8 %collective-permute-start.4 = (bf16[8,7168]{1,0:T(8,128)(2,1)S(1)}, bf16[8,7168]{1,0:T(8,128)(2,1)S(1)}, u32[]{:S(2)}, u32[]{:S(2)}) collective-permute-start(bf16[8,7168]{1,0:T(8,128)(2,1)S(1)} %get-tuple-element.31), channel_id=1, source_target_pairs={{0,2},{1,3},{2,0},{3,1},{4,6},{5,7},{6,4},{7,5},{8,10},{9,11},{10,... | collective-permute-start | bytes 344072 | tf_op jit(solution)/shard_map/ppermute | solution.py:298
  33.1 3.3 %collective-permute-done.1 = bf16[8,7168]{1,0:T(8,128)(2,1)S(1)} collective-permute-done((bf16[8,7168]{1,0:T(8,128)(2,1)S(1)}, bf16[8,7168]{1,0:T(8,128)(2,1)S(1)}, u32[]{:S(2)}, u32[]{:S(2)}) %collective-permute-start.1) | collective-permute-done | bytes 114720 | tf_op jit(solution)/shard_map/ppermute | solution.py:298
  36.9 1.1 %collective-permute-done.4 = bf16[8,7168]{1,0:T(8,128)(2,1)S(1)} collective-permute-done((bf16[8,7168]{1,0:T(8,128)(2,1)S(1)}, bf16[8,7168]{1,0:T(8,128)(2,1)S(1)}, u32[]{:S(2)}, u32[]{:S(2)}) %collective-permute-start.4) | collective-permute-done | bytes 114720 | tf_op jit(solution)/shard_map/ppermute | solution.py:298
  38.1 1.1 %collective-permute-start.5 = (bf16[8,7168]{1,0:T(8,128)(2,1)S(1)}, bf16[8,7168]{1,0:T(8,128)(2,1)S(1)}, u32[]{:S(2)}, u32[]{:S(2)}) collective-permute-start(bf16[8,7168]{1,0:T(8,128)(2,1)S(1)} %fusion.2), channel_id=1, source_target_pairs={{0,8},{1,9},{2,10},{3,11},{4,12},{5,13},{6,14},{7,15},{8,0},{9,1},... | collective-permute-start | bytes 344072 | tf_op jit(solution)/shard_map/ppermute | solution.py:298
  39.2 7.3 %collective-permute-done.5 = bf16[8,7168]{1,0:T(8,128)(2,1)S(1)} collective-permute-done((bf16[8,7168]{1,0:T(8,128)(2,1)S(1)}, bf16[8,7168]{1,0:T(8,128)(2,1)S(1)}, u32[]{:S(2)}, u32[]{:S(2)}) %collective-permute-start.5) | collective-permute-done | bytes 114720 | tf_op jit(solution)/shard_map/ppermute | solution.py:298
  46.8 1.3 %collective-permute-start.7 = (bf16[8,7168]{1,0:T(8,128)(2,1)S(1)}, bf16[8,7168]{1,0:T(8,128)(2,1)S(1)}, u32[]{:S(2)}, u32[]{:S(2)}) collective-permute-start(bf16[8,7168]{1,0:T(8,128)(2,1)S(1)} %add_convert_fusion.3.refs_0_), channel_id=1, source_target_pairs={{0,4},{1,5},{2,6},{3,7},{4,0},{5,1},{6,2},{7,3},{8,12},{9,13},{10,... | collective-permute-start | bytes 344072 | tf_op jit(solution)/shard_map/ppermute | solution.py:298
  48.2 2.1 %collective-permute-start.8 = (bf16[8,7168]{1,0:T(8,128)(2,1)S(1)}, bf16[8,7168]{1,0:T(8,128)(2,1)S(1)}, u32[]{:S(2)}, u32[]{:S(2)}) collective-permute-start(bf16[8,7168]{1,0:T(8,128)(2,1)S(1)} %add_convert_fusion.3.refs_0_), channel_id=1, source_target_pairs={{0,2},{1,3},{2,0},{3,1},{4,6},{5,7},{6,4},{7,5},{8,10},{9,11},{10,... | collective-permute-start | bytes 344072 | tf_op jit(solution)/shard_map/ppermute | solution.py:298
  50.3 3.4 %collective-permute-done.6.refs_1_ = bf16[8,7168]{1,0:T(8,128)(2,1)S(1)} collective-permute-done((bf16[8,7168]{1,0:T(8,128)(2,1)S(1)}, bf16[8,7168]{1,0:T(8,128)(2,1)S(1)}, u32[]{:S(2)}, u32[]{:S(2)}) %collective-permute-start.6) | collective-permute-done | bytes 114720 | tf_op jit(solution)/shard_map/ppermute | solution.py:298
  54.3 1.0 %collective-permute-done.8.refs_3_ = bf16[8,7168]{1,0:T(8,128)(2,1)S(1)} collective-permute-done((bf16[8,7168]{1,0:T(8,128)(2,1)S(1)}, bf16[8,7168]{1,0:T(8,128)(2,1)S(1)}, u32[]{:S(2)}, u32[]{:S(2)}) %collective-permute-start.8) | collective-permute-done | bytes 114720 | tf_op jit(solution)/shard_map/ppermute | solution.py:298
  55.3 1.3 %collective-permute-done.12.refs_7_ = bf16[8,7168]{1,0:T(8,128)(2,1)S(1)} collective-permute-done((bf16[8,7168]{1,0:T(8,128)(2,1)S(1)}, bf16[8,7168]{1,0:T(8,128)(2,1)S(1)}, u32[]{:S(2)}, u32[]{:S(2)}) %collective-permute-start.12) | collective-permute-done | bytes 114720 | tf_op jit(solution)/shard_map/ppermute | solution.py:298
  56.6 2.3 %expert.1 = (f32[8,7168]{1,0:T(8,128)S(1)}, f32[8,7168]{1,0:T(8,128)S(1)}, f32[8,7168]{1,0:T(8,128)S(1)}, f32[8,7168]{1,0:T(8,128)S(1)}, bf16[8,7168]{1,0:T(8,128)(2,1)S(1)}, /*index=5*/bf16[24,7168]{1,0:T(8,128)(2,1)S(1)}) custom-call(bf16[8,7168]{1,0:T(8,128)(2,1)S(1)} %add_convert_fusion.3.refs_0_, bf16[8,7168]{1,0:T(8,128)(2,1)S(1)} %collective-permute-done.6.refs_1_, ...), custom_call_target="tpu_custom_call" | custom-call | flops 704643072 | bytes 11010048 | tf_op jit(solution)/shard_map/expert/pallas_call | solution.py:281
  59.6 0.8 %collective-permute-done.13 = bf16[8,7168]{1,0:T(8,128)(2,1)S(1)} collective-permute-done((bf16[8,7168]{1,0:T(8,128)(2,1)S(1)}, bf16[8,7168]{1,0:T(8,128)(2,1)S(1)}, u32[]{:S(2)}, u32[]{:S(2)}) %collective-permute-start.13) | collective-permute-done | bytes 114720 | tf_op jit(solution)/shard_map/ppermute | solution.py:298
  60.9 1.9 %collective-permute-start.16 = (bf16[8,7168]{1,0:T(8,128)(2,1)S(1)}, bf16[8,7168]{1,0:T(8,128)(2,1)S(1)}, u32[]{:S(2)}, u32[]{:S(2)}) collective-permute-start(bf16[8,7168]{1,0:T(8,128)(2,1)S(1)} %get-tuple-element.28), channel_id=1, source_target_pairs={{0,4},{1,5},{2,6},{3,7},{4,0},{5,1},{6,2},{7,3},{8,12},{9,13},{10,... | collective-permute-start | bytes 344072 | tf_op jit(solution)/shard_map/ppermute | solution.py:298
  62.8 1.3 %collective-permute-start.17 = (bf16[8,7168]{1,0:T(8,128)(2,1)S(1)}, bf16[8,7168]{1,0:T(8,128)(2,1)S(1)}, u32[]{:S(2)}, u32[]{:S(2)}) collective-permute-start(bf16[8,7168]{1,0:T(8,128)(2,1)S(1)} %get-tuple-element.29), channel_id=1, source_target_pairs={{0,2},{1,3},{2,0},{3,1},{4,6},{5,7},{6,4},{7,5},{8,10},{9,11},{10,... | collective-permute-start | bytes 344072 | tf_op jit(solution)/shard_map/ppermute | solution.py:298
  64.8 2.5 %collective-permute-done.14 = bf16[8,7168]{1,0:T(8,128)(2,1)S(1)} collective-permute-done((bf16[8,7168]{1,0:T(8,128)(2,1)S(1)}, bf16[8,7168]{1,0:T(8,128)(2,1)S(1)}, u32[]{:S(2)}, u32[]{:S(2)}) %collective-permute-start.14) | collective-permute-done | bytes 114720 | tf_op jit(solution)/shard_map/ppermute | solution.py:298
  67.4 1.1 %collective-permute-done.16 = bf16[8,7168]{1,0:T(8,128)(2,1)S(1)} collective-permute-done((bf16[8,7168]{1,0:T(8,128)(2,1)S(1)}, bf16[8,7168]{1,0:T(8,128)(2,1)S(1)}, u32[]{:S(2)}, u32[]{:S(2)}) %collective-permute-start.16) | collective-permute-done | bytes 114720 | tf_op jit(solution)/shard_map/ppermute | solution.py:298
  69.3 5.1 %collective-permute-done.18 = bf16[4,7168]{1,0:T(4,128)(2,1)S(1)} collective-permute-done((bf16[4,7168]{1,0:T(4,128)(2,1)S(1)}, bf16[4,7168]{1,0:T(4,128)(2,1)S(1)}, u32[]{:S(2)}, u32[]{:S(2)}) %collective-permute-start.18) | collective-permute-done | bytes 57376 | tf_op jit(solution)/shard_map/ppermute | solution.py:298
  74.4 0.7 add_convert_fusion.7
  (52 shorter events, 4.8 us)
Async XLA Ops:
  0.6 25.6 %slice-start = ((s8[7340032]{0:T(1024)(128)(4,1)}), s8[4194304]{0:T(1024)(128)(4,1)S(1)}, s32[]{:S(2)}) async-start(s8[7340032]{0:T(1024)(128)(4,1)} %bitcast.3), calls=%async_computation.1 | async-start | bytes 8388608
  26.2 30.4 %copy-start = (bf16[7168,256]{1,0:T(8,128)(2,1)S(1)}, bf16[7168,256]{1,0:T(8,128)(2,1)}, u32[]{:S(2)}) copy-start(bf16[7168,256]{1,0:T(8,128)(2,1)} %refs_9_.1) | copy-start | bytes 11010052
  26.2 30.4 %copy-start.1 = (bf16[7168,256]{1,0:T(8,128)(2,1)S(1)}, bf16[7168,256]{1,0:T(8,128)(2,1)}, u32[]{:S(2)}) copy-start(bf16[7168,256]{1,0:T(8,128)(2,1)} %refs_10_.1) | copy-start | bytes 11010052
  26.3 30.3 %copy-start.2 = (bf16[256,7168]{1,0:T(8,128)(2,1)S(1)}, bf16[256,7168]{1,0:T(8,128)(2,1)}, u32[]{:S(2)}) copy-start(bf16[256,7168]{1,0:T(8,128)(2,1)} %refs_11_.1) | copy-start | bytes 11010052
  26.3 30.3 %copy-start.5 = (f32[7168]{0:T(1024)S(1)}, f32[7168]{0:T(1024)}, u32[]{:S(2)}) copy-start(f32[7168]{0:T(1024)} %param.18) | copy-start | bytes 86020
  28.0 1.4 %collective-permute-start = (bf16[8,7168]{1,0:T(8,128)(2,1)S(1)}, bf16[8,7168]{1,0:T(8,128)(2,1)S(1)}, u32[]{:S(2)}, u32[]{:S(2)}) collective-permute-start(bf16[8,7168]{1,0:T(8,128)(2,1)S(1)} %get-tuple-element.15), channel_id=1, source_target_pairs={{0,1},{1,0},{2,3},{3,2},{4,5},{5,4},{6,7},{7,6},{8,9},{9,8},{10,11... | collective-permute-start | bytes 344072 | tf_op jit(solution)/shard_map/ppermute | solution.py:298
  28.1 2.0 %collective-permute-start.2 = (bf16[24,7168]{1,0:T(8,128)(2,1)S(1)}, bf16[24,7168]{1,0:T(8,128)(2,1)S(1)}, u32[]{:S(2)}, u32[]{:S(2)}) collective-permute-start(bf16[24,7168]{1,0:T(8,128)(2,1)S(1)} %get-tuple-element.17), channel_id=1, source_target_pairs={{0,1},{1,0},{2,3},{3,2},{4,5},{5,4},{6,7},{7,6},{8,9},{9,8},{10,11... | collective-permute-start | bytes 1032200 | tf_op jit(solution)/shard_map/ppermute | solution.py:298
  29.4 7.0 %collective-permute-start.1 = (bf16[8,7168]{1,0:T(8,128)(2,1)S(1)}, bf16[8,7168]{1,0:T(8,128)(2,1)S(1)}, u32[]{:S(2)}, u32[]{:S(2)}) collective-permute-start(bf16[8,7168]{1,0:T(8,128)(2,1)S(1)} %add_convert_fusion.6), channel_id=1, source_target_pairs={{0,6},{1,7},{2,4},{3,5},{4,2},{5,3},{6,0},{7,1},{8,14},{9,15},{10,... | collective-permute-start | bytes 344072 | tf_op jit(solution)/shard_map/ppermute | solution.py:298
  30.1 6.8 %collective-permute-start.3 = (bf16[8,7168]{1,0:T(8,128)(2,1)S(1)}, bf16[8,7168]{1,0:T(8,128)(2,1)S(1)}, u32[]{:S(2)}, u32[]{:S(2)}) collective-permute-start(bf16[8,7168]{1,0:T(8,128)(2,1)S(1)} %get-tuple-element.30), channel_id=1, source_target_pairs={{0,4},{1,5},{2,6},{3,7},{4,0},{5,1},{6,2},{7,3},{8,12},{9,13},{10,... | collective-permute-start | bytes 344072 | tf_op jit(solution)/shard_map/ppermute | solution.py:298
  31.2 6.8 %collective-permute-start.4 = (bf16[8,7168]{1,0:T(8,128)(2,1)S(1)}, bf16[8,7168]{1,0:T(8,128)(2,1)S(1)}, u32[]{:S(2)}, u32[]{:S(2)}) collective-permute-start(bf16[8,7168]{1,0:T(8,128)(2,1)S(1)} %get-tuple-element.31), channel_id=1, source_target_pairs={{0,2},{1,3},{2,0},{3,1},{4,6},{5,7},{6,4},{7,5},{8,10},{9,11},{10,... | collective-permute-start | bytes 344072 | tf_op jit(solution)/shard_map/ppermute | solution.py:298
  38.1 8.5 %collective-permute-start.5 = (bf16[8,7168]{1,0:T(8,128)(2,1)S(1)}, bf16[8,7168]{1,0:T(8,128)(2,1)S(1)}, u32[]{:S(2)}, u32[]{:S(2)}) collective-permute-start(bf16[8,7168]{1,0:T(8,128)(2,1)S(1)} %fusion.2), channel_id=1, source_target_pairs={{0,8},{1,9},{2,10},{3,11},{4,12},{5,13},{6,14},{7,15},{8,0},{9,1},... | collective-permute-start | bytes 344072 | tf_op jit(solution)/shard_map/ppermute | solution.py:298
  46.8 7.0 %collective-permute-start.6 = (bf16[8,7168]{1,0:T(8,128)(2,1)S(1)}, bf16[8,7168]{1,0:T(8,128)(2,1)S(1)}, u32[]{:S(2)}, u32[]{:S(2)}) collective-permute-start(bf16[8,7168]{1,0:T(8,128)(2,1)S(1)} %add_convert_fusion.3.refs_0_), channel_id=1, source_target_pairs={{0,6},{1,7},{2,4},{3,5},{4,2},{5,3},{6,0},{7,1},{8,14},{9,15},{10,... | collective-permute-start | bytes 344072 | tf_op jit(solution)/shard_map/ppermute | solution.py:298
  46.8 6.9 %collective-permute-start.7 = (bf16[8,7168]{1,0:T(8,128)(2,1)S(1)}, bf16[8,7168]{1,0:T(8,128)(2,1)S(1)}, u32[]{:S(2)}, u32[]{:S(2)}) collective-permute-start(bf16[8,7168]{1,0:T(8,128)(2,1)S(1)} %add_convert_fusion.3.refs_0_), channel_id=1, source_target_pairs={{0,4},{1,5},{2,6},{3,7},{4,0},{5,1},{6,2},{7,3},{8,12},{9,13},{10,... | collective-permute-start | bytes 344072 | tf_op jit(solution)/shard_map/ppermute | solution.py:298
  48.2 7.1 %collective-permute-start.8 = (bf16[8,7168]{1,0:T(8,128)(2,1)S(1)}, bf16[8,7168]{1,0:T(8,128)(2,1)S(1)}, u32[]{:S(2)}, u32[]{:S(2)}) collective-permute-start(bf16[8,7168]{1,0:T(8,128)(2,1)S(1)} %add_convert_fusion.3.refs_0_), channel_id=1, source_target_pairs={{0,2},{1,3},{2,0},{3,1},{4,6},{5,7},{6,4},{7,5},{8,10},{9,11},{10,... | collective-permute-start | bytes 344072 | tf_op jit(solution)/shard_map/ppermute | solution.py:298
  50.3 5.0 %collective-permute-start.9 = (bf16[8,7168]{1,0:T(8,128)(2,1)S(1)}, bf16[8,7168]{1,0:T(8,128)(2,1)S(1)}, u32[]{:S(2)}, u32[]{:S(2)}) collective-permute-start(bf16[8,7168]{1,0:T(8,128)(2,1)S(1)} %add_convert_fusion.3.refs_0_), channel_id=1, source_target_pairs={{0,1},{1,0},{2,3},{3,2},{4,5},{5,4},{6,7},{7,6},{8,9},{9,8},{10,11... | collective-permute-start | bytes 344072 | tf_op jit(solution)/shard_map/ppermute | solution.py:298
  53.7 1.5 %collective-permute-start.10 = (bf16[8,7168]{1,0:T(8,128)(2,1)S(1)}, bf16[8,7168]{1,0:T(8,128)(2,1)S(1)}, u32[]{:S(2)}, u32[]{:S(2)}) collective-permute-start(bf16[8,7168]{1,0:T(8,128)(2,1)S(1)} %collective-permute-done.6.refs_1_), channel_id=1, source_target_pairs={{0,1},{1,0},{2,3},{3,2},{4,5},{5,4},{6,7},{7,6},{8,9},{9,8},{10,11... | collective-permute-start | bytes 344072 | tf_op jit(solution)/shard_map/ppermute | solution.py:298
  53.7 1.5 %collective-permute-start.11 = (bf16[8,7168]{1,0:T(8,128)(2,1)S(1)}, bf16[8,7168]{1,0:T(8,128)(2,1)S(1)}, u32[]{:S(2)}, u32[]{:S(2)}) collective-permute-start(bf16[8,7168]{1,0:T(8,128)(2,1)S(1)} %collective-permute-done.7.refs_2_), channel_id=1, source_target_pairs={{0,1},{1,0},{2,3},{3,2},{4,5},{5,4},{6,7},{7,6},{8,9},{9,8},{10,11... | collective-permute-start | bytes 344072 | tf_op jit(solution)/shard_map/ppermute | solution.py:298
  55.3 1.3 %collective-permute-start.12 = (bf16[8,7168]{1,0:T(8,128)(2,1)S(1)}, bf16[8,7168]{1,0:T(8,128)(2,1)S(1)}, u32[]{:S(2)}, u32[]{:S(2)}) collective-permute-start(bf16[8,7168]{1,0:T(8,128)(2,1)S(1)} %collective-permute-done.8.refs_3_), channel_id=1, source_target_pairs={{0,1},{1,0},{2,3},{3,2},{4,5},{5,4},{6,7},{7,6},{8,9},{9,8},{10,11... | collective-permute-start | bytes 344072 | tf_op jit(solution)/shard_map/ppermute | solution.py:298
  59.0 1.4 %collective-permute-start.13 = (bf16[8,7168]{1,0:T(8,128)(2,1)S(1)}, bf16[8,7168]{1,0:T(8,128)(2,1)S(1)}, u32[]{:S(2)}, u32[]{:S(2)}) collective-permute-start(bf16[8,7168]{1,0:T(8,128)(2,1)S(1)} %get-tuple-element.21), channel_id=1, source_target_pairs={{0,1},{1,0},{2,3},{3,2},{4,5},{5,4},{6,7},{7,6},{8,9},{9,8},{10,11... | collective-permute-start | bytes 344072 | tf_op jit(solution)/shard_map/ppermute | solution.py:298
  59.2 1.7 %collective-permute-start.15 = (bf16[24,7168]{1,0:T(8,128)(2,1)S(1)}, bf16[24,7168]{1,0:T(8,128)(2,1)S(1)}, u32[]{:S(2)}, u32[]{:S(2)}) collective-permute-start(bf16[24,7168]{1,0:T(8,128)(2,1)S(1)} %get-tuple-element.23), channel_id=1, source_target_pairs={{0,1},{1,0},{2,3},{3,2},{4,5},{5,4},{6,7},{7,6},{8,9},{9,8},{10,11... | collective-permute-start | bytes 1032200 | tf_op jit(solution)/shard_map/ppermute | solution.py:298
  60.4 7.0 %collective-permute-start.14 = (bf16[8,7168]{1,0:T(8,128)(2,1)S(1)}, bf16[8,7168]{1,0:T(8,128)(2,1)S(1)}, u32[]{:S(2)}, u32[]{:S(2)}) collective-permute-start(bf16[8,7168]{1,0:T(8,128)(2,1)S(1)} %add_convert_fusion.2), channel_id=1, source_target_pairs={{0,6},{1,7},{2,4},{3,5},{4,2},{5,3},{6,0},{7,1},{8,14},{9,15},{10,... | collective-permute-start | bytes 344072 | tf_op jit(solution)/shard_map/ppermute | solution.py:298
  60.9 7.6 %collective-permute-start.16 = (bf16[8,7168]{1,0:T(8,128)(2,1)S(1)}, bf16[8,7168]{1,0:T(8,128)(2,1)S(1)}, u32[]{:S(2)}, u32[]{:S(2)}) collective-permute-start(bf16[8,7168]{1,0:T(8,128)(2,1)S(1)} %get-tuple-element.28), channel_id=1, source_target_pairs={{0,4},{1,5},{2,6},{3,7},{4,0},{5,1},{6,2},{7,3},{8,12},{9,13},{10,... | collective-permute-start | bytes 344072 | tf_op jit(solution)/shard_map/ppermute | solution.py:298
  62.8 6.3 %collective-permute-start.17 = (bf16[8,7168]{1,0:T(8,128)(2,1)S(1)}, bf16[8,7168]{1,0:T(8,128)(2,1)S(1)}, u32[]{:S(2)}, u32[]{:S(2)}) collective-permute-start(bf16[8,7168]{1,0:T(8,128)(2,1)S(1)} %get-tuple-element.29), channel_id=1, source_target_pairs={{0,2},{1,3},{2,0},{3,1},{4,6},{5,7},{6,4},{7,5},{8,10},{9,11},{10,... | collective-permute-start | bytes 344072 | tf_op jit(solution)/shard_map/ppermute | solution.py:298
  69.1 5.2 %collective-permute-start.18 = (bf16[4,7168]{1,0:T(4,128)(2,1)S(1)}, bf16[4,7168]{1,0:T(4,128)(2,1)S(1)}, u32[]{:S(2)}, u32[]{:S(2)}) collective-permute-start(bf16[4,7168]{1,0:T(4,128)(2,1)S(1)} %slice.68), channel_id=1, source_target_pairs={{0,8},{1,9},{2,10},{3,11},{4,12},{5,13},{6,14},{7,15},{8,0},{9,1},... | collective-permute-start | bytes 172040 | tf_op jit(solution)/shard_map/ppermute | solution.py:298
  (5 other events, 91.6 us)

commit v14 on v13

--- a/solution.py
+++ b/solution.py
@@ -9,9 +9,9 @@
 
 QK = 192
 FF = 2048
-BLOCK = 512
+BLOCK = 256
 LOWEST = -3e38
-GROUP = 4
+GROUP = 8
 LANES = 128
 TILE = 256
 PARTS = 4
@@ -120,13 +120,17 @@
                 )
 
     def visit_group(group, _):
-        visit(group * GROUP, GROUP)
+        visit(own_rows + group * GROUP, GROUP)
         return 0
 
-    whole = items // GROUP
-    lax.fori_loop(0, whole, visit_group, 0)
-    pl.when((items & 2) != 0)(lambda: visit(whole * GROUP, 2))
-    pl.when((items & 1) != 0)(lambda: visit(items - 1, 1))
+    visit(0, own_rows)
+    rest = items - own_rows
+    lax.fori_loop(0, rest // GROUP, visit_group, 0)
+    many = GROUP // 2
+    while many:
+        first = own_rows + rest // (2 * many) * (2 * many)
+        pl.when((rest & many) != 0)(functools.partial(visit, first, many))
+        many //= 2
     for row in range(own_rows):
         latent = summed[row] * (1.0 / jnp.sum(sums[row], axis=1, keepdims=True))
         for device in range(devices):

time: 75.3 us -> 76.3 us (1.013)
  Pallas kernels: 10.7 us -> 11.5 us
    pallas_call x1, Pallas kernels: 6.66 us -> 7.47 us  [attend(): pl.pallas_call(attend_kernel, out_shape=jax.ShapeDtypeStruct((devices, pa...]
where the time goes in v14:
time: 76.3 us; the launch traced here: 76.2 us
  waiting for transfers between devices  29 us (38%)
  blocking collectives  19.1 us (25%)
  starting transfers between devices  13.5 us (18%)
  Pallas kernels  11.5 us (15%)
  other arithmetic  1.33 us (2%)
  between operations  0.85 us (1%)
  local copies, waits for them, and re-layouts  0.77 us (1%)
    ppermute x19, waiting for transfers between devices, swap(): return lax.ppermute(array, 'experts', pairs)  29 us
    all_to_all x1, blocking collectives, shards(): lax.all_to_all(latent, 'experts', split_axis=0, concat_axis=0, tiled=True)  19.1 us
    ppermute x19, starting transfers between devices, swap(): return lax.ppermute(array, 'experts', pairs)  13.5 us
    pallas_call x1, Pallas kernels, attend(): pl.pallas_call(attend_kernel, out_shape=jax.ShapeDtypeStruct((devices, pa...  7.47 us
    pallas_call x1, Pallas kernels, run_expert(): pl.pallas_call(expert_kernel, out_shape=term_shapes(rows, width), in_spec...  2.34 us
    pallas_call x1, Pallas kernels, project(): pl.pallas_call(functools.partial(project_kernel, own_rows, far), out_shap...  1.69 us
  transfers between devices with their start and end apart: 19, of which 14 were waited for; matrix products, arithmetic and copies ran while one was open for 1% of the time, Pallas kernels for 0%

profile of v14, /device:TPU:0, one launch (start us, length us, event | category | flops | bytes accessed | tf_op | source)
XLA Modules:
  0.0 76.2 jit_solution(3274370735806352638)
XLA Ops:
  0.7 7.5 %attend.1 = bf16[16,16,512]{2,1,0:T(8,128)(2,1)} custom-call(s32[4]{0:T(128)} %len_ref.1, bf16[4,64,576]{2,1,0:T(8,128)(2,1)} %bitcast.7, bf16[4,576,4096]{2,1,0:T(8,128)(2,1)} %cache_ref.1), custom_call_target="tpu_custom_call" | custom-call | flops 1140850688 | bytes 9437184 | tf_op jit(solution)/shard_map/attend/pallas_call | solution.py:148
  8.1 19.1 %all_to_all.5 = bf16[16,16,512]{2,1,0:T(8,128)(2,1)S(1)} all-to-all(bf16[16,16,512]{2,1,0:T(8,128)(2,1)} %attend.1), channel_id=1, replica_groups=mesh['groups'=2,'experts'=16] {'experts'}, dimensions={0} | all-to-all | bytes 524288 | tf_op jit(solution)/shard_map/all_to_all | solution.py:366
  27.4 1.7 %project.1 = (f32[8,7168]{1,0:T(8,128)S(1)}, f32[8,7168]{1,0:T(8,128)S(1)}, f32[8,7168]{1,0:T(8,128)S(1)}, f32[8,7168]{1,0:T(8,128)S(1)}, bf16[8,7168]{1,0:T(8,128)(2,1)S(1)}, /*index=5*/bf16[24,7168]{1,0:T(8,128)(2,1)S(1)}) custom-call(bf16[256,512]{1,0:T(8,128)(2,1)S(1)} %bitcast.5, bf16[4,7168]{1,0:T(4,128)(2,1)S(1)} %copy-done.4, ...), custom_call_target="tpu_custom_call" | custom-call | flops 469762048 | bytes 7340032 | tf_op jit(solution)/shard_map/project/pallas_call | solution.py:232
  29.6 0.8 %collective-permute-done = bf16[8,7168]{1,0:T(8,128)(2,1)S(1)} collective-permute-done((bf16[8,7168]{1,0:T(8,128)(2,1)S(1)}, bf16[8,7168]{1,0:T(8,128)(2,1)S(1)}, u32[]{:S(2)}, u32[]{:S(2)}) %collective-permute-start) | collective-permute-done | bytes 114720 | tf_op jit(solution)/shard_map/ppermute | solution.py:302
  30.5 0.7 collective-permute-start.1
  31.2 1.1 %collective-permute-start.3 = (bf16[8,7168]{1,0:T(8,128)(2,1)S(1)}, bf16[8,7168]{1,0:T(8,128)(2,1)S(1)}, u32[]{:S(2)}, u32[]{:S(2)}) collective-permute-start(bf16[8,7168]{1,0:T(8,128)(2,1)S(1)} %get-tuple-element.30), channel_id=1, source_target_pairs={{0,4},{1,5},{2,6},{3,7},{4,0},{5,1},{6,2},{7,3},{8,12},{9,13},{10,... | collective-permute-start | bytes 344072 | tf_op jit(solution)/shard_map/ppermute | solution.py:302
  32.3 1.8 %collective-permute-start.4 = (bf16[8,7168]{1,0:T(8,128)(2,1)S(1)}, bf16[8,7168]{1,0:T(8,128)(2,1)S(1)}, u32[]{:S(2)}, u32[]{:S(2)}) collective-permute-start(bf16[8,7168]{1,0:T(8,128)(2,1)S(1)} %get-tuple-element.31), channel_id=1, source_target_pairs={{0,2},{1,3},{2,0},{3,1},{4,6},{5,7},{6,4},{7,5},{8,10},{9,11},{10,... | collective-permute-start | bytes 344072 | tf_op jit(solution)/shard_map/ppermute | solution.py:302
  34.2 3.3 %collective-permute-done.1 = bf16[8,7168]{1,0:T(8,128)(2,1)S(1)} collective-permute-done((bf16[8,7168]{1,0:T(8,128)(2,1)S(1)}, bf16[8,7168]{1,0:T(8,128)(2,1)S(1)}, u32[]{:S(2)}, u32[]{:S(2)}) %collective-permute-start.1) | collective-permute-done | bytes 114720 | tf_op jit(solution)/shard_map/ppermute | solution.py:302
  38.0 1.1 %collective-permute-done.4 = bf16[8,7168]{1,0:T(8,128)(2,1)S(1)} collective-permute-done((bf16[8,7168]{1,0:T(8,128)(2,1)S(1)}, bf16[8,7168]{1,0:T(8,128)(2,1)S(1)}, u32[]{:S(2)}, u32[]{:S(2)}) %collective-permute-start.4) | collective-permute-done | bytes 114720 | tf_op jit(solution)/shard_map/ppermute | solution.py:302
  39.2 1.1 %collective-permute-start.5 = (bf16[8,7168]{1,0:T(8,128)(2,1)S(1)}, bf16[8,7168]{1,0:T(8,128)(2,1)S(1)}, u32[]{:S(2)}, u32[]{:S(2)}) collective-permute-start(bf16[8,7168]{1,0:T(8,128)(2,1)S(1)} %fusion.2), channel_id=1, source_target_pairs={{0,8},{1,9},{2,10},{3,11},{4,12},{5,13},{6,14},{7,15},{8,0},{9,1},... | collective-permute-start | bytes 344072 | tf_op jit(solution)/shard_map/ppermute | solution.py:302
  40.3 7.3 %collective-permute-done.5 = bf16[8,7168]{1,0:T(8,128)(2,1)S(1)} collective-permute-done((bf16[8,7168]{1,0:T(8,128)(2,1)S(1)}, bf16[8,7168]{1,0:T(8,128)(2,1)S(1)}, u32[]{:S(2)}, u32[]{:S(2)}) %collective-permute-start.5) | collective-permute-done | bytes 114720 | tf_op jit(solution)/shard_map/ppermute | solution.py:302
  47.9 1.3 %collective-permute-start.7 = (bf16[8,7168]{1,0:T(8,128)(2,1)S(1)}, bf16[8,7168]{1,0:T(8,128)(2,1)S(1)}, u32[]{:S(2)}, u32[]{:S(2)}) collective-permute-start(bf16[8,7168]{1,0:T(8,128)(2,1)S(1)} %add_convert_fusion.3.refs_0_), channel_id=1, source_target_pairs={{0,4},{1,5},{2,6},{3,7},{4,0},{5,1},{6,2},{7,3},{8,12},{9,13},{10,... | collective-permute-start | bytes 344072 | tf_op jit(solution)/shard_map/ppermute | solution.py:302
  49.3 2.1 %collective-permute-start.8 = (bf16[8,7168]{1,0:T(8,128)(2,1)S(1)}, bf16[8,7168]{1,0:T(8,128)(2,1)S(1)}, u32[]{:S(2)}, u32[]{:S(2)}) collective-permute-start(bf16[8,7168]{1,0:T(8,128)(2,1)S(1)} %add_convert_fusion.3.refs_0_), channel_id=1, source_target_pairs={{0,2},{1,3},{2,0},{3,1},{4,6},{5,7},{6,4},{7,5},{8,10},{9,11},{10,... | collective-permute-start | bytes 344072 | tf_op jit(solution)/shard_map/ppermute | solution.py:302
  51.4 3.4 %collective-permute-done.6.refs_1_ = bf16[8,7168]{1,0:T(8,128)(2,1)S(1)} collective-permute-done((bf16[8,7168]{1,0:T(8,128)(2,1)S(1)}, bf16[8,7168]{1,0:T(8,128)(2,1)S(1)}, u32[]{:S(2)}, u32[]{:S(2)}) %collective-permute-start.6) | collective-permute-done | bytes 114720 | tf_op jit(solution)/shard_map/ppermute | solution.py:302
  55.3 1.0 %collective-permute-done.8.refs_3_ = bf16[8,7168]{1,0:T(8,128)(2,1)S(1)} collective-permute-done((bf16[8,7168]{1,0:T(8,128)(2,1)S(1)}, bf16[8,7168]{1,0:T(8,128)(2,1)S(1)}, u32[]{:S(2)}, u32[]{:S(2)}) %collective-permute-start.8) | collective-permute-done | bytes 114720 | tf_op jit(solution)/shard_map/ppermute | solution.py:302
  56.4 1.3 %collective-permute-done.12.refs_7_ = bf16[8,7168]{1,0:T(8,128)(2,1)S(1)} collective-permute-done((bf16[8,7168]{1,0:T(8,128)(2,1)S(1)}, bf16[8,7168]{1,0:T(8,128)(2,1)S(1)}, u32[]{:S(2)}, u32[]{:S(2)}) %collective-permute-start.12) | collective-permute-done | bytes 114720 | tf_op jit(solution)/shard_map/ppermute | solution.py:302
  57.7 2.3 %expert.1 = (f32[8,7168]{1,0:T(8,128)S(1)}, f32[8,7168]{1,0:T(8,128)S(1)}, f32[8,7168]{1,0:T(8,128)S(1)}, f32[8,7168]{1,0:T(8,128)S(1)}, bf16[8,7168]{1,0:T(8,128)(2,1)S(1)}, /*index=5*/bf16[24,7168]{1,0:T(8,128)(2,1)S(1)}) custom-call(bf16[8,7168]{1,0:T(8,128)(2,1)S(1)} %add_convert_fusion.3.refs_0_, bf16[8,7168]{1,0:T(8,128)(2,1)S(1)} %collective-permute-done.6.refs_1_, ...), custom_call_target="tpu_custom_call" | custom-call | flops 704643072 | bytes 11010048 | tf_op jit(solution)/shard_map/expert/pallas_call | solution.py:285
  60.6 0.8 %collective-permute-done.13 = bf16[8,7168]{1,0:T(8,128)(2,1)S(1)} collective-permute-done((bf16[8,7168]{1,0:T(8,128)(2,1)S(1)}, bf16[8,7168]{1,0:T(8,128)(2,1)S(1)}, u32[]{:S(2)}, u32[]{:S(2)}) %collective-permute-start.13) | collective-permute-done | bytes 114720 | tf_op jit(solution)/shard_map/ppermute | solution.py:302
  62.0 1.9 %collective-permute-start.16 = (bf16[8,7168]{1,0:T(8,128)(2,1)S(1)}, bf16[8,7168]{1,0:T(8,128)(2,1)S(1)}, u32[]{:S(2)}, u32[]{:S(2)}) collective-permute-start(bf16[8,7168]{1,0:T(8,128)(2,1)S(1)} %get-tuple-element.28), channel_id=1, source_target_pairs={{0,4},{1,5},{2,6},{3,7},{4,0},{5,1},{6,2},{7,3},{8,12},{9,13},{10,... | collective-permute-start | bytes 344072 | tf_op jit(solution)/shard_map/ppermute | solution.py:302
  63.8 1.3 %collective-permute-start.17 = (bf16[8,7168]{1,0:T(8,128)(2,1)S(1)}, bf16[8,7168]{1,0:T(8,128)(2,1)S(1)}, u32[]{:S(2)}, u32[]{:S(2)}) collective-permute-start(bf16[8,7168]{1,0:T(8,128)(2,1)S(1)} %get-tuple-element.29), channel_id=1, source_target_pairs={{0,2},{1,3},{2,0},{3,1},{4,6},{5,7},{6,4},{7,5},{8,10},{9,11},{10,... | collective-permute-start | bytes 344072 | tf_op jit(solution)/shard_map/ppermute | solution.py:302
  65.9 2.5 %collective-permute-done.14 = bf16[8,7168]{1,0:T(8,128)(2,1)S(1)} collective-permute-done((bf16[8,7168]{1,0:T(8,128)(2,1)S(1)}, bf16[8,7168]{1,0:T(8,128)(2,1)S(1)}, u32[]{:S(2)}, u32[]{:S(2)}) %collective-permute-start.14) | collective-permute-done | bytes 114720 | tf_op jit(solution)/shard_map/ppermute | solution.py:302
  68.4 1.1 %collective-permute-done.16 = bf16[8,7168]{1,0:T(8,128)(2,1)S(1)} collective-permute-done((bf16[8,7168]{1,0:T(8,128)(2,1)S(1)}, bf16[8,7168]{1,0:T(8,128)(2,1)S(1)}, u32[]{:S(2)}, u32[]{:S(2)}) %collective-permute-start.16) | collective-permute-done | bytes 114720 | tf_op jit(solution)/shard_map/ppermute | solution.py:302
  70.4 5.1 %collective-permute-done.18 = bf16[4,7168]{1,0:T(4,128)(2,1)S(1)} collective-permute-done((bf16[4,7168]{1,0:T(4,128)(2,1)S(1)}, bf16[4,7168]{1,0:T(4,128)(2,1)S(1)}, u32[]{:S(2)}, u32[]{:S(2)}) %collective-permute-start.18) | collective-permute-done | bytes 57376 | tf_op jit(solution)/shard_map/ppermute | solution.py:302
  75.4 0.7 add_convert_fusion.7
  (52 shorter events, 4.8 us)
Async XLA Ops:
  0.6 26.6 %slice-start = ((s8[7340032]{0:T(1024)(128)(4,1)}), s8[4194304]{0:T(1024)(128)(4,1)S(1)}, s32[]{:S(2)}) async-start(s8[7340032]{0:T(1024)(128)(4,1)} %bitcast.3), calls=%async_computation.1 | async-start | bytes 8388608
  27.3 30.4 %copy-start = (bf16[7168,256]{1,0:T(8,128)(2,1)S(1)}, bf16[7168,256]{1,0:T(8,128)(2,1)}, u32[]{:S(2)}) copy-start(bf16[7168,256]{1,0:T(8,128)(2,1)} %refs_9_.1) | copy-start | bytes 11010052
  27.3 30.3 %copy-start.1 = (bf16[7168,256]{1,0:T(8,128)(2,1)S(1)}, bf16[7168,256]{1,0:T(8,128)(2,1)}, u32[]{:S(2)}) copy-start(bf16[7168,256]{1,0:T(8,128)(2,1)} %refs_10_.1) | copy-start | bytes 11010052
  27.3 30.3 %copy-start.2 = (bf16[256,7168]{1,0:T(8,128)(2,1)S(1)}, bf16[256,7168]{1,0:T(8,128)(2,1)}, u32[]{:S(2)}) copy-start(bf16[256,7168]{1,0:T(8,128)(2,1)} %refs_11_.1) | copy-start | bytes 11010052
  27.3 30.3 %copy-start.5 = (f32[7168]{0:T(1024)S(1)}, f32[7168]{0:T(1024)}, u32[]{:S(2)}) copy-start(f32[7168]{0:T(1024)} %param.18) | copy-start | bytes 86020
  29.1 1.4 %collective-permute-start = (bf16[8,7168]{1,0:T(8,128)(2,1)S(1)}, bf16[8,7168]{1,0:T(8,128)(2,1)S(1)}, u32[]{:S(2)}, u32[]{:S(2)}) collective-permute-start(bf16[8,7168]{1,0:T(8,128)(2,1)S(1)} %get-tuple-element.15), channel_id=1, source_target_pairs={{0,1},{1,0},{2,3},{3,2},{4,5},{5,4},{6,7},{7,6},{8,9},{9,8},{10,11... | collective-permute-start | bytes 344072 | tf_op jit(solution)/shard_map/ppermute | solution.py:302
  29.1 2.0 %collective-permute-start.2 = (bf16[24,7168]{1,0:T(8,128)(2,1)S(1)}, bf16[24,7168]{1,0:T(8,128)(2,1)S(1)}, u32[]{:S(2)}, u32[]{:S(2)}) collective-permute-start(bf16[24,7168]{1,0:T(8,128)(2,1)S(1)} %get-tuple-element.17), channel_id=1, source_target_pairs={{0,1},{1,0},{2,3},{3,2},{4,5},{5,4},{6,7},{7,6},{8,9},{9,8},{10,11... | collective-permute-start | bytes 1032200 | tf_op jit(solution)/shard_map/ppermute | solution.py:302
  30.5 7.0 %collective-permute-start.1 = (bf16[8,7168]{1,0:T(8,128)(2,1)S(1)}, bf16[8,7168]{1,0:T(8,128)(2,1)S(1)}, u32[]{:S(2)}, u32[]{:S(2)}) collective-permute-start(bf16[8,7168]{1,0:T(8,128)(2,1)S(1)} %add_convert_fusion.6), channel_id=1, source_target_pairs={{0,6},{1,7},{2,4},{3,5},{4,2},{5,3},{6,0},{7,1},{8,14},{9,15},{10,... | collective-permute-start | bytes 344072 | tf_op jit(solution)/shard_map/ppermute | solution.py:302
  31.2 6.8 %collective-permute-start.3 = (bf16[8,7168]{1,0:T(8,128)(2,1)S(1)}, bf16[8,7168]{1,0:T(8,128)(2,1)S(1)}, u32[]{:S(2)}, u32[]{:S(2)}) collective-permute-start(bf16[8,7168]{1,0:T(8,128)(2,1)S(1)} %get-tuple-element.30), channel_id=1, source_target_pairs={{0,4},{1,5},{2,6},{3,7},{4,0},{5,1},{6,2},{7,3},{8,12},{9,13},{10,... | collective-permute-start | bytes 344072 | tf_op jit(solution)/shard_map/ppermute | solution.py:302
  32.3 6.8 %collective-permute-start.4 = (bf16[8,7168]{1,0:T(8,128)(2,1)S(1)}, bf16[8,7168]{1,0:T(8,128)(2,1)S(1)}, u32[]{:S(2)}, u32[]{:S(2)}) collective-permute-start(bf16[8,7168]{1,0:T(8,128)(2,1)S(1)} %get-tuple-element.31), channel_id=1, source_target_pairs={{0,2},{1,3},{2,0},{3,1},{4,6},{5,7},{6,4},{7,5},{8,10},{9,11},{10,... | collective-permute-start | bytes 344072 | tf_op jit(solution)/shard_map/ppermute | solution.py:302
  39.2 8.5 %collective-permute-start.5 = (bf16[8,7168]{1,0:T(8,128)(2,1)S(1)}, bf16[8,7168]{1,0:T(8,128)(2,1)S(1)}, u32[]{:S(2)}, u32[]{:S(2)}) collective-permute-start(bf16[8,7168]{1,0:T(8,128)(2,1)S(1)} %fusion.2), channel_id=1, source_target_pairs={{0,8},{1,9},{2,10},{3,11},{4,12},{5,13},{6,14},{7,15},{8,0},{9,1},... | collective-permute-start | bytes 344072 | tf_op jit(solution)/shard_map/ppermute | solution.py:302
  47.8 7.0 %collective-permute-start.6 = (bf16[8,7168]{1,0:T(8,128)(2,1)S(1)}, bf16[8,7168]{1,0:T(8,128)(2,1)S(1)}, u32[]{:S(2)}, u32[]{:S(2)}) collective-permute-start(bf16[8,7168]{1,0:T(8,128)(2,1)S(1)} %add_convert_fusion.3.refs_0_), channel_id=1, source_target_pairs={{0,6},{1,7},{2,4},{3,5},{4,2},{5,3},{6,0},{7,1},{8,14},{9,15},{10,... | collective-permute-start | bytes 344072 | tf_op jit(solution)/shard_map/ppermute | solution.py:302
  47.9 6.9 %collective-permute-start.7 = (bf16[8,7168]{1,0:T(8,128)(2,1)S(1)}, bf16[8,7168]{1,0:T(8,128)(2,1)S(1)}, u32[]{:S(2)}, u32[]{:S(2)}) collective-permute-start(bf16[8,7168]{1,0:T(8,128)(2,1)S(1)} %add_convert_fusion.3.refs_0_), channel_id=1, source_target_pairs={{0,4},{1,5},{2,6},{3,7},{4,0},{5,1},{6,2},{7,3},{8,12},{9,13},{10,... | collective-permute-start | bytes 344072 | tf_op jit(solution)/shard_map/ppermute | solution.py:302
  49.3 7.1 %collective-permute-start.8 = (bf16[8,7168]{1,0:T(8,128)(2,1)S(1)}, bf16[8,7168]{1,0:T(8,128)(2,1)S(1)}, u32[]{:S(2)}, u32[]{:S(2)}) collective-permute-start(bf16[8,7168]{1,0:T(8,128)(2,1)S(1)} %add_convert_fusion.3.refs_0_), channel_id=1, source_target_pairs={{0,2},{1,3},{2,0},{3,1},{4,6},{5,7},{6,4},{7,5},{8,10},{9,11},{10,... | collective-permute-start | bytes 344072 | tf_op jit(solution)/shard_map/ppermute | solution.py:302
  51.4 5.0 %collective-permute-start.9 = (bf16[8,7168]{1,0:T(8,128)(2,1)S(1)}, bf16[8,7168]{1,0:T(8,128)(2,1)S(1)}, u32[]{:S(2)}, u32[]{:S(2)}) collective-permute-start(bf16[8,7168]{1,0:T(8,128)(2,1)S(1)} %add_convert_fusion.3.refs_0_), channel_id=1, source_target_pairs={{0,1},{1,0},{2,3},{3,2},{4,5},{5,4},{6,7},{7,6},{8,9},{9,8},{10,11... | collective-permute-start | bytes 344072 | tf_op jit(solution)/shard_map/ppermute | solution.py:302
  54.8 1.5 %collective-permute-start.10 = (bf16[8,7168]{1,0:T(8,128)(2,1)S(1)}, bf16[8,7168]{1,0:T(8,128)(2,1)S(1)}, u32[]{:S(2)}, u32[]{:S(2)}) collective-permute-start(bf16[8,7168]{1,0:T(8,128)(2,1)S(1)} %collective-permute-done.6.refs_1_), channel_id=1, source_target_pairs={{0,1},{1,0},{2,3},{3,2},{4,5},{5,4},{6,7},{7,6},{8,9},{9,8},{10,11... | collective-permute-start | bytes 344072 | tf_op jit(solution)/shard_map/ppermute | solution.py:302
  54.8 1.5 %collective-permute-start.11 = (bf16[8,7168]{1,0:T(8,128)(2,1)S(1)}, bf16[8,7168]{1,0:T(8,128)(2,1)S(1)}, u32[]{:S(2)}, u32[]{:S(2)}) collective-permute-start(bf16[8,7168]{1,0:T(8,128)(2,1)S(1)} %collective-permute-done.7.refs_2_), channel_id=1, source_target_pairs={{0,1},{1,0},{2,3},{3,2},{4,5},{5,4},{6,7},{7,6},{8,9},{9,8},{10,11... | collective-permute-start | bytes 344072 | tf_op jit(solution)/shard_map/ppermute | solution.py:302
  56.3 1.3 %collective-permute-start.12 = (bf16[8,7168]{1,0:T(8,128)(2,1)S(1)}, bf16[8,7168]{1,0:T(8,128)(2,1)S(1)}, u32[]{:S(2)}, u32[]{:S(2)}) collective-permute-start(bf16[8,7168]{1,0:T(8,128)(2,1)S(1)} %collective-permute-done.8.refs_3_), channel_id=1, source_target_pairs={{0,1},{1,0},{2,3},{3,2},{4,5},{5,4},{6,7},{7,6},{8,9},{9,8},{10,11... | collective-permute-start | bytes 344072 | tf_op jit(solution)/shard_map/ppermute | solution.py:302
  60.1 1.4 %collective-permute-start.13 = (bf16[8,7168]{1,0:T(8,128)(2,1)S(1)}, bf16[8,7168]{1,0:T(8,128)(2,1)S(1)}, u32[]{:S(2)}, u32[]{:S(2)}) collective-permute-start(bf16[8,7168]{1,0:T(8,128)(2,1)S(1)} %get-tuple-element.21), channel_id=1, source_target_pairs={{0,1},{1,0},{2,3},{3,2},{4,5},{5,4},{6,7},{7,6},{8,9},{9,8},{10,11... | collective-permute-start | bytes 344072 | tf_op jit(solution)/shard_map/ppermute | solution.py:302
  60.3 1.7 %collective-permute-start.15 = (bf16[24,7168]{1,0:T(8,128)(2,1)S(1)}, bf16[24,7168]{1,0:T(8,128)(2,1)S(1)}, u32[]{:S(2)}, u32[]{:S(2)}) collective-permute-start(bf16[24,7168]{1,0:T(8,128)(2,1)S(1)} %get-tuple-element.23), channel_id=1, source_target_pairs={{0,1},{1,0},{2,3},{3,2},{4,5},{5,4},{6,7},{7,6},{8,9},{9,8},{10,11... | collective-permute-start | bytes 1032200 | tf_op jit(solution)/shard_map/ppermute | solution.py:302
  61.5 7.0 %collective-permute-start.14 = (bf16[8,7168]{1,0:T(8,128)(2,1)S(1)}, bf16[8,7168]{1,0:T(8,128)(2,1)S(1)}, u32[]{:S(2)}, u32[]{:S(2)}) collective-permute-start(bf16[8,7168]{1,0:T(8,128)(2,1)S(1)} %add_convert_fusion.2), channel_id=1, source_target_pairs={{0,6},{1,7},{2,4},{3,5},{4,2},{5,3},{6,0},{7,1},{8,14},{9,15},{10,... | collective-permute-start | bytes 344072 | tf_op jit(solution)/shard_map/ppermute | solution.py:302
  62.0 7.6 %collective-permute-start.16 = (bf16[8,7168]{1,0:T(8,128)(2,1)S(1)}, bf16[8,7168]{1,0:T(8,128)(2,1)S(1)}, u32[]{:S(2)}, u32[]{:S(2)}) collective-permute-start(bf16[8,7168]{1,0:T(8,128)(2,1)S(1)} %get-tuple-element.28), channel_id=1, source_target_pairs={{0,4},{1,5},{2,6},{3,7},{4,0},{5,1},{6,2},{7,3},{8,12},{9,13},{10,... | collective-permute-start | bytes 344072 | tf_op jit(solution)/shard_map/ppermute | solution.py:302
  63.8 6.3 %collective-permute-start.17 = (bf16[8,7168]{1,0:T(8,128)(2,1)S(1)}, bf16[8,7168]{1,0:T(8,128)(2,1)S(1)}, u32[]{:S(2)}, u32[]{:S(2)}) collective-permute-start(bf16[8,7168]{1,0:T(8,128)(2,1)S(1)} %get-tuple-element.29), channel_id=1, source_target_pairs={{0,2},{1,3},{2,0},{3,1},{4,6},{5,7},{6,4},{7,5},{8,10},{9,11},{10,... | collective-permute-start | bytes 344072 | tf_op jit(solution)/shard_map/ppermute | solution.py:302
  70.2 5.2 %collective-permute-start.18 = (bf16[4,7168]{1,0:T(4,128)(2,1)S(1)}, bf16[4,7168]{1,0:T(4,128)(2,1)S(1)}, u32[]{:S(2)}, u32[]{:S(2)}) collective-permute-start(bf16[4,7168]{1,0:T(4,128)(2,1)S(1)} %slice.68), channel_id=1, source_target_pairs={{0,8},{1,9},{2,10},{3,11},{4,12},{5,13},{6,14},{7,15},{8,0},{9,1},... | collective-permute-start | bytes 172040 | tf_op jit(solution)/shard_map/ppermute | solution.py:302
  (5 other events, 94.8 us)

commit v15 on v14

--- a/solution.py
+++ b/solution.py
@@ -9,7 +9,7 @@
 
 QK = 192
 FF = 2048
-BLOCK = 256
+BLOCK = 512
 LOWEST = -3e38
 GROUP = 8
 LANES = 128
@@ -313,13 +313,13 @@
     others = [swap(first, 1)] + [
         rest[at * rows : (at + 1) * rows] for at in range(PIECES - 1)
     ]
-    total = 0.0
+    found = []
     for keep, other, distance in zip(keeps, others, SQUARE):
         part = keep + wide(other)
         if distance:
-            part = wide(swap(part.astype(jnp.bfloat16), distance))
-        total = total + part
-    return total
+            part = swap(part.astype(jnp.bfloat16), distance)
+        found.append(part)
+    return found
 
 
 def exchange(total, far):
@@ -366,10 +366,17 @@
     joined = lax.all_to_all(latent, "experts", split_axis=0, concat_axis=0, tiled=True)
     joined = joined.reshape(-1, joined.shape[-1])
     terms = project(joined, w_absorb, residual_in, w_out, all_rows, far)
-    stream = exchange(collect(terms), far)
+    stream = exchange(sum(wide(part) for part in collect(terms)), far)
     attended = stream[:own_rows]
 
-    total = collect(run_expert(spread(stream), norm_gain, w_gate, w_up, w_down))
+    parts = collect(run_expert(spread(stream), norm_gain, w_gate, w_up, w_down))
+    sent = [
+        sum(wide(part[at * own_rows : (at + 1) * own_rows]) for part in parts).astype(
+            jnp.bfloat16
+        )
+        for at in range(1, far)
+    ]
+    *sent, parts = lax.optimization_barrier((*sent, parts))
     own_ids = lax.dynamic_slice_in_dim(expert_ids, rank_here * own_rows, own_rows, 0)
     mixings = []
     for at in range(far):
@@ -379,10 +386,10 @@
                 route_gates * (own_ids == expert).astype(jnp.float32), axis=1, keepdims=True
             )
         )
-    expert_out = lax.optimization_barrier(mixings[0] * total[:own_rows])
+    kept = sum(wide(part[:own_rows]) for part in parts)
+    expert_out = lax.optimization_barrier(mixings[0] * kept)
     for at in range(1, far):
-        block = total[at * own_rows : (at + 1) * own_rows].astype(jnp.bfloat16)
-        expert_out = expert_out + mixings[at] * wide(swap(block, 8 * at))
+        expert_out = expert_out + mixings[at] * wide(swap(sent[at - 1], 8 * at))
     return (attended, expert_out.astype(jnp.bfloat16))
 
 

time: 76.3 us -> 74.4 us (0.975); the launches traced: 76.2 us -> 73.3 us
  blocking collectives: 19.1 us -> 16.5 us
    all_to_all x1, blocking collectives: 19.1 us -> 16.5 us  [shards(): lax.all_to_all(latent, 'experts', split_axis=0, concat_axis=0, tiled=True)]
where the time goes in v15:
time: 74.4 us; the launch traced here: 73.3 us
  waiting for transfers between devices  29 us (39%)
  blocking collectives  16.5 us (22%)
  starting transfers between devices  13.5 us (18%)
  Pallas kernels  11.3 us (15%)
  other arithmetic  1.42 us (2%)
  between operations  0.84 us (1%)
    ppermute x19, waiting for transfers between devices, swap(): return lax.ppermute(array, 'experts', pairs)  29 us
    all_to_all x1, blocking collectives, shards(): lax.all_to_all(latent, 'experts', split_axis=0, concat_axis=0, tiled=True)  16.5 us
    ppermute x19, starting transfers between devices, swap(): return lax.ppermute(array, 'experts', pairs)  13.5 us
    pallas_call x1, Pallas kernels, attend(): pl.pallas_call(attend_kernel, out_shape=jax.ShapeDtypeStruct((devices, pa...  7.24 us
    pallas_call x1, Pallas kernels, run_expert(): pl.pallas_call(expert_kernel, out_shape=term_shapes(rows, width), in_spec...  2.35 us
    pallas_call x1, Pallas kernels, project(): pl.pallas_call(functools.partial(project_kernel, own_rows, far), out_shap...  1.69 us
  transfers between devices with their start and end apart: 19, of which 14 were waited for; matrix products, arithmetic and copies ran while one was open for 1% of the time, Pallas kernels for 0%

profile of v15, /device:TPU:0, one launch (start us, length us, event | category | flops | bytes accessed | tf_op | source)
XLA Modules:
  0.0 73.3 jit_solution(14800520790265105262)
XLA Ops:
  0.7 7.2 %attend.1 = bf16[16,16,512]{2,1,0:T(8,128)(2,1)} custom-call(s32[4]{0:T(128)} %len_ref.1, bf16[4,64,576]{2,1,0:T(8,128)(2,1)} %bitcast.7, bf16[4,576,4096]{2,1,0:T(8,128)(2,1)} %cache_ref.1), custom_call_target="tpu_custom_call" | custom-call | flops 1140850688 | bytes 9437184 | tf_op jit(solution)/shard_map/attend/pallas_call | solution.py:148
  7.9 16.5 %all_to_all.5 = bf16[16,16,512]{2,1,0:T(8,128)(2,1)S(1)} all-to-all(bf16[16,16,512]{2,1,0:T(8,128)(2,1)} %attend.1), channel_id=1, replica_groups=mesh['groups'=2,'experts'=16] {'experts'}, dimensions={0} | all-to-all | bytes 524288 | tf_op jit(solution)/shard_map/all_to_all | solution.py:366
  24.5 1.7 %project.1 = (f32[8,7168]{1,0:T(8,128)S(1)}, f32[8,7168]{1,0:T(8,128)S(1)}, f32[8,7168]{1,0:T(8,128)S(1)}, f32[8,7168]{1,0:T(8,128)S(1)}, bf16[8,7168]{1,0:T(8,128)(2,1)S(1)}, /*index=5*/bf16[24,7168]{1,0:T(8,128)(2,1)S(1)}) custom-call(bf16[256,512]{1,0:T(8,128)(2,1)S(1)} %bitcast.5, bf16[4,7168]{1,0:T(4,128)(2,1)S(1)} %copy-done.4, ...), custom_call_target="tpu_custom_call" | custom-call | flops 469762048 | bytes 7340032 | tf_op jit(solution)/shard_map/project/pallas_call | solution.py:232
  26.7 0.8 %collective-permute-done = bf16[8,7168]{1,0:T(8,128)(2,1)S(1)} collective-permute-done((bf16[8,7168]{1,0:T(8,128)(2,1)S(1)}, bf16[8,7168]{1,0:T(8,128)(2,1)S(1)}, u32[]{:S(2)}, u32[]{:S(2)}) %collective-permute-start) | collective-permute-done | bytes 114720 | tf_op jit(solution)/shard_map/ppermute | solution.py:302
  27.6 0.6 collective-permute-start.1
  28.3 1.1 %collective-permute-start.3 = (bf16[8,7168]{1,0:T(8,128)(2,1)S(1)}, bf16[8,7168]{1,0:T(8,128)(2,1)S(1)}, u32[]{:S(2)}, u32[]{:S(2)}) collective-permute-start(bf16[8,7168]{1,0:T(8,128)(2,1)S(1)} %get-tuple-element.41), channel_id=1, source_target_pairs={{0,4},{1,5},{2,6},{3,7},{4,0},{5,1},{6,2},{7,3},{8,12},{9,13},{10,... | collective-permute-start | bytes 344072 | tf_op jit(solution)/shard_map/ppermute | solution.py:302
  29.4 1.8 %collective-permute-start.4 = (bf16[8,7168]{1,0:T(8,128)(2,1)S(1)}, bf16[8,7168]{1,0:T(8,128)(2,1)S(1)}, u32[]{:S(2)}, u32[]{:S(2)}) collective-permute-start(bf16[8,7168]{1,0:T(8,128)(2,1)S(1)} %get-tuple-element.42), channel_id=1, source_target_pairs={{0,2},{1,3},{2,0},{3,1},{4,6},{5,7},{6,4},{7,5},{8,10},{9,11},{10,... | collective-permute-start | bytes 344072 | tf_op jit(solution)/shard_map/ppermute | solution.py:302
  31.3 3.3 %collective-permute-done.1 = bf16[8,7168]{1,0:T(8,128)(2,1)S(1)} collective-permute-done((bf16[8,7168]{1,0:T(8,128)(2,1)S(1)}, bf16[8,7168]{1,0:T(8,128)(2,1)S(1)}, u32[]{:S(2)}, u32[]{:S(2)}) %collective-permute-start.1) | collective-permute-done | bytes 114720 | tf_op jit(solution)/shard_map/ppermute | solution.py:302
  35.1 1.1 %collective-permute-done.4 = bf16[8,7168]{1,0:T(8,128)(2,1)S(1)} collective-permute-done((bf16[8,7168]{1,0:T(8,128)(2,1)S(1)}, bf16[8,7168]{1,0:T(8,128)(2,1)S(1)}, u32[]{:S(2)}, u32[]{:S(2)}) %collective-permute-start.4) | collective-permute-done | bytes 114720 | tf_op jit(solution)/shard_map/ppermute | solution.py:302
  36.3 1.1 %collective-permute-start.5 = (bf16[8,7168]{1,0:T(8,128)(2,1)S(1)}, bf16[8,7168]{1,0:T(8,128)(2,1)S(1)}, u32[]{:S(2)}, u32[]{:S(2)}) collective-permute-start(bf16[8,7168]{1,0:T(8,128)(2,1)S(1)} %fusion.3), channel_id=1, source_target_pairs={{0,8},{1,9},{2,10},{3,11},{4,12},{5,13},{6,14},{7,15},{8,0},{9,1},... | collective-permute-start | bytes 344072 | tf_op jit(solution)/shard_map/ppermute | solution.py:302
  37.4 7.3 %collective-permute-done.5 = bf16[8,7168]{1,0:T(8,128)(2,1)S(1)} collective-permute-done((bf16[8,7168]{1,0:T(8,128)(2,1)S(1)}, bf16[8,7168]{1,0:T(8,128)(2,1)S(1)}, u32[]{:S(2)}, u32[]{:S(2)}) %collective-permute-start.5) | collective-permute-done | bytes 114720 | tf_op jit(solution)/shard_map/ppermute | solution.py:302
  45.0 1.3 %collective-permute-start.7 = (bf16[8,7168]{1,0:T(8,128)(2,1)S(1)}, bf16[8,7168]{1,0:T(8,128)(2,1)S(1)}, u32[]{:S(2)}, u32[]{:S(2)}) collective-permute-start(bf16[8,7168]{1,0:T(8,128)(2,1)S(1)} %add_convert_fusion.3.refs_0_), channel_id=1, source_target_pairs={{0,4},{1,5},{2,6},{3,7},{4,0},{5,1},{6,2},{7,3},{8,12},{9,13},{10,... | collective-permute-start | bytes 344072 | tf_op jit(solution)/shard_map/ppermute | solution.py:302
  46.4 2.1 %collective-permute-start.8 = (bf16[8,7168]{1,0:T(8,128)(2,1)S(1)}, bf16[8,7168]{1,0:T(8,128)(2,1)S(1)}, u32[]{:S(2)}, u32[]{:S(2)}) collective-permute-start(bf16[8,7168]{1,0:T(8,128)(2,1)S(1)} %add_convert_fusion.3.refs_0_), channel_id=1, source_target_pairs={{0,2},{1,3},{2,0},{3,1},{4,6},{5,7},{6,4},{7,5},{8,10},{9,11},{10,... | collective-permute-start | bytes 344072 | tf_op jit(solution)/shard_map/ppermute | solution.py:302
  48.5 3.4 %collective-permute-done.6.refs_1_ = bf16[8,7168]{1,0:T(8,128)(2,1)S(1)} collective-permute-done((bf16[8,7168]{1,0:T(8,128)(2,1)S(1)}, bf16[8,7168]{1,0:T(8,128)(2,1)S(1)}, u32[]{:S(2)}, u32[]{:S(2)}) %collective-permute-start.6) | collective-permute-done | bytes 114720 | tf_op jit(solution)/shard_map/ppermute | solution.py:302
  52.4 1.0 %collective-permute-done.8.refs_3_ = bf16[8,7168]{1,0:T(8,128)(2,1)S(1)} collective-permute-done((bf16[8,7168]{1,0:T(8,128)(2,1)S(1)}, bf16[8,7168]{1,0:T(8,128)(2,1)S(1)}, u32[]{:S(2)}, u32[]{:S(2)}) %collective-permute-start.8) | collective-permute-done | bytes 114720 | tf_op jit(solution)/shard_map/ppermute | solution.py:302
  53.5 1.3 %collective-permute-done.12.refs_7_ = bf16[8,7168]{1,0:T(8,128)(2,1)S(1)} collective-permute-done((bf16[8,7168]{1,0:T(8,128)(2,1)S(1)}, bf16[8,7168]{1,0:T(8,128)(2,1)S(1)}, u32[]{:S(2)}, u32[]{:S(2)}) %collective-permute-start.12) | collective-permute-done | bytes 114720 | tf_op jit(solution)/shard_map/ppermute | solution.py:302
  54.8 2.3 %expert.1 = (f32[8,7168]{1,0:T(8,128)S(1)}, f32[8,7168]{1,0:T(8,128)S(1)}, f32[8,7168]{1,0:T(8,128)S(1)}, f32[8,7168]{1,0:T(8,128)S(1)}, bf16[8,7168]{1,0:T(8,128)(2,1)S(1)}, /*index=5*/bf16[24,7168]{1,0:T(8,128)(2,1)S(1)}) custom-call(bf16[8,7168]{1,0:T(8,128)(2,1)S(1)} %add_convert_fusion.3.refs_0_, bf16[8,7168]{1,0:T(8,128)(2,1)S(1)} %collective-permute-done.6.refs_1_, ...), custom_call_target="tpu_custom_call" | custom-call | flops 704643072 | bytes 11010048 | tf_op jit(solution)/shard_map/expert/pallas_call | solution.py:285
  57.7 0.8 %collective-permute-done.13 = bf16[8,7168]{1,0:T(8,128)(2,1)S(1)} collective-permute-done((bf16[8,7168]{1,0:T(8,128)(2,1)S(1)}, bf16[8,7168]{1,0:T(8,128)(2,1)S(1)}, u32[]{:S(2)}, u32[]{:S(2)}) %collective-permute-start.13) | collective-permute-done | bytes 114720 | tf_op jit(solution)/shard_map/ppermute | solution.py:302
  59.1 1.9 %collective-permute-start.16 = (bf16[8,7168]{1,0:T(8,128)(2,1)S(1)}, bf16[8,7168]{1,0:T(8,128)(2,1)S(1)}, u32[]{:S(2)}, u32[]{:S(2)}) collective-permute-start(bf16[8,7168]{1,0:T(8,128)(2,1)S(1)} %get-tuple-element.38), channel_id=1, source_target_pairs={{0,4},{1,5},{2,6},{3,7},{4,0},{5,1},{6,2},{7,3},{8,12},{9,13},{10,... | collective-permute-start | bytes 344072 | tf_op jit(solution)/shard_map/ppermute | solution.py:302
  61.0 1.3 %collective-permute-start.17 = (bf16[8,7168]{1,0:T(8,128)(2,1)S(1)}, bf16[8,7168]{1,0:T(8,128)(2,1)S(1)}, u32[]{:S(2)}, u32[]{:S(2)}) collective-permute-start(bf16[8,7168]{1,0:T(8,128)(2,1)S(1)} %get-tuple-element.40), channel_id=1, source_target_pairs={{0,2},{1,3},{2,0},{3,1},{4,6},{5,7},{6,4},{7,5},{8,10},{9,11},{10,... | collective-permute-start | bytes 344072 | tf_op jit(solution)/shard_map/ppermute | solution.py:302
  63.0 2.5 %collective-permute-done.14 = bf16[8,7168]{1,0:T(8,128)(2,1)S(1)} collective-permute-done((bf16[8,7168]{1,0:T(8,128)(2,1)S(1)}, bf16[8,7168]{1,0:T(8,128)(2,1)S(1)}, u32[]{:S(2)}, u32[]{:S(2)}) %collective-permute-start.14) | collective-permute-done | bytes 114720 | tf_op jit(solution)/shard_map/ppermute | solution.py:302
  65.5 1.1 %collective-permute-done.16 = bf16[8,7168]{1,0:T(8,128)(2,1)S(1)} collective-permute-done((bf16[8,7168]{1,0:T(8,128)(2,1)S(1)}, bf16[8,7168]{1,0:T(8,128)(2,1)S(1)}, u32[]{:S(2)}, u32[]{:S(2)}) %collective-permute-start.16) | collective-permute-done | bytes 114720 | tf_op jit(solution)/shard_map/ppermute | solution.py:302
  67.5 5.1 %collective-permute-done.18 = bf16[4,7168]{1,0:T(4,128)(2,1)S(1)} collective-permute-done((bf16[4,7168]{1,0:T(4,128)(2,1)S(1)}, bf16[4,7168]{1,0:T(4,128)(2,1)S(1)}, u32[]{:S(2)}, u32[]{:S(2)}) %collective-permute-start.18) | collective-permute-done | bytes 57376 | tf_op jit(solution)/shard_map/ppermute | solution.py:302
  72.5 0.7 add_convert_fusion.7
  (51 shorter events, 4.9 us)
Async XLA Ops:
  0.6 23.8 %slice-start = ((s8[7340032]{0:T(1024)(128)(4,1)}), s8[4194304]{0:T(1024)(128)(4,1)S(1)}, s32[]{:S(2)}) async-start(s8[7340032]{0:T(1024)(128)(4,1)} %bitcast.3), calls=%async_computation.1 | async-start | bytes 8388608
  24.4 30.4 %copy-start = (bf16[7168,256]{1,0:T(8,128)(2,1)S(1)}, bf16[7168,256]{1,0:T(8,128)(2,1)}, u32[]{:S(2)}) copy-start(bf16[7168,256]{1,0:T(8,128)(2,1)} %refs_9_.1) | copy-start | bytes 11010052
  24.4 30.4 %copy-start.1 = (bf16[7168,256]{1,0:T(8,128)(2,1)S(1)}, bf16[7168,256]{1,0:T(8,128)(2,1)}, u32[]{:S(2)}) copy-start(bf16[7168,256]{1,0:T(8,128)(2,1)} %refs_10_.1) | copy-start | bytes 11010052
  24.4 30.3 %copy-start.2 = (bf16[256,7168]{1,0:T(8,128)(2,1)S(1)}, bf16[256,7168]{1,0:T(8,128)(2,1)}, u32[]{:S(2)}) copy-start(bf16[256,7168]{1,0:T(8,128)(2,1)} %refs_11_.1) | copy-start | bytes 11010052
  24.4 30.3 %copy-start.5 = (f32[7168]{0:T(1024)S(1)}, f32[7168]{0:T(1024)}, u32[]{:S(2)}) copy-start(f32[7168]{0:T(1024)} %param.18) | copy-start | bytes 86020
  26.2 1.4 %collective-permute-start = (bf16[8,7168]{1,0:T(8,128)(2,1)S(1)}, bf16[8,7168]{1,0:T(8,128)(2,1)S(1)}, u32[]{:S(2)}, u32[]{:S(2)}) collective-permute-start(bf16[8,7168]{1,0:T(8,128)(2,1)S(1)} %get-tuple-element.20), channel_id=1, source_target_pairs={{0,1},{1,0},{2,3},{3,2},{4,5},{5,4},{6,7},{7,6},{8,9},{9,8},{10,11... | collective-permute-start | bytes 344072 | tf_op jit(solution)/shard_map/ppermute | solution.py:302
  26.2 2.0 %collective-permute-start.2 = (bf16[24,7168]{1,0:T(8,128)(2,1)S(1)}, bf16[24,7168]{1,0:T(8,128)(2,1)S(1)}, u32[]{:S(2)}, u32[]{:S(2)}) collective-permute-start(bf16[24,7168]{1,0:T(8,128)(2,1)S(1)} %get-tuple-element.22), channel_id=1, source_target_pairs={{0,1},{1,0},{2,3},{3,2},{4,5},{5,4},{6,7},{7,6},{8,9},{9,8},{10,11... | collective-permute-start | bytes 1032200 | tf_op jit(solution)/shard_map/ppermute | solution.py:302
  27.6 7.0 %collective-permute-start.1 = (bf16[8,7168]{1,0:T(8,128)(2,1)S(1)}, bf16[8,7168]{1,0:T(8,128)(2,1)S(1)}, u32[]{:S(2)}, u32[]{:S(2)}) collective-permute-start(bf16[8,7168]{1,0:T(8,128)(2,1)S(1)} %add_convert_fusion.6), channel_id=1, source_target_pairs={{0,6},{1,7},{2,4},{3,5},{4,2},{5,3},{6,0},{7,1},{8,14},{9,15},{10,... | collective-permute-start | bytes 344072 | tf_op jit(solution)/shard_map/ppermute | solution.py:302
  28.3 6.8 %collective-permute-start.3 = (bf16[8,7168]{1,0:T(8,128)(2,1)S(1)}, bf16[8,7168]{1,0:T(8,128)(2,1)S(1)}, u32[]{:S(2)}, u32[]{:S(2)}) collective-permute-start(bf16[8,7168]{1,0:T(8,128)(2,1)S(1)} %get-tuple-element.41), channel_id=1, source_target_pairs={{0,4},{1,5},{2,6},{3,7},{4,0},{5,1},{6,2},{7,3},{8,12},{9,13},{10,... | collective-permute-start | bytes 344072 | tf_op jit(solution)/shard_map/ppermute | solution.py:302
  29.4 6.8 %collective-permute-start.4 = (bf16[8,7168]{1,0:T(8,128)(2,1)S(1)}, bf16[8,7168]{1,0:T(8,128)(2,1)S(1)}, u32[]{:S(2)}, u32[]{:S(2)}) collective-permute-start(bf16[8,7168]{1,0:T(8,128)(2,1)S(1)} %get-tuple-element.42), channel_id=1, source_target_pairs={{0,2},{1,3},{2,0},{3,1},{4,6},{5,7},{6,4},{7,5},{8,10},{9,11},{10,... | collective-permute-start | bytes 344072 | tf_op jit(solution)/shard_map/ppermute | solution.py:302
  36.3 8.5 %collective-permute-start.5 = (bf16[8,7168]{1,0:T(8,128)(2,1)S(1)}, bf16[8,7168]{1,0:T(8,128)(2,1)S(1)}, u32[]{:S(2)}, u32[]{:S(2)}) collective-permute-start(bf16[8,7168]{1,0:T(8,128)(2,1)S(1)} %fusion.3), channel_id=1, source_target_pairs={{0,8},{1,9},{2,10},{3,11},{4,12},{5,13},{6,14},{7,15},{8,0},{9,1},... | collective-permute-start | bytes 344072 | tf_op jit(solution)/shard_map/ppermute | solution.py:302
  44.9 7.0 %collective-permute-start.6 = (bf16[8,7168]{1,0:T(8,128)(2,1)S(1)}, bf16[8,7168]{1,0:T(8,128)(2,1)S(1)}, u32[]{:S(2)}, u32[]{:S(2)}) collective-permute-start(bf16[8,7168]{1,0:T(8,128)(2,1)S(1)} %add_convert_fusion.3.refs_0_), channel_id=1, source_target_pairs={{0,6},{1,7},{2,4},{3,5},{4,2},{5,3},{6,0},{7,1},{8,14},{9,15},{10,... | collective-permute-start | bytes 344072 | tf_op jit(solution)/shard_map/ppermute | solution.py:302
  45.0 6.9 %collective-permute-start.7 = (bf16[8,7168]{1,0:T(8,128)(2,1)S(1)}, bf16[8,7168]{1,0:T(8,128)(2,1)S(1)}, u32[]{:S(2)}, u32[]{:S(2)}) collective-permute-start(bf16[8,7168]{1,0:T(8,128)(2,1)S(1)} %add_convert_fusion.3.refs_0_), channel_id=1, source_target_pairs={{0,4},{1,5},{2,6},{3,7},{4,0},{5,1},{6,2},{7,3},{8,12},{9,13},{10,... | collective-permute-start | bytes 344072 | tf_op jit(solution)/shard_map/ppermute | solution.py:302
  46.4 7.1 %collective-permute-start.8 = (bf16[8,7168]{1,0:T(8,128)(2,1)S(1)}, bf16[8,7168]{1,0:T(8,128)(2,1)S(1)}, u32[]{:S(2)}, u32[]{:S(2)}) collective-permute-start(bf16[8,7168]{1,0:T(8,128)(2,1)S(1)} %add_convert_fusion.3.refs_0_), channel_id=1, source_target_pairs={{0,2},{1,3},{2,0},{3,1},{4,6},{5,7},{6,4},{7,5},{8,10},{9,11},{10,... | collective-permute-start | bytes 344072 | tf_op jit(solution)/shard_map/ppermute | solution.py:302
  48.5 5.0 %collective-permute-start.9 = (bf16[8,7168]{1,0:T(8,128)(2,1)S(1)}, bf16[8,7168]{1,0:T(8,128)(2,1)S(1)}, u32[]{:S(2)}, u32[]{:S(2)}) collective-permute-start(bf16[8,7168]{1,0:T(8,128)(2,1)S(1)} %add_convert_fusion.3.refs_0_), channel_id=1, source_target_pairs={{0,1},{1,0},{2,3},{3,2},{4,5},{5,4},{6,7},{7,6},{8,9},{9,8},{10,11... | collective-permute-start | bytes 344072 | tf_op jit(solution)/shard_map/ppermute | solution.py:302
  51.9 1.5 %collective-permute-start.10 = (bf16[8,7168]{1,0:T(8,128)(2,1)S(1)}, bf16[8,7168]{1,0:T(8,128)(2,1)S(1)}, u32[]{:S(2)}, u32[]{:S(2)}) collective-permute-start(bf16[8,7168]{1,0:T(8,128)(2,1)S(1)} %collective-permute-done.6.refs_1_), channel_id=1, source_target_pairs={{0,1},{1,0},{2,3},{3,2},{4,5},{5,4},{6,7},{7,6},{8,9},{9,8},{10,11... | collective-permute-start | bytes 344072 | tf_op jit(solution)/shard_map/ppermute | solution.py:302
  51.9 1.5 %collective-permute-start.11 = (bf16[8,7168]{1,0:T(8,128)(2,1)S(1)}, bf16[8,7168]{1,0:T(8,128)(2,1)S(1)}, u32[]{:S(2)}, u32[]{:S(2)}) collective-permute-start(bf16[8,7168]{1,0:T(8,128)(2,1)S(1)} %collective-permute-done.7.refs_2_), channel_id=1, source_target_pairs={{0,1},{1,0},{2,3},{3,2},{4,5},{5,4},{6,7},{7,6},{8,9},{9,8},{10,11... | collective-permute-start | bytes 344072 | tf_op jit(solution)/shard_map/ppermute | solution.py:302
  53.4 1.3 %collective-permute-start.12 = (bf16[8,7168]{1,0:T(8,128)(2,1)S(1)}, bf16[8,7168]{1,0:T(8,128)(2,1)S(1)}, u32[]{:S(2)}, u32[]{:S(2)}) collective-permute-start(bf16[8,7168]{1,0:T(8,128)(2,1)S(1)} %collective-permute-done.8.refs_3_), channel_id=1, source_target_pairs={{0,1},{1,0},{2,3},{3,2},{4,5},{5,4},{6,7},{7,6},{8,9},{9,8},{10,11... | collective-permute-start | bytes 344072 | tf_op jit(solution)/shard_map/ppermute | solution.py:302
  57.2 1.4 %collective-permute-start.13 = (bf16[8,7168]{1,0:T(8,128)(2,1)S(1)}, bf16[8,7168]{1,0:T(8,128)(2,1)S(1)}, u32[]{:S(2)}, u32[]{:S(2)}) collective-permute-start(bf16[8,7168]{1,0:T(8,128)(2,1)S(1)} %get-tuple-element.26), channel_id=1, source_target_pairs={{0,1},{1,0},{2,3},{3,2},{4,5},{5,4},{6,7},{7,6},{8,9},{9,8},{10,11... | collective-permute-start | bytes 344072 | tf_op jit(solution)/shard_map/ppermute | solution.py:302
  57.4 1.7 %collective-permute-start.15 = (bf16[24,7168]{1,0:T(8,128)(2,1)S(1)}, bf16[24,7168]{1,0:T(8,128)(2,1)S(1)}, u32[]{:S(2)}, u32[]{:S(2)}) collective-permute-start(bf16[24,7168]{1,0:T(8,128)(2,1)S(1)} %get-tuple-element.28), channel_id=1, source_target_pairs={{0,1},{1,0},{2,3},{3,2},{4,5},{5,4},{6,7},{7,6},{8,9},{9,8},{10,11... | collective-permute-start | bytes 1032200 | tf_op jit(solution)/shard_map/ppermute | solution.py:302
  58.6 7.0 %collective-permute-start.14 = (bf16[8,7168]{1,0:T(8,128)(2,1)S(1)}, bf16[8,7168]{1,0:T(8,128)(2,1)S(1)}, u32[]{:S(2)}, u32[]{:S(2)}) collective-permute-start(bf16[8,7168]{1,0:T(8,128)(2,1)S(1)} %add_convert_fusion.2), channel_id=1, source_target_pairs={{0,6},{1,7},{2,4},{3,5},{4,2},{5,3},{6,0},{7,1},{8,14},{9,15},{10,... | collective-permute-start | bytes 344072 | tf_op jit(solution)/shard_map/ppermute | solution.py:302
  59.1 7.5 %collective-permute-start.16 = (bf16[8,7168]{1,0:T(8,128)(2,1)S(1)}, bf16[8,7168]{1,0:T(8,128)(2,1)S(1)}, u32[]{:S(2)}, u32[]{:S(2)}) collective-permute-start(bf16[8,7168]{1,0:T(8,128)(2,1)S(1)} %get-tuple-element.38), channel_id=1, source_target_pairs={{0,4},{1,5},{2,6},{3,7},{4,0},{5,1},{6,2},{7,3},{8,12},{9,13},{10,... | collective-permute-start | bytes 344072 | tf_op jit(solution)/shard_map/ppermute | solution.py:302
  61.0 6.2 %collective-permute-start.17 = (bf16[8,7168]{1,0:T(8,128)(2,1)S(1)}, bf16[8,7168]{1,0:T(8,128)(2,1)S(1)}, u32[]{:S(2)}, u32[]{:S(2)}) collective-permute-start(bf16[8,7168]{1,0:T(8,128)(2,1)S(1)} %get-tuple-element.40), channel_id=1, source_target_pairs={{0,2},{1,3},{2,0},{3,1},{4,6},{5,7},{6,4},{7,5},{8,10},{9,11},{10,... | collective-permute-start | bytes 344072 | tf_op jit(solution)/shard_map/ppermute | solution.py:302
  67.3 5.2 %collective-permute-start.18 = (bf16[4,7168]{1,0:T(4,128)(2,1)S(1)}, bf16[4,7168]{1,0:T(4,128)(2,1)S(1)}, u32[]{:S(2)}, u32[]{:S(2)}) collective-permute-start(bf16[4,7168]{1,0:T(4,128)(2,1)S(1)} %fusion), channel_id=1, source_target_pairs={{0,8},{1,9},{2,10},{3,11},{4,12},{5,13},{6,14},{7,15},{8,0},{9,1},... | collective-permute-start | bytes 172040 | tf_op jit(solution)/shard_map/ppermute | solution.py:302
  (5 other events, 86.2 us)

commit v16 on v15

--- a/solution.py
+++ b/solution.py
@@ -126,11 +126,9 @@
     visit(0, own_rows)
     rest = items - own_rows
     lax.fori_loop(0, rest // GROUP, visit_group, 0)
-    many = GROUP // 2
-    while many:
-        first = own_rows + rest // (2 * many) * (2 * many)
-        pl.when((rest & many) != 0)(functools.partial(visit, first, many))
-        many //= 2
+    left = rest % GROUP
+    for many in range(1, GROUP):
+        pl.when(left == many)(functools.partial(visit, items - many, many))
     for row in range(own_rows):
         latent = summed[row] * (1.0 / jnp.sum(sums[row], axis=1, keepdims=True))
         for device in range(devices):

time: 74.4 us -> 74.7 us (level)
  Pallas kernels: 11.3 us -> 12.5 us
    pallas_call x1, Pallas kernels: 7.24 us -> 8.46 us  [attend(): pl.pallas_call(attend_kernel, out_shape=jax.ShapeDtypeStruct((devices, pa...]
where the time goes in v16:
time: 74.7 us; the launch traced here: 74.3 us
  waiting for transfers between devices  29 us (39%)
  blocking collectives  16.2 us (22%)
  starting transfers between devices  13.5 us (18%)
  Pallas kernels  12.5 us (17%)
  other arithmetic  1.42 us (2%)
  between operations  0.84 us (1%)
    ppermute x19, waiting for transfers between devices, swap(): return lax.ppermute(array, 'experts', pairs)  29 us
    all_to_all x1, blocking collectives, shards(): lax.all_to_all(latent, 'experts', split_axis=0, concat_axis=0, tiled=True)  16.2 us
    ppermute x19, starting transfers between devices, swap(): return lax.ppermute(array, 'experts', pairs)  13.5 us
    pallas_call x1, Pallas kernels, attend(): pl.pallas_call(attend_kernel, out_shape=jax.ShapeDtypeStruct((devices, pa...  8.46 us
    pallas_call x1, Pallas kernels, run_expert(): pl.pallas_call(expert_kernel, out_shape=term_shapes(rows, width), in_spec...  2.34 us
    pallas_call x1, Pallas kernels, project(): pl.pallas_call(functools.partial(project_kernel, own_rows, far), out_shap...  1.69 us
  transfers between devices with their start and end apart: 19, of which 14 were waited for; matrix products, arithmetic and copies ran while one was open for 1% of the time, Pallas kernels for 0%

profile of v16, /device:TPU:0, one launch (start us, length us, event | category | flops | bytes accessed | tf_op | source)
XLA Modules:
  0.0 74.3 jit_solution(1694960992671009460)
XLA Ops:
  0.7 8.5 %attend.1 = bf16[16,16,512]{2,1,0:T(8,128)(2,1)} custom-call(s32[4]{0:T(128)} %len_ref.1, bf16[4,64,576]{2,1,0:T(8,128)(2,1)} %bitcast.7, bf16[4,576,4096]{2,1,0:T(8,128)(2,1)} %cache_ref.1), custom_call_target="tpu_custom_call" | custom-call | flops 1140850688 | bytes 9437184 | tf_op jit(solution)/shard_map/attend/pallas_call | solution.py:146
  9.1 16.2 %all_to_all.5 = bf16[16,16,512]{2,1,0:T(8,128)(2,1)S(1)} all-to-all(bf16[16,16,512]{2,1,0:T(8,128)(2,1)} %attend.1), channel_id=1, replica_groups=mesh['groups'=2,'experts'=16] {'experts'}, dimensions={0} | all-to-all | bytes 524288 | tf_op jit(solution)/shard_map/all_to_all | solution.py:364
  25.5 1.7 %project.1 = (f32[8,7168]{1,0:T(8,128)S(1)}, f32[8,7168]{1,0:T(8,128)S(1)}, f32[8,7168]{1,0:T(8,128)S(1)}, f32[8,7168]{1,0:T(8,128)S(1)}, bf16[8,7168]{1,0:T(8,128)(2,1)S(1)}, /*index=5*/bf16[24,7168]{1,0:T(8,128)(2,1)S(1)}) custom-call(bf16[256,512]{1,0:T(8,128)(2,1)S(1)} %bitcast.5, bf16[4,7168]{1,0:T(4,128)(2,1)S(1)} %copy-done.4, ...), custom_call_target="tpu_custom_call" | custom-call | flops 469762048 | bytes 7340032 | tf_op jit(solution)/shard_map/project/pallas_call | solution.py:230
  27.7 0.8 %collective-permute-done = bf16[8,7168]{1,0:T(8,128)(2,1)S(1)} collective-permute-done((bf16[8,7168]{1,0:T(8,128)(2,1)S(1)}, bf16[8,7168]{1,0:T(8,128)(2,1)S(1)}, u32[]{:S(2)}, u32[]{:S(2)}) %collective-permute-start) | collective-permute-done | bytes 114720 | tf_op jit(solution)/shard_map/ppermute | solution.py:300
  28.6 0.7 collective-permute-start.1
  29.3 1.1 %collective-permute-start.3 = (bf16[8,7168]{1,0:T(8,128)(2,1)S(1)}, bf16[8,7168]{1,0:T(8,128)(2,1)S(1)}, u32[]{:S(2)}, u32[]{:S(2)}) collective-permute-start(bf16[8,7168]{1,0:T(8,128)(2,1)S(1)} %get-tuple-element.41), channel_id=1, source_target_pairs={{0,4},{1,5},{2,6},{3,7},{4,0},{5,1},{6,2},{7,3},{8,12},{9,13},{10,... | collective-permute-start | bytes 344072 | tf_op jit(solution)/shard_map/ppermute | solution.py:300
  30.4 1.8 %collective-permute-start.4 = (bf16[8,7168]{1,0:T(8,128)(2,1)S(1)}, bf16[8,7168]{1,0:T(8,128)(2,1)S(1)}, u32[]{:S(2)}, u32[]{:S(2)}) collective-permute-start(bf16[8,7168]{1,0:T(8,128)(2,1)S(1)} %get-tuple-element.42), channel_id=1, source_target_pairs={{0,2},{1,3},{2,0},{3,1},{4,6},{5,7},{6,4},{7,5},{8,10},{9,11},{10,... | collective-permute-start | bytes 344072 | tf_op jit(solution)/shard_map/ppermute | solution.py:300
  32.3 3.3 %collective-permute-done.1 = bf16[8,7168]{1,0:T(8,128)(2,1)S(1)} collective-permute-done((bf16[8,7168]{1,0:T(8,128)(2,1)S(1)}, bf16[8,7168]{1,0:T(8,128)(2,1)S(1)}, u32[]{:S(2)}, u32[]{:S(2)}) %collective-permute-start.1) | collective-permute-done | bytes 114720 | tf_op jit(solution)/shard_map/ppermute | solution.py:300
  36.1 1.1 %collective-permute-done.4 = bf16[8,7168]{1,0:T(8,128)(2,1)S(1)} collective-permute-done((bf16[8,7168]{1,0:T(8,128)(2,1)S(1)}, bf16[8,7168]{1,0:T(8,128)(2,1)S(1)}, u32[]{:S(2)}, u32[]{:S(2)}) %collective-permute-start.4) | collective-permute-done | bytes 114720 | tf_op jit(solution)/shard_map/ppermute | solution.py:300
  37.3 1.1 %collective-permute-start.5 = (bf16[8,7168]{1,0:T(8,128)(2,1)S(1)}, bf16[8,7168]{1,0:T(8,128)(2,1)S(1)}, u32[]{:S(2)}, u32[]{:S(2)}) collective-permute-start(bf16[8,7168]{1,0:T(8,128)(2,1)S(1)} %fusion.3), channel_id=1, source_target_pairs={{0,8},{1,9},{2,10},{3,11},{4,12},{5,13},{6,14},{7,15},{8,0},{9,1},... | collective-permute-start | bytes 344072 | tf_op jit(solution)/shard_map/ppermute | solution.py:300
  38.4 7.3 %collective-permute-done.5 = bf16[8,7168]{1,0:T(8,128)(2,1)S(1)} collective-permute-done((bf16[8,7168]{1,0:T(8,128)(2,1)S(1)}, bf16[8,7168]{1,0:T(8,128)(2,1)S(1)}, u32[]{:S(2)}, u32[]{:S(2)}) %collective-permute-start.5) | collective-permute-done | bytes 114720 | tf_op jit(solution)/shard_map/ppermute | solution.py:300
  46.0 1.3 %collective-permute-start.7 = (bf16[8,7168]{1,0:T(8,128)(2,1)S(1)}, bf16[8,7168]{1,0:T(8,128)(2,1)S(1)}, u32[]{:S(2)}, u32[]{:S(2)}) collective-permute-start(bf16[8,7168]{1,0:T(8,128)(2,1)S(1)} %add_convert_fusion.3.refs_0_), channel_id=1, source_target_pairs={{0,4},{1,5},{2,6},{3,7},{4,0},{5,1},{6,2},{7,3},{8,12},{9,13},{10,... | collective-permute-start | bytes 344072 | tf_op jit(solution)/shard_map/ppermute | solution.py:300
  47.4 2.1 %collective-permute-start.8 = (bf16[8,7168]{1,0:T(8,128)(2,1)S(1)}, bf16[8,7168]{1,0:T(8,128)(2,1)S(1)}, u32[]{:S(2)}, u32[]{:S(2)}) collective-permute-start(bf16[8,7168]{1,0:T(8,128)(2,1)S(1)} %add_convert_fusion.3.refs_0_), channel_id=1, source_target_pairs={{0,2},{1,3},{2,0},{3,1},{4,6},{5,7},{6,4},{7,5},{8,10},{9,11},{10,... | collective-permute-start | bytes 344072 | tf_op jit(solution)/shard_map/ppermute | solution.py:300
  49.5 3.4 %collective-permute-done.6.refs_1_ = bf16[8,7168]{1,0:T(8,128)(2,1)S(1)} collective-permute-done((bf16[8,7168]{1,0:T(8,128)(2,1)S(1)}, bf16[8,7168]{1,0:T(8,128)(2,1)S(1)}, u32[]{:S(2)}, u32[]{:S(2)}) %collective-permute-start.6) | collective-permute-done | bytes 114720 | tf_op jit(solution)/shard_map/ppermute | solution.py:300
  53.4 1.0 %collective-permute-done.8.refs_3_ = bf16[8,7168]{1,0:T(8,128)(2,1)S(1)} collective-permute-done((bf16[8,7168]{1,0:T(8,128)(2,1)S(1)}, bf16[8,7168]{1,0:T(8,128)(2,1)S(1)}, u32[]{:S(2)}, u32[]{:S(2)}) %collective-permute-start.8) | collective-permute-done | bytes 114720 | tf_op jit(solution)/shard_map/ppermute | solution.py:300
  54.5 1.3 %collective-permute-done.12.refs_7_ = bf16[8,7168]{1,0:T(8,128)(2,1)S(1)} collective-permute-done((bf16[8,7168]{1,0:T(8,128)(2,1)S(1)}, bf16[8,7168]{1,0:T(8,128)(2,1)S(1)}, u32[]{:S(2)}, u32[]{:S(2)}) %collective-permute-start.12) | collective-permute-done | bytes 114720 | tf_op jit(solution)/shard_map/ppermute | solution.py:300
  55.8 2.3 %expert.1 = (f32[8,7168]{1,0:T(8,128)S(1)}, f32[8,7168]{1,0:T(8,128)S(1)}, f32[8,7168]{1,0:T(8,128)S(1)}, f32[8,7168]{1,0:T(8,128)S(1)}, bf16[8,7168]{1,0:T(8,128)(2,1)S(1)}, /*index=5*/bf16[24,7168]{1,0:T(8,128)(2,1)S(1)}) custom-call(bf16[8,7168]{1,0:T(8,128)(2,1)S(1)} %add_convert_fusion.3.refs_0_, bf16[8,7168]{1,0:T(8,128)(2,1)S(1)} %collective-permute-done.6.refs_1_, ...), custom_call_target="tpu_custom_call" | custom-call | flops 704643072 | bytes 11010048 | tf_op jit(solution)/shard_map/expert/pallas_call | solution.py:283
  58.7 0.8 %collective-permute-done.13 = bf16[8,7168]{1,0:T(8,128)(2,1)S(1)} collective-permute-done((bf16[8,7168]{1,0:T(8,128)(2,1)S(1)}, bf16[8,7168]{1,0:T(8,128)(2,1)S(1)}, u32[]{:S(2)}, u32[]{:S(2)}) %collective-permute-start.13) | collective-permute-done | bytes 114720 | tf_op jit(solution)/shard_map/ppermute | solution.py:300
  60.1 1.9 %collective-permute-start.16 = (bf16[8,7168]{1,0:T(8,128)(2,1)S(1)}, bf16[8,7168]{1,0:T(8,128)(2,1)S(1)}, u32[]{:S(2)}, u32[]{:S(2)}) collective-permute-start(bf16[8,7168]{1,0:T(8,128)(2,1)S(1)} %get-tuple-element.38), channel_id=1, source_target_pairs={{0,4},{1,5},{2,6},{3,7},{4,0},{5,1},{6,2},{7,3},{8,12},{9,13},{10,... | collective-permute-start | bytes 344072 | tf_op jit(solution)/shard_map/ppermute | solution.py:300
  62.0 1.3 %collective-permute-start.17 = (bf16[8,7168]{1,0:T(8,128)(2,1)S(1)}, bf16[8,7168]{1,0:T(8,128)(2,1)S(1)}, u32[]{:S(2)}, u32[]{:S(2)}) collective-permute-start(bf16[8,7168]{1,0:T(8,128)(2,1)S(1)} %get-tuple-element.40), channel_id=1, source_target_pairs={{0,2},{1,3},{2,0},{3,1},{4,6},{5,7},{6,4},{7,5},{8,10},{9,11},{10,... | collective-permute-start | bytes 344072 | tf_op jit(solution)/shard_map/ppermute | solution.py:300
  64.0 2.5 %collective-permute-done.14 = bf16[8,7168]{1,0:T(8,128)(2,1)S(1)} collective-permute-done((bf16[8,7168]{1,0:T(8,128)(2,1)S(1)}, bf16[8,7168]{1,0:T(8,128)(2,1)S(1)}, u32[]{:S(2)}, u32[]{:S(2)}) %collective-permute-start.14) | collective-permute-done | bytes 114720 | tf_op jit(solution)/shard_map/ppermute | solution.py:300
  66.5 1.1 %collective-permute-done.16 = bf16[8,7168]{1,0:T(8,128)(2,1)S(1)} collective-permute-done((bf16[8,7168]{1,0:T(8,128)(2,1)S(1)}, bf16[8,7168]{1,0:T(8,128)(2,1)S(1)}, u32[]{:S(2)}, u32[]{:S(2)}) %collective-permute-start.16) | collective-permute-done | bytes 114720 | tf_op jit(solution)/shard_map/ppermute | solution.py:300
  68.5 5.1 %collective-permute-done.18 = bf16[4,7168]{1,0:T(4,128)(2,1)S(1)} collective-permute-done((bf16[4,7168]{1,0:T(4,128)(2,1)S(1)}, bf16[4,7168]{1,0:T(4,128)(2,1)S(1)}, u32[]{:S(2)}, u32[]{:S(2)}) %collective-permute-start.18) | collective-permute-done | bytes 57376 | tf_op jit(solution)/shard_map/ppermute | solution.py:300
  73.5 0.7 add_convert_fusion.7
  (51 shorter events, 4.9 us)
Async XLA Ops:
  0.6 24.8 %slice-start = ((s8[7340032]{0:T(1024)(128)(4,1)}), s8[4194304]{0:T(1024)(128)(4,1)S(1)}, s32[]{:S(2)}) async-start(s8[7340032]{0:T(1024)(128)(4,1)} %bitcast.3), calls=%async_computation.1 | async-start | bytes 8388608
  25.4 30.4 %copy-start = (bf16[7168,256]{1,0:T(8,128)(2,1)S(1)}, bf16[7168,256]{1,0:T(8,128)(2,1)}, u32[]{:S(2)}) copy-start(bf16[7168,256]{1,0:T(8,128)(2,1)} %refs_9_.1) | copy-start | bytes 11010052
  25.4 30.3 %copy-start.1 = (bf16[7168,256]{1,0:T(8,128)(2,1)S(1)}, bf16[7168,256]{1,0:T(8,128)(2,1)}, u32[]{:S(2)}) copy-start(bf16[7168,256]{1,0:T(8,128)(2,1)} %refs_10_.1) | copy-start | bytes 11010052
  25.4 30.3 %copy-start.2 = (bf16[256,7168]{1,0:T(8,128)(2,1)S(1)}, bf16[256,7168]{1,0:T(8,128)(2,1)}, u32[]{:S(2)}) copy-start(bf16[256,7168]{1,0:T(8,128)(2,1)} %refs_11_.1) | copy-start | bytes 11010052
  25.5 30.3 %copy-start.5 = (f32[7168]{0:T(1024)S(1)}, f32[7168]{0:T(1024)}, u32[]{:S(2)}) copy-start(f32[7168]{0:T(1024)} %param.18) | copy-start | bytes 86020
  27.2 1.4 %collective-permute-start = (bf16[8,7168]{1,0:T(8,128)(2,1)S(1)}, bf16[8,7168]{1,0:T(8,128)(2,1)S(1)}, u32[]{:S(2)}, u32[]{:S(2)}) collective-permute-start(bf16[8,7168]{1,0:T(8,128)(2,1)S(1)} %get-tuple-element.20), channel_id=1, source_target_pairs={{0,1},{1,0},{2,3},{3,2},{4,5},{5,4},{6,7},{7,6},{8,9},{9,8},{10,11... | collective-permute-start | bytes 344072 | tf_op jit(solution)/shard_map/ppermute | solution.py:300
  27.2 2.0 %collective-permute-start.2 = (bf16[24,7168]{1,0:T(8,128)(2,1)S(1)}, bf16[24,7168]{1,0:T(8,128)(2,1)S(1)}, u32[]{:S(2)}, u32[]{:S(2)}) collective-permute-start(bf16[24,7168]{1,0:T(8,128)(2,1)S(1)} %get-tuple-element.22), channel_id=1, source_target_pairs={{0,1},{1,0},{2,3},{3,2},{4,5},{5,4},{6,7},{7,6},{8,9},{9,8},{10,11... | collective-permute-start | bytes 1032200 | tf_op jit(solution)/shard_map/ppermute | solution.py:300
  28.6 7.0 %collective-permute-start.1 = (bf16[8,7168]{1,0:T(8,128)(2,1)S(1)}, bf16[8,7168]{1,0:T(8,128)(2,1)S(1)}, u32[]{:S(2)}, u32[]{:S(2)}) collective-permute-start(bf16[8,7168]{1,0:T(8,128)(2,1)S(1)} %add_convert_fusion.6), channel_id=1, source_target_pairs={{0,6},{1,7},{2,4},{3,5},{4,2},{5,3},{6,0},{7,1},{8,14},{9,15},{10,... | collective-permute-start | bytes 344072 | tf_op jit(solution)/shard_map/ppermute | solution.py:300
  29.3 6.8 %collective-permute-start.3 = (bf16[8,7168]{1,0:T(8,128)(2,1)S(1)}, bf16[8,7168]{1,0:T(8,128)(2,1)S(1)}, u32[]{:S(2)}, u32[]{:S(2)}) collective-permute-start(bf16[8,7168]{1,0:T(8,128)(2,1)S(1)} %get-tuple-element.41), channel_id=1, source_target_pairs={{0,4},{1,5},{2,6},{3,7},{4,0},{5,1},{6,2},{7,3},{8,12},{9,13},{10,... | collective-permute-start | bytes 344072 | tf_op jit(solution)/shard_map/ppermute | solution.py:300
  30.4 6.8 %collective-permute-start.4 = (bf16[8,7168]{1,0:T(8,128)(2,1)S(1)}, bf16[8,7168]{1,0:T(8,128)(2,1)S(1)}, u32[]{:S(2)}, u32[]{:S(2)}) collective-permute-start(bf16[8,7168]{1,0:T(8,128)(2,1)S(1)} %get-tuple-element.42), channel_id=1, source_target_pairs={{0,2},{1,3},{2,0},{3,1},{4,6},{5,7},{6,4},{7,5},{8,10},{9,11},{10,... | collective-permute-start | bytes 344072 | tf_op jit(solution)/shard_map/ppermute | solution.py:300
  37.3 8.5 %collective-permute-start.5 = (bf16[8,7168]{1,0:T(8,128)(2,1)S(1)}, bf16[8,7168]{1,0:T(8,128)(2,1)S(1)}, u32[]{:S(2)}, u32[]{:S(2)}) collective-permute-start(bf16[8,7168]{1,0:T(8,128)(2,1)S(1)} %fusion.3), channel_id=1, source_target_pairs={{0,8},{1,9},{2,10},{3,11},{4,12},{5,13},{6,14},{7,15},{8,0},{9,1},... | collective-permute-start | bytes 344072 | tf_op jit(solution)/shard_map/ppermute | solution.py:300
  46.0 7.0 %collective-permute-start.6 = (bf16[8,7168]{1,0:T(8,128)(2,1)S(1)}, bf16[8,7168]{1,0:T(8,128)(2,1)S(1)}, u32[]{:S(2)}, u32[]{:S(2)}) collective-permute-start(bf16[8,7168]{1,0:T(8,128)(2,1)S(1)} %add_convert_fusion.3.refs_0_), channel_id=1, source_target_pairs={{0,6},{1,7},{2,4},{3,5},{4,2},{5,3},{6,0},{7,1},{8,14},{9,15},{10,... | collective-permute-start | bytes 344072 | tf_op jit(solution)/shard_map/ppermute | solution.py:300
  46.0 6.9 %collective-permute-start.7 = (bf16[8,7168]{1,0:T(8,128)(2,1)S(1)}, bf16[8,7168]{1,0:T(8,128)(2,1)S(1)}, u32[]{:S(2)}, u32[]{:S(2)}) collective-permute-start(bf16[8,7168]{1,0:T(8,128)(2,1)S(1)} %add_convert_fusion.3.refs_0_), channel_id=1, source_target_pairs={{0,4},{1,5},{2,6},{3,7},{4,0},{5,1},{6,2},{7,3},{8,12},{9,13},{10,... | collective-permute-start | bytes 344072 | tf_op jit(solution)/shard_map/ppermute | solution.py:300
  47.4 7.1 %collective-permute-start.8 = (bf16[8,7168]{1,0:T(8,128)(2,1)S(1)}, bf16[8,7168]{1,0:T(8,128)(2,1)S(1)}, u32[]{:S(2)}, u32[]{:S(2)}) collective-permute-start(bf16[8,7168]{1,0:T(8,128)(2,1)S(1)} %add_convert_fusion.3.refs_0_), channel_id=1, source_target_pairs={{0,2},{1,3},{2,0},{3,1},{4,6},{5,7},{6,4},{7,5},{8,10},{9,11},{10,... | collective-permute-start | bytes 344072 | tf_op jit(solution)/shard_map/ppermute | solution.py:300
  49.5 5.0 %collective-permute-start.9 = (bf16[8,7168]{1,0:T(8,128)(2,1)S(1)}, bf16[8,7168]{1,0:T(8,128)(2,1)S(1)}, u32[]{:S(2)}, u32[]{:S(2)}) collective-permute-start(bf16[8,7168]{1,0:T(8,128)(2,1)S(1)} %add_convert_fusion.3.refs_0_), channel_id=1, source_target_pairs={{0,1},{1,0},{2,3},{3,2},{4,5},{5,4},{6,7},{7,6},{8,9},{9,8},{10,11... | collective-permute-start | bytes 344072 | tf_op jit(solution)/shard_map/ppermute | solution.py:300
  52.9 1.5 %collective-permute-start.10 = (bf16[8,7168]{1,0:T(8,128)(2,1)S(1)}, bf16[8,7168]{1,0:T(8,128)(2,1)S(1)}, u32[]{:S(2)}, u32[]{:S(2)}) collective-permute-start(bf16[8,7168]{1,0:T(8,128)(2,1)S(1)} %collective-permute-done.6.refs_1_), channel_id=1, source_target_pairs={{0,1},{1,0},{2,3},{3,2},{4,5},{5,4},{6,7},{7,6},{8,9},{9,8},{10,11... | collective-permute-start | bytes 344072 | tf_op jit(solution)/shard_map/ppermute | solution.py:300
  52.9 1.5 %collective-permute-start.11 = (bf16[8,7168]{1,0:T(8,128)(2,1)S(1)}, bf16[8,7168]{1,0:T(8,128)(2,1)S(1)}, u32[]{:S(2)}, u32[]{:S(2)}) collective-permute-start(bf16[8,7168]{1,0:T(8,128)(2,1)S(1)} %collective-permute-done.7.refs_2_), channel_id=1, source_target_pairs={{0,1},{1,0},{2,3},{3,2},{4,5},{5,4},{6,7},{7,6},{8,9},{9,8},{10,11... | collective-permute-start | bytes 344072 | tf_op jit(solution)/shard_map/ppermute | solution.py:300
  54.4 1.3 %collective-permute-start.12 = (bf16[8,7168]{1,0:T(8,128)(2,1)S(1)}, bf16[8,7168]{1,0:T(8,128)(2,1)S(1)}, u32[]{:S(2)}, u32[]{:S(2)}) collective-permute-start(bf16[8,7168]{1,0:T(8,128)(2,1)S(1)} %collective-permute-done.8.refs_3_), channel_id=1, source_target_pairs={{0,1},{1,0},{2,3},{3,2},{4,5},{5,4},{6,7},{7,6},{8,9},{9,8},{10,11... | collective-permute-start | bytes 344072 | tf_op jit(solution)/shard_map/ppermute | solution.py:300
  58.2 1.4 %collective-permute-start.13 = (bf16[8,7168]{1,0:T(8,128)(2,1)S(1)}, bf16[8,7168]{1,0:T(8,128)(2,1)S(1)}, u32[]{:S(2)}, u32[]{:S(2)}) collective-permute-start(bf16[8,7168]{1,0:T(8,128)(2,1)S(1)} %get-tuple-element.26), channel_id=1, source_target_pairs={{0,1},{1,0},{2,3},{3,2},{4,5},{5,4},{6,7},{7,6},{8,9},{9,8},{10,11... | collective-permute-start | bytes 344072 | tf_op jit(solution)/shard_map/ppermute | solution.py:300
  58.4 1.7 %collective-permute-start.15 = (bf16[24,7168]{1,0:T(8,128)(2,1)S(1)}, bf16[24,7168]{1,0:T(8,128)(2,1)S(1)}, u32[]{:S(2)}, u32[]{:S(2)}) collective-permute-start(bf16[24,7168]{1,0:T(8,128)(2,1)S(1)} %get-tuple-element.28), channel_id=1, source_target_pairs={{0,1},{1,0},{2,3},{3,2},{4,5},{5,4},{6,7},{7,6},{8,9},{9,8},{10,11... | collective-permute-start | bytes 1032200 | tf_op jit(solution)/shard_map/ppermute | solution.py:300
  59.6 7.0 %collective-permute-start.14 = (bf16[8,7168]{1,0:T(8,128)(2,1)S(1)}, bf16[8,7168]{1,0:T(8,128)(2,1)S(1)}, u32[]{:S(2)}, u32[]{:S(2)}) collective-permute-start(bf16[8,7168]{1,0:T(8,128)(2,1)S(1)} %add_convert_fusion.2), channel_id=1, source_target_pairs={{0,6},{1,7},{2,4},{3,5},{4,2},{5,3},{6,0},{7,1},{8,14},{9,15},{10,... | collective-permute-start | bytes 344072 | tf_op jit(solution)/shard_map/ppermute | solution.py:300
  60.1 7.5 %collective-permute-start.16 = (bf16[8,7168]{1,0:T(8,128)(2,1)S(1)}, bf16[8,7168]{1,0:T(8,128)(2,1)S(1)}, u32[]{:S(2)}, u32[]{:S(2)}) collective-permute-start(bf16[8,7168]{1,0:T(8,128)(2,1)S(1)} %get-tuple-element.38), channel_id=1, source_target_pairs={{0,4},{1,5},{2,6},{3,7},{4,0},{5,1},{6,2},{7,3},{8,12},{9,13},{10,... | collective-permute-start | bytes 344072 | tf_op jit(solution)/shard_map/ppermute | solution.py:300
  62.0 6.2 %collective-permute-start.17 = (bf16[8,7168]{1,0:T(8,128)(2,1)S(1)}, bf16[8,7168]{1,0:T(8,128)(2,1)S(1)}, u32[]{:S(2)}, u32[]{:S(2)}) collective-permute-start(bf16[8,7168]{1,0:T(8,128)(2,1)S(1)} %get-tuple-element.40), channel_id=1, source_target_pairs={{0,2},{1,3},{2,0},{3,1},{4,6},{5,7},{6,4},{7,5},{8,10},{9,11},{10,... | collective-permute-start | bytes 344072 | tf_op jit(solution)/shard_map/ppermute | solution.py:300
  68.3 5.2 %collective-permute-start.18 = (bf16[4,7168]{1,0:T(4,128)(2,1)S(1)}, bf16[4,7168]{1,0:T(4,128)(2,1)S(1)}, u32[]{:S(2)}, u32[]{:S(2)}) collective-permute-start(bf16[4,7168]{1,0:T(4,128)(2,1)S(1)} %fusion), channel_id=1, source_target_pairs={{0,8},{1,9},{2,10},{3,11},{4,12},{5,13},{6,14},{7,15},{8,0},{9,1},... | collective-permute-start | bytes 172040 | tf_op jit(solution)/shard_map/ppermute | solution.py:300
  (5 other events, 89.2 us)

commit v17 on v16

--- a/solution.py
+++ b/solution.py
@@ -11,7 +11,7 @@
 FF = 2048
 BLOCK = 512
 LOWEST = -3e38
-GROUP = 8
+GROUP = 4
 LANES = 128
 TILE = 256
 PARTS = 4

time: 74.7 us -> 73.8 us (0.988)
  Pallas kernels: 12.5 us -> 10.2 us
    pallas_call x1, Pallas kernels: 8.46 us -> 6.19 us  [attend(): pl.pallas_call(attend_kernel, out_shape=jax.ShapeDtypeStruct((devices, pa...]
where the time goes in v17:
time: 73.8 us; the launch traced here: 72.6 us
  waiting for transfers between devices  29 us (39%)
  blocking collectives  16.9 us (23%)
  starting transfers between devices  13.5 us (18%)
  Pallas kernels  10.2 us (14%)
  other arithmetic  1.42 us (2%)
  between operations  0.84 us (1%)
  local copies, waits for them, and re-layouts  0.74 us (1%)
    ppermute x19, waiting for transfers between devices, swap(): return lax.ppermute(array, 'experts', pairs)  29 us
    all_to_all x1, blocking collectives, shards(): lax.all_to_all(latent, 'experts', split_axis=0, concat_axis=0, tiled=True)  16.9 us
    ppermute x19, starting transfers between devices, swap(): return lax.ppermute(array, 'experts', pairs)  13.5 us
    pallas_call x1, Pallas kernels, attend(): pl.pallas_call(attend_kernel, out_shape=jax.ShapeDtypeStruct((devices, pa...  6.19 us
    pallas_call x1, Pallas kernels, run_expert(): pl.pallas_call(expert_kernel, out_shape=term_shapes(rows, width), in_spec...  2.34 us
    pallas_call x1, Pallas kernels, project(): pl.pallas_call(functools.partial(project_kernel, own_rows, far), out_shap...  1.69 us
  transfers between devices with their start and end apart: 19, of which 14 were waited for; matrix products, arithmetic and copies ran while one was open for 1% of the time, Pallas kernels for 0%

profile of v17, /device:TPU:0, one launch (start us, length us, event | category | flops | bytes accessed | tf_op | source)
XLA Modules:
  0.0 72.6 jit_solution(10718817730750822032)
XLA Ops:
  0.7 6.2 %attend.1 = bf16[16,16,512]{2,1,0:T(8,128)(2,1)} custom-call(s32[4]{0:T(128)} %len_ref.1, bf16[4,64,576]{2,1,0:T(8,128)(2,1)} %bitcast.7, bf16[4,576,4096]{2,1,0:T(8,128)(2,1)} %cache_ref.1), custom_call_target="tpu_custom_call" | custom-call | flops 1140850688 | bytes 9437184 | tf_op jit(solution)/shard_map/attend/pallas_call | solution.py:146
  6.9 16.9 %all_to_all.5 = bf16[16,16,512]{2,1,0:T(8,128)(2,1)S(1)} all-to-all(bf16[16,16,512]{2,1,0:T(8,128)(2,1)} %attend.1), channel_id=1, replica_groups=mesh['groups'=2,'experts'=16] {'experts'}, dimensions={0} | all-to-all | bytes 524288 | tf_op jit(solution)/shard_map/all_to_all | solution.py:364
  23.8 1.7 %project.1 = (f32[8,7168]{1,0:T(8,128)S(1)}, f32[8,7168]{1,0:T(8,128)S(1)}, f32[8,7168]{1,0:T(8,128)S(1)}, f32[8,7168]{1,0:T(8,128)S(1)}, bf16[8,7168]{1,0:T(8,128)(2,1)S(1)}, /*index=5*/bf16[24,7168]{1,0:T(8,128)(2,1)S(1)}) custom-call(bf16[256,512]{1,0:T(8,128)(2,1)S(1)} %bitcast.5, bf16[4,7168]{1,0:T(4,128)(2,1)S(1)} %copy-done.4, ...), custom_call_target="tpu_custom_call" | custom-call | flops 469762048 | bytes 7340032 | tf_op jit(solution)/shard_map/project/pallas_call | solution.py:230
  26.1 0.8 %collective-permute-done = bf16[8,7168]{1,0:T(8,128)(2,1)S(1)} collective-permute-done((bf16[8,7168]{1,0:T(8,128)(2,1)S(1)}, bf16[8,7168]{1,0:T(8,128)(2,1)S(1)}, u32[]{:S(2)}, u32[]{:S(2)}) %collective-permute-start) | collective-permute-done | bytes 114720 | tf_op jit(solution)/shard_map/ppermute | solution.py:300
  27.0 0.7 collective-permute-start.1
  27.7 1.1 %collective-permute-start.3 = (bf16[8,7168]{1,0:T(8,128)(2,1)S(1)}, bf16[8,7168]{1,0:T(8,128)(2,1)S(1)}, u32[]{:S(2)}, u32[]{:S(2)}) collective-permute-start(bf16[8,7168]{1,0:T(8,128)(2,1)S(1)} %get-tuple-element.41), channel_id=1, source_target_pairs={{0,4},{1,5},{2,6},{3,7},{4,0},{5,1},{6,2},{7,3},{8,12},{9,13},{10,... | collective-permute-start | bytes 344072 | tf_op jit(solution)/shard_map/ppermute | solution.py:300
  28.8 1.8 %collective-permute-start.4 = (bf16[8,7168]{1,0:T(8,128)(2,1)S(1)}, bf16[8,7168]{1,0:T(8,128)(2,1)S(1)}, u32[]{:S(2)}, u32[]{:S(2)}) collective-permute-start(bf16[8,7168]{1,0:T(8,128)(2,1)S(1)} %get-tuple-element.42), channel_id=1, source_target_pairs={{0,2},{1,3},{2,0},{3,1},{4,6},{5,7},{6,4},{7,5},{8,10},{9,11},{10,... | collective-permute-start | bytes 344072 | tf_op jit(solution)/shard_map/ppermute | solution.py:300
  30.6 3.3 %collective-permute-done.1 = bf16[8,7168]{1,0:T(8,128)(2,1)S(1)} collective-permute-done((bf16[8,7168]{1,0:T(8,128)(2,1)S(1)}, bf16[8,7168]{1,0:T(8,128)(2,1)S(1)}, u32[]{:S(2)}, u32[]{:S(2)}) %collective-permute-start.1) | collective-permute-done | bytes 114720 | tf_op jit(solution)/shard_map/ppermute | solution.py:300
  34.5 1.1 %collective-permute-done.4 = bf16[8,7168]{1,0:T(8,128)(2,1)S(1)} collective-permute-done((bf16[8,7168]{1,0:T(8,128)(2,1)S(1)}, bf16[8,7168]{1,0:T(8,128)(2,1)S(1)}, u32[]{:S(2)}, u32[]{:S(2)}) %collective-permute-start.4) | collective-permute-done | bytes 114720 | tf_op jit(solution)/shard_map/ppermute | solution.py:300
  35.7 1.1 %collective-permute-start.5 = (bf16[8,7168]{1,0:T(8,128)(2,1)S(1)}, bf16[8,7168]{1,0:T(8,128)(2,1)S(1)}, u32[]{:S(2)}, u32[]{:S(2)}) collective-permute-start(bf16[8,7168]{1,0:T(8,128)(2,1)S(1)} %fusion.3), channel_id=1, source_target_pairs={{0,8},{1,9},{2,10},{3,11},{4,12},{5,13},{6,14},{7,15},{8,0},{9,1},... | collective-permute-start | bytes 344072 | tf_op jit(solution)/shard_map/ppermute | solution.py:300
  36.8 7.3 %collective-permute-done.5 = bf16[8,7168]{1,0:T(8,128)(2,1)S(1)} collective-permute-done((bf16[8,7168]{1,0:T(8,128)(2,1)S(1)}, bf16[8,7168]{1,0:T(8,128)(2,1)S(1)}, u32[]{:S(2)}, u32[]{:S(2)}) %collective-permute-start.5) | collective-permute-done | bytes 114720 | tf_op jit(solution)/shard_map/ppermute | solution.py:300
  44.4 1.3 %collective-permute-start.7 = (bf16[8,7168]{1,0:T(8,128)(2,1)S(1)}, bf16[8,7168]{1,0:T(8,128)(2,1)S(1)}, u32[]{:S(2)}, u32[]{:S(2)}) collective-permute-start(bf16[8,7168]{1,0:T(8,128)(2,1)S(1)} %add_convert_fusion.3.refs_0_), channel_id=1, source_target_pairs={{0,4},{1,5},{2,6},{3,7},{4,0},{5,1},{6,2},{7,3},{8,12},{9,13},{10,... | collective-permute-start | bytes 344072 | tf_op jit(solution)/shard_map/ppermute | solution.py:300
  45.7 2.1 %collective-permute-start.8 = (bf16[8,7168]{1,0:T(8,128)(2,1)S(1)}, bf16[8,7168]{1,0:T(8,128)(2,1)S(1)}, u32[]{:S(2)}, u32[]{:S(2)}) collective-permute-start(bf16[8,7168]{1,0:T(8,128)(2,1)S(1)} %add_convert_fusion.3.refs_0_), channel_id=1, source_target_pairs={{0,2},{1,3},{2,0},{3,1},{4,6},{5,7},{6,4},{7,5},{8,10},{9,11},{10,... | collective-permute-start | bytes 344072 | tf_op jit(solution)/shard_map/ppermute | solution.py:300
  47.9 3.4 %collective-permute-done.6.refs_1_ = bf16[8,7168]{1,0:T(8,128)(2,1)S(1)} collective-permute-done((bf16[8,7168]{1,0:T(8,128)(2,1)S(1)}, bf16[8,7168]{1,0:T(8,128)(2,1)S(1)}, u32[]{:S(2)}, u32[]{:S(2)}) %collective-permute-start.6) | collective-permute-done | bytes 114720 | tf_op jit(solution)/shard_map/ppermute | solution.py:300
  51.8 1.0 %collective-permute-done.8.refs_3_ = bf16[8,7168]{1,0:T(8,128)(2,1)S(1)} collective-permute-done((bf16[8,7168]{1,0:T(8,128)(2,1)S(1)}, bf16[8,7168]{1,0:T(8,128)(2,1)S(1)}, u32[]{:S(2)}, u32[]{:S(2)}) %collective-permute-start.8) | collective-permute-done | bytes 114720 | tf_op jit(solution)/shard_map/ppermute | solution.py:300
  52.8 1.3 %collective-permute-done.12.refs_7_ = bf16[8,7168]{1,0:T(8,128)(2,1)S(1)} collective-permute-done((bf16[8,7168]{1,0:T(8,128)(2,1)S(1)}, bf16[8,7168]{1,0:T(8,128)(2,1)S(1)}, u32[]{:S(2)}, u32[]{:S(2)}) %collective-permute-start.12) | collective-permute-done | bytes 114720 | tf_op jit(solution)/shard_map/ppermute | solution.py:300
  54.2 2.3 %expert.1 = (f32[8,7168]{1,0:T(8,128)S(1)}, f32[8,7168]{1,0:T(8,128)S(1)}, f32[8,7168]{1,0:T(8,128)S(1)}, f32[8,7168]{1,0:T(8,128)S(1)}, bf16[8,7168]{1,0:T(8,128)(2,1)S(1)}, /*index=5*/bf16[24,7168]{1,0:T(8,128)(2,1)S(1)}) custom-call(bf16[8,7168]{1,0:T(8,128)(2,1)S(1)} %add_convert_fusion.3.refs_0_, bf16[8,7168]{1,0:T(8,128)(2,1)S(1)} %collective-permute-done.6.refs_1_, ...), custom_call_target="tpu_custom_call" | custom-call | flops 704643072 | bytes 11010048 | tf_op jit(solution)/shard_map/expert/pallas_call | solution.py:283
  57.1 0.8 %collective-permute-done.13 = bf16[8,7168]{1,0:T(8,128)(2,1)S(1)} collective-permute-done((bf16[8,7168]{1,0:T(8,128)(2,1)S(1)}, bf16[8,7168]{1,0:T(8,128)(2,1)S(1)}, u32[]{:S(2)}, u32[]{:S(2)}) %collective-permute-start.13) | collective-permute-done | bytes 114720 | tf_op jit(solution)/shard_map/ppermute | solution.py:300
  58.5 1.9 %collective-permute-start.16 = (bf16[8,7168]{1,0:T(8,128)(2,1)S(1)}, bf16[8,7168]{1,0:T(8,128)(2,1)S(1)}, u32[]{:S(2)}, u32[]{:S(2)}) collective-permute-start(bf16[8,7168]{1,0:T(8,128)(2,1)S(1)} %get-tuple-element.38), channel_id=1, source_target_pairs={{0,4},{1,5},{2,6},{3,7},{4,0},{5,1},{6,2},{7,3},{8,12},{9,13},{10,... | collective-permute-start | bytes 344072 | tf_op jit(solution)/shard_map/ppermute | solution.py:300
  60.4 1.3 %collective-permute-start.17 = (bf16[8,7168]{1,0:T(8,128)(2,1)S(1)}, bf16[8,7168]{1,0:T(8,128)(2,1)S(1)}, u32[]{:S(2)}, u32[]{:S(2)}) collective-permute-start(bf16[8,7168]{1,0:T(8,128)(2,1)S(1)} %get-tuple-element.40), channel_id=1, source_target_pairs={{0,2},{1,3},{2,0},{3,1},{4,6},{5,7},{6,4},{7,5},{8,10},{9,11},{10,... | collective-permute-start | bytes 344072 | tf_op jit(solution)/shard_map/ppermute | solution.py:300
  62.4 2.5 %collective-permute-done.14 = bf16[8,7168]{1,0:T(8,128)(2,1)S(1)} collective-permute-done((bf16[8,7168]{1,0:T(8,128)(2,1)S(1)}, bf16[8,7168]{1,0:T(8,128)(2,1)S(1)}, u32[]{:S(2)}, u32[]{:S(2)}) %collective-permute-start.14) | collective-permute-done | bytes 114720 | tf_op jit(solution)/shard_map/ppermute | solution.py:300
  64.9 1.1 %collective-permute-done.16 = bf16[8,7168]{1,0:T(8,128)(2,1)S(1)} collective-permute-done((bf16[8,7168]{1,0:T(8,128)(2,1)S(1)}, bf16[8,7168]{1,0:T(8,128)(2,1)S(1)}, u32[]{:S(2)}, u32[]{:S(2)}) %collective-permute-start.16) | collective-permute-done | bytes 114720 | tf_op jit(solution)/shard_map/ppermute | solution.py:300
  66.9 5.1 %collective-permute-done.18 = bf16[4,7168]{1,0:T(4,128)(2,1)S(1)} collective-permute-done((bf16[4,7168]{1,0:T(4,128)(2,1)S(1)}, bf16[4,7168]{1,0:T(4,128)(2,1)S(1)}, u32[]{:S(2)}, u32[]{:S(2)}) %collective-permute-start.18) | collective-permute-done | bytes 57376 | tf_op jit(solution)/shard_map/ppermute | solution.py:300
  71.9 0.7 add_convert_fusion.7
  (51 shorter events, 4.8 us)
Async XLA Ops:
  0.6 23.1 %slice-start = ((s8[7340032]{0:T(1024)(128)(4,1)}), s8[4194304]{0:T(1024)(128)(4,1)S(1)}, s32[]{:S(2)}) async-start(s8[7340032]{0:T(1024)(128)(4,1)} %bitcast.3), calls=%async_computation.1 | async-start | bytes 8388608
  23.8 30.4 %copy-start = (bf16[7168,256]{1,0:T(8,128)(2,1)S(1)}, bf16[7168,256]{1,0:T(8,128)(2,1)}, u32[]{:S(2)}) copy-start(bf16[7168,256]{1,0:T(8,128)(2,1)} %refs_9_.1) | copy-start | bytes 11010052
  23.8 30.3 %copy-start.1 = (bf16[7168,256]{1,0:T(8,128)(2,1)S(1)}, bf16[7168,256]{1,0:T(8,128)(2,1)}, u32[]{:S(2)}) copy-start(bf16[7168,256]{1,0:T(8,128)(2,1)} %refs_10_.1) | copy-start | bytes 11010052
  23.8 30.3 %copy-start.2 = (bf16[256,7168]{1,0:T(8,128)(2,1)S(1)}, bf16[256,7168]{1,0:T(8,128)(2,1)}, u32[]{:S(2)}) copy-start(bf16[256,7168]{1,0:T(8,128)(2,1)} %refs_11_.1) | copy-start | bytes 11010052
  23.8 30.3 %copy-start.5 = (f32[7168]{0:T(1024)S(1)}, f32[7168]{0:T(1024)}, u32[]{:S(2)}) copy-start(f32[7168]{0:T(1024)} %param.18) | copy-start | bytes 86020
  25.5 1.4 %collective-permute-start = (bf16[8,7168]{1,0:T(8,128)(2,1)S(1)}, bf16[8,7168]{1,0:T(8,128)(2,1)S(1)}, u32[]{:S(2)}, u32[]{:S(2)}) collective-permute-start(bf16[8,7168]{1,0:T(8,128)(2,1)S(1)} %get-tuple-element.20), channel_id=1, source_target_pairs={{0,1},{1,0},{2,3},{3,2},{4,5},{5,4},{6,7},{7,6},{8,9},{9,8},{10,11... | collective-permute-start | bytes 344072 | tf_op jit(solution)/shard_map/ppermute | solution.py:300
  25.6 2.0 %collective-permute-start.2 = (bf16[24,7168]{1,0:T(8,128)(2,1)S(1)}, bf16[24,7168]{1,0:T(8,128)(2,1)S(1)}, u32[]{:S(2)}, u32[]{:S(2)}) collective-permute-start(bf16[24,7168]{1,0:T(8,128)(2,1)S(1)} %get-tuple-element.22), channel_id=1, source_target_pairs={{0,1},{1,0},{2,3},{3,2},{4,5},{5,4},{6,7},{7,6},{8,9},{9,8},{10,11... | collective-permute-start | bytes 1032200 | tf_op jit(solution)/shard_map/ppermute | solution.py:300
  27.0 7.0 %collective-permute-start.1 = (bf16[8,7168]{1,0:T(8,128)(2,1)S(1)}, bf16[8,7168]{1,0:T(8,128)(2,1)S(1)}, u32[]{:S(2)}, u32[]{:S(2)}) collective-permute-start(bf16[8,7168]{1,0:T(8,128)(2,1)S(1)} %add_convert_fusion.6), channel_id=1, source_target_pairs={{0,6},{1,7},{2,4},{3,5},{4,2},{5,3},{6,0},{7,1},{8,14},{9,15},{10,... | collective-permute-start | bytes 344072 | tf_op jit(solution)/shard_map/ppermute | solution.py:300
  27.7 6.8 %collective-permute-start.3 = (bf16[8,7168]{1,0:T(8,128)(2,1)S(1)}, bf16[8,7168]{1,0:T(8,128)(2,1)S(1)}, u32[]{:S(2)}, u32[]{:S(2)}) collective-permute-start(bf16[8,7168]{1,0:T(8,128)(2,1)S(1)} %get-tuple-element.41), channel_id=1, source_target_pairs={{0,4},{1,5},{2,6},{3,7},{4,0},{5,1},{6,2},{7,3},{8,12},{9,13},{10,... | collective-permute-start | bytes 344072 | tf_op jit(solution)/shard_map/ppermute | solution.py:300
  28.8 6.8 %collective-permute-start.4 = (bf16[8,7168]{1,0:T(8,128)(2,1)S(1)}, bf16[8,7168]{1,0:T(8,128)(2,1)S(1)}, u32[]{:S(2)}, u32[]{:S(2)}) collective-permute-start(bf16[8,7168]{1,0:T(8,128)(2,1)S(1)} %get-tuple-element.42), channel_id=1, source_target_pairs={{0,2},{1,3},{2,0},{3,1},{4,6},{5,7},{6,4},{7,5},{8,10},{9,11},{10,... | collective-permute-start | bytes 344072 | tf_op jit(solution)/shard_map/ppermute | solution.py:300
  35.7 8.5 %collective-permute-start.5 = (bf16[8,7168]{1,0:T(8,128)(2,1)S(1)}, bf16[8,7168]{1,0:T(8,128)(2,1)S(1)}, u32[]{:S(2)}, u32[]{:S(2)}) collective-permute-start(bf16[8,7168]{1,0:T(8,128)(2,1)S(1)} %fusion.3), channel_id=1, source_target_pairs={{0,8},{1,9},{2,10},{3,11},{4,12},{5,13},{6,14},{7,15},{8,0},{9,1},... | collective-permute-start | bytes 344072 | tf_op jit(solution)/shard_map/ppermute | solution.py:300
  44.3 7.0 %collective-permute-start.6 = (bf16[8,7168]{1,0:T(8,128)(2,1)S(1)}, bf16[8,7168]{1,0:T(8,128)(2,1)S(1)}, u32[]{:S(2)}, u32[]{:S(2)}) collective-permute-start(bf16[8,7168]{1,0:T(8,128)(2,1)S(1)} %add_convert_fusion.3.refs_0_), channel_id=1, source_target_pairs={{0,6},{1,7},{2,4},{3,5},{4,2},{5,3},{6,0},{7,1},{8,14},{9,15},{10,... | collective-permute-start | bytes 344072 | tf_op jit(solution)/shard_map/ppermute | solution.py:300
  44.4 6.9 %collective-permute-start.7 = (bf16[8,7168]{1,0:T(8,128)(2,1)S(1)}, bf16[8,7168]{1,0:T(8,128)(2,1)S(1)}, u32[]{:S(2)}, u32[]{:S(2)}) collective-permute-start(bf16[8,7168]{1,0:T(8,128)(2,1)S(1)} %add_convert_fusion.3.refs_0_), channel_id=1, source_target_pairs={{0,4},{1,5},{2,6},{3,7},{4,0},{5,1},{6,2},{7,3},{8,12},{9,13},{10,... | collective-permute-start | bytes 344072 | tf_op jit(solution)/shard_map/ppermute | solution.py:300
  45.7 7.1 %collective-permute-start.8 = (bf16[8,7168]{1,0:T(8,128)(2,1)S(1)}, bf16[8,7168]{1,0:T(8,128)(2,1)S(1)}, u32[]{:S(2)}, u32[]{:S(2)}) collective-permute-start(bf16[8,7168]{1,0:T(8,128)(2,1)S(1)} %add_convert_fusion.3.refs_0_), channel_id=1, source_target_pairs={{0,2},{1,3},{2,0},{3,1},{4,6},{5,7},{6,4},{7,5},{8,10},{9,11},{10,... | collective-permute-start | bytes 344072 | tf_op jit(solution)/shard_map/ppermute | solution.py:300
  47.9 5.0 %collective-permute-start.9 = (bf16[8,7168]{1,0:T(8,128)(2,1)S(1)}, bf16[8,7168]{1,0:T(8,128)(2,1)S(1)}, u32[]{:S(2)}, u32[]{:S(2)}) collective-permute-start(bf16[8,7168]{1,0:T(8,128)(2,1)S(1)} %add_convert_fusion.3.refs_0_), channel_id=1, source_target_pairs={{0,1},{1,0},{2,3},{3,2},{4,5},{5,4},{6,7},{7,6},{8,9},{9,8},{10,11... | collective-permute-start | bytes 344072 | tf_op jit(solution)/shard_map/ppermute | solution.py:300
  51.3 1.5 %collective-permute-start.10 = (bf16[8,7168]{1,0:T(8,128)(2,1)S(1)}, bf16[8,7168]{1,0:T(8,128)(2,1)S(1)}, u32[]{:S(2)}, u32[]{:S(2)}) collective-permute-start(bf16[8,7168]{1,0:T(8,128)(2,1)S(1)} %collective-permute-done.6.refs_1_), channel_id=1, source_target_pairs={{0,1},{1,0},{2,3},{3,2},{4,5},{5,4},{6,7},{7,6},{8,9},{9,8},{10,11... | collective-permute-start | bytes 344072 | tf_op jit(solution)/shard_map/ppermute | solution.py:300
  51.3 1.5 %collective-permute-start.11 = (bf16[8,7168]{1,0:T(8,128)(2,1)S(1)}, bf16[8,7168]{1,0:T(8,128)(2,1)S(1)}, u32[]{:S(2)}, u32[]{:S(2)}) collective-permute-start(bf16[8,7168]{1,0:T(8,128)(2,1)S(1)} %collective-permute-done.7.refs_2_), channel_id=1, source_target_pairs={{0,1},{1,0},{2,3},{3,2},{4,5},{5,4},{6,7},{7,6},{8,9},{9,8},{10,11... | collective-permute-start | bytes 344072 | tf_op jit(solution)/shard_map/ppermute | solution.py:300
  52.8 1.3 %collective-permute-start.12 = (bf16[8,7168]{1,0:T(8,128)(2,1)S(1)}, bf16[8,7168]{1,0:T(8,128)(2,1)S(1)}, u32[]{:S(2)}, u32[]{:S(2)}) collective-permute-start(bf16[8,7168]{1,0:T(8,128)(2,1)S(1)} %collective-permute-done.8.refs_3_), channel_id=1, source_target_pairs={{0,1},{1,0},{2,3},{3,2},{4,5},{5,4},{6,7},{7,6},{8,9},{9,8},{10,11... | collective-permute-start | bytes 344072 | tf_op jit(solution)/shard_map/ppermute | solution.py:300
  56.5 1.4 %collective-permute-start.13 = (bf16[8,7168]{1,0:T(8,128)(2,1)S(1)}, bf16[8,7168]{1,0:T(8,128)(2,1)S(1)}, u32[]{:S(2)}, u32[]{:S(2)}) collective-permute-start(bf16[8,7168]{1,0:T(8,128)(2,1)S(1)} %get-tuple-element.26), channel_id=1, source_target_pairs={{0,1},{1,0},{2,3},{3,2},{4,5},{5,4},{6,7},{7,6},{8,9},{9,8},{10,11... | collective-permute-start | bytes 344072 | tf_op jit(solution)/shard_map/ppermute | solution.py:300
  56.7 1.7 %collective-permute-start.15 = (bf16[24,7168]{1,0:T(8,128)(2,1)S(1)}, bf16[24,7168]{1,0:T(8,128)(2,1)S(1)}, u32[]{:S(2)}, u32[]{:S(2)}) collective-permute-start(bf16[24,7168]{1,0:T(8,128)(2,1)S(1)} %get-tuple-element.28), channel_id=1, source_target_pairs={{0,1},{1,0},{2,3},{3,2},{4,5},{5,4},{6,7},{7,6},{8,9},{9,8},{10,11... | collective-permute-start | bytes 1032200 | tf_op jit(solution)/shard_map/ppermute | solution.py:300
  58.0 7.0 %collective-permute-start.14 = (bf16[8,7168]{1,0:T(8,128)(2,1)S(1)}, bf16[8,7168]{1,0:T(8,128)(2,1)S(1)}, u32[]{:S(2)}, u32[]{:S(2)}) collective-permute-start(bf16[8,7168]{1,0:T(8,128)(2,1)S(1)} %add_convert_fusion.2), channel_id=1, source_target_pairs={{0,6},{1,7},{2,4},{3,5},{4,2},{5,3},{6,0},{7,1},{8,14},{9,15},{10,... | collective-permute-start | bytes 344072 | tf_op jit(solution)/shard_map/ppermute | solution.py:300
  58.5 7.5 %collective-permute-start.16 = (bf16[8,7168]{1,0:T(8,128)(2,1)S(1)}, bf16[8,7168]{1,0:T(8,128)(2,1)S(1)}, u32[]{:S(2)}, u32[]{:S(2)}) collective-permute-start(bf16[8,7168]{1,0:T(8,128)(2,1)S(1)} %get-tuple-element.38), channel_id=1, source_target_pairs={{0,4},{1,5},{2,6},{3,7},{4,0},{5,1},{6,2},{7,3},{8,12},{9,13},{10,... | collective-permute-start | bytes 344072 | tf_op jit(solution)/shard_map/ppermute | solution.py:300
  60.4 6.2 %collective-permute-start.17 = (bf16[8,7168]{1,0:T(8,128)(2,1)S(1)}, bf16[8,7168]{1,0:T(8,128)(2,1)S(1)}, u32[]{:S(2)}, u32[]{:S(2)}) collective-permute-start(bf16[8,7168]{1,0:T(8,128)(2,1)S(1)} %get-tuple-element.40), channel_id=1, source_target_pairs={{0,2},{1,3},{2,0},{3,1},{4,6},{5,7},{6,4},{7,5},{8,10},{9,11},{10,... | collective-permute-start | bytes 344072 | tf_op jit(solution)/shard_map/ppermute | solution.py:300
  66.7 5.2 %collective-permute-start.18 = (bf16[4,7168]{1,0:T(4,128)(2,1)S(1)}, bf16[4,7168]{1,0:T(4,128)(2,1)S(1)}, u32[]{:S(2)}, u32[]{:S(2)}) collective-permute-start(bf16[4,7168]{1,0:T(4,128)(2,1)S(1)} %fusion), channel_id=1, source_target_pairs={{0,8},{1,9},{2,10},{3,11},{4,12},{5,13},{6,14},{7,15},{8,0},{9,1},... | collective-permute-start | bytes 172040 | tf_op jit(solution)/shard_map/ppermute | solution.py:300
  (5 other events, 84.3 us)

commit v18 on v17

--- a/solution.py
+++ b/solution.py
@@ -162,7 +162,7 @@
             pltpu.SemaphoreType.DMA,
             pltpu.SemaphoreType.DMA((own_rows, blocks)),
         ],
-        compiler_params=pltpu.CompilerParams(vmem_limit_bytes=55 * MIB),
+        compiler_params=pltpu.CompilerParams(vmem_limit_bytes=107 * MIB // 2),
         cost_estimate=pl.CostEstimate(
             flops=own_rows * heads * cache.shape[2] * (depth + rank),
             bytes_accessed=cache.size,

time: 73.8 us -> 76 us (1.030); the launches traced: 72.6 us -> 75.7 us
  blocking collectives: 16.9 us -> 19.2 us
  local copies, waits for them, and re-layouts: 0.74 us -> 1.53 us
    all_to_all x1, blocking collectives: 16.9 us -> 19.2 us  [shards(): lax.all_to_all(latent, 'experts', split_axis=0, concat_axis=0, tiled=True)]
    unnamed x20 -> x22, local copies, waits for them, and re-layouts: 0.06 us -> 0.85 us
where the time goes in v18:
time: 76 us; the launch traced here: 75.7 us
  waiting for transfers between devices  29 us (38%)
  blocking collectives  19.2 us (25%)
  starting transfers between devices  13.5 us (18%)
  Pallas kernels  10.3 us (14%)
  local copies, waits for them, and re-layouts  1.53 us (2%)
  other arithmetic  1.4 us (2%)
  between operations  0.83 us (1%)
    ppermute x19, waiting for transfers between devices, swap(): return lax.ppermute(array, 'experts', pairs)  29 us
    all_to_all x1, blocking collectives, shards(): lax.all_to_all(latent, 'experts', split_axis=0, concat_axis=0, tiled=True)  19.2 us
    ppermute x19, starting transfers between devices, swap(): return lax.ppermute(array, 'experts', pairs)  13.5 us
    pallas_call x1, Pallas kernels, attend(): pl.pallas_call(attend_kernel, out_shape=jax.ShapeDtypeStruct((devices, pa...  6.22 us
    pallas_call x1, Pallas kernels, run_expert(): pl.pallas_call(expert_kernel, out_shape=term_shapes(rows, width), in_spec...  2.36 us
    pallas_call x1, Pallas kernels, project(): pl.pallas_call(functools.partial(project_kernel, own_rows, far), out_shap...  1.69 us
  transfers between devices with their start and end apart: 19, of which 14 were waited for; matrix products, arithmetic and copies ran while one was open for 1% of the time, Pallas kernels for 0%

profile of v18, /device:TPU:0, one launch (start us, length us, event | category | flops | bytes accessed | tf_op | source)
XLA Modules:
  0.0 75.7 jit_solution(8200780425602173501)
XLA Ops:
  0.7 0.8 %copy-done.6 = s32[4]{0:T(128)S(1)} copy-done((s32[4]{0:T(128)S(1)}, s32[4]{0:T(128)}, u32[]{:S(2)}) %copy-start.6) | copy-done | bytes 40
  1.5 6.2 %attend.1 = bf16[16,16,512]{2,1,0:T(8,128)(2,1)S(1)} custom-call(s32[4]{0:T(128)S(1)} %copy-done.6, bf16[4,64,576]{2,1,0:T(8,128)(2,1)} %bitcast.7, bf16[4,576,4096]{2,1,0:T(8,128)(2,1)} %cache_ref.1), custom_call_target="tpu_custom_call" | custom-call | flops 1140850688 | bytes 9437184 | tf_op jit(solution)/shard_map/attend/pallas_call | solution.py:146
  7.7 19.2 %all_to_all.5 = bf16[16,16,512]{2,1,0:T(8,128)(2,1)S(1)} all-to-all(bf16[16,16,512]{2,1,0:T(8,128)(2,1)S(1)} %attend.1), channel_id=1, replica_groups=mesh['groups'=2,'experts'=16] {'experts'}, dimensions={0} | all-to-all | bytes 524288 | tf_op jit(solution)/shard_map/all_to_all | solution.py:364
  26.9 1.7 %project.1 = (f32[8,7168]{1,0:T(8,128)S(1)}, f32[8,7168]{1,0:T(8,128)S(1)}, f32[8,7168]{1,0:T(8,128)S(1)}, f32[8,7168]{1,0:T(8,128)S(1)}, bf16[8,7168]{1,0:T(8,128)(2,1)S(1)}, /*index=5*/bf16[24,7168]{1,0:T(8,128)(2,1)S(1)}) custom-call(bf16[256,512]{1,0:T(8,128)(2,1)S(1)} %bitcast.5, bf16[4,7168]{1,0:T(4,128)(2,1)S(1)} %copy-done.4, ...), custom_call_target="tpu_custom_call" | custom-call | flops 469762048 | bytes 7340032 | tf_op jit(solution)/shard_map/project/pallas_call | solution.py:230
  29.2 0.8 %collective-permute-done = bf16[8,7168]{1,0:T(8,128)(2,1)S(1)} collective-permute-done((bf16[8,7168]{1,0:T(8,128)(2,1)S(1)}, bf16[8,7168]{1,0:T(8,128)(2,1)S(1)}, u32[]{:S(2)}, u32[]{:S(2)}) %collective-permute-start) | collective-permute-done | bytes 114720 | tf_op jit(solution)/shard_map/ppermute | solution.py:300
  30.7 1.1 %collective-permute-start.3 = (bf16[8,7168]{1,0:T(8,128)(2,1)S(1)}, bf16[8,7168]{1,0:T(8,128)(2,1)S(1)}, u32[]{:S(2)}, u32[]{:S(2)}) collective-permute-start(bf16[8,7168]{1,0:T(8,128)(2,1)S(1)} %get-tuple-element.41), channel_id=1, source_target_pairs={{0,4},{1,5},{2,6},{3,7},{4,0},{5,1},{6,2},{7,3},{8,12},{9,13},{10,... | collective-permute-start | bytes 344072 | tf_op jit(solution)/shard_map/ppermute | solution.py:300
  31.9 1.8 %collective-permute-start.4 = (bf16[8,7168]{1,0:T(8,128)(2,1)S(1)}, bf16[8,7168]{1,0:T(8,128)(2,1)S(1)}, u32[]{:S(2)}, u32[]{:S(2)}) collective-permute-start(bf16[8,7168]{1,0:T(8,128)(2,1)S(1)} %get-tuple-element.42), channel_id=1, source_target_pairs={{0,2},{1,3},{2,0},{3,1},{4,6},{5,7},{6,4},{7,5},{8,10},{9,11},{10,... | collective-permute-start | bytes 344072 | tf_op jit(solution)/shard_map/ppermute | solution.py:300
  33.7 3.3 %collective-permute-done.1 = bf16[8,7168]{1,0:T(8,128)(2,1)S(1)} collective-permute-done((bf16[8,7168]{1,0:T(8,128)(2,1)S(1)}, bf16[8,7168]{1,0:T(8,128)(2,1)S(1)}, u32[]{:S(2)}, u32[]{:S(2)}) %collective-permute-start.1) | collective-permute-done | bytes 114720 | tf_op jit(solution)/shard_map/ppermute | solution.py:300
  37.6 1.1 %collective-permute-done.4 = bf16[8,7168]{1,0:T(8,128)(2,1)S(1)} collective-permute-done((bf16[8,7168]{1,0:T(8,128)(2,1)S(1)}, bf16[8,7168]{1,0:T(8,128)(2,1)S(1)}, u32[]{:S(2)}, u32[]{:S(2)}) %collective-permute-start.4) | collective-permute-done | bytes 114720 | tf_op jit(solution)/shard_map/ppermute | solution.py:300
  38.7 1.1 %collective-permute-start.5 = (bf16[8,7168]{1,0:T(8,128)(2,1)S(1)}, bf16[8,7168]{1,0:T(8,128)(2,1)S(1)}, u32[]{:S(2)}, u32[]{:S(2)}) collective-permute-start(bf16[8,7168]{1,0:T(8,128)(2,1)S(1)} %fusion.3), channel_id=1, source_target_pairs={{0,8},{1,9},{2,10},{3,11},{4,12},{5,13},{6,14},{7,15},{8,0},{9,1},... | collective-permute-start | bytes 344072 | tf_op jit(solution)/shard_map/ppermute | solution.py:300
  39.9 7.4 %collective-permute-done.5 = bf16[8,7168]{1,0:T(8,128)(2,1)S(1)} collective-permute-done((bf16[8,7168]{1,0:T(8,128)(2,1)S(1)}, bf16[8,7168]{1,0:T(8,128)(2,1)S(1)}, u32[]{:S(2)}, u32[]{:S(2)}) %collective-permute-start.5) | collective-permute-done | bytes 114720 | tf_op jit(solution)/shard_map/ppermute | solution.py:300
  47.5 1.3 %collective-permute-start.7 = (bf16[8,7168]{1,0:T(8,128)(2,1)S(1)}, bf16[8,7168]{1,0:T(8,128)(2,1)S(1)}, u32[]{:S(2)}, u32[]{:S(2)}) collective-permute-start(bf16[8,7168]{1,0:T(8,128)(2,1)S(1)} %add_convert_fusion.3.refs_0_), channel_id=1, source_target_pairs={{0,4},{1,5},{2,6},{3,7},{4,0},{5,1},{6,2},{7,3},{8,12},{9,13},{10,... | collective-permute-start | bytes 344072 | tf_op jit(solution)/shard_map/ppermute | solution.py:300
  48.8 2.1 %collective-permute-start.8 = (bf16[8,7168]{1,0:T(8,128)(2,1)S(1)}, bf16[8,7168]{1,0:T(8,128)(2,1)S(1)}, u32[]{:S(2)}, u32[]{:S(2)}) collective-permute-start(bf16[8,7168]{1,0:T(8,128)(2,1)S(1)} %add_convert_fusion.3.refs_0_), channel_id=1, source_target_pairs={{0,2},{1,3},{2,0},{3,1},{4,6},{5,7},{6,4},{7,5},{8,10},{9,11},{10,... | collective-permute-start | bytes 344072 | tf_op jit(solution)/shard_map/ppermute | solution.py:300
  51.0 3.4 %collective-permute-done.6.refs_1_ = bf16[8,7168]{1,0:T(8,128)(2,1)S(1)} collective-permute-done((bf16[8,7168]{1,0:T(8,128)(2,1)S(1)}, bf16[8,7168]{1,0:T(8,128)(2,1)S(1)}, u32[]{:S(2)}, u32[]{:S(2)}) %collective-permute-start.6) | collective-permute-done | bytes 114720 | tf_op jit(solution)/shard_map/ppermute | solution.py:300
  54.9 1.0 %collective-permute-done.8.refs_3_ = bf16[8,7168]{1,0:T(8,128)(2,1)S(1)} collective-permute-done((bf16[8,7168]{1,0:T(8,128)(2,1)S(1)}, bf16[8,7168]{1,0:T(8,128)(2,1)S(1)}, u32[]{:S(2)}, u32[]{:S(2)}) %collective-permute-start.8) | collective-permute-done | bytes 114720 | tf_op jit(solution)/shard_map/ppermute | solution.py:300
  55.9 1.3 %collective-permute-done.12.refs_7_ = bf16[8,7168]{1,0:T(8,128)(2,1)S(1)} collective-permute-done((bf16[8,7168]{1,0:T(8,128)(2,1)S(1)}, bf16[8,7168]{1,0:T(8,128)(2,1)S(1)}, u32[]{:S(2)}, u32[]{:S(2)}) %collective-permute-start.12) | collective-permute-done | bytes 114720 | tf_op jit(solution)/shard_map/ppermute | solution.py:300
  57.3 2.4 %expert.1 = (f32[8,7168]{1,0:T(8,128)S(1)}, f32[8,7168]{1,0:T(8,128)S(1)}, f32[8,7168]{1,0:T(8,128)S(1)}, f32[8,7168]{1,0:T(8,128)S(1)}, bf16[8,7168]{1,0:T(8,128)(2,1)S(1)}, /*index=5*/bf16[24,7168]{1,0:T(8,128)(2,1)S(1)}) custom-call(bf16[8,7168]{1,0:T(8,128)(2,1)S(1)} %add_convert_fusion.3.refs_0_, bf16[8,7168]{1,0:T(8,128)(2,1)S(1)} %collective-permute-done.6.refs_1_, ...), custom_call_target="tpu_custom_call" | custom-call | flops 704643072 | bytes 11010048 | tf_op jit(solution)/shard_map/expert/pallas_call | solution.py:283
  60.2 0.8 %collective-permute-done.13 = bf16[8,7168]{1,0:T(8,128)(2,1)S(1)} collective-permute-done((bf16[8,7168]{1,0:T(8,128)(2,1)S(1)}, bf16[8,7168]{1,0:T(8,128)(2,1)S(1)}, u32[]{:S(2)}, u32[]{:S(2)}) %collective-permute-start.13) | collective-permute-done | bytes 114720 | tf_op jit(solution)/shard_map/ppermute | solution.py:300
  61.6 1.9 %collective-permute-start.16 = (bf16[8,7168]{1,0:T(8,128)(2,1)S(1)}, bf16[8,7168]{1,0:T(8,128)(2,1)S(1)}, u32[]{:S(2)}, u32[]{:S(2)}) collective-permute-start(bf16[8,7168]{1,0:T(8,128)(2,1)S(1)} %get-tuple-element.38), channel_id=1, source_target_pairs={{0,4},{1,5},{2,6},{3,7},{4,0},{5,1},{6,2},{7,3},{8,12},{9,13},{10,... | collective-permute-start | bytes 344072 | tf_op jit(solution)/shard_map/ppermute | solution.py:300
  63.4 1.3 %collective-permute-start.17 = (bf16[8,7168]{1,0:T(8,128)(2,1)S(1)}, bf16[8,7168]{1,0:T(8,128)(2,1)S(1)}, u32[]{:S(2)}, u32[]{:S(2)}) collective-permute-start(bf16[8,7168]{1,0:T(8,128)(2,1)S(1)} %get-tuple-element.40), channel_id=1, source_target_pairs={{0,2},{1,3},{2,0},{3,1},{4,6},{5,7},{6,4},{7,5},{8,10},{9,11},{10,... | collective-permute-start | bytes 344072 | tf_op jit(solution)/shard_map/ppermute | solution.py:300
  65.5 2.5 %collective-permute-done.14 = bf16[8,7168]{1,0:T(8,128)(2,1)S(1)} collective-permute-done((bf16[8,7168]{1,0:T(8,128)(2,1)S(1)}, bf16[8,7168]{1,0:T(8,128)(2,1)S(1)}, u32[]{:S(2)}, u32[]{:S(2)}) %collective-permute-start.14) | collective-permute-done | bytes 114720 | tf_op jit(solution)/shard_map/ppermute | solution.py:300
  68.0 1.1 %collective-permute-done.16 = bf16[8,7168]{1,0:T(8,128)(2,1)S(1)} collective-permute-done((bf16[8,7168]{1,0:T(8,128)(2,1)S(1)}, bf16[8,7168]{1,0:T(8,128)(2,1)S(1)}, u32[]{:S(2)}, u32[]{:S(2)}) %collective-permute-start.16) | collective-permute-done | bytes 114720 | tf_op jit(solution)/shard_map/ppermute | solution.py:300
  70.0 5.1 %collective-permute-done.18 = bf16[4,7168]{1,0:T(4,128)(2,1)S(1)} collective-permute-done((bf16[4,7168]{1,0:T(4,128)(2,1)S(1)}, bf16[4,7168]{1,0:T(4,128)(2,1)S(1)}, u32[]{:S(2)}, u32[]{:S(2)}) %collective-permute-start.18) | collective-permute-done | bytes 57376 | tf_op jit(solution)/shard_map/ppermute | solution.py:300
  75.0 0.7 add_convert_fusion.7
  (53 shorter events, 5.5 us)
Async XLA Ops:
  0.6 26.2 %slice-start = ((s8[7340032]{0:T(1024)(128)(4,1)}), s8[4194304]{0:T(1024)(128)(4,1)S(1)}, s32[]{:S(2)}) async-start(s8[7340032]{0:T(1024)(128)(4,1)} %bitcast.3), calls=%async_computation.1 | async-start | bytes 8388608
  26.9 30.3 %copy-start = (bf16[7168,256]{1,0:T(8,128)(2,1)S(1)}, bf16[7168,256]{1,0:T(8,128)(2,1)}, u32[]{:S(2)}) copy-start(bf16[7168,256]{1,0:T(8,128)(2,1)} %refs_9_.1) | copy-start | bytes 11010052
  26.9 30.3 %copy-start.1 = (bf16[7168,256]{1,0:T(8,128)(2,1)S(1)}, bf16[7168,256]{1,0:T(8,128)(2,1)}, u32[]{:S(2)}) copy-start(bf16[7168,256]{1,0:T(8,128)(2,1)} %refs_10_.1) | copy-start | bytes 11010052
  26.9 30.3 %copy-start.2 = (bf16[256,7168]{1,0:T(8,128)(2,1)S(1)}, bf16[256,7168]{1,0:T(8,128)(2,1)}, u32[]{:S(2)}) copy-start(bf16[256,7168]{1,0:T(8,128)(2,1)} %refs_11_.1) | copy-start | bytes 11010052
  26.9 30.3 %copy-start.5 = (f32[7168]{0:T(1024)S(1)}, f32[7168]{0:T(1024)}, u32[]{:S(2)}) copy-start(f32[7168]{0:T(1024)} %param.18) | copy-start | bytes 86020
  28.6 1.4 %collective-permute-start = (bf16[8,7168]{1,0:T(8,128)(2,1)S(1)}, bf16[8,7168]{1,0:T(8,128)(2,1)S(1)}, u32[]{:S(2)}, u32[]{:S(2)}) collective-permute-start(bf16[8,7168]{1,0:T(8,128)(2,1)S(1)} %get-tuple-element.20), channel_id=1, source_target_pairs={{0,1},{1,0},{2,3},{3,2},{4,5},{5,4},{6,7},{7,6},{8,9},{9,8},{10,11... | collective-permute-start | bytes 344072 | tf_op jit(solution)/shard_map/ppermute | solution.py:300
  28.7 2.0 %collective-permute-start.2 = (bf16[24,7168]{1,0:T(8,128)(2,1)S(1)}, bf16[24,7168]{1,0:T(8,128)(2,1)S(1)}, u32[]{:S(2)}, u32[]{:S(2)}) collective-permute-start(bf16[24,7168]{1,0:T(8,128)(2,1)S(1)} %get-tuple-element.22), channel_id=1, source_target_pairs={{0,1},{1,0},{2,3},{3,2},{4,5},{5,4},{6,7},{7,6},{8,9},{9,8},{10,11... | collective-permute-start | bytes 1032200 | tf_op jit(solution)/shard_map/ppermute | solution.py:300
  30.0 7.0 %collective-permute-start.1 = (bf16[8,7168]{1,0:T(8,128)(2,1)S(1)}, bf16[8,7168]{1,0:T(8,128)(2,1)S(1)}, u32[]{:S(2)}, u32[]{:S(2)}) collective-permute-start(bf16[8,7168]{1,0:T(8,128)(2,1)S(1)} %add_convert_fusion.6), channel_id=1, source_target_pairs={{0,6},{1,7},{2,4},{3,5},{4,2},{5,3},{6,0},{7,1},{8,14},{9,15},{10,... | collective-permute-start | bytes 344072 | tf_op jit(solution)/shard_map/ppermute | solution.py:300
  30.7 6.8 %collective-permute-start.3 = (bf16[8,7168]{1,0:T(8,128)(2,1)S(1)}, bf16[8,7168]{1,0:T(8,128)(2,1)S(1)}, u32[]{:S(2)}, u32[]{:S(2)}) collective-permute-start(bf16[8,7168]{1,0:T(8,128)(2,1)S(1)} %get-tuple-element.41), channel_id=1, source_target_pairs={{0,4},{1,5},{2,6},{3,7},{4,0},{5,1},{6,2},{7,3},{8,12},{9,13},{10,... | collective-permute-start | bytes 344072 | tf_op jit(solution)/shard_map/ppermute | solution.py:300
  31.9 6.8 %collective-permute-start.4 = (bf16[8,7168]{1,0:T(8,128)(2,1)S(1)}, bf16[8,7168]{1,0:T(8,128)(2,1)S(1)}, u32[]{:S(2)}, u32[]{:S(2)}) collective-permute-start(bf16[8,7168]{1,0:T(8,128)(2,1)S(1)} %get-tuple-element.42), channel_id=1, source_target_pairs={{0,2},{1,3},{2,0},{3,1},{4,6},{5,7},{6,4},{7,5},{8,10},{9,11},{10,... | collective-permute-start | bytes 344072 | tf_op jit(solution)/shard_map/ppermute | solution.py:300
  38.7 8.5 %collective-permute-start.5 = (bf16[8,7168]{1,0:T(8,128)(2,1)S(1)}, bf16[8,7168]{1,0:T(8,128)(2,1)S(1)}, u32[]{:S(2)}, u32[]{:S(2)}) collective-permute-start(bf16[8,7168]{1,0:T(8,128)(2,1)S(1)} %fusion.3), channel_id=1, source_target_pairs={{0,8},{1,9},{2,10},{3,11},{4,12},{5,13},{6,14},{7,15},{8,0},{9,1},... | collective-permute-start | bytes 344072 | tf_op jit(solution)/shard_map/ppermute | solution.py:300
  47.4 7.0 %collective-permute-start.6 = (bf16[8,7168]{1,0:T(8,128)(2,1)S(1)}, bf16[8,7168]{1,0:T(8,128)(2,1)S(1)}, u32[]{:S(2)}, u32[]{:S(2)}) collective-permute-start(bf16[8,7168]{1,0:T(8,128)(2,1)S(1)} %add_convert_fusion.3.refs_0_), channel_id=1, source_target_pairs={{0,6},{1,7},{2,4},{3,5},{4,2},{5,3},{6,0},{7,1},{8,14},{9,15},{10,... | collective-permute-start | bytes 344072 | tf_op jit(solution)/shard_map/ppermute | solution.py:300
  47.5 6.9 %collective-permute-start.7 = (bf16[8,7168]{1,0:T(8,128)(2,1)S(1)}, bf16[8,7168]{1,0:T(8,128)(2,1)S(1)}, u32[]{:S(2)}, u32[]{:S(2)}) collective-permute-start(bf16[8,7168]{1,0:T(8,128)(2,1)S(1)} %add_convert_fusion.3.refs_0_), channel_id=1, source_target_pairs={{0,4},{1,5},{2,6},{3,7},{4,0},{5,1},{6,2},{7,3},{8,12},{9,13},{10,... | collective-permute-start | bytes 344072 | tf_op jit(solution)/shard_map/ppermute | solution.py:300
  48.8 7.1 %collective-permute-start.8 = (bf16[8,7168]{1,0:T(8,128)(2,1)S(1)}, bf16[8,7168]{1,0:T(8,128)(2,1)S(1)}, u32[]{:S(2)}, u32[]{:S(2)}) collective-permute-start(bf16[8,7168]{1,0:T(8,128)(2,1)S(1)} %add_convert_fusion.3.refs_0_), channel_id=1, source_target_pairs={{0,2},{1,3},{2,0},{3,1},{4,6},{5,7},{6,4},{7,5},{8,10},{9,11},{10,... | collective-permute-start | bytes 344072 | tf_op jit(solution)/shard_map/ppermute | solution.py:300
  51.0 5.0 %collective-permute-start.9 = (bf16[8,7168]{1,0:T(8,128)(2,1)S(1)}, bf16[8,7168]{1,0:T(8,128)(2,1)S(1)}, u32[]{:S(2)}, u32[]{:S(2)}) collective-permute-start(bf16[8,7168]{1,0:T(8,128)(2,1)S(1)} %add_convert_fusion.3.refs_0_), channel_id=1, source_target_pairs={{0,1},{1,0},{2,3},{3,2},{4,5},{5,4},{6,7},{7,6},{8,9},{9,8},{10,11... | collective-permute-start | bytes 344072 | tf_op jit(solution)/shard_map/ppermute | solution.py:300
  54.4 1.5 %collective-permute-start.10 = (bf16[8,7168]{1,0:T(8,128)(2,1)S(1)}, bf16[8,7168]{1,0:T(8,128)(2,1)S(1)}, u32[]{:S(2)}, u32[]{:S(2)}) collective-permute-start(bf16[8,7168]{1,0:T(8,128)(2,1)S(1)} %collective-permute-done.6.refs_1_), channel_id=1, source_target_pairs={{0,1},{1,0},{2,3},{3,2},{4,5},{5,4},{6,7},{7,6},{8,9},{9,8},{10,11... | collective-permute-start | bytes 344072 | tf_op jit(solution)/shard_map/ppermute | solution.py:300
  54.4 1.5 %collective-permute-start.11 = (bf16[8,7168]{1,0:T(8,128)(2,1)S(1)}, bf16[8,7168]{1,0:T(8,128)(2,1)S(1)}, u32[]{:S(2)}, u32[]{:S(2)}) collective-permute-start(bf16[8,7168]{1,0:T(8,128)(2,1)S(1)} %collective-permute-done.7.refs_2_), channel_id=1, source_target_pairs={{0,1},{1,0},{2,3},{3,2},{4,5},{5,4},{6,7},{7,6},{8,9},{9,8},{10,11... | collective-permute-start | bytes 344072 | tf_op jit(solution)/shard_map/ppermute | solution.py:300
  55.9 1.3 %collective-permute-start.12 = (bf16[8,7168]{1,0:T(8,128)(2,1)S(1)}, bf16[8,7168]{1,0:T(8,128)(2,1)S(1)}, u32[]{:S(2)}, u32[]{:S(2)}) collective-permute-start(bf16[8,7168]{1,0:T(8,128)(2,1)S(1)} %collective-permute-done.8.refs_3_), channel_id=1, source_target_pairs={{0,1},{1,0},{2,3},{3,2},{4,5},{5,4},{6,7},{7,6},{8,9},{9,8},{10,11... | collective-permute-start | bytes 344072 | tf_op jit(solution)/shard_map/ppermute | solution.py:300
  59.6 1.4 %collective-permute-start.13 = (bf16[8,7168]{1,0:T(8,128)(2,1)S(1)}, bf16[8,7168]{1,0:T(8,128)(2,1)S(1)}, u32[]{:S(2)}, u32[]{:S(2)}) collective-permute-start(bf16[8,7168]{1,0:T(8,128)(2,1)S(1)} %get-tuple-element.26), channel_id=1, source_target_pairs={{0,1},{1,0},{2,3},{3,2},{4,5},{5,4},{6,7},{7,6},{8,9},{9,8},{10,11... | collective-permute-start | bytes 344072 | tf_op jit(solution)/shard_map/ppermute | solution.py:300
  59.8 1.7 %collective-permute-start.15 = (bf16[24,7168]{1,0:T(8,128)(2,1)S(1)}, bf16[24,7168]{1,0:T(8,128)(2,1)S(1)}, u32[]{:S(2)}, u32[]{:S(2)}) collective-permute-start(bf16[24,7168]{1,0:T(8,128)(2,1)S(1)} %get-tuple-element.28), channel_id=1, source_target_pairs={{0,1},{1,0},{2,3},{3,2},{4,5},{5,4},{6,7},{7,6},{8,9},{9,8},{10,11... | collective-permute-start | bytes 1032200 | tf_op jit(solution)/shard_map/ppermute | solution.py:300
  61.0 7.0 %collective-permute-start.14 = (bf16[8,7168]{1,0:T(8,128)(2,1)S(1)}, bf16[8,7168]{1,0:T(8,128)(2,1)S(1)}, u32[]{:S(2)}, u32[]{:S(2)}) collective-permute-start(bf16[8,7168]{1,0:T(8,128)(2,1)S(1)} %add_convert_fusion.2), channel_id=1, source_target_pairs={{0,6},{1,7},{2,4},{3,5},{4,2},{5,3},{6,0},{7,1},{8,14},{9,15},{10,... | collective-permute-start | bytes 344072 | tf_op jit(solution)/shard_map/ppermute | solution.py:300
  61.6 7.5 %collective-permute-start.16 = (bf16[8,7168]{1,0:T(8,128)(2,1)S(1)}, bf16[8,7168]{1,0:T(8,128)(2,1)S(1)}, u32[]{:S(2)}, u32[]{:S(2)}) collective-permute-start(bf16[8,7168]{1,0:T(8,128)(2,1)S(1)} %get-tuple-element.38), channel_id=1, source_target_pairs={{0,4},{1,5},{2,6},{3,7},{4,0},{5,1},{6,2},{7,3},{8,12},{9,13},{10,... | collective-permute-start | bytes 344072 | tf_op jit(solution)/shard_map/ppermute | solution.py:300
  63.4 6.2 %collective-permute-start.17 = (bf16[8,7168]{1,0:T(8,128)(2,1)S(1)}, bf16[8,7168]{1,0:T(8,128)(2,1)S(1)}, u32[]{:S(2)}, u32[]{:S(2)}) collective-permute-start(bf16[8,7168]{1,0:T(8,128)(2,1)S(1)} %get-tuple-element.40), channel_id=1, source_target_pairs={{0,2},{1,3},{2,0},{3,1},{4,6},{5,7},{6,4},{7,5},{8,10},{9,11},{10,... | collective-permute-start | bytes 344072 | tf_op jit(solution)/shard_map/ppermute | solution.py:300
  69.8 5.2 %collective-permute-start.18 = (bf16[4,7168]{1,0:T(4,128)(2,1)S(1)}, bf16[4,7168]{1,0:T(4,128)(2,1)S(1)}, u32[]{:S(2)}, u32[]{:S(2)}) collective-permute-start(bf16[4,7168]{1,0:T(4,128)(2,1)S(1)} %fusion), channel_id=1, source_target_pairs={{0,8},{1,9},{2,10},{3,11},{4,12},{5,13},{6,14},{7,15},{8,0},{9,1},... | collective-permute-start | bytes 172040 | tf_op jit(solution)/shard_map/ppermute | solution.py:300
  (6 other events, 92.0 us)

commit v19 on v14

--- a/solution.py
+++ b/solution.py
@@ -9,9 +9,9 @@
 
 QK = 192
 FF = 2048
-BLOCK = 256
+BLOCK = 512
 LOWEST = -3e38
-GROUP = 8
+GROUP = 4
 LANES = 128
 TILE = 256
 PARTS = 4
@@ -126,11 +126,9 @@
     visit(0, own_rows)
     rest = items - own_rows
     lax.fori_loop(0, rest // GROUP, visit_group, 0)
-    many = GROUP // 2
-    while many:
-        first = own_rows + rest // (2 * many) * (2 * many)
-        pl.when((rest & many) != 0)(functools.partial(visit, first, many))
-        many //= 2
+    left = rest % GROUP
+    for many in range(1, GROUP):
+        pl.when(left == many)(functools.partial(visit, items - many, many))
     for row in range(own_rows):
         latent = summed[row] * (1.0 / jnp.sum(sums[row], axis=1, keepdims=True))
         for device in range(devices):

time: 76.3 us -> 75.6 us (level); the launches traced: 76.2 us -> 76.2 us
  blocking collectives: 19.1 us -> 20.3 us
  Pallas kernels: 11.5 us -> 10.4 us
    all_to_all x1, blocking collectives: 19.1 us -> 20.3 us  [shards(): lax.all_to_all(latent, 'experts', split_axis=0, concat_axis=0, tiled=True)]
    pallas_call x1, Pallas kernels: 7.47 us -> 6.4 us  [attend(): pl.pallas_call(attend_kernel, out_shape=jax.ShapeDtypeStruct((devices, pa...]
where the time goes in v19:
time: 75.6 us; the launch traced here: 76.2 us
  waiting for transfers between devices  29 us (38%)
  blocking collectives  20.3 us (27%)
  starting transfers between devices  13.5 us (18%)
  Pallas kernels  10.4 us (14%)
  other arithmetic  1.33 us (2%)
  between operations  0.85 us (1%)
  local copies, waits for them, and re-layouts  0.77 us (1%)
    ppermute x19, waiting for transfers between devices, swap(): return lax.ppermute(array, 'experts', pairs)  29 us
    all_to_all x1, blocking collectives, shards(): lax.all_to_all(latent, 'experts', split_axis=0, concat_axis=0, tiled=True)  20.3 us
    ppermute x19, starting transfers between devices, swap(): return lax.ppermute(array, 'experts', pairs)  13.5 us
    pallas_call x1, Pallas kernels, attend(): pl.pallas_call(attend_kernel, out_shape=jax.ShapeDtypeStruct((devices, pa...  6.4 us
    pallas_call x1, Pallas kernels, run_expert(): pl.pallas_call(expert_kernel, out_shape=term_shapes(rows, width), in_spec...  2.34 us
    pallas_call x1, Pallas kernels, project(): pl.pallas_call(functools.partial(project_kernel, own_rows, far), out_shap...  1.69 us
  transfers between devices with their start and end apart: 19, of which 14 were waited for; matrix products, arithmetic and copies ran while one was open for 1% of the time, Pallas kernels for 0%

profile of v19, /device:TPU:0, one launch (start us, length us, event | category | flops | bytes accessed | tf_op | source)
XLA Modules:
  0.0 76.2 jit_solution(16309563765328250795)
XLA Ops:
  0.7 6.4 %attend.1 = bf16[16,16,512]{2,1,0:T(8,128)(2,1)} custom-call(s32[4]{0:T(128)} %len_ref.1, bf16[4,64,576]{2,1,0:T(8,128)(2,1)} %bitcast.7, bf16[4,576,4096]{2,1,0:T(8,128)(2,1)} %cache_ref.1), custom_call_target="tpu_custom_call" | custom-call | flops 1140850688 | bytes 9437184 | tf_op jit(solution)/shard_map/attend/pallas_call | solution.py:146
  7.1 20.3 %all_to_all.5 = bf16[16,16,512]{2,1,0:T(8,128)(2,1)S(1)} all-to-all(bf16[16,16,512]{2,1,0:T(8,128)(2,1)} %attend.1), channel_id=1, replica_groups=mesh['groups'=2,'experts'=16] {'experts'}, dimensions={0} | all-to-all | bytes 524288 | tf_op jit(solution)/shard_map/all_to_all | solution.py:364
  27.4 1.7 %project.1 = (f32[8,7168]{1,0:T(8,128)S(1)}, f32[8,7168]{1,0:T(8,128)S(1)}, f32[8,7168]{1,0:T(8,128)S(1)}, f32[8,7168]{1,0:T(8,128)S(1)}, bf16[8,7168]{1,0:T(8,128)(2,1)S(1)}, /*index=5*/bf16[24,7168]{1,0:T(8,128)(2,1)S(1)}) custom-call(bf16[256,512]{1,0:T(8,128)(2,1)S(1)} %bitcast.5, bf16[4,7168]{1,0:T(4,128)(2,1)S(1)} %copy-done.4, ...), custom_call_target="tpu_custom_call" | custom-call | flops 469762048 | bytes 7340032 | tf_op jit(solution)/shard_map/project/pallas_call | solution.py:230
  29.7 0.8 %collective-permute-done = bf16[8,7168]{1,0:T(8,128)(2,1)S(1)} collective-permute-done((bf16[8,7168]{1,0:T(8,128)(2,1)S(1)}, bf16[8,7168]{1,0:T(8,128)(2,1)S(1)}, u32[]{:S(2)}, u32[]{:S(2)}) %collective-permute-start) | collective-permute-done | bytes 114720 | tf_op jit(solution)/shard_map/ppermute | solution.py:300
  30.6 0.7 collective-permute-start.1
  31.3 1.1 %collective-permute-start.3 = (bf16[8,7168]{1,0:T(8,128)(2,1)S(1)}, bf16[8,7168]{1,0:T(8,128)(2,1)S(1)}, u32[]{:S(2)}, u32[]{:S(2)}) collective-permute-start(bf16[8,7168]{1,0:T(8,128)(2,1)S(1)} %get-tuple-element.30), channel_id=1, source_target_pairs={{0,4},{1,5},{2,6},{3,7},{4,0},{5,1},{6,2},{7,3},{8,12},{9,13},{10,... | collective-permute-start | bytes 344072 | tf_op jit(solution)/shard_map/ppermute | solution.py:300
  32.4 1.8 %collective-permute-start.4 = (bf16[8,7168]{1,0:T(8,128)(2,1)S(1)}, bf16[8,7168]{1,0:T(8,128)(2,1)S(1)}, u32[]{:S(2)}, u32[]{:S(2)}) collective-permute-start(bf16[8,7168]{1,0:T(8,128)(2,1)S(1)} %get-tuple-element.31), channel_id=1, source_target_pairs={{0,2},{1,3},{2,0},{3,1},{4,6},{5,7},{6,4},{7,5},{8,10},{9,11},{10,... | collective-permute-start | bytes 344072 | tf_op jit(solution)/shard_map/ppermute | solution.py:300
  34.3 3.3 %collective-permute-done.1 = bf16[8,7168]{1,0:T(8,128)(2,1)S(1)} collective-permute-done((bf16[8,7168]{1,0:T(8,128)(2,1)S(1)}, bf16[8,7168]{1,0:T(8,128)(2,1)S(1)}, u32[]{:S(2)}, u32[]{:S(2)}) %collective-permute-start.1) | collective-permute-done | bytes 114720 | tf_op jit(solution)/shard_map/ppermute | solution.py:300
  38.1 1.1 %collective-permute-done.4 = bf16[8,7168]{1,0:T(8,128)(2,1)S(1)} collective-permute-done((bf16[8,7168]{1,0:T(8,128)(2,1)S(1)}, bf16[8,7168]{1,0:T(8,128)(2,1)S(1)}, u32[]{:S(2)}, u32[]{:S(2)}) %collective-permute-start.4) | collective-permute-done | bytes 114720 | tf_op jit(solution)/shard_map/ppermute | solution.py:300
  39.3 1.1 %collective-permute-start.5 = (bf16[8,7168]{1,0:T(8,128)(2,1)S(1)}, bf16[8,7168]{1,0:T(8,128)(2,1)S(1)}, u32[]{:S(2)}, u32[]{:S(2)}) collective-permute-start(bf16[8,7168]{1,0:T(8,128)(2,1)S(1)} %fusion.2), channel_id=1, source_target_pairs={{0,8},{1,9},{2,10},{3,11},{4,12},{5,13},{6,14},{7,15},{8,0},{9,1},... | collective-permute-start | bytes 344072 | tf_op jit(solution)/shard_map/ppermute | solution.py:300
  40.4 7.3 %collective-permute-done.5 = bf16[8,7168]{1,0:T(8,128)(2,1)S(1)} collective-permute-done((bf16[8,7168]{1,0:T(8,128)(2,1)S(1)}, bf16[8,7168]{1,0:T(8,128)(2,1)S(1)}, u32[]{:S(2)}, u32[]{:S(2)}) %collective-permute-start.5) | collective-permute-done | bytes 114720 | tf_op jit(solution)/shard_map/ppermute | solution.py:300
  48.0 1.3 %collective-permute-start.7 = (bf16[8,7168]{1,0:T(8,128)(2,1)S(1)}, bf16[8,7168]{1,0:T(8,128)(2,1)S(1)}, u32[]{:S(2)}, u32[]{:S(2)}) collective-permute-start(bf16[8,7168]{1,0:T(8,128)(2,1)S(1)} %add_convert_fusion.3.refs_0_), channel_id=1, source_target_pairs={{0,4},{1,5},{2,6},{3,7},{4,0},{5,1},{6,2},{7,3},{8,12},{9,13},{10,... | collective-permute-start | bytes 344072 | tf_op jit(solution)/shard_map/ppermute | solution.py:300
  49.3 2.1 %collective-permute-start.8 = (bf16[8,7168]{1,0:T(8,128)(2,1)S(1)}, bf16[8,7168]{1,0:T(8,128)(2,1)S(1)}, u32[]{:S(2)}, u32[]{:S(2)}) collective-permute-start(bf16[8,7168]{1,0:T(8,128)(2,1)S(1)} %add_convert_fusion.3.refs_0_), channel_id=1, source_target_pairs={{0,2},{1,3},{2,0},{3,1},{4,6},{5,7},{6,4},{7,5},{8,10},{9,11},{10,... | collective-permute-start | bytes 344072 | tf_op jit(solution)/shard_map/ppermute | solution.py:300
  51.5 3.4 %collective-permute-done.6.refs_1_ = bf16[8,7168]{1,0:T(8,128)(2,1)S(1)} collective-permute-done((bf16[8,7168]{1,0:T(8,128)(2,1)S(1)}, bf16[8,7168]{1,0:T(8,128)(2,1)S(1)}, u32[]{:S(2)}, u32[]{:S(2)}) %collective-permute-start.6) | collective-permute-done | bytes 114720 | tf_op jit(solution)/shard_map/ppermute | solution.py:300
  55.4 1.0 %collective-permute-done.8.refs_3_ = bf16[8,7168]{1,0:T(8,128)(2,1)S(1)} collective-permute-done((bf16[8,7168]{1,0:T(8,128)(2,1)S(1)}, bf16[8,7168]{1,0:T(8,128)(2,1)S(1)}, u32[]{:S(2)}, u32[]{:S(2)}) %collective-permute-start.8) | collective-permute-done | bytes 114720 | tf_op jit(solution)/shard_map/ppermute | solution.py:300
  56.5 1.3 %collective-permute-done.12.refs_7_ = bf16[8,7168]{1,0:T(8,128)(2,1)S(1)} collective-permute-done((bf16[8,7168]{1,0:T(8,128)(2,1)S(1)}, bf16[8,7168]{1,0:T(8,128)(2,1)S(1)}, u32[]{:S(2)}, u32[]{:S(2)}) %collective-permute-start.12) | collective-permute-done | bytes 114720 | tf_op jit(solution)/shard_map/ppermute | solution.py:300
  57.8 2.3 %expert.1 = (f32[8,7168]{1,0:T(8,128)S(1)}, f32[8,7168]{1,0:T(8,128)S(1)}, f32[8,7168]{1,0:T(8,128)S(1)}, f32[8,7168]{1,0:T(8,128)S(1)}, bf16[8,7168]{1,0:T(8,128)(2,1)S(1)}, /*index=5*/bf16[24,7168]{1,0:T(8,128)(2,1)S(1)}) custom-call(bf16[8,7168]{1,0:T(8,128)(2,1)S(1)} %add_convert_fusion.3.refs_0_, bf16[8,7168]{1,0:T(8,128)(2,1)S(1)} %collective-permute-done.6.refs_1_, ...), custom_call_target="tpu_custom_call" | custom-call | flops 704643072 | bytes 11010048 | tf_op jit(solution)/shard_map/expert/pallas_call | solution.py:283
  60.7 0.8 %collective-permute-done.13 = bf16[8,7168]{1,0:T(8,128)(2,1)S(1)} collective-permute-done((bf16[8,7168]{1,0:T(8,128)(2,1)S(1)}, bf16[8,7168]{1,0:T(8,128)(2,1)S(1)}, u32[]{:S(2)}, u32[]{:S(2)}) %collective-permute-start.13) | collective-permute-done | bytes 114720 | tf_op jit(solution)/shard_map/ppermute | solution.py:300
  62.1 1.9 %collective-permute-start.16 = (bf16[8,7168]{1,0:T(8,128)(2,1)S(1)}, bf16[8,7168]{1,0:T(8,128)(2,1)S(1)}, u32[]{:S(2)}, u32[]{:S(2)}) collective-permute-start(bf16[8,7168]{1,0:T(8,128)(2,1)S(1)} %get-tuple-element.28), channel_id=1, source_target_pairs={{0,4},{1,5},{2,6},{3,7},{4,0},{5,1},{6,2},{7,3},{8,12},{9,13},{10,... | collective-permute-start | bytes 344072 | tf_op jit(solution)/shard_map/ppermute | solution.py:300
  63.9 1.3 %collective-permute-start.17 = (bf16[8,7168]{1,0:T(8,128)(2,1)S(1)}, bf16[8,7168]{1,0:T(8,128)(2,1)S(1)}, u32[]{:S(2)}, u32[]{:S(2)}) collective-permute-start(bf16[8,7168]{1,0:T(8,128)(2,1)S(1)} %get-tuple-element.29), channel_id=1, source_target_pairs={{0,2},{1,3},{2,0},{3,1},{4,6},{5,7},{6,4},{7,5},{8,10},{9,11},{10,... | collective-permute-start | bytes 344072 | tf_op jit(solution)/shard_map/ppermute | solution.py:300
  66.0 2.5 %collective-permute-done.14 = bf16[8,7168]{1,0:T(8,128)(2,1)S(1)} collective-permute-done((bf16[8,7168]{1,0:T(8,128)(2,1)S(1)}, bf16[8,7168]{1,0:T(8,128)(2,1)S(1)}, u32[]{:S(2)}, u32[]{:S(2)}) %collective-permute-start.14) | collective-permute-done | bytes 114720 | tf_op jit(solution)/shard_map/ppermute | solution.py:300
  68.5 1.1 %collective-permute-done.16 = bf16[8,7168]{1,0:T(8,128)(2,1)S(1)} collective-permute-done((bf16[8,7168]{1,0:T(8,128)(2,1)S(1)}, bf16[8,7168]{1,0:T(8,128)(2,1)S(1)}, u32[]{:S(2)}, u32[]{:S(2)}) %collective-permute-start.16) | collective-permute-done | bytes 114720 | tf_op jit(solution)/shard_map/ppermute | solution.py:300
  70.5 5.1 %collective-permute-done.18 = bf16[4,7168]{1,0:T(4,128)(2,1)S(1)} collective-permute-done((bf16[4,7168]{1,0:T(4,128)(2,1)S(1)}, bf16[4,7168]{1,0:T(4,128)(2,1)S(1)}, u32[]{:S(2)}, u32[]{:S(2)}) %collective-permute-start.18) | collective-permute-done | bytes 57376 | tf_op jit(solution)/shard_map/ppermute | solution.py:300
  75.5 0.7 add_convert_fusion.7
  (52 shorter events, 4.8 us)
Async XLA Ops:
  0.6 26.7 %slice-start = ((s8[7340032]{0:T(1024)(128)(4,1)}), s8[4194304]{0:T(1024)(128)(4,1)S(1)}, s32[]{:S(2)}) async-start(s8[7340032]{0:T(1024)(128)(4,1)} %bitcast.3), calls=%async_computation.1 | async-start | bytes 8388608
  27.4 30.4 %copy-start = (bf16[7168,256]{1,0:T(8,128)(2,1)S(1)}, bf16[7168,256]{1,0:T(8,128)(2,1)}, u32[]{:S(2)}) copy-start(bf16[7168,256]{1,0:T(8,128)(2,1)} %refs_9_.1) | copy-start | bytes 11010052
  27.4 30.3 %copy-start.1 = (bf16[7168,256]{1,0:T(8,128)(2,1)S(1)}, bf16[7168,256]{1,0:T(8,128)(2,1)}, u32[]{:S(2)}) copy-start(bf16[7168,256]{1,0:T(8,128)(2,1)} %refs_10_.1) | copy-start | bytes 11010052
  27.4 30.3 %copy-start.2 = (bf16[256,7168]{1,0:T(8,128)(2,1)S(1)}, bf16[256,7168]{1,0:T(8,128)(2,1)}, u32[]{:S(2)}) copy-start(bf16[256,7168]{1,0:T(8,128)(2,1)} %refs_11_.1) | copy-start | bytes 11010052
  27.4 30.3 %copy-start.5 = (f32[7168]{0:T(1024)S(1)}, f32[7168]{0:T(1024)}, u32[]{:S(2)}) copy-start(f32[7168]{0:T(1024)} %param.18) | copy-start | bytes 86020
  29.1 1.4 %collective-permute-start = (bf16[8,7168]{1,0:T(8,128)(2,1)S(1)}, bf16[8,7168]{1,0:T(8,128)(2,1)S(1)}, u32[]{:S(2)}, u32[]{:S(2)}) collective-permute-start(bf16[8,7168]{1,0:T(8,128)(2,1)S(1)} %get-tuple-element.15), channel_id=1, source_target_pairs={{0,1},{1,0},{2,3},{3,2},{4,5},{5,4},{6,7},{7,6},{8,9},{9,8},{10,11... | collective-permute-start | bytes 344072 | tf_op jit(solution)/shard_map/ppermute | solution.py:300
  29.2 2.0 %collective-permute-start.2 = (bf16[24,7168]{1,0:T(8,128)(2,1)S(1)}, bf16[24,7168]{1,0:T(8,128)(2,1)S(1)}, u32[]{:S(2)}, u32[]{:S(2)}) collective-permute-start(bf16[24,7168]{1,0:T(8,128)(2,1)S(1)} %get-tuple-element.17), channel_id=1, source_target_pairs={{0,1},{1,0},{2,3},{3,2},{4,5},{5,4},{6,7},{7,6},{8,9},{9,8},{10,11... | collective-permute-start | bytes 1032200 | tf_op jit(solution)/shard_map/ppermute | solution.py:300
  30.6 7.0 %collective-permute-start.1 = (bf16[8,7168]{1,0:T(8,128)(2,1)S(1)}, bf16[8,7168]{1,0:T(8,128)(2,1)S(1)}, u32[]{:S(2)}, u32[]{:S(2)}) collective-permute-start(bf16[8,7168]{1,0:T(8,128)(2,1)S(1)} %add_convert_fusion.6), channel_id=1, source_target_pairs={{0,6},{1,7},{2,4},{3,5},{4,2},{5,3},{6,0},{7,1},{8,14},{9,15},{10,... | collective-permute-start | bytes 344072 | tf_op jit(solution)/shard_map/ppermute | solution.py:300
  31.3 6.8 %collective-permute-start.3 = (bf16[8,7168]{1,0:T(8,128)(2,1)S(1)}, bf16[8,7168]{1,0:T(8,128)(2,1)S(1)}, u32[]{:S(2)}, u32[]{:S(2)}) collective-permute-start(bf16[8,7168]{1,0:T(8,128)(2,1)S(1)} %get-tuple-element.30), channel_id=1, source_target_pairs={{0,4},{1,5},{2,6},{3,7},{4,0},{5,1},{6,2},{7,3},{8,12},{9,13},{10,... | collective-permute-start | bytes 344072 | tf_op jit(solution)/shard_map/ppermute | solution.py:300
  32.4 6.8 %collective-permute-start.4 = (bf16[8,7168]{1,0:T(8,128)(2,1)S(1)}, bf16[8,7168]{1,0:T(8,128)(2,1)S(1)}, u32[]{:S(2)}, u32[]{:S(2)}) collective-permute-start(bf16[8,7168]{1,0:T(8,128)(2,1)S(1)} %get-tuple-element.31), channel_id=1, source_target_pairs={{0,2},{1,3},{2,0},{3,1},{4,6},{5,7},{6,4},{7,5},{8,10},{9,11},{10,... | collective-permute-start | bytes 344072 | tf_op jit(solution)/shard_map/ppermute | solution.py:300
  39.3 8.5 %collective-permute-start.5 = (bf16[8,7168]{1,0:T(8,128)(2,1)S(1)}, bf16[8,7168]{1,0:T(8,128)(2,1)S(1)}, u32[]{:S(2)}, u32[]{:S(2)}) collective-permute-start(bf16[8,7168]{1,0:T(8,128)(2,1)S(1)} %fusion.2), channel_id=1, source_target_pairs={{0,8},{1,9},{2,10},{3,11},{4,12},{5,13},{6,14},{7,15},{8,0},{9,1},... | collective-permute-start | bytes 344072 | tf_op jit(solution)/shard_map/ppermute | solution.py:300
  47.9 7.0 %collective-permute-start.6 = (bf16[8,7168]{1,0:T(8,128)(2,1)S(1)}, bf16[8,7168]{1,0:T(8,128)(2,1)S(1)}, u32[]{:S(2)}, u32[]{:S(2)}) collective-permute-start(bf16[8,7168]{1,0:T(8,128)(2,1)S(1)} %add_convert_fusion.3.refs_0_), channel_id=1, source_target_pairs={{0,6},{1,7},{2,4},{3,5},{4,2},{5,3},{6,0},{7,1},{8,14},{9,15},{10,... | collective-permute-start | bytes 344072 | tf_op jit(solution)/shard_map/ppermute | solution.py:300
  48.0 6.9 %collective-permute-start.7 = (bf16[8,7168]{1,0:T(8,128)(2,1)S(1)}, bf16[8,7168]{1,0:T(8,128)(2,1)S(1)}, u32[]{:S(2)}, u32[]{:S(2)}) collective-permute-start(bf16[8,7168]{1,0:T(8,128)(2,1)S(1)} %add_convert_fusion.3.refs_0_), channel_id=1, source_target_pairs={{0,4},{1,5},{2,6},{3,7},{4,0},{5,1},{6,2},{7,3},{8,12},{9,13},{10,... | collective-permute-start | bytes 344072 | tf_op jit(solution)/shard_map/ppermute | solution.py:300
  49.3 7.1 %collective-permute-start.8 = (bf16[8,7168]{1,0:T(8,128)(2,1)S(1)}, bf16[8,7168]{1,0:T(8,128)(2,1)S(1)}, u32[]{:S(2)}, u32[]{:S(2)}) collective-permute-start(bf16[8,7168]{1,0:T(8,128)(2,1)S(1)} %add_convert_fusion.3.refs_0_), channel_id=1, source_target_pairs={{0,2},{1,3},{2,0},{3,1},{4,6},{5,7},{6,4},{7,5},{8,10},{9,11},{10,... | collective-permute-start | bytes 344072 | tf_op jit(solution)/shard_map/ppermute | solution.py:300
  51.5 5.0 %collective-permute-start.9 = (bf16[8,7168]{1,0:T(8,128)(2,1)S(1)}, bf16[8,7168]{1,0:T(8,128)(2,1)S(1)}, u32[]{:S(2)}, u32[]{:S(2)}) collective-permute-start(bf16[8,7168]{1,0:T(8,128)(2,1)S(1)} %add_convert_fusion.3.refs_0_), channel_id=1, source_target_pairs={{0,1},{1,0},{2,3},{3,2},{4,5},{5,4},{6,7},{7,6},{8,9},{9,8},{10,11... | collective-permute-start | bytes 344072 | tf_op jit(solution)/shard_map/ppermute | solution.py:300
  54.9 1.5 %collective-permute-start.10 = (bf16[8,7168]{1,0:T(8,128)(2,1)S(1)}, bf16[8,7168]{1,0:T(8,128)(2,1)S(1)}, u32[]{:S(2)}, u32[]{:S(2)}) collective-permute-start(bf16[8,7168]{1,0:T(8,128)(2,1)S(1)} %collective-permute-done.6.refs_1_), channel_id=1, source_target_pairs={{0,1},{1,0},{2,3},{3,2},{4,5},{5,4},{6,7},{7,6},{8,9},{9,8},{10,11... | collective-permute-start | bytes 344072 | tf_op jit(solution)/shard_map/ppermute | solution.py:300
  54.9 1.5 %collective-permute-start.11 = (bf16[8,7168]{1,0:T(8,128)(2,1)S(1)}, bf16[8,7168]{1,0:T(8,128)(2,1)S(1)}, u32[]{:S(2)}, u32[]{:S(2)}) collective-permute-start(bf16[8,7168]{1,0:T(8,128)(2,1)S(1)} %collective-permute-done.7.refs_2_), channel_id=1, source_target_pairs={{0,1},{1,0},{2,3},{3,2},{4,5},{5,4},{6,7},{7,6},{8,9},{9,8},{10,11... | collective-permute-start | bytes 344072 | tf_op jit(solution)/shard_map/ppermute | solution.py:300
  56.4 1.3 %collective-permute-start.12 = (bf16[8,7168]{1,0:T(8,128)(2,1)S(1)}, bf16[8,7168]{1,0:T(8,128)(2,1)S(1)}, u32[]{:S(2)}, u32[]{:S(2)}) collective-permute-start(bf16[8,7168]{1,0:T(8,128)(2,1)S(1)} %collective-permute-done.8.refs_3_), channel_id=1, source_target_pairs={{0,1},{1,0},{2,3},{3,2},{4,5},{5,4},{6,7},{7,6},{8,9},{9,8},{10,11... | collective-permute-start | bytes 344072 | tf_op jit(solution)/shard_map/ppermute | solution.py:300
  60.1 1.4 %collective-permute-start.13 = (bf16[8,7168]{1,0:T(8,128)(2,1)S(1)}, bf16[8,7168]{1,0:T(8,128)(2,1)S(1)}, u32[]{:S(2)}, u32[]{:S(2)}) collective-permute-start(bf16[8,7168]{1,0:T(8,128)(2,1)S(1)} %get-tuple-element.21), channel_id=1, source_target_pairs={{0,1},{1,0},{2,3},{3,2},{4,5},{5,4},{6,7},{7,6},{8,9},{9,8},{10,11... | collective-permute-start | bytes 344072 | tf_op jit(solution)/shard_map/ppermute | solution.py:300
  60.4 1.7 %collective-permute-start.15 = (bf16[24,7168]{1,0:T(8,128)(2,1)S(1)}, bf16[24,7168]{1,0:T(8,128)(2,1)S(1)}, u32[]{:S(2)}, u32[]{:S(2)}) collective-permute-start(bf16[24,7168]{1,0:T(8,128)(2,1)S(1)} %get-tuple-element.23), channel_id=1, source_target_pairs={{0,1},{1,0},{2,3},{3,2},{4,5},{5,4},{6,7},{7,6},{8,9},{9,8},{10,11... | collective-permute-start | bytes 1032200 | tf_op jit(solution)/shard_map/ppermute | solution.py:300
  61.6 7.0 %collective-permute-start.14 = (bf16[8,7168]{1,0:T(8,128)(2,1)S(1)}, bf16[8,7168]{1,0:T(8,128)(2,1)S(1)}, u32[]{:S(2)}, u32[]{:S(2)}) collective-permute-start(bf16[8,7168]{1,0:T(8,128)(2,1)S(1)} %add_convert_fusion.2), channel_id=1, source_target_pairs={{0,6},{1,7},{2,4},{3,5},{4,2},{5,3},{6,0},{7,1},{8,14},{9,15},{10,... | collective-permute-start | bytes 344072 | tf_op jit(solution)/shard_map/ppermute | solution.py:300
  62.1 7.6 %collective-permute-start.16 = (bf16[8,7168]{1,0:T(8,128)(2,1)S(1)}, bf16[8,7168]{1,0:T(8,128)(2,1)S(1)}, u32[]{:S(2)}, u32[]{:S(2)}) collective-permute-start(bf16[8,7168]{1,0:T(8,128)(2,1)S(1)} %get-tuple-element.28), channel_id=1, source_target_pairs={{0,4},{1,5},{2,6},{3,7},{4,0},{5,1},{6,2},{7,3},{8,12},{9,13},{10,... | collective-permute-start | bytes 344072 | tf_op jit(solution)/shard_map/ppermute | solution.py:300
  63.9 6.3 %collective-permute-start.17 = (bf16[8,7168]{1,0:T(8,128)(2,1)S(1)}, bf16[8,7168]{1,0:T(8,128)(2,1)S(1)}, u32[]{:S(2)}, u32[]{:S(2)}) collective-permute-start(bf16[8,7168]{1,0:T(8,128)(2,1)S(1)} %get-tuple-element.29), channel_id=1, source_target_pairs={{0,2},{1,3},{2,0},{3,1},{4,6},{5,7},{6,4},{7,5},{8,10},{9,11},{10,... | collective-permute-start | bytes 344072 | tf_op jit(solution)/shard_map/ppermute | solution.py:300
  70.3 5.2 %collective-permute-start.18 = (bf16[4,7168]{1,0:T(4,128)(2,1)S(1)}, bf16[4,7168]{1,0:T(4,128)(2,1)S(1)}, u32[]{:S(2)}, u32[]{:S(2)}) collective-permute-start(bf16[4,7168]{1,0:T(4,128)(2,1)S(1)} %slice.68), channel_id=1, source_target_pairs={{0,8},{1,9},{2,10},{3,11},{4,12},{5,13},{6,14},{7,15},{8,0},{9,1},... | collective-permute-start | bytes 172040 | tf_op jit(solution)/shard_map/ppermute | solution.py:300
  (5 other events, 95.1 us)

commit v20 on v19

--- a/solution.py
+++ b/solution.py
@@ -123,7 +123,8 @@
         visit(own_rows + group * GROUP, GROUP)
         return 0
 
-    visit(0, own_rows)
+    visit(0, own_rows // 2)
+    visit(own_rows // 2, own_rows - own_rows // 2)
     rest = items - own_rows
     lax.fori_loop(0, rest // GROUP, visit_group, 0)
     left = rest % GROUP

time: 75.6 us -> 74.7 us (0.988)
  blocking collectives: 20.3 us -> 18 us
  Pallas kernels: 10.4 us -> 12 us
    all_to_all x1, blocking collectives: 20.3 us -> 18 us  [shards(): lax.all_to_all(latent, 'experts', split_axis=0, concat_axis=0, tiled=True)]
    pallas_call x1, Pallas kernels: 6.4 us -> 7.93 us  [attend(): pl.pallas_call(attend_kernel, out_shape=jax.ShapeDtypeStruct((devices, pa...]
where the time goes in v20:
time: 74.7 us; the launch traced here: 75.5 us
  waiting for transfers between devices  29 us (39%)
  blocking collectives  18 us (24%)
  starting transfers between devices  13.5 us (18%)
  Pallas kernels  12 us (16%)
  other arithmetic  1.33 us (2%)
  between operations  0.85 us (1%)
  local copies, waits for them, and re-layouts  0.77 us (1%)
    ppermute x19, waiting for transfers between devices, swap(): return lax.ppermute(array, 'experts', pairs)  29 us
    all_to_all x1, blocking collectives, shards(): lax.all_to_all(latent, 'experts', split_axis=0, concat_axis=0, tiled=True)  18 us
    ppermute x19, starting transfers between devices, swap(): return lax.ppermute(array, 'experts', pairs)  13.5 us
    pallas_call x1, Pallas kernels, attend(): pl.pallas_call(attend_kernel, out_shape=jax.ShapeDtypeStruct((devices, pa...  7.93 us
    pallas_call x1, Pallas kernels, run_expert(): pl.pallas_call(expert_kernel, out_shape=term_shapes(rows, width), in_spec...  2.35 us
    pallas_call x1, Pallas kernels, project(): pl.pallas_call(functools.partial(project_kernel, own_rows, far), out_shap...  1.69 us
  transfers between devices with their start and end apart: 19, of which 14 were waited for; matrix products, arithmetic and copies ran while one was open for 1% of the time, Pallas kernels for 0%

profile of v20, /device:TPU:0, one launch (start us, length us, event | category | flops | bytes accessed | tf_op | source)
XLA Modules:
  0.0 75.5 jit_solution(6373780103538802420)
XLA Ops:
  0.7 7.9 %attend.1 = bf16[16,16,512]{2,1,0:T(8,128)(2,1)} custom-call(s32[4]{0:T(128)} %len_ref.1, bf16[4,64,576]{2,1,0:T(8,128)(2,1)} %bitcast.7, bf16[4,576,4096]{2,1,0:T(8,128)(2,1)} %cache_ref.1), custom_call_target="tpu_custom_call" | custom-call | flops 1140850688 | bytes 9437184 | tf_op jit(solution)/shard_map/attend/pallas_call | solution.py:147
  8.6 18.0 %all_to_all.5 = bf16[16,16,512]{2,1,0:T(8,128)(2,1)S(1)} all-to-all(bf16[16,16,512]{2,1,0:T(8,128)(2,1)} %attend.1), channel_id=1, replica_groups=mesh['groups'=2,'experts'=16] {'experts'}, dimensions={0} | all-to-all | bytes 524288 | tf_op jit(solution)/shard_map/all_to_all | solution.py:365
  26.7 1.7 %project.1 = (f32[8,7168]{1,0:T(8,128)S(1)}, f32[8,7168]{1,0:T(8,128)S(1)}, f32[8,7168]{1,0:T(8,128)S(1)}, f32[8,7168]{1,0:T(8,128)S(1)}, bf16[8,7168]{1,0:T(8,128)(2,1)S(1)}, /*index=5*/bf16[24,7168]{1,0:T(8,128)(2,1)S(1)}) custom-call(bf16[256,512]{1,0:T(8,128)(2,1)S(1)} %bitcast.5, bf16[4,7168]{1,0:T(4,128)(2,1)S(1)} %copy-done.4, ...), custom_call_target="tpu_custom_call" | custom-call | flops 469762048 | bytes 7340032 | tf_op jit(solution)/shard_map/project/pallas_call | solution.py:231
  28.9 0.8 %collective-permute-done = bf16[8,7168]{1,0:T(8,128)(2,1)S(1)} collective-permute-done((bf16[8,7168]{1,0:T(8,128)(2,1)S(1)}, bf16[8,7168]{1,0:T(8,128)(2,1)S(1)}, u32[]{:S(2)}, u32[]{:S(2)}) %collective-permute-start) | collective-permute-done | bytes 114720 | tf_op jit(solution)/shard_map/ppermute | solution.py:301
  29.8 0.6 collective-permute-start.1
  30.5 1.1 %collective-permute-start.3 = (bf16[8,7168]{1,0:T(8,128)(2,1)S(1)}, bf16[8,7168]{1,0:T(8,128)(2,1)S(1)}, u32[]{:S(2)}, u32[]{:S(2)}) collective-permute-start(bf16[8,7168]{1,0:T(8,128)(2,1)S(1)} %get-tuple-element.30), channel_id=1, source_target_pairs={{0,4},{1,5},{2,6},{3,7},{4,0},{5,1},{6,2},{7,3},{8,12},{9,13},{10,... | collective-permute-start | bytes 344072 | tf_op jit(solution)/shard_map/ppermute | solution.py:301
  31.6 1.8 %collective-permute-start.4 = (bf16[8,7168]{1,0:T(8,128)(2,1)S(1)}, bf16[8,7168]{1,0:T(8,128)(2,1)S(1)}, u32[]{:S(2)}, u32[]{:S(2)}) collective-permute-start(bf16[8,7168]{1,0:T(8,128)(2,1)S(1)} %get-tuple-element.31), channel_id=1, source_target_pairs={{0,2},{1,3},{2,0},{3,1},{4,6},{5,7},{6,4},{7,5},{8,10},{9,11},{10,... | collective-permute-start | bytes 344072 | tf_op jit(solution)/shard_map/ppermute | solution.py:301
  33.5 3.3 %collective-permute-done.1 = bf16[8,7168]{1,0:T(8,128)(2,1)S(1)} collective-permute-done((bf16[8,7168]{1,0:T(8,128)(2,1)S(1)}, bf16[8,7168]{1,0:T(8,128)(2,1)S(1)}, u32[]{:S(2)}, u32[]{:S(2)}) %collective-permute-start.1) | collective-permute-done | bytes 114720 | tf_op jit(solution)/shard_map/ppermute | solution.py:301
  37.3 1.1 %collective-permute-done.4 = bf16[8,7168]{1,0:T(8,128)(2,1)S(1)} collective-permute-done((bf16[8,7168]{1,0:T(8,128)(2,1)S(1)}, bf16[8,7168]{1,0:T(8,128)(2,1)S(1)}, u32[]{:S(2)}, u32[]{:S(2)}) %collective-permute-start.4) | collective-permute-done | bytes 114720 | tf_op jit(solution)/shard_map/ppermute | solution.py:301
  38.5 1.1 %collective-permute-start.5 = (bf16[8,7168]{1,0:T(8,128)(2,1)S(1)}, bf16[8,7168]{1,0:T(8,128)(2,1)S(1)}, u32[]{:S(2)}, u32[]{:S(2)}) collective-permute-start(bf16[8,7168]{1,0:T(8,128)(2,1)S(1)} %fusion.2), channel_id=1, source_target_pairs={{0,8},{1,9},{2,10},{3,11},{4,12},{5,13},{6,14},{7,15},{8,0},{9,1},... | collective-permute-start | bytes 344072 | tf_op jit(solution)/shard_map/ppermute | solution.py:301
  39.6 7.3 %collective-permute-done.5 = bf16[8,7168]{1,0:T(8,128)(2,1)S(1)} collective-permute-done((bf16[8,7168]{1,0:T(8,128)(2,1)S(1)}, bf16[8,7168]{1,0:T(8,128)(2,1)S(1)}, u32[]{:S(2)}, u32[]{:S(2)}) %collective-permute-start.5) | collective-permute-done | bytes 114720 | tf_op jit(solution)/shard_map/ppermute | solution.py:301
  47.2 1.3 %collective-permute-start.7 = (bf16[8,7168]{1,0:T(8,128)(2,1)S(1)}, bf16[8,7168]{1,0:T(8,128)(2,1)S(1)}, u32[]{:S(2)}, u32[]{:S(2)}) collective-permute-start(bf16[8,7168]{1,0:T(8,128)(2,1)S(1)} %add_convert_fusion.3.refs_0_), channel_id=1, source_target_pairs={{0,4},{1,5},{2,6},{3,7},{4,0},{5,1},{6,2},{7,3},{8,12},{9,13},{10,... | collective-permute-start | bytes 344072 | tf_op jit(solution)/shard_map/ppermute | solution.py:301
  48.6 2.1 %collective-permute-start.8 = (bf16[8,7168]{1,0:T(8,128)(2,1)S(1)}, bf16[8,7168]{1,0:T(8,128)(2,1)S(1)}, u32[]{:S(2)}, u32[]{:S(2)}) collective-permute-start(bf16[8,7168]{1,0:T(8,128)(2,1)S(1)} %add_convert_fusion.3.refs_0_), channel_id=1, source_target_pairs={{0,2},{1,3},{2,0},{3,1},{4,6},{5,7},{6,4},{7,5},{8,10},{9,11},{10,... | collective-permute-start | bytes 344072 | tf_op jit(solution)/shard_map/ppermute | solution.py:301
  50.7 3.4 %collective-permute-done.6.refs_1_ = bf16[8,7168]{1,0:T(8,128)(2,1)S(1)} collective-permute-done((bf16[8,7168]{1,0:T(8,128)(2,1)S(1)}, bf16[8,7168]{1,0:T(8,128)(2,1)S(1)}, u32[]{:S(2)}, u32[]{:S(2)}) %collective-permute-start.6) | collective-permute-done | bytes 114720 | tf_op jit(solution)/shard_map/ppermute | solution.py:301
  54.6 1.0 %collective-permute-done.8.refs_3_ = bf16[8,7168]{1,0:T(8,128)(2,1)S(1)} collective-permute-done((bf16[8,7168]{1,0:T(8,128)(2,1)S(1)}, bf16[8,7168]{1,0:T(8,128)(2,1)S(1)}, u32[]{:S(2)}, u32[]{:S(2)}) %collective-permute-start.8) | collective-permute-done | bytes 114720 | tf_op jit(solution)/shard_map/ppermute | solution.py:301
  55.7 1.3 %collective-permute-done.12.refs_7_ = bf16[8,7168]{1,0:T(8,128)(2,1)S(1)} collective-permute-done((bf16[8,7168]{1,0:T(8,128)(2,1)S(1)}, bf16[8,7168]{1,0:T(8,128)(2,1)S(1)}, u32[]{:S(2)}, u32[]{:S(2)}) %collective-permute-start.12) | collective-permute-done | bytes 114720 | tf_op jit(solution)/shard_map/ppermute | solution.py:301
  57.0 2.3 %expert.1 = (f32[8,7168]{1,0:T(8,128)S(1)}, f32[8,7168]{1,0:T(8,128)S(1)}, f32[8,7168]{1,0:T(8,128)S(1)}, f32[8,7168]{1,0:T(8,128)S(1)}, bf16[8,7168]{1,0:T(8,128)(2,1)S(1)}, /*index=5*/bf16[24,7168]{1,0:T(8,128)(2,1)S(1)}) custom-call(bf16[8,7168]{1,0:T(8,128)(2,1)S(1)} %add_convert_fusion.3.refs_0_, bf16[8,7168]{1,0:T(8,128)(2,1)S(1)} %collective-permute-done.6.refs_1_, ...), custom_call_target="tpu_custom_call" | custom-call | flops 704643072 | bytes 11010048 | tf_op jit(solution)/shard_map/expert/pallas_call | solution.py:284
  59.9 0.8 %collective-permute-done.13 = bf16[8,7168]{1,0:T(8,128)(2,1)S(1)} collective-permute-done((bf16[8,7168]{1,0:T(8,128)(2,1)S(1)}, bf16[8,7168]{1,0:T(8,128)(2,1)S(1)}, u32[]{:S(2)}, u32[]{:S(2)}) %collective-permute-start.13) | collective-permute-done | bytes 114720 | tf_op jit(solution)/shard_map/ppermute | solution.py:301
  61.3 1.9 %collective-permute-start.16 = (bf16[8,7168]{1,0:T(8,128)(2,1)S(1)}, bf16[8,7168]{1,0:T(8,128)(2,1)S(1)}, u32[]{:S(2)}, u32[]{:S(2)}) collective-permute-start(bf16[8,7168]{1,0:T(8,128)(2,1)S(1)} %get-tuple-element.28), channel_id=1, source_target_pairs={{0,4},{1,5},{2,6},{3,7},{4,0},{5,1},{6,2},{7,3},{8,12},{9,13},{10,... | collective-permute-start | bytes 344072 | tf_op jit(solution)/shard_map/ppermute | solution.py:301
  63.2 1.3 %collective-permute-start.17 = (bf16[8,7168]{1,0:T(8,128)(2,1)S(1)}, bf16[8,7168]{1,0:T(8,128)(2,1)S(1)}, u32[]{:S(2)}, u32[]{:S(2)}) collective-permute-start(bf16[8,7168]{1,0:T(8,128)(2,1)S(1)} %get-tuple-element.29), channel_id=1, source_target_pairs={{0,2},{1,3},{2,0},{3,1},{4,6},{5,7},{6,4},{7,5},{8,10},{9,11},{10,... | collective-permute-start | bytes 344072 | tf_op jit(solution)/shard_map/ppermute | solution.py:301
  65.2 2.5 %collective-permute-done.14 = bf16[8,7168]{1,0:T(8,128)(2,1)S(1)} collective-permute-done((bf16[8,7168]{1,0:T(8,128)(2,1)S(1)}, bf16[8,7168]{1,0:T(8,128)(2,1)S(1)}, u32[]{:S(2)}, u32[]{:S(2)}) %collective-permute-start.14) | collective-permute-done | bytes 114720 | tf_op jit(solution)/shard_map/ppermute | solution.py:301
  67.7 1.1 %collective-permute-done.16 = bf16[8,7168]{1,0:T(8,128)(2,1)S(1)} collective-permute-done((bf16[8,7168]{1,0:T(8,128)(2,1)S(1)}, bf16[8,7168]{1,0:T(8,128)(2,1)S(1)}, u32[]{:S(2)}, u32[]{:S(2)}) %collective-permute-start.16) | collective-permute-done | bytes 114720 | tf_op jit(solution)/shard_map/ppermute | solution.py:301
  69.7 5.1 %collective-permute-done.18 = bf16[4,7168]{1,0:T(4,128)(2,1)S(1)} collective-permute-done((bf16[4,7168]{1,0:T(4,128)(2,1)S(1)}, bf16[4,7168]{1,0:T(4,128)(2,1)S(1)}, u32[]{:S(2)}, u32[]{:S(2)}) %collective-permute-start.18) | collective-permute-done | bytes 57376 | tf_op jit(solution)/shard_map/ppermute | solution.py:301
  74.8 0.7 add_convert_fusion.7
  (52 shorter events, 4.8 us)
Async XLA Ops:
  0.6 26.0 %slice-start = ((s8[7340032]{0:T(1024)(128)(4,1)}), s8[4194304]{0:T(1024)(128)(4,1)S(1)}, s32[]{:S(2)}) async-start(s8[7340032]{0:T(1024)(128)(4,1)} %bitcast.3), calls=%async_computation.1 | async-start | bytes 8388608
  26.6 30.4 %copy-start = (bf16[7168,256]{1,0:T(8,128)(2,1)S(1)}, bf16[7168,256]{1,0:T(8,128)(2,1)}, u32[]{:S(2)}) copy-start(bf16[7168,256]{1,0:T(8,128)(2,1)} %refs_9_.1) | copy-start | bytes 11010052
  26.6 30.4 %copy-start.1 = (bf16[7168,256]{1,0:T(8,128)(2,1)S(1)}, bf16[7168,256]{1,0:T(8,128)(2,1)}, u32[]{:S(2)}) copy-start(bf16[7168,256]{1,0:T(8,128)(2,1)} %refs_10_.1) | copy-start | bytes 11010052
  26.6 30.3 %copy-start.2 = (bf16[256,7168]{1,0:T(8,128)(2,1)S(1)}, bf16[256,7168]{1,0:T(8,128)(2,1)}, u32[]{:S(2)}) copy-start(bf16[256,7168]{1,0:T(8,128)(2,1)} %refs_11_.1) | copy-start | bytes 11010052
  26.7 30.3 %copy-start.5 = (f32[7168]{0:T(1024)S(1)}, f32[7168]{0:T(1024)}, u32[]{:S(2)}) copy-start(f32[7168]{0:T(1024)} %param.18) | copy-start | bytes 86020
  28.4 1.4 %collective-permute-start = (bf16[8,7168]{1,0:T(8,128)(2,1)S(1)}, bf16[8,7168]{1,0:T(8,128)(2,1)S(1)}, u32[]{:S(2)}, u32[]{:S(2)}) collective-permute-start(bf16[8,7168]{1,0:T(8,128)(2,1)S(1)} %get-tuple-element.15), channel_id=1, source_target_pairs={{0,1},{1,0},{2,3},{3,2},{4,5},{5,4},{6,7},{7,6},{8,9},{9,8},{10,11... | collective-permute-start | bytes 344072 | tf_op jit(solution)/shard_map/ppermute | solution.py:301
  28.4 2.0 %collective-permute-start.2 = (bf16[24,7168]{1,0:T(8,128)(2,1)S(1)}, bf16[24,7168]{1,0:T(8,128)(2,1)S(1)}, u32[]{:S(2)}, u32[]{:S(2)}) collective-permute-start(bf16[24,7168]{1,0:T(8,128)(2,1)S(1)} %get-tuple-element.17), channel_id=1, source_target_pairs={{0,1},{1,0},{2,3},{3,2},{4,5},{5,4},{6,7},{7,6},{8,9},{9,8},{10,11... | collective-permute-start | bytes 1032200 | tf_op jit(solution)/shard_map/ppermute | solution.py:301
  29.8 7.0 %collective-permute-start.1 = (bf16[8,7168]{1,0:T(8,128)(2,1)S(1)}, bf16[8,7168]{1,0:T(8,128)(2,1)S(1)}, u32[]{:S(2)}, u32[]{:S(2)}) collective-permute-start(bf16[8,7168]{1,0:T(8,128)(2,1)S(1)} %add_convert_fusion.6), channel_id=1, source_target_pairs={{0,6},{1,7},{2,4},{3,5},{4,2},{5,3},{6,0},{7,1},{8,14},{9,15},{10,... | collective-permute-start | bytes 344072 | tf_op jit(solution)/shard_map/ppermute | solution.py:301
  30.5 6.8 %collective-permute-start.3 = (bf16[8,7168]{1,0:T(8,128)(2,1)S(1)}, bf16[8,7168]{1,0:T(8,128)(2,1)S(1)}, u32[]{:S(2)}, u32[]{:S(2)}) collective-permute-start(bf16[8,7168]{1,0:T(8,128)(2,1)S(1)} %get-tuple-element.30), channel_id=1, source_target_pairs={{0,4},{1,5},{2,6},{3,7},{4,0},{5,1},{6,2},{7,3},{8,12},{9,13},{10,... | collective-permute-start | bytes 344072 | tf_op jit(solution)/shard_map/ppermute | solution.py:301
  31.6 6.8 %collective-permute-start.4 = (bf16[8,7168]{1,0:T(8,128)(2,1)S(1)}, bf16[8,7168]{1,0:T(8,128)(2,1)S(1)}, u32[]{:S(2)}, u32[]{:S(2)}) collective-permute-start(bf16[8,7168]{1,0:T(8,128)(2,1)S(1)} %get-tuple-element.31), channel_id=1, source_target_pairs={{0,2},{1,3},{2,0},{3,1},{4,6},{5,7},{6,4},{7,5},{8,10},{9,11},{10,... | collective-permute-start | bytes 344072 | tf_op jit(solution)/shard_map/ppermute | solution.py:301
  38.5 8.5 %collective-permute-start.5 = (bf16[8,7168]{1,0:T(8,128)(2,1)S(1)}, bf16[8,7168]{1,0:T(8,128)(2,1)S(1)}, u32[]{:S(2)}, u32[]{:S(2)}) collective-permute-start(bf16[8,7168]{1,0:T(8,128)(2,1)S(1)} %fusion.2), channel_id=1, source_target_pairs={{0,8},{1,9},{2,10},{3,11},{4,12},{5,13},{6,14},{7,15},{8,0},{9,1},... | collective-permute-start | bytes 344072 | tf_op jit(solution)/shard_map/ppermute | solution.py:301
  47.2 7.0 %collective-permute-start.6 = (bf16[8,7168]{1,0:T(8,128)(2,1)S(1)}, bf16[8,7168]{1,0:T(8,128)(2,1)S(1)}, u32[]{:S(2)}, u32[]{:S(2)}) collective-permute-start(bf16[8,7168]{1,0:T(8,128)(2,1)S(1)} %add_convert_fusion.3.refs_0_), channel_id=1, source_target_pairs={{0,6},{1,7},{2,4},{3,5},{4,2},{5,3},{6,0},{7,1},{8,14},{9,15},{10,... | collective-permute-start | bytes 344072 | tf_op jit(solution)/shard_map/ppermute | solution.py:301
  47.2 6.9 %collective-permute-start.7 = (bf16[8,7168]{1,0:T(8,128)(2,1)S(1)}, bf16[8,7168]{1,0:T(8,128)(2,1)S(1)}, u32[]{:S(2)}, u32[]{:S(2)}) collective-permute-start(bf16[8,7168]{1,0:T(8,128)(2,1)S(1)} %add_convert_fusion.3.refs_0_), channel_id=1, source_target_pairs={{0,4},{1,5},{2,6},{3,7},{4,0},{5,1},{6,2},{7,3},{8,12},{9,13},{10,... | collective-permute-start | bytes 344072 | tf_op jit(solution)/shard_map/ppermute | solution.py:301
  48.6 7.1 %collective-permute-start.8 = (bf16[8,7168]{1,0:T(8,128)(2,1)S(1)}, bf16[8,7168]{1,0:T(8,128)(2,1)S(1)}, u32[]{:S(2)}, u32[]{:S(2)}) collective-permute-start(bf16[8,7168]{1,0:T(8,128)(2,1)S(1)} %add_convert_fusion.3.refs_0_), channel_id=1, source_target_pairs={{0,2},{1,3},{2,0},{3,1},{4,6},{5,7},{6,4},{7,5},{8,10},{9,11},{10,... | collective-permute-start | bytes 344072 | tf_op jit(solution)/shard_map/ppermute | solution.py:301
  50.7 5.0 %collective-permute-start.9 = (bf16[8,7168]{1,0:T(8,128)(2,1)S(1)}, bf16[8,7168]{1,0:T(8,128)(2,1)S(1)}, u32[]{:S(2)}, u32[]{:S(2)}) collective-permute-start(bf16[8,7168]{1,0:T(8,128)(2,1)S(1)} %add_convert_fusion.3.refs_0_), channel_id=1, source_target_pairs={{0,1},{1,0},{2,3},{3,2},{4,5},{5,4},{6,7},{7,6},{8,9},{9,8},{10,11... | collective-permute-start | bytes 344072 | tf_op jit(solution)/shard_map/ppermute | solution.py:301
  54.1 1.5 %collective-permute-start.10 = (bf16[8,7168]{1,0:T(8,128)(2,1)S(1)}, bf16[8,7168]{1,0:T(8,128)(2,1)S(1)}, u32[]{:S(2)}, u32[]{:S(2)}) collective-permute-start(bf16[8,7168]{1,0:T(8,128)(2,1)S(1)} %collective-permute-done.6.refs_1_), channel_id=1, source_target_pairs={{0,1},{1,0},{2,3},{3,2},{4,5},{5,4},{6,7},{7,6},{8,9},{9,8},{10,11... | collective-permute-start | bytes 344072 | tf_op jit(solution)/shard_map/ppermute | solution.py:301
  54.1 1.5 %collective-permute-start.11 = (bf16[8,7168]{1,0:T(8,128)(2,1)S(1)}, bf16[8,7168]{1,0:T(8,128)(2,1)S(1)}, u32[]{:S(2)}, u32[]{:S(2)}) collective-permute-start(bf16[8,7168]{1,0:T(8,128)(2,1)S(1)} %collective-permute-done.7.refs_2_), channel_id=1, source_target_pairs={{0,1},{1,0},{2,3},{3,2},{4,5},{5,4},{6,7},{7,6},{8,9},{9,8},{10,11... | collective-permute-start | bytes 344072 | tf_op jit(solution)/shard_map/ppermute | solution.py:301
  55.7 1.3 %collective-permute-start.12 = (bf16[8,7168]{1,0:T(8,128)(2,1)S(1)}, bf16[8,7168]{1,0:T(8,128)(2,1)S(1)}, u32[]{:S(2)}, u32[]{:S(2)}) collective-permute-start(bf16[8,7168]{1,0:T(8,128)(2,1)S(1)} %collective-permute-done.8.refs_3_), channel_id=1, source_target_pairs={{0,1},{1,0},{2,3},{3,2},{4,5},{5,4},{6,7},{7,6},{8,9},{9,8},{10,11... | collective-permute-start | bytes 344072 | tf_op jit(solution)/shard_map/ppermute | solution.py:301
  59.4 1.4 %collective-permute-start.13 = (bf16[8,7168]{1,0:T(8,128)(2,1)S(1)}, bf16[8,7168]{1,0:T(8,128)(2,1)S(1)}, u32[]{:S(2)}, u32[]{:S(2)}) collective-permute-start(bf16[8,7168]{1,0:T(8,128)(2,1)S(1)} %get-tuple-element.21), channel_id=1, source_target_pairs={{0,1},{1,0},{2,3},{3,2},{4,5},{5,4},{6,7},{7,6},{8,9},{9,8},{10,11... | collective-permute-start | bytes 344072 | tf_op jit(solution)/shard_map/ppermute | solution.py:301
  59.6 1.7 %collective-permute-start.15 = (bf16[24,7168]{1,0:T(8,128)(2,1)S(1)}, bf16[24,7168]{1,0:T(8,128)(2,1)S(1)}, u32[]{:S(2)}, u32[]{:S(2)}) collective-permute-start(bf16[24,7168]{1,0:T(8,128)(2,1)S(1)} %get-tuple-element.23), channel_id=1, source_target_pairs={{0,1},{1,0},{2,3},{3,2},{4,5},{5,4},{6,7},{7,6},{8,9},{9,8},{10,11... | collective-permute-start | bytes 1032200 | tf_op jit(solution)/shard_map/ppermute | solution.py:301
  60.8 7.0 %collective-permute-start.14 = (bf16[8,7168]{1,0:T(8,128)(2,1)S(1)}, bf16[8,7168]{1,0:T(8,128)(2,1)S(1)}, u32[]{:S(2)}, u32[]{:S(2)}) collective-permute-start(bf16[8,7168]{1,0:T(8,128)(2,1)S(1)} %add_convert_fusion.2), channel_id=1, source_target_pairs={{0,6},{1,7},{2,4},{3,5},{4,2},{5,3},{6,0},{7,1},{8,14},{9,15},{10,... | collective-permute-start | bytes 344072 | tf_op jit(solution)/shard_map/ppermute | solution.py:301
  61.3 7.6 %collective-permute-start.16 = (bf16[8,7168]{1,0:T(8,128)(2,1)S(1)}, bf16[8,7168]{1,0:T(8,128)(2,1)S(1)}, u32[]{:S(2)}, u32[]{:S(2)}) collective-permute-start(bf16[8,7168]{1,0:T(8,128)(2,1)S(1)} %get-tuple-element.28), channel_id=1, source_target_pairs={{0,4},{1,5},{2,6},{3,7},{4,0},{5,1},{6,2},{7,3},{8,12},{9,13},{10,... | collective-permute-start | bytes 344072 | tf_op jit(solution)/shard_map/ppermute | solution.py:301
  63.2 6.3 %collective-permute-start.17 = (bf16[8,7168]{1,0:T(8,128)(2,1)S(1)}, bf16[8,7168]{1,0:T(8,128)(2,1)S(1)}, u32[]{:S(2)}, u32[]{:S(2)}) collective-permute-start(bf16[8,7168]{1,0:T(8,128)(2,1)S(1)} %get-tuple-element.29), channel_id=1, source_target_pairs={{0,2},{1,3},{2,0},{3,1},{4,6},{5,7},{6,4},{7,5},{8,10},{9,11},{10,... | collective-permute-start | bytes 344072 | tf_op jit(solution)/shard_map/ppermute | solution.py:301
  69.5 5.2 %collective-permute-start.18 = (bf16[4,7168]{1,0:T(4,128)(2,1)S(1)}, bf16[4,7168]{1,0:T(4,128)(2,1)S(1)}, u32[]{:S(2)}, u32[]{:S(2)}) collective-permute-start(bf16[4,7168]{1,0:T(4,128)(2,1)S(1)} %slice.68), channel_id=1, source_target_pairs={{0,8},{1,9},{2,10},{3,11},{4,12},{5,13},{6,14},{7,15},{8,0},{9,1},... | collective-permute-start | bytes 172040 | tf_op jit(solution)/shard_map/ppermute | solution.py:301
  (5 other events, 92.8 us)

commit v21 on v13

--- a/solution.py
+++ b/solution.py
@@ -15,7 +15,7 @@
 LANES = 128
 TILE = 256
 PARTS = 4
-SQUARE = (6, 4, 2, 0)
+SQUARE = (2, 4, 6, 0)
 PIECES = len(SQUARE)
 MIB = 2**20
 
@@ -194,7 +194,7 @@
     far_bits = far.bit_length() - 1
     request, slot = row & (own_rows - 1), row >> turn
     far_at, slot = slot & (far - 1), slot >> far_bits
-    distance = (far_at << 3) + ((3 - (slot & 3)) << 1) + (slot >> 2)
+    distance = (far_at << 3) + ((slot + 1 & 3) << 1) + (slot >> 2)
     device = distance ^ lax.axis_index("experts")
     choices = []
     for head in range(own_heads):

time: 75.3 us -> 74.5 us (0.989)
  blocking collectives: 18.9 us -> 16.8 us
  Pallas kernels: 10.7 us -> 11.9 us
    all_to_all x1, blocking collectives: 18.9 us -> 16.8 us  [shards(): lax.all_to_all(latent, 'experts', split_axis=0, concat_axis=0, tiled=True)]
    pallas_call x1, Pallas kernels: 6.66 us -> 7.86 us  [attend(): pl.pallas_call(attend_kernel, out_shape=jax.ShapeDtypeStruct((devices, pa...]
  transfers between devices with their start and end apart: 19 -> 19, of which waited for: 14 -> 15; matrix products, arithmetic and copies ran while one was open for 1% -> 1% of each run, Pallas kernels for 0% -> 0%
where the time goes in v21:
time: 74.5 us; the launch traced here: 74.1 us
  waiting for transfers between devices  29 us (39%)
  blocking collectives  16.8 us (23%)
  starting transfers between devices  13.5 us (18%)
  Pallas kernels  11.9 us (16%)
  other arithmetic  1.33 us (2%)
  between operations  0.84 us (1%)
  local copies, waits for them, and re-layouts  0.77 us (1%)
    ppermute x19, waiting for transfers between devices, swap(): return lax.ppermute(array, 'experts', pairs)  29 us
    all_to_all x1, blocking collectives, shards(): lax.all_to_all(latent, 'experts', split_axis=0, concat_axis=0, tiled=True)  16.8 us
    ppermute x19, starting transfers between devices, swap(): return lax.ppermute(array, 'experts', pairs)  13.5 us
    pallas_call x1, Pallas kernels, attend(): pl.pallas_call(attend_kernel, out_shape=jax.ShapeDtypeStruct((devices, pa...  7.86 us
    pallas_call x1, Pallas kernels, run_expert(): pl.pallas_call(expert_kernel, out_shape=term_shapes(rows, width), in_spec...  2.35 us
    pallas_call x1, Pallas kernels, project(): pl.pallas_call(functools.partial(project_kernel, own_rows, far), out_shap...  1.69 us
  transfers between devices with their start and end apart: 19, of which 15 were waited for; matrix products, arithmetic and copies ran while one was open for 1% of the time, Pallas kernels for 0%

profile of v21, /device:TPU:0, one launch (start us, length us, event | category | flops | bytes accessed | tf_op | source)
XLA Modules:
  0.0 74.1 jit_solution(12341296928146579378)
XLA Ops:
  0.7 7.9 %attend.1 = bf16[16,16,512]{2,1,0:T(8,128)(2,1)} custom-call(s32[4]{0:T(128)} %len_ref.1, bf16[4,64,576]{2,1,0:T(8,128)(2,1)} %bitcast.7, bf16[4,576,4096]{2,1,0:T(8,128)(2,1)} %cache_ref.1), custom_call_target="tpu_custom_call" | custom-call | flops 1140850688 | bytes 9437184 | tf_op jit(solution)/shard_map/attend/pallas_call | solution.py:144
  8.5 16.8 %all_to_all.5 = bf16[16,16,512]{2,1,0:T(8,128)(2,1)S(1)} all-to-all(bf16[16,16,512]{2,1,0:T(8,128)(2,1)} %attend.1), channel_id=1, replica_groups=mesh['groups'=2,'experts'=16] {'experts'}, dimensions={0} | all-to-all | bytes 524288 | tf_op jit(solution)/shard_map/all_to_all | solution.py:362
  25.4 1.7 %project.1 = (f32[8,7168]{1,0:T(8,128)S(1)}, f32[8,7168]{1,0:T(8,128)S(1)}, f32[8,7168]{1,0:T(8,128)S(1)}, f32[8,7168]{1,0:T(8,128)S(1)}, bf16[8,7168]{1,0:T(8,128)(2,1)S(1)}, /*index=5*/bf16[24,7168]{1,0:T(8,128)(2,1)S(1)}) custom-call(bf16[256,512]{1,0:T(8,128)(2,1)S(1)} %bitcast.5, bf16[4,7168]{1,0:T(4,128)(2,1)S(1)} %copy-done.4, ...), custom_call_target="tpu_custom_call" | custom-call | flops 469762048 | bytes 7340032 | tf_op jit(solution)/shard_map/project/pallas_call | solution.py:228
  27.7 0.8 %collective-permute-done = bf16[8,7168]{1,0:T(8,128)(2,1)S(1)} collective-permute-done((bf16[8,7168]{1,0:T(8,128)(2,1)S(1)}, bf16[8,7168]{1,0:T(8,128)(2,1)S(1)}, u32[]{:S(2)}, u32[]{:S(2)}) %collective-permute-start) | collective-permute-done | bytes 114720 | tf_op jit(solution)/shard_map/ppermute | solution.py:298
  29.0 0.8 %collective-permute-start.3 = (bf16[8,7168]{1,0:T(8,128)(2,1)S(1)}, bf16[8,7168]{1,0:T(8,128)(2,1)S(1)}, u32[]{:S(2)}, u32[]{:S(2)}) collective-permute-start(bf16[8,7168]{1,0:T(8,128)(2,1)S(1)} %get-tuple-element.30), channel_id=1, source_target_pairs={{0,4},{1,5},{2,6},{3,7},{4,0},{5,1},{6,2},{7,3},{8,12},{9,13},{10,... | collective-permute-start | bytes 344072 | tf_op jit(solution)/shard_map/ppermute | solution.py:298
  29.9 2.3 %collective-permute-start.4 = (bf16[8,7168]{1,0:T(8,128)(2,1)S(1)}, bf16[8,7168]{1,0:T(8,128)(2,1)S(1)}, u32[]{:S(2)}, u32[]{:S(2)}) collective-permute-start(bf16[8,7168]{1,0:T(8,128)(2,1)S(1)} %get-tuple-element.31), channel_id=1, source_target_pairs={{0,6},{1,7},{2,4},{3,5},{4,2},{5,3},{6,0},{7,1},{8,14},{9,15},{10,... | collective-permute-start | bytes 344072 | tf_op jit(solution)/shard_map/ppermute | solution.py:298
  32.2 1.6 %collective-permute-done.1 = bf16[8,7168]{1,0:T(8,128)(2,1)S(1)} collective-permute-done((bf16[8,7168]{1,0:T(8,128)(2,1)S(1)}, bf16[8,7168]{1,0:T(8,128)(2,1)S(1)}, u32[]{:S(2)}, u32[]{:S(2)}) %collective-permute-start.1) | collective-permute-done | bytes 114720 | tf_op jit(solution)/shard_map/ppermute | solution.py:298
  33.8 1.3 %collective-permute-done.3 = bf16[8,7168]{1,0:T(8,128)(2,1)S(1)} collective-permute-done((bf16[8,7168]{1,0:T(8,128)(2,1)S(1)}, bf16[8,7168]{1,0:T(8,128)(2,1)S(1)}, u32[]{:S(2)}, u32[]{:S(2)}) %collective-permute-start.3) | collective-permute-done | bytes 114720 | tf_op jit(solution)/shard_map/ppermute | solution.py:298
  35.1 2.5 %collective-permute-done.4 = bf16[8,7168]{1,0:T(8,128)(2,1)S(1)} collective-permute-done((bf16[8,7168]{1,0:T(8,128)(2,1)S(1)}, bf16[8,7168]{1,0:T(8,128)(2,1)S(1)}, u32[]{:S(2)}, u32[]{:S(2)}) %collective-permute-start.4) | collective-permute-done | bytes 114720 | tf_op jit(solution)/shard_map/ppermute | solution.py:298
  37.6 1.1 %collective-permute-start.5 = (bf16[8,7168]{1,0:T(8,128)(2,1)S(1)}, bf16[8,7168]{1,0:T(8,128)(2,1)S(1)}, u32[]{:S(2)}, u32[]{:S(2)}) collective-permute-start(bf16[8,7168]{1,0:T(8,128)(2,1)S(1)} %fusion.2), channel_id=1, source_target_pairs={{0,8},{1,9},{2,10},{3,11},{4,12},{5,13},{6,14},{7,15},{8,0},{9,1},... | collective-permute-start | bytes 344072 | tf_op jit(solution)/shard_map/ppermute | solution.py:298
  38.8 6.3 %collective-permute-done.5 = bf16[8,7168]{1,0:T(8,128)(2,1)S(1)} collective-permute-done((bf16[8,7168]{1,0:T(8,128)(2,1)S(1)}, bf16[8,7168]{1,0:T(8,128)(2,1)S(1)}, u32[]{:S(2)}, u32[]{:S(2)}) %collective-permute-start.5) | collective-permute-done | bytes 114720 | tf_op jit(solution)/shard_map/ppermute | solution.py:298
  45.3 1.0 %collective-permute-start.6 = (bf16[8,7168]{1,0:T(8,128)(2,1)S(1)}, bf16[8,7168]{1,0:T(8,128)(2,1)S(1)}, u32[]{:S(2)}, u32[]{:S(2)}) collective-permute-start(bf16[8,7168]{1,0:T(8,128)(2,1)S(1)} %add_convert_fusion.3.refs_0_), channel_id=1, source_target_pairs={{0,2},{1,3},{2,0},{3,1},{4,6},{5,7},{6,4},{7,5},{8,10},{9,11},{10,... | collective-permute-start | bytes 344072 | tf_op jit(solution)/shard_map/ppermute | solution.py:298
  46.3 2.5 %collective-permute-start.8 = (bf16[8,7168]{1,0:T(8,128)(2,1)S(1)}, bf16[8,7168]{1,0:T(8,128)(2,1)S(1)}, u32[]{:S(2)}, u32[]{:S(2)}) collective-permute-start(bf16[8,7168]{1,0:T(8,128)(2,1)S(1)} %add_convert_fusion.3.refs_0_), channel_id=1, source_target_pairs={{0,6},{1,7},{2,4},{3,5},{4,2},{5,3},{6,0},{7,1},{8,14},{9,15},{10,... | collective-permute-start | bytes 344072 | tf_op jit(solution)/shard_map/ppermute | solution.py:298
  48.9 2.5 %collective-permute-done.6.refs_1_ = bf16[8,7168]{1,0:T(8,128)(2,1)S(1)} collective-permute-done((bf16[8,7168]{1,0:T(8,128)(2,1)S(1)}, bf16[8,7168]{1,0:T(8,128)(2,1)S(1)}, u32[]{:S(2)}, u32[]{:S(2)}) %collective-permute-start.6) | collective-permute-done | bytes 114720 | tf_op jit(solution)/shard_map/ppermute | solution.py:298
  51.9 1.5 %collective-permute-done.8.refs_3_ = bf16[8,7168]{1,0:T(8,128)(2,1)S(1)} collective-permute-done((bf16[8,7168]{1,0:T(8,128)(2,1)S(1)}, bf16[8,7168]{1,0:T(8,128)(2,1)S(1)}, u32[]{:S(2)}, u32[]{:S(2)}) %collective-permute-start.8) | collective-permute-done | bytes 114720 | tf_op jit(solution)/shard_map/ppermute | solution.py:298
  53.4 1.3 %collective-permute-done.12.refs_7_ = bf16[8,7168]{1,0:T(8,128)(2,1)S(1)} collective-permute-done((bf16[8,7168]{1,0:T(8,128)(2,1)S(1)}, bf16[8,7168]{1,0:T(8,128)(2,1)S(1)}, u32[]{:S(2)}, u32[]{:S(2)}) %collective-permute-start.12) | collective-permute-done | bytes 114720 | tf_op jit(solution)/shard_map/ppermute | solution.py:298
  54.7 2.3 %expert.1 = (f32[8,7168]{1,0:T(8,128)S(1)}, f32[8,7168]{1,0:T(8,128)S(1)}, f32[8,7168]{1,0:T(8,128)S(1)}, f32[8,7168]{1,0:T(8,128)S(1)}, bf16[8,7168]{1,0:T(8,128)(2,1)S(1)}, /*index=5*/bf16[24,7168]{1,0:T(8,128)(2,1)S(1)}) custom-call(bf16[8,7168]{1,0:T(8,128)(2,1)S(1)} %add_convert_fusion.3.refs_0_, bf16[8,7168]{1,0:T(8,128)(2,1)S(1)} %collective-permute-done.6.refs_1_, ...), custom_call_target="tpu_custom_call" | custom-call | flops 704643072 | bytes 11010048 | tf_op jit(solution)/shard_map/expert/pallas_call | solution.py:281
  57.7 0.8 %collective-permute-done.13 = bf16[8,7168]{1,0:T(8,128)(2,1)S(1)} collective-permute-done((bf16[8,7168]{1,0:T(8,128)(2,1)S(1)}, bf16[8,7168]{1,0:T(8,128)(2,1)S(1)}, u32[]{:S(2)}, u32[]{:S(2)}) %collective-permute-start.13) | collective-permute-done | bytes 114720 | tf_op jit(solution)/shard_map/ppermute | solution.py:298
  58.5 1.2 %collective-permute-start.14 = (bf16[8,7168]{1,0:T(8,128)(2,1)S(1)}, bf16[8,7168]{1,0:T(8,128)(2,1)S(1)}, u32[]{:S(2)}, u32[]{:S(2)}) collective-permute-start(bf16[8,7168]{1,0:T(8,128)(2,1)S(1)} %add_convert_fusion.2), channel_id=1, source_target_pairs={{0,2},{1,3},{2,0},{3,1},{4,6},{5,7},{6,4},{7,5},{8,10},{9,11},{10,... | collective-permute-start | bytes 344072 | tf_op jit(solution)/shard_map/ppermute | solution.py:298
  60.4 1.8 %collective-permute-start.17 = (bf16[8,7168]{1,0:T(8,128)(2,1)S(1)}, bf16[8,7168]{1,0:T(8,128)(2,1)S(1)}, u32[]{:S(2)}, u32[]{:S(2)}) collective-permute-start(bf16[8,7168]{1,0:T(8,128)(2,1)S(1)} %get-tuple-element.29), channel_id=1, source_target_pairs={{0,6},{1,7},{2,4},{3,5},{4,2},{5,3},{6,0},{7,1},{8,14},{9,15},{10,... | collective-permute-start | bytes 344072 | tf_op jit(solution)/shard_map/ppermute | solution.py:298
  62.9 0.9 %collective-permute-done.14 = bf16[8,7168]{1,0:T(8,128)(2,1)S(1)} collective-permute-done((bf16[8,7168]{1,0:T(8,128)(2,1)S(1)}, bf16[8,7168]{1,0:T(8,128)(2,1)S(1)}, u32[]{:S(2)}, u32[]{:S(2)}) %collective-permute-start.14) | collective-permute-done | bytes 114720 | tf_op jit(solution)/shard_map/ppermute | solution.py:298
  63.8 2.1 %collective-permute-done.16 = bf16[8,7168]{1,0:T(8,128)(2,1)S(1)} collective-permute-done((bf16[8,7168]{1,0:T(8,128)(2,1)S(1)}, bf16[8,7168]{1,0:T(8,128)(2,1)S(1)}, u32[]{:S(2)}, u32[]{:S(2)}) %collective-permute-start.16) | collective-permute-done | bytes 114720 | tf_op jit(solution)/shard_map/ppermute | solution.py:298
  65.9 1.7 %collective-permute-done.17 = bf16[8,7168]{1,0:T(8,128)(2,1)S(1)} collective-permute-done((bf16[8,7168]{1,0:T(8,128)(2,1)S(1)}, bf16[8,7168]{1,0:T(8,128)(2,1)S(1)}, u32[]{:S(2)}, u32[]{:S(2)}) %collective-permute-start.17) | collective-permute-done | bytes 114720 | tf_op jit(solution)/shard_map/ppermute | solution.py:298
  68.4 5.0 %collective-permute-done.18 = bf16[4,7168]{1,0:T(4,128)(2,1)S(1)} collective-permute-done((bf16[4,7168]{1,0:T(4,128)(2,1)S(1)}, bf16[4,7168]{1,0:T(4,128)(2,1)S(1)}, u32[]{:S(2)}, u32[]{:S(2)}) %collective-permute-start.18) | collective-permute-done | bytes 57376 | tf_op jit(solution)/shard_map/ppermute | solution.py:298
  (52 shorter events, 5.5 us)
Async XLA Ops:
  0.6 24.7 %slice-start = ((s8[7340032]{0:T(1024)(128)(4,1)}), s8[4194304]{0:T(1024)(128)(4,1)S(1)}, s32[]{:S(2)}) async-start(s8[7340032]{0:T(1024)(128)(4,1)} %bitcast.3), calls=%async_computation.1 | async-start | bytes 8388608
  25.3 29.4 %copy-start = (bf16[7168,256]{1,0:T(8,128)(2,1)S(1)}, bf16[7168,256]{1,0:T(8,128)(2,1)}, u32[]{:S(2)}) copy-start(bf16[7168,256]{1,0:T(8,128)(2,1)} %refs_9_.1) | copy-start | bytes 11010052
  25.4 29.3 %copy-start.1 = (bf16[7168,256]{1,0:T(8,128)(2,1)S(1)}, bf16[7168,256]{1,0:T(8,128)(2,1)}, u32[]{:S(2)}) copy-start(bf16[7168,256]{1,0:T(8,128)(2,1)} %refs_10_.1) | copy-start | bytes 11010052
  25.4 29.3 %copy-start.2 = (bf16[256,7168]{1,0:T(8,128)(2,1)S(1)}, bf16[256,7168]{1,0:T(8,128)(2,1)}, u32[]{:S(2)}) copy-start(bf16[256,7168]{1,0:T(8,128)(2,1)} %refs_11_.1) | copy-start | bytes 11010052
  25.4 29.3 %copy-start.5 = (f32[7168]{0:T(1024)S(1)}, f32[7168]{0:T(1024)}, u32[]{:S(2)}) copy-start(f32[7168]{0:T(1024)} %param.18) | copy-start | bytes 86020
  27.1 1.4 %collective-permute-start = (bf16[8,7168]{1,0:T(8,128)(2,1)S(1)}, bf16[8,7168]{1,0:T(8,128)(2,1)S(1)}, u32[]{:S(2)}, u32[]{:S(2)}) collective-permute-start(bf16[8,7168]{1,0:T(8,128)(2,1)S(1)} %get-tuple-element.15), channel_id=1, source_target_pairs={{0,1},{1,0},{2,3},{3,2},{4,5},{5,4},{6,7},{7,6},{8,9},{9,8},{10,11... | collective-permute-start | bytes 344072 | tf_op jit(solution)/shard_map/ppermute | solution.py:298
  27.2 1.8 %collective-permute-start.2 = (bf16[24,7168]{1,0:T(8,128)(2,1)S(1)}, bf16[24,7168]{1,0:T(8,128)(2,1)S(1)}, u32[]{:S(2)}, u32[]{:S(2)}) collective-permute-start(bf16[24,7168]{1,0:T(8,128)(2,1)S(1)} %get-tuple-element.17), channel_id=1, source_target_pairs={{0,1},{1,0},{2,3},{3,2},{4,5},{5,4},{6,7},{7,6},{8,9},{9,8},{10,11... | collective-permute-start | bytes 1032200 | tf_op jit(solution)/shard_map/ppermute | solution.py:298
  28.5 5.3 %collective-permute-start.1 = (bf16[8,7168]{1,0:T(8,128)(2,1)S(1)}, bf16[8,7168]{1,0:T(8,128)(2,1)S(1)}, u32[]{:S(2)}, u32[]{:S(2)}) collective-permute-start(bf16[8,7168]{1,0:T(8,128)(2,1)S(1)} %add_convert_fusion.6), channel_id=1, source_target_pairs={{0,2},{1,3},{2,0},{3,1},{4,6},{5,7},{6,4},{7,5},{8,10},{9,11},{10,... | collective-permute-start | bytes 344072 | tf_op jit(solution)/shard_map/ppermute | solution.py:298
  29.0 6.0 %collective-permute-start.3 = (bf16[8,7168]{1,0:T(8,128)(2,1)S(1)}, bf16[8,7168]{1,0:T(8,128)(2,1)S(1)}, u32[]{:S(2)}, u32[]{:S(2)}) collective-permute-start(bf16[8,7168]{1,0:T(8,128)(2,1)S(1)} %get-tuple-element.30), channel_id=1, source_target_pairs={{0,4},{1,5},{2,6},{3,7},{4,0},{5,1},{6,2},{7,3},{8,12},{9,13},{10,... | collective-permute-start | bytes 344072 | tf_op jit(solution)/shard_map/ppermute | solution.py:298
  29.9 7.7 %collective-permute-start.4 = (bf16[8,7168]{1,0:T(8,128)(2,1)S(1)}, bf16[8,7168]{1,0:T(8,128)(2,1)S(1)}, u32[]{:S(2)}, u32[]{:S(2)}) collective-permute-start(bf16[8,7168]{1,0:T(8,128)(2,1)S(1)} %get-tuple-element.31), channel_id=1, source_target_pairs={{0,6},{1,7},{2,4},{3,5},{4,2},{5,3},{6,0},{7,1},{8,14},{9,15},{10,... | collective-permute-start | bytes 344072 | tf_op jit(solution)/shard_map/ppermute | solution.py:298
  37.6 7.5 %collective-permute-start.5 = (bf16[8,7168]{1,0:T(8,128)(2,1)S(1)}, bf16[8,7168]{1,0:T(8,128)(2,1)S(1)}, u32[]{:S(2)}, u32[]{:S(2)}) collective-permute-start(bf16[8,7168]{1,0:T(8,128)(2,1)S(1)} %fusion.2), channel_id=1, source_target_pairs={{0,8},{1,9},{2,10},{3,11},{4,12},{5,13},{6,14},{7,15},{8,0},{9,1},... | collective-permute-start | bytes 344072 | tf_op jit(solution)/shard_map/ppermute | solution.py:298
  45.3 6.1 %collective-permute-start.6 = (bf16[8,7168]{1,0:T(8,128)(2,1)S(1)}, bf16[8,7168]{1,0:T(8,128)(2,1)S(1)}, u32[]{:S(2)}, u32[]{:S(2)}) collective-permute-start(bf16[8,7168]{1,0:T(8,128)(2,1)S(1)} %add_convert_fusion.3.refs_0_), channel_id=1, source_target_pairs={{0,2},{1,3},{2,0},{3,1},{4,6},{5,7},{6,4},{7,5},{8,10},{9,11},{10,... | collective-permute-start | bytes 344072 | tf_op jit(solution)/shard_map/ppermute | solution.py:298
  46.3 5.5 %collective-permute-start.7 = (bf16[8,7168]{1,0:T(8,128)(2,1)S(1)}, bf16[8,7168]{1,0:T(8,128)(2,1)S(1)}, u32[]{:S(2)}, u32[]{:S(2)}) collective-permute-start(bf16[8,7168]{1,0:T(8,128)(2,1)S(1)} %add_convert_fusion.3.refs_0_), channel_id=1, source_target_pairs={{0,4},{1,5},{2,6},{3,7},{4,0},{5,1},{6,2},{7,3},{8,12},{9,13},{10,... | collective-permute-start | bytes 344072 | tf_op jit(solution)/shard_map/ppermute | solution.py:298
  46.3 7.0 %collective-permute-start.8 = (bf16[8,7168]{1,0:T(8,128)(2,1)S(1)}, bf16[8,7168]{1,0:T(8,128)(2,1)S(1)}, u32[]{:S(2)}, u32[]{:S(2)}) collective-permute-start(bf16[8,7168]{1,0:T(8,128)(2,1)S(1)} %add_convert_fusion.3.refs_0_), channel_id=1, source_target_pairs={{0,6},{1,7},{2,4},{3,5},{4,2},{5,3},{6,0},{7,1},{8,14},{9,15},{10,... | collective-permute-start | bytes 344072 | tf_op jit(solution)/shard_map/ppermute | solution.py:298
  48.9 4.5 %collective-permute-start.9 = (bf16[8,7168]{1,0:T(8,128)(2,1)S(1)}, bf16[8,7168]{1,0:T(8,128)(2,1)S(1)}, u32[]{:S(2)}, u32[]{:S(2)}) collective-permute-start(bf16[8,7168]{1,0:T(8,128)(2,1)S(1)} %add_convert_fusion.3.refs_0_), channel_id=1, source_target_pairs={{0,1},{1,0},{2,3},{3,2},{4,5},{5,4},{6,7},{7,6},{8,9},{9,8},{10,11... | collective-permute-start | bytes 344072 | tf_op jit(solution)/shard_map/ppermute | solution.py:298
  51.4 2.0 %collective-permute-start.10 = (bf16[8,7168]{1,0:T(8,128)(2,1)S(1)}, bf16[8,7168]{1,0:T(8,128)(2,1)S(1)}, u32[]{:S(2)}, u32[]{:S(2)}) collective-permute-start(bf16[8,7168]{1,0:T(8,128)(2,1)S(1)} %collective-permute-done.6.refs_1_), channel_id=1, source_target_pairs={{0,1},{1,0},{2,3},{3,2},{4,5},{5,4},{6,7},{7,6},{8,9},{9,8},{10,11... | collective-permute-start | bytes 344072 | tf_op jit(solution)/shard_map/ppermute | solution.py:298
  51.9 1.5 %collective-permute-start.11 = (bf16[8,7168]{1,0:T(8,128)(2,1)S(1)}, bf16[8,7168]{1,0:T(8,128)(2,1)S(1)}, u32[]{:S(2)}, u32[]{:S(2)}) collective-permute-start(bf16[8,7168]{1,0:T(8,128)(2,1)S(1)} %collective-permute-done.7.refs_2_), channel_id=1, source_target_pairs={{0,1},{1,0},{2,3},{3,2},{4,5},{5,4},{6,7},{7,6},{8,9},{9,8},{10,11... | collective-permute-start | bytes 344072 | tf_op jit(solution)/shard_map/ppermute | solution.py:298
  53.4 1.3 %collective-permute-start.12 = (bf16[8,7168]{1,0:T(8,128)(2,1)S(1)}, bf16[8,7168]{1,0:T(8,128)(2,1)S(1)}, u32[]{:S(2)}, u32[]{:S(2)}) collective-permute-start(bf16[8,7168]{1,0:T(8,128)(2,1)S(1)} %collective-permute-done.8.refs_3_), channel_id=1, source_target_pairs={{0,1},{1,0},{2,3},{3,2},{4,5},{5,4},{6,7},{7,6},{8,9},{9,8},{10,11... | collective-permute-start | bytes 344072 | tf_op jit(solution)/shard_map/ppermute | solution.py:298
  57.1 1.4 %collective-permute-start.13 = (bf16[8,7168]{1,0:T(8,128)(2,1)S(1)}, bf16[8,7168]{1,0:T(8,128)(2,1)S(1)}, u32[]{:S(2)}, u32[]{:S(2)}) collective-permute-start(bf16[8,7168]{1,0:T(8,128)(2,1)S(1)} %get-tuple-element.21), channel_id=1, source_target_pairs={{0,1},{1,0},{2,3},{3,2},{4,5},{5,4},{6,7},{7,6},{8,9},{9,8},{10,11... | collective-permute-start | bytes 344072 | tf_op jit(solution)/shard_map/ppermute | solution.py:298
  57.3 2.5 %collective-permute-start.15 = (bf16[24,7168]{1,0:T(8,128)(2,1)S(1)}, bf16[24,7168]{1,0:T(8,128)(2,1)S(1)}, u32[]{:S(2)}, u32[]{:S(2)}) collective-permute-start(bf16[24,7168]{1,0:T(8,128)(2,1)S(1)} %get-tuple-element.23), channel_id=1, source_target_pairs={{0,1},{1,0},{2,3},{3,2},{4,5},{5,4},{6,7},{7,6},{8,9},{9,8},{10,11... | collective-permute-start | bytes 1032200 | tf_op jit(solution)/shard_map/ppermute | solution.py:298
  58.5 5.3 %collective-permute-start.14 = (bf16[8,7168]{1,0:T(8,128)(2,1)S(1)}, bf16[8,7168]{1,0:T(8,128)(2,1)S(1)}, u32[]{:S(2)}, u32[]{:S(2)}) collective-permute-start(bf16[8,7168]{1,0:T(8,128)(2,1)S(1)} %add_convert_fusion.2), channel_id=1, source_target_pairs={{0,2},{1,3},{2,0},{3,1},{4,6},{5,7},{6,4},{7,5},{8,10},{9,11},{10,... | collective-permute-start | bytes 344072 | tf_op jit(solution)/shard_map/ppermute | solution.py:298
  59.8 6.1 %collective-permute-start.16 = (bf16[8,7168]{1,0:T(8,128)(2,1)S(1)}, bf16[8,7168]{1,0:T(8,128)(2,1)S(1)}, u32[]{:S(2)}, u32[]{:S(2)}) collective-permute-start(bf16[8,7168]{1,0:T(8,128)(2,1)S(1)} %get-tuple-element.28), channel_id=1, source_target_pairs={{0,4},{1,5},{2,6},{3,7},{4,0},{5,1},{6,2},{7,3},{8,12},{9,13},{10,... | collective-permute-start | bytes 344072 | tf_op jit(solution)/shard_map/ppermute | solution.py:298
  60.4 7.1 %collective-permute-start.17 = (bf16[8,7168]{1,0:T(8,128)(2,1)S(1)}, bf16[8,7168]{1,0:T(8,128)(2,1)S(1)}, u32[]{:S(2)}, u32[]{:S(2)}) collective-permute-start(bf16[8,7168]{1,0:T(8,128)(2,1)S(1)} %get-tuple-element.29), channel_id=1, source_target_pairs={{0,6},{1,7},{2,4},{3,5},{4,2},{5,3},{6,0},{7,1},{8,14},{9,15},{10,... | collective-permute-start | bytes 344072 | tf_op jit(solution)/shard_map/ppermute | solution.py:298
  67.7 5.8 %collective-permute-start.18 = (bf16[4,7168]{1,0:T(4,128)(2,1)S(1)}, bf16[4,7168]{1,0:T(4,128)(2,1)S(1)}, u32[]{:S(2)}, u32[]{:S(2)}) collective-permute-start(bf16[4,7168]{1,0:T(4,128)(2,1)S(1)} %slice.68), channel_id=1, source_target_pairs={{0,8},{1,9},{2,10},{3,11},{4,12},{5,13},{6,14},{7,15},{8,0},{9,1},... | collective-permute-start | bytes 172040 | tf_op jit(solution)/shard_map/ppermute | solution.py:298
  (5 other events, 88.9 us)
